TPU v7x, 256 devices: a whole 4x4x8 slice. The times are simulated.
256 devices in a mesh: dom: 32 (over x, y, core), row: 8 (over z).
Axes of the slice: x: 4, y: 4, z: 8, core: 2. Of those that a mesh axis runs over, the one named last changes fastest.
Arguments:
- basis: float32 [16, 1048576], P(None, ('dom', 'row')), may hold values from -6 to 6
- previous: float32 [16, 1048576], P(None, ('dom', 'row')), may hold values from -3 to 3
- previous_image: float32 [16, 1048576], P(None, ('dom', 'row')), may hold values from -12 to 12
- degree: float32 [1048576], P(('dom', 'row')), may hold values from 1 to 8
- coupling: bfloat16 [65536, 128, 128], P(('dom', 'row')), may hold values from -0.1875 to 0.1875
- slot_row: int32 [65536], P(('dom', 'row')), may hold values from 0 to 31
- slot_column: int32 [65536], P(('dom', 'row')), may hold values from 0 to 511
- send_lists: int32 [32, 32, 8], P('dom'), may hold values from 0 to 255
- live_slots: int32 [256], P(('dom', 'row')), may hold values from 32 to 256, as said below
Outputs:
- new_basis: float32 [16, 1048576], P(None, ('dom', 'row'))
- new_image: float32 [16, 1048576], P(None, ('dom', 'row'))
Inputs may be any that keep to these rules, and one draw needn't show every extreme that they name: `live_slots`: each device has a block count; some device uses all 256 of its slots and some device uses 256 // 8.
All inputs are finite; a program needn't handle non-finite values. Where the computation divides by a largest or mean magnitude, that divisor is 1e-20 or more.
Results may differ from a plain program's by a relative error of at most 0.002.
Values may be sent and summed in bfloat16 or wider, within the bound.
No kernel may reach another device: no remote copies, remote signals or barrier semaphores. Data moves between devices by JAX's collectives and lax.ppermute only.
A program may use at most 64 MiB of HBM per device.

v0:
```python
import math

import jax
import jax.numpy as jnp
from jax import lax
from jax.sharding import PartitionSpec as P

K = 16
BS = 128
RB = 32


def apply_slots(lookup, coupling, slot_rows, slot_cols, live):
    picked = lookup[slot_cols]
    product = jnp.einsum("skc,sjc->skj", picked, coupling, preferred_element_type=jnp.float32)
    positions = jnp.arange(slot_rows.shape[0], dtype=jnp.int32)
    live_mask = positions < live
    onehot = (
        (slot_rows[None, :] == jnp.arange(RB, dtype=jnp.int32)[:, None]) & live_mask[None, :]
    ).astype(jnp.float32)
    return jnp.einsum(
        "rs,skj->rkj",
        onehot,
        product,
        precision=lax.Precision.HIGHEST,
        preferred_element_type=jnp.float32,
    )


def couple(field_half, coupling, slot_row, slot_column, send_lists, live_slots):
    tile_rows = field_half.reshape(K, RB, BS).transpose(1, 0, 2)
    own_part = lax.all_gather(tile_rows, "row", axis=0, tiled=True)
    selection = send_lists[0]
    incoming = lax.all_to_all(own_part[selection], "dom", split_axis=0, concat_axis=0, tiled=True)
    halo_tiles = incoming.reshape(-1, K, BS)
    lookup = jnp.concatenate([own_part, halo_tiles], axis=0)
    live = live_slots[0]
    result = apply_slots(lookup, coupling, slot_row, slot_column, live)
    return result.transpose(1, 0, 2).reshape(K, RB * BS)


def ritz(gram_a, gram_b, count):
    highest = lax.Precision.HIGHEST
    symmetric = 0.5 * (gram_a + gram_a.T)
    factor = jnp.linalg.cholesky(gram_b)
    partial_solve = lax.linalg.triangular_solve(factor, symmetric, left_side=True, lower=True)
    reduced = lax.linalg.triangular_solve(factor, partial_solve.T, left_side=True, lower=True)
    reduced = 0.5 * (reduced + reduced.T)
    spread = jnp.max(jnp.sum(jnp.abs(reduced), axis=1))
    dimension = reduced.shape[0]
    filter_mat = (spread * jnp.eye(dimension, dtype=jnp.float32) - reduced) / (2.0 * spread)
    subspace = jnp.eye(dimension, count, dtype=jnp.float32)
    for repeat in range(4):
        subspace = jnp.dot(
            filter_mat, subspace, precision=highest, preferred_element_type=jnp.float32
        )
    inner_gram = jnp.dot(
        subspace.T, subspace, precision=highest, preferred_element_type=jnp.float32
    )
    sub_factor = jnp.linalg.cholesky(inner_gram)
    orthonormal = lax.linalg.triangular_solve(sub_factor, subspace.T, left_side=True, lower=True).T
    return lax.linalg.triangular_solve(
        factor, orthonormal, left_side=True, lower=True, transpose_a=True
    )


def inner_rows(left, right):
    return jnp.dot(
        left, right.T, precision=lax.Precision.HIGHEST, preferred_element_type=jnp.float32
    )


def body(
    basis, previous, previous_image, degree, coupling, slot_row, slot_column, send_lists, live_slots
):
    highest = lax.Precision.HIGHEST
    image = degree * basis - couple(
        basis.astype(jnp.bfloat16), coupling, slot_row, slot_column, send_lists, live_slots
    )
    totals = lax.psum(
        (jnp.sum(basis * image, axis=1), jnp.sum(basis * basis, axis=1)), ("dom", "row")
    )
    theta = totals[0] / totals[1]
    residual = (image - theta[:, None] * basis) / degree
    residual_image = degree * residual - couple(
        residual.astype(jnp.bfloat16), coupling, slot_row, slot_column, send_lists, live_slots
    )
    stacked = jnp.concatenate([basis, residual, previous], axis=0)
    stacked_image = jnp.concatenate([image, residual_image, previous_image], axis=0)
    gram_b, gram_a = lax.psum(
        (inner_rows(stacked, stacked), inner_rows(stacked, stacked_image)), ("dom", "row")
    )
    coeff = ritz(gram_a, gram_b, basis.shape[0])
    root_rows = math.sqrt(basis.shape[1] * lax.axis_size("dom") * lax.axis_size("row"))
    new_basis = root_rows * jnp.dot(
        coeff.T, stacked, precision=highest, preferred_element_type=jnp.float32
    )
    new_image = root_rows * jnp.dot(
        coeff.T, stacked_image, precision=highest, preferred_element_type=jnp.float32
    )
    return (new_basis, new_image)


def solution(mesh):
    placed = (
        P(None, ("dom", "row")),
        P(None, ("dom", "row")),
        P(None, ("dom", "row")),
        P(("dom", "row")),
        P(("dom", "row"), None, None),
        P(("dom", "row")),
        P(("dom", "row")),
        P("dom", None, None),
        P(("dom", "row")),
    )
    return jax.shard_map(
        body,
        mesh=mesh,
        in_specs=placed,
        out_specs=(P(None, ("dom", "row")), P(None, ("dom", "row"))),
        check_vma=False,
    )
```

profile of v0, /device:TPU:1, one launch (start us, length us, event | category | flops | bytes accessed | tf_op | source)
XLA Modules:
  0.0 342.6 jit_solution(16421815786798126711)
XLA Ops:
  7.2 1.0 convert_bitcast_fusion.1
  8.2 0.7 copy.35
  8.9 0.7 compare_select_fusion
  9.8 38.0 %all-gather.3.cloned.1.call-done = bf16[256,16,128]{2,1,0:T(8,128)(2,1)} async-done(((bf16[32,16,128]{2,1,0:T(8,128)(2,1)}), bf16[256,16,128]{2,1,0:T(8,128)(2,1)}) %all-gather.3.cloned.1.call-update) | async-done | bytes 1048592 | tf_op jit(solution)/shard_map/all_gather | solution.py:32
  47.8 3.1 gather_fusion
  51.0 12.6 %all-to-all-start = ((bf16[32,8,16,128]{3,2,1,0:T(8,128)(2,1)}), bf16[32,8,16,128]{3,2,1,0:T(8,128)(2,1)S(1)}, u32[]{:S(2)}, u32[]{:S(2)}) async-start(bf16[32,8,16,128]{3,2,1,0:T(8,128)(2,1)} %bitcast.4), calls=%async_computation | async-start | bytes 2097152 | tf_op jit(solution)/shard_map/all_to_all | solution.py:34
  64.3 16.2 %all-to-all-done = bf16[32,8,16,128]{3,2,1,0:T(8,128)(2,1)S(1)} async-done(((bf16[32,8,16,128]{3,2,1,0:T(8,128)(2,1)}), bf16[32,8,16,128]{3,2,1,0:T(8,128)(2,1)S(1)}, u32[]{:S(2)}, u32[]{:S(2)}) %all-to-all-start) | async-done | bytes 1048608 | tf_op jit(solution)/shard_map/all_to_all | solution.py:34
  80.5 1.0 copy-done.3
  81.5 1.4 pad_maximum_fusion
  83.0 0.8 gather_fusion.1
  83.8 6.8 %fusion.35 = f32[256,16,128]{2,1,0:T(8,128)S(1)} fusion(bf16[256,16,128]{2,1,0:T(8,128)(2,1)S(1)} %gather_fusion.1, bf16[256,128,128]{2,1,0:T(8,128)(2,1)} %param.15), kind=kOutput, calls=%fused_computation.73 | convolution fusion | flops 134217728 | bytes 11534336 | tf_op jit(solution)/shard_map/skc,sjc->skj/dot_general | solution.py:15
  90.6 1.4 fusion.2
  92.3 73.5 %all-reduce.1 = (f32[16]{0:T(128)S(1)}, f32[16]{0:T(128)S(1)}) all-reduce(f32[16]{0:T(128)S(1)} %get-tuple-element.4, f32[16]{0:T(128)S(1)} %get-tuple-element.3), channel_id=1, replica_groups=mesh['dom'=32,'row'=8] {'dom','row'}, use_global_device_ids=true, to_apply=%region_1.0 | all-reduce | flops 32 | bytes 256 | tf_op jit(solution)/shard_map/psum | solution.py:80
  166.0 0.7 copy.40
  166.8 29.8 %all-gather.5.cloned.1.call-done = bf16[256,16,128]{2,1,0:T(8,128)(2,1)} async-done(((bf16[32,16,128]{2,1,0:T(8,128)(2,1)}), bf16[256,16,128]{2,1,0:T(8,128)(2,1)}) %all-gather.5.cloned.1.call-update) | async-done | bytes 1048592 | tf_op jit(solution)/shard_map/all_gather | solution.py:32
  196.6 3.0 gather_fusion.2
  199.6 12.8 %all-to-all-start.1 = ((bf16[32,8,16,128]{3,2,1,0:T(8,128)(2,1)}), bf16[32,8,16,128]{3,2,1,0:T(8,128)(2,1)S(1)}, u32[]{:S(2)}, u32[]{:S(2)}) async-start(bf16[32,8,16,128]{3,2,1,0:T(8,128)(2,1)} %bitcast.15), calls=%async_computation.1 | async-start | bytes 2097152 | tf_op jit(solution)/shard_map/all_to_all | solution.py:34
  212.4 0.8 fusion.5
  213.2 16.1 %all-to-all-done.1 = bf16[32,8,16,128]{3,2,1,0:T(8,128)(2,1)S(1)} async-done(((bf16[32,8,16,128]{3,2,1,0:T(8,128)(2,1)}), bf16[32,8,16,128]{3,2,1,0:T(8,128)(2,1)S(1)}, u32[]{:S(2)}, u32[]{:S(2)}) %all-to-all-start.1) | async-done | bytes 1048608 | tf_op jit(solution)/shard_map/all_to_all | solution.py:34
  229.3 1.0 copy-done.4
  230.3 1.4 pad_maximum_fusion.1
  231.7 0.8 gather_fusion.3
  232.6 6.8 %fusion.36 = f32[256,16,128]{2,1,0:T(8,128)S(1)} fusion(bf16[256,16,128]{2,1,0:T(8,128)(2,1)S(1)} %gather_fusion.3, bf16[256,128,128]{2,1,0:T(8,128)(2,1)} %param.15), kind=kOutput, calls=%fused_computation.74 | convolution fusion | flops 134217728 | bytes 11534336 | tf_op jit(solution)/shard_map/skc,sjc->skj/dot_general | solution.py:15
  239.4 1.4 fusion
  241.0 0.8 fusion.4
  241.8 74.1 %all-reduce = (f32[48,48]{0,1:T(8,128)S(1)}, f32[48,48]{0,1:T(8,128)S(1)}) all-reduce(f32[48,48]{0,1:T(8,128)S(1)} %fusion.4, f32[48,48]{0,1:T(8,128)S(1)} %fusion.5), channel_id=1, replica_groups=mesh['dom'=32,'row'=8] {'dom','row'}, use_global_device_ids=true, to_apply=%region_7.8 | all-reduce | flops 4608 | bytes 36864 | tf_op jit(solution)/shard_map/psum | solution.py:90
  316.0 4.4 %cholesky.30 = f32[48,48]{1,0:T(8,128)S(1)} custom-call(f32[48,48]{1,0:T(8,128)S(1)} %fusion.19), custom_call_target="Cholesky" | custom-call | tf_op jit(solution)/shard_map/jit(cholesky)/cholesky | solution.py:45
  321.7 3.7 %custom-call.15 = f32[1,48,48]{1,2,0:T(8,128)S(1)} custom-call(f32[1,48,48]{2,1,0:T(8,128)S(1)} %fusion.10), custom_call_target="InvertDiagBlocksLowerTriangular" | custom-call | tf_op jit(solution)/shard_map/triangular_solve | solution.py:62
  329.0 1.5 cholesky.63
  331.8 1.2 custom-call.16
  333.4 1.2 convolution_multiply_fusion
  334.6 1.2 convolution_multiply_fusion.1
  (68 shorter events, 7.0 us)
Async XLA Ops:
  7.2 40.7 %all-gather.3.cloned.1.call-start = ((), (), s32[]{:S(2)}) async-start(), calls=%async_computation.2 | async-start | bytes 1179648 | tf_op jit(solution)/shard_map/all_gather | solution.py:32
  9.8 54.5 %copy-start.14 = (s32[256]{0:T(256)S(1)}, s32[256]{0:T(256)}, u32[]{:S(2)}) copy-start(s32[256]{0:T(256)} %param.17) | copy-start | bytes 3076
  47.8 33.7 %copy-start.1 = (bf16[256,16,128]{2,1,0:T(8,128)(2,1)S(1)}, bf16[256,16,128]{2,1,0:T(8,128)(2,1)}, u32[]{:S(2)}) copy-start(bf16[256,16,128]{2,1,0:T(8,128)(2,1)} %all-gather.3.cloned.1.call-done) | copy-start | bytes 3145732
  51.0 29.6 %all-to-all-start = ((bf16[32,8,16,128]{3,2,1,0:T(8,128)(2,1)}), bf16[32,8,16,128]{3,2,1,0:T(8,128)(2,1)S(1)}, u32[]{:S(2)}, u32[]{:S(2)}) async-start(bf16[32,8,16,128]{3,2,1,0:T(8,128)(2,1)} %bitcast.4), calls=%async_computation | async-start | bytes 2097152 | tf_op jit(solution)/shard_map/all_to_all | solution.py:34
  63.6 133.0 %all-gather.5.cloned.1.call-start = ((), (), s32[]{:S(2)}) async-start(), calls=%async_computation.3 | async-start | bytes 1179648 | tf_op jit(solution)/shard_map/all_gather | solution.py:32
  80.5 1.0 copy-start.3
  83.8 6.8 %copy-start.13 = (s32[256]{0:T(256)S(1)}, s32[256]{0:T(256)}, u32[]{:S(2)}) copy-start(s32[256]{0:T(256)} %param.16) | copy-start | bytes 3076
  90.6 1.4 copy-start
  90.6 1.5 copy-start.12
  92.3 104.2 %copy-start.7 = (f32[16,4096]{1,0:T(8,128)}, f32[16,4096]{1,0:T(8,128)S(1)}, u32[]{:S(2)}) copy-start(f32[16,4096]{1,0:T(8,128)S(1)} %get-tuple-element.11) | copy-start | bytes 786436
  165.9 46.4 %copy-start.5 = (f32[16,4096]{1,0:T(8,128)}, f32[16,4096]{1,0:T(8,128)S(1)}, u32[]{:S(2)}) copy-start(f32[16,4096]{1,0:T(8,128)S(1)} %get-tuple-element.10) | copy-start | bytes 786436
  166.7 45.6 %copy-start.10 = (f32[16,4096]{1,0:T(8,128)S(1)}, f32[16,4096]{1,0:T(8,128)}, u32[]{:S(2)}) copy-start(f32[16,4096]{1,0:T(8,128)} %param.12) | copy-start | bytes 786436
  199.6 30.7 %copy-start.2 = (bf16[256,16,128]{2,1,0:T(8,128)(2,1)S(1)}, bf16[256,16,128]{2,1,0:T(8,128)(2,1)}, u32[]{:S(2)}) copy-start(bf16[256,16,128]{2,1,0:T(8,128)(2,1)} %all-gather.5.cloned.1.call-done) | copy-start | bytes 3145732
  199.6 29.7 %all-to-all-start.1 = ((bf16[32,8,16,128]{3,2,1,0:T(8,128)(2,1)}), bf16[32,8,16,128]{3,2,1,0:T(8,128)(2,1)S(1)}, u32[]{:S(2)}, u32[]{:S(2)}) async-start(bf16[32,8,16,128]{3,2,1,0:T(8,128)(2,1)} %bitcast.15), calls=%async_computation.1 | async-start | bytes 2097152 | tf_op jit(solution)/shard_map/all_to_all | solution.py:34
  229.3 1.0 copy-start.4
  239.3 1.5 copy-start.6
  239.3 1.6 copy-start.8
  239.3 1.6 copy-start.9
  239.4 1.6 copy-start.11
Sparse Core Ops, SparseCore 0:
  10.4 37.4 all-gather.2
  166.9 29.6 all-gather.4
where the time goes:
time: 343 us
  blocking collectives  148 us (43%)
  waiting for transfers between devices  100 us (29%)
  starting transfers between devices  25.5 us (7%)
  matrix products  21.9 us (6%)
  other arithmetic  19.9 us (6%)
  between operations  15.7 us (5%)
  local copies, waits for them, and re-layouts  12 us (3%)
    psum x1, blocking collectives, body(): lax.psum((inner_rows(stacked, stacked), inner_rows(stacked, stacked_image...  74.1 us
    psum x1, blocking collectives, body(): lax.psum((jnp.sum(basis * image, axis=1), jnp.sum(basis * basis, axis=1))...  73.5 us
    all_gather x2, waiting for transfers between devices, couple(): own_part = lax.all_gather(tile_rows, 'row', axis=0, tiled=True)  67.8 us
    all_to_all x2, waiting for transfers between devices, couple(): lax.all_to_all(own_part[selection], 'dom', split_axis=0, concat_axis=0, t...  32.3 us
    all_to_all x2, starting transfers between devices, couple(): lax.all_to_all(own_part[selection], 'dom', split_axis=0, concat_axis=0, t...  25.4 us
    dot_general x2, matrix products, apply_slots(): jnp.einsum('skc,sjc->skj', picked, coupling, preferred_element_type=jnp.f...  13.5 us
  transfers between devices with their start and end apart: 4, of which 4 were waited for; matrix products, arithmetic and copies ran while one was open for 0% of the time, Pallas kernels for 0%

commit v1 on v0

v1 whole, which is shorter than its diff:
```python
import functools
import math

import jax
import jax.numpy as jnp
from jax import lax
from jax.experimental import pallas as pl
from jax.experimental.pallas import tpu as pltpu
from jax.sharding import PartitionSpec as P

K = 16
BS = 128
RB = 32
SLOTS = 256
SEND = 8
LEN = SLOTS + 8
F32 = jnp.float32
BF16 = jnp.bfloat16
HIGHEST = lax.Precision.HIGHEST
VMEM_LIMIT = 48 * 1024 * 1024
SMEM = pl.BlockSpec(memory_space=pltpu.SMEM)
HBM = pl.BlockSpec(memory_space=pl.ANY)
VMEM = pl.BlockSpec(memory_space=pltpu.VMEM)


def call(kernel, out_shape, in_specs, out_specs, scratch=(), flops=0, moved=0):
    return pl.pallas_call(
        kernel,
        out_shape=out_shape,
        in_specs=in_specs,
        out_specs=out_specs,
        scratch_shapes=scratch,
        compiler_params=pltpu.CompilerParams(vmem_limit_bytes=VMEM_LIMIT),
        cost_estimate=pl.CostEstimate(flops=flops, bytes_accessed=moved, transcendentals=0),
    )


def shaped(shape, dtype):
    return jax.ShapeDtypeStruct(shape, dtype)


def dot_nt(left, right, precision=None):
    return lax.dot_general(
        left, right, (((1,), (1,)), ((), ())), precision=precision, preferred_element_type=F32
    )


def dot_nn(left, right, precision=None):
    return lax.dot_general(
        left, right, (((1,), (0,)), ((), ())), precision=precision, preferred_element_type=F32
    )


def columns(block):
    return slice(block * BS, (block + 1) * BS)


def list_kernel(part, row_ref, column_ref, live_ref, own_ref, halo_ref, count_ref):
    live = live_ref[0]

    def step(slot, counts):
        n_own, n_halo = counts
        column = column_ref[slot]
        row = row_ref[slot]
        own_ref[0, n_own] = slot
        own_ref[1, n_own] = column
        own_ref[2, n_own] = row
        halo_ref[0, n_halo] = slot
        halo_ref[1, n_halo] = column - part
        halo_ref[2, n_halo] = row
        used = slot < live
        is_own = column < part
        n_own = n_own + jnp.where(used & is_own, 1, 0)
        n_halo = n_halo + jnp.where(used & (column >= part), 1, 0)
        return n_own, n_halo

    n_own, n_halo = lax.fori_loop(0, SLOTS, step, (jnp.int32(0), jnp.int32(0)))
    for ref, count in ((own_ref, n_own), (halo_ref, n_halo)):
        for extra in range(8):
            ref[0, count + extra] = 0
            ref[1, count + extra] = 0
            ref[2, count + extra] = RB
    count_ref[0] = n_own
    count_ref[1] = n_halo


def make_lists(slot_row, slot_column, live_slots, part):
    return call(
        functools.partial(list_kernel, part),
        (shaped((3, LEN), jnp.int32), shaped((3, LEN), jnp.int32), shaped((2,), jnp.int32)),
        [SMEM, SMEM, SMEM],
        (SMEM, SMEM, SMEM),
        moved=20000,
    )(slot_row, slot_column, live_slots)


def cast_kernel(field_ref, tiles_ref):
    for block in range(RB):
        tiles_ref[block] = field_ref[:, columns(block)].astype(BF16)


def cast_tiles(field):
    return call(cast_kernel, shaped((RB, K, BS), BF16), [VMEM], VMEM, moved=400000)(field)


def gather_row(tiles, n_row):
    up = [(i, (i + 1) % n_row) for i in range(n_row)]
    down = [(i, (i - 1) % n_row) for i in range(n_row)]
    pieces = [(0, tiles)]
    from_below = from_above = tiles
    for step in range(1, n_row // 2):
        from_below = lax.ppermute(from_below, "row", up)
        from_above = lax.ppermute(from_above, "row", down)
        pieces += [(-step, from_below), (step, from_above)]
    half = RB // 2
    far_low = lax.ppermute(from_below[:half], "row", up)
    far_high = lax.ppermute(from_above[half:], "row", down)
    return pieces, far_low, far_high


def select_kernel(offsets, n_row, place_ref, send_ref, *refs):
    pieces, (far_low, far_high, part_ref, chosen_ref) = refs[: len(offsets)], refs[len(offsets) :]
    place = place_ref[0]
    half = RB // 2
    for offset, piece in zip(offsets, pieces):
        owner = lax.rem(place + offset + n_row, n_row)
        part_ref[pl.ds(owner * RB, RB)] = piece[...]
    owner = lax.rem(place + n_row // 2, n_row)
    part_ref[pl.ds(owner * RB, half)] = far_low[...]
    part_ref[pl.ds(owner * RB + half, half)] = far_high[...]

    def step(group, carry):
        for j in range(8):
            chosen_ref[group * 8 + j] = part_ref[send_ref[group * 8 + j]]
        return carry

    lax.fori_loop(0, chosen_ref.shape[0] // 8, step, 0)


def select(gathered, place, send_list, n_row):
    pieces, far_low, far_high = gathered
    offsets = [offset for offset, _ in pieces]
    count = send_list.shape[0]
    return call(
        functools.partial(select_kernel, offsets, n_row),
        (shaped((n_row * RB, K, BS), BF16), shaped((count, K, BS), BF16)),
        [SMEM, SMEM] + [VMEM] * (len(pieces) + 2),
        (VMEM, VMEM),
        moved=3000000,
    )(place, send_list, *[piece for _, piece in pieces], far_low, far_high)


def apply_list(count, list_ref, lookup_ref, coupling_ref, held, sems, acc_ref):
    groups = lax.div(count + 7, 8)

    def issue(group, carry):
        for j in range(8):
            at = group * 8 + j
            pltpu.make_async_copy(
                coupling_ref.at[list_ref[0, at]], held.at[at], sems.at[group]
            ).start()
        return carry

    lax.fori_loop(0, groups, issue, 0)

    def work(group, carry):
        base = group * 8
        pltpu.make_async_copy(
            coupling_ref.at[pl.ds(0, 8)], held.at[pl.ds(base, 8)], sems.at[group]
        ).wait()
        products = [
            dot_nt(lookup_ref[list_ref[1, base + j]], held[base + j]) for j in range(8)
        ]
        for j in range(8):
            row = list_ref[2, base + j]
            acc_ref[row] = acc_ref[row] + products[j]
        return carry

    lax.fori_loop(0, groups, work, 0)


HELD = (pltpu.VMEM((SLOTS, BS, BS), BF16), pltpu.SemaphoreType.DMA((SLOTS // 8,)))


def own_kernel(list_ref, count_ref, lookup_ref, coupling_ref, acc_ref, held, sems):
    acc_ref[...] = jnp.zeros_like(acc_ref)
    apply_list(count_ref[0], list_ref, lookup_ref, coupling_ref, held, sems, acc_ref)


def couple_own(own_list, counts, part_tiles, coupling):
    return call(
        own_kernel,
        shaped((RB + 1, K, BS), F32),
        [SMEM, SMEM, VMEM, HBM],
        VMEM,
        HELD,
        flops=2 * SLOTS * K * BS * BS,
        moved=8000000,
    )(own_list, counts, part_tiles, coupling)


def image_kernel(
    list_ref, count_ref, lookup_ref, coupling_ref, own_ref, basis_ref, degree_ref,
    image_ref, sums_ref, acc_ref, held, sems,
):
    acc_ref[...] = own_ref[...]
    apply_list(count_ref[1], list_ref, lookup_ref, coupling_ref, held, sems, acc_ref)
    top = jnp.zeros((K, BS), F32)
    bottom = jnp.zeros((K, BS), F32)
    for block in range(RB):
        at = columns(block)
        basis = basis_ref[:, at]
        image = degree_ref[:, at] * basis - acc_ref[block]
        image_ref[:, at] = image
        top = top + basis * image
        bottom = bottom + basis * basis
    lane = lax.broadcasted_iota(jnp.int32, (K, BS), 1)
    sums = jnp.where(
        lane == 0, jnp.sum(top, axis=1, keepdims=True), jnp.sum(bottom, axis=1, keepdims=True)
    )
    for peer in range(sums_ref.shape[0]):
        sums_ref[peer] = sums


def make_image(halo_list, counts, halo_tiles, coupling, own, basis, degree, n_dom):
    return call(
        image_kernel,
        (shaped(basis.shape, F32), shaped((n_dom, K, BS), F32)),
        [SMEM, SMEM, VMEM, HBM, VMEM, VMEM, VMEM],
        (VMEM, VMEM),
        (pltpu.VMEM((RB + 1, K, BS), F32),) + HELD,
        flops=2 * SLOTS * K * BS * BS,
        moved=8000000,
    )(halo_list, counts, halo_tiles, coupling, own, basis, degree)


def spread_kernel(taken_ref, given_ref):
    total = taken_ref[0]
    for peer in range(1, taken_ref.shape[0]):
        total = total + taken_ref[peer]
    for peer in range(given_ref.shape[0]):
        given_ref[peer] = total


def add_and_repeat(taken, peers):
    return call(
        spread_kernel, shaped((peers,) + taken.shape[1:], F32), [VMEM], VMEM, moved=400000
    )(taken)


def residual_kernel(sums_ref, basis_ref, image_ref, degree_ref, residual_ref, tiles_ref):
    sums = sums_ref[0]
    for peer in range(1, sums_ref.shape[0]):
        sums = sums + sums_ref[peer]
    theta = sums[:, 0:1] / sums[:, 1:2]
    for block in range(RB):
        at = columns(block)
        residual = (image_ref[:, at] - theta * basis_ref[:, at]) / degree_ref[:, at]
        residual_ref[:, at] = residual
        tiles_ref[block] = residual.astype(BF16)


def make_residual(sums, basis, image, degree):
    return call(
        residual_kernel,
        (shaped(basis.shape, F32), shaped((RB, K, BS), BF16)),
        [VMEM] * 4,
        (VMEM, VMEM),
        moved=1000000,
    )(sums, basis, image, degree)


def iota2(shape, axis):
    return lax.broadcasted_iota(jnp.int32, shape, axis)


def square(value, wide_ref):
    rows, cols = value.shape
    wide_ref[...] = jnp.zeros_like(wide_ref)
    wide_ref[0:rows, 0:cols] = value
    return wide_ref[...]


def pack_grams(gram_b, gram_a, wide_ref):
    wide_a = square(gram_a, wide_ref)
    both = 0.5 * (wide_a + wide_a.T)
    wide_b = square(gram_b, wide_ref)
    row = iota2((BS, BS), 0)
    lane = iota2((BS, BS), 1)
    packed = jnp.where(row <= lane, wide_b, both)
    diagonal = jnp.sum(jnp.where(row == lane, both, 0.0), axis=1, keepdims=True)
    low, high = packed[0:24], pltpu.roll(packed[24:48], 48, 1)
    at = iota2((24, BS), 1)
    out = jnp.where(at < 48, low, high)
    out = jnp.where(at == 96, diagonal[0:24], out)
    return jnp.where(at == 97, diagonal[24:48], out)


def unpack_grams(packed, wide_ref):
    wide_ref[...] = jnp.zeros_like(wide_ref)
    at = iota2((24, BS), 1)
    wide_ref[0:24] = jnp.where(at < 48, packed, 0.0)
    wide_ref[24:48] = jnp.where(at < 48, pltpu.roll(packed, 80, 1), 0.0)
    wide = wide_ref[...]
    flipped = wide.T
    row = iota2((48, BS), 0)
    lane = iota2((48, BS), 1)
    wide, flipped = wide[0:48], flipped[0:48]
    diagonal = jnp.concatenate([packed[:, 96:97], packed[:, 97:98]], axis=0)
    gram_b = jnp.where(row <= lane, wide, flipped)
    gram_a = jnp.where(row == lane, diagonal, jnp.where(row > lane, wide, flipped))
    return gram_b, gram_a


def gram_kernel(
    list_ref, count_ref, lookup_ref, coupling_ref, own_ref, basis_ref, image_ref, residual_ref, degree_ref,
    previous_ref, previous_image_ref, residual_image_ref, packed_ref, acc_ref, held, sems, stacked, stacked_image,
    wide_ref,
):
    acc_ref[...] = own_ref[...]
    apply_list(count_ref[1], list_ref, lookup_ref, coupling_ref, held, sems, acc_ref)
    stacked[0:16] = basis_ref[...]
    stacked[16:32] = residual_ref[...]
    stacked[32:48] = previous_ref[...]
    stacked_image[0:16] = image_ref[...]
    stacked_image[32:48] = previous_image_ref[...]
    for block in range(RB):
        at = columns(block)
        value = degree_ref[:, at] * residual_ref[:, at] - acc_ref[block]
        residual_image_ref[:, at] = value
        stacked_image[16:32, at] = value
    gram_b = dot_nt(stacked[...], stacked[...], HIGHEST)
    gram_a = dot_nt(stacked[...], stacked_image[...], HIGHEST)
    packed = pack_grams(gram_b, gram_a, wide_ref)
    for peer in range(packed_ref.shape[0]):
        packed_ref[peer] = packed


def make_grams(
    halo_list, counts, halo_tiles, coupling, own, basis, image, residual, degree, previous, previous_image, n_dom
):
    width = basis.shape[1]
    return call(
        gram_kernel,
        (shaped(basis.shape, F32), shaped((n_dom, 24, BS), F32)),
        [SMEM, SMEM, VMEM, HBM] + [VMEM] * 7,
        (VMEM, VMEM),
        (pltpu.VMEM((RB + 1, K, BS), F32),)
        + HELD
        + (pltpu.VMEM((48, width), F32), pltpu.VMEM((48, width), F32), pltpu.VMEM((BS, BS), F32)),
        flops=2 * SLOTS * K * BS * BS,
        moved=10000000,
    )(halo_list, counts, halo_tiles, coupling, own, basis, image, residual, degree, previous, previous_image)


def inverse_factor(gram, n):
    row = iota2((n, BS), 0)
    lane = iota2((n, BS), 1)
    work = jnp.where(lane < n, gram, jnp.where(lane == row + n, 1.0, 0.0))
    for j in range(n):
        column = work[:, j : j + 1]
        pivot = work[j : j + 1, :]
        scale = lax.rsqrt(work[j : j + 1, j : j + 1])
        scaled = pivot * scale
        below = jnp.where(row[:, 0:1] > j, column * scale, 0.0)
        work = jnp.where(row == j, scaled, work - below * scaled)
    return pltpu.roll(work, BS - n, 1)


def final_kernel(
    root_rows, taken_ref, basis_ref, residual_ref, previous_ref, image_ref, residual_image_ref, previous_image_ref,
    new_basis_ref, new_image_ref, wide_ref, stacked,
):
    packed = taken_ref[0]
    for peer in range(1, taken_ref.shape[0]):
        packed = packed + taken_ref[peer]
    gram_b, gram_a = unpack_grams(packed, wide_ref)
    inverse = inverse_factor(gram_b, 48)[:, 0:48]
    symmetric = gram_a[:, 0:48]
    reduced = dot_nt(dot_nn(inverse, symmetric, HIGHEST), inverse, HIGHEST)
    wide = square(reduced, wide_ref)
    reduced = 0.5 * (wide + wide.T)[0:48, 0:48]
    spread = jnp.max(jnp.sum(jnp.abs(reduced), axis=1, keepdims=True), axis=0, keepdims=True)
    row = iota2((48, 48), 0)
    lane = iota2((48, 48), 1)
    filter_mat = (jnp.where(row == lane, spread, 0.0) - reduced) / (2.0 * spread)
    subspace = filter_mat[:, 0:16]
    for repeat in range(3):
        subspace = dot_nn(filter_mat, subspace, HIGHEST)
    wide_ref[...] = jnp.zeros_like(wide_ref)
    wide_ref[0:48, 0:16] = subspace
    turned = wide_ref[...].T[0:16, 0:48]
    inner = dot_nt(turned, turned, HIGHEST)
    wide_ref[...] = jnp.zeros_like(wide_ref)
    wide_ref[0:16, 0:16] = inner
    sub_inverse = inverse_factor(wide_ref[0:16, :], 16)[:, 0:16]
    coeff = dot_nn(dot_nn(sub_inverse, turned, HIGHEST), inverse, HIGHEST) * root_rows
    stacked[0:16] = basis_ref[...]
    stacked[16:32] = residual_ref[...]
    stacked[32:48] = previous_ref[...]
    new_basis_ref[...] = dot_nn(coeff, stacked[...], HIGHEST)
    stacked[0:16] = image_ref[...]
    stacked[16:32] = residual_image_ref[...]
    stacked[32:48] = previous_image_ref[...]
    new_image_ref[...] = dot_nn(coeff, stacked[...], HIGHEST)


def finish(root_rows, packed, basis, residual, previous, image, residual_image, previous_image):
    return call(
        functools.partial(final_kernel, root_rows),
        (shaped(basis.shape, F32), shaped(basis.shape, F32)),
        [VMEM] * 7,
        (VMEM, VMEM),
        (pltpu.VMEM((BS, BS), F32), pltpu.VMEM((48, basis.shape[1]), F32)),
        flops=1000000,
        moved=3000000,
    )(packed, basis, residual, previous, image, residual_image, previous_image)


def to_all(value, axis):
    return lax.all_to_all(value, axis, split_axis=0, concat_axis=0, tiled=True)


def body(
    n_dom, n_row,
    basis, previous, previous_image, degree, coupling, slot_row, slot_column, send_lists, live_slots,
):
    part = n_row * RB
    place = lax.axis_index("row").astype(jnp.int32).reshape(1)
    send_list = send_lists.reshape(n_dom * SEND)
    degree = degree.reshape(1, -1)
    own_list, halo_list, counts = make_lists(slot_row, slot_column, live_slots, part)

    part_tiles, chosen = select(gather_row(cast_tiles(basis), n_row), place, send_list, n_row)
    halo_tiles = to_all(chosen, "dom")
    own = couple_own(own_list, counts, part_tiles, coupling)
    image, sums = make_image(halo_list, counts, halo_tiles, coupling, own, basis, degree, n_dom)
    sums = to_all(add_and_repeat(to_all(sums, "dom"), n_row), "row")
    residual, tiles = make_residual(sums, basis, image, degree)

    part_tiles, chosen = select(gather_row(tiles, n_row), place, send_list, n_row)
    halo_tiles = to_all(chosen, "dom")
    own = couple_own(own_list, counts, part_tiles, coupling)
    residual_image, packed = make_grams(
        halo_list, counts, halo_tiles, coupling, own, basis, image, residual, degree, previous, previous_image, n_dom
    )
    packed = to_all(add_and_repeat(to_all(packed, "dom"), n_row), "row")
    root_rows = math.sqrt(basis.shape[1] * n_dom * n_row)
    return finish(root_rows, packed, basis, residual, previous, image, residual_image, previous_image)


def solution(mesh):
    split = P(None, ("dom", "row"))
    flat = P(("dom", "row"))
    return jax.shard_map(
        functools.partial(body, mesh.shape["dom"], mesh.shape["row"]),
        mesh=mesh,
        in_specs=(
            split, split, split, flat, P(("dom", "row"), None, None), flat, flat, P("dom", None, None), flat,
        ),
        out_specs=(split, split),
        check_vma=False,
    )
```

time: 343 us -> 182 us (0.53)
  blocking collectives: 148 us -> 54.9 us
  waiting for transfers between devices: 100 us -> 36.9 us
  Pallas kernels: 0 us -> 33.5 us
  matrix products: 21.9 us -> 0 us
  starting transfers between devices: 25.5 us -> 47 us
  other arithmetic: 19.9 us -> 0 us
  between operations: 15.7 us -> 1.49 us
  local copies, waits for them, and re-layouts: 12 us -> 6.08 us
    psum x2 -> x0, blocking collectives: 148 us -> none  [the longest x1 74.1 us: body(): lax.psum((inner_rows(stacked, stacked), inner_rows(stacked, stacked_image...]
    all_gather x2 -> x0, waiting for transfers between devices: 67.8 us -> none  [couple(): own_part = lax.all_gather(tile_rows, 'row', axis=0, tiled=True)]
    all_to_all x0 -> x4, blocking collectives: none -> 54.9 us  [to_all(): return lax.all_to_all(value, axis, split_axis=0, concat_axis=0, tiled=True)]
    pallas_call x0 -> x12, Pallas kernels: none -> 33.5 us  [the longest x1 8.67 us: finish(): call(functools.partial(final_kernel, root_rows), (shaped(basis.shape, F32...]
    ppermute x0 -> x16, starting transfers between devices: none -> 25.5 us  [the longest x6 17.1 us: gather_row(): from_above = lax.ppermute(from_above, 'row', down)]
    dot_general x13 -> x0, matrix products: 21.1 us -> none  [the longest x2 13.5 us: apply_slots(): jnp.einsum('skc,sjc->skj', picked, coupling, preferred_element_type=jnp.f...]
    ppermute x0 -> x16, waiting for transfers between devices: none -> 18.1 us  [the longest x6 14.9 us: gather_row(): from_below = lax.ppermute(from_below, 'row', up)]
    all_to_all x2, waiting for transfers between devices: 32.3 us -> 18.8 us  [to_all(): return lax.all_to_all(value, axis, split_axis=0, concat_axis=0, tiled=True)]
  transfers between devices with their start and end apart: 4 -> 18, of which waited for: 4 -> 10; matrix products, arithmetic and copies ran while one was open for 0% -> 0% of each run, Pallas kernels for 0% -> 7%
where the time goes in v1:
time: 182 us; the launch traced here: 180 us
  blocking collectives  54.9 us (30%)
  starting transfers between devices  47 us (26%)
  waiting for transfers between devices  36.9 us (20%)
  Pallas kernels  33.5 us (18%)
  local copies, waits for them, and re-layouts  6.08 us (3%)
    all_to_all x4, blocking collectives, to_all(): return lax.all_to_all(value, axis, split_axis=0, concat_axis=0, tiled=True)  54.9 us
    all_to_all x2, starting transfers between devices, to_all(): return lax.all_to_all(value, axis, split_axis=0, concat_axis=0, tiled=True)  21.5 us
    all_to_all x2, waiting for transfers between devices, to_all(): return lax.all_to_all(value, axis, split_axis=0, concat_axis=0, tiled=True)  18.8 us
    ppermute x6, starting transfers between devices, gather_row(): from_above = lax.ppermute(from_above, 'row', down)  17.1 us
    ppermute x6, waiting for transfers between devices, gather_row(): from_below = lax.ppermute(from_below, 'row', up)  14.9 us
    pallas_call x1, Pallas kernels, finish(): call(functools.partial(final_kernel, root_rows), (shaped(basis.shape, F32...  8.67 us
    pallas_call x2, Pallas kernels, couple_own(): call(own_kernel, shaped((RB + 1, K, BS), F32), [SMEM, SMEM, VMEM, HBM], V...  8.25 us
    unnamed x25, local copies, waits for them, and re-layouts  5.97 us
  transfers between devices with their start and end apart: 18, of which 10 were waited for; matrix products, arithmetic and copies ran while one was open for 0% of the time, Pallas kernels for 7%

profile of v1, /device:TPU:1, one launch (start us, length us, event | category | flops | bytes accessed | tf_op | source)
XLA Modules:
  0.0 179.9 jit_solution(17676835726351369785)
XLA Ops:
  1.6 2.5 %collective-permute-start = (bf16[32,16,128]{2,1,0:T(8,128)(2,1)S(1)}, bf16[32,16,128]{2,1,0:T(8,128)(2,1)S(1)}, u32[]{:S(2)}, u32[]{:S(2)}) collective-permute-start(bf16[32,16,128]{2,1,0:T(8,128)(2,1)S(1)} %shard_map.105.refs_0_), channel_id=1, source_target_pairs={{0,1},{1,2},{2,3},{3,4},{4,5},{5,6},{6,7},{7,0},{8,9},{9,10},{10,1... | collective-permute-start | bytes 393224 | tf_op jit(solution)/shard_map/ppermute | solution.py:112
  4.1 4.0 %collective-permute-start.1 = (bf16[32,16,128]{2,1,0:T(8,128)(2,1)S(1)}, bf16[32,16,128]{2,1,0:T(8,128)(2,1)S(1)}, u32[]{:S(2)}, u32[]{:S(2)}) collective-permute-start(bf16[32,16,128]{2,1,0:T(8,128)(2,1)S(1)} %shard_map.105.refs_0_), channel_id=1, source_target_pairs={{0,7},{1,0},{2,1},{3,2},{4,3},{5,4},{6,5},{7,6},{8,15},{9,8},{10,9... | collective-permute-start | bytes 393224 | tf_op jit(solution)/shard_map/ppermute | solution.py:113
  8.2 3.1 %collective-permute-done.refs_1_ = bf16[32,16,128]{2,1,0:T(8,128)(2,1)S(1)} collective-permute-done((bf16[32,16,128]{2,1,0:T(8,128)(2,1)S(1)}, bf16[32,16,128]{2,1,0:T(8,128)(2,1)S(1)}, u32[]{:S(2)}, u32[]{:S(2)}) %collective-permute-start) | collective-permute-done | bytes 131104 | tf_op jit(solution)/shard_map/ppermute | solution.py:112
  11.3 2.7 %collective-permute-start.3 = (bf16[32,16,128]{2,1,0:T(8,128)(2,1)S(1)}, bf16[32,16,128]{2,1,0:T(8,128)(2,1)S(1)}, u32[]{:S(2)}, u32[]{:S(2)}) collective-permute-start(bf16[32,16,128]{2,1,0:T(8,128)(2,1)S(1)} %collective-permute-done.1.refs_2_), channel_id=1, source_target_pairs={{0,7},{1,0},{2,1},{3,2},{4,3},{5,4},{6,5},{7,6},{8,15},{9,8},{10,9... | collective-permute-start | bytes 393224 | tf_op jit(solution)/shard_map/ppermute | solution.py:113
  14.0 2.3 %collective-permute-done.2.refs_3_ = bf16[32,16,128]{2,1,0:T(8,128)(2,1)S(1)} collective-permute-done((bf16[32,16,128]{2,1,0:T(8,128)(2,1)S(1)}, bf16[32,16,128]{2,1,0:T(8,128)(2,1)S(1)}, u32[]{:S(2)}, u32[]{:S(2)}) %collective-permute-start.2) | collective-permute-done | bytes 131104 | tf_op jit(solution)/shard_map/ppermute | solution.py:112
  16.3 2.7 %collective-permute-start.5 = (bf16[32,16,128]{2,1,0:T(8,128)(2,1)S(1)}, bf16[32,16,128]{2,1,0:T(8,128)(2,1)S(1)}, u32[]{:S(2)}, u32[]{:S(2)}) collective-permute-start(bf16[32,16,128]{2,1,0:T(8,128)(2,1)S(1)} %collective-permute-done.3.refs_4_), channel_id=1, source_target_pairs={{0,7},{1,0},{2,1},{3,2},{4,3},{5,4},{6,5},{7,6},{8,15},{9,8},{10,9... | collective-permute-start | bytes 393224 | tf_op jit(solution)/shard_map/ppermute | solution.py:113
  19.0 2.3 %collective-permute-done.4.refs_5_ = bf16[32,16,128]{2,1,0:T(8,128)(2,1)S(1)} collective-permute-done((bf16[32,16,128]{2,1,0:T(8,128)(2,1)S(1)}, bf16[32,16,128]{2,1,0:T(8,128)(2,1)S(1)}, u32[]{:S(2)}, u32[]{:S(2)}) %collective-permute-start.4) | collective-permute-done | bytes 131104 | tf_op jit(solution)/shard_map/ppermute | solution.py:112
  21.4 2.7 %collective-permute-start.7 = (bf16[16,16,128]{2,1,0:T(8,128)(2,1)S(1)}, bf16[16,16,128]{2,1,0:T(8,128)(2,1)S(1)}, u32[]{:S(2)}, u32[]{:S(2)}) collective-permute-start(bf16[16,16,128]{2,1,0:T(8,128)(2,1)S(1)} %slice.17), channel_id=1, source_target_pairs={{0,7},{1,0},{2,1},{3,2},{4,3},{5,4},{6,5},{7,6},{8,15},{9,8},{10,9... | collective-permute-start | bytes 196616 | tf_op jit(solution)/shard_map/ppermute | solution.py:117
  25.7 1.1 shard_map.106
  27.7 11.8 %all-to-all-start = ((bf16[256,16,128]{2,1,0:T(8,128)(2,1)}), bf16[256,16,128]{2,1,0:T(8,128)(2,1)S(1)}, u32[]{:S(2)}, u32[]{:S(2)}) async-start(bf16[256,16,128]{2,1,0:T(8,128)(2,1)} %copy-done.7), calls=%async_computation | async-start | bytes 2097152 | tf_op jit(solution)/shard_map/all_to_all | solution.py:421
  41.5 4.7 %shard_map.104 = (s32[3,264]{1,0:T(4,128)S(1)}, s32[3,264]{1,0:T(4,128)S(1)}, s32[2]{0:T(128)S(1)}) custom-call(s32[256]{0:T(256)S(1)} %copy-done.10, s32[256]{0:T(256)S(1)} %copy-done.11, s32[1]{0:T(128)S(6)} %copy.12.live_ref), custom_call_target="tpu_custom_call" | custom-call | bytes 20000 | tf_op jit(solution)/shard_map/pallas_call | solution.py:88
  46.3 4.1 %shard_map.107.own_ref = f32[33,16,128]{2,1,0:T(8,128)S(1)} custom-call(s32[3,264]{1,0:T(4,128)S(1)} %get-tuple-element.18.list_ref, s32[2]{0:T(128)S(1)} %get-tuple-element.16.count_ref, bf16[256,16,128]{2,1,0:T(8,128)(2,1)S(1)} %get-tuple-element.19.lookup_ref, bf16[256,128,128]{2,1,0:T(8,128)(2,1)} %coupling_ref.7), custom_call_target="tpu_custom_call" | custom-call | flops 134217728 | bytes 8000000 | tf_op jit(solution)/shard_map/pallas_call | solution.py:191
  50.4 6.0 %all-to-all-done.lookup_ref = bf16[256,16,128]{2,1,0:T(8,128)(2,1)S(1)} async-done(((bf16[256,16,128]{2,1,0:T(8,128)(2,1)}), bf16[256,16,128]{2,1,0:T(8,128)(2,1)S(1)}, u32[]{:S(2)}, u32[]{:S(2)}) %all-to-all-start) | async-done | bytes 1048608 | tf_op jit(solution)/shard_map/all_to_all | solution.py:421
  56.4 4.0 %shard_map.108 = (f32[16,4096]{1,0:T(8,128)S(1)}, f32[32,16,128]{2,1,0:T(8,128)S(1)}) custom-call(s32[3,264]{1,0:T(4,128)S(1)} %get-tuple-element.15.list_ref, s32[2]{0:T(128)S(1)} %get-tuple-element.16.count_ref, bf16[256,16,128]{2,1,0:T(8,128)(2,1)S(1)} %all-to-all-done.lookup_ref, bf16[256,128,128]{2,1,0:T(8,128)(2,1)} %coupling_ref.7, ...), custom_call_target="tpu_custom_call" | custom-call | flops 134217728 | bytes 8000000 | tf_op jit(solution)/shard_map/pallas_call | solution.py:226
  60.5 15.4 %all_to_all.30.taken_ref = f32[32,16,128]{2,1,0:T(8,128)S(1)} all-to-all(f32[32,16,128]{2,1,0:T(8,128)S(1)} %get-tuple-element.20), channel_id=1, replica_groups=mesh['dom'=32,'row'=8] {'dom'}, dimensions={0} | all-to-all | bytes 524288 | tf_op jit(solution)/shard_map/all_to_all | solution.py:421
  75.9 12.4 %all_to_all.31.sums_ref = f32[8,16,128]{2,1,0:T(8,128)S(1)} all-to-all(f32[8,16,128]{2,1,0:T(8,128)S(1)} %shard_map.109), channel_id=1, replica_groups=mesh['dom'=32,'row'=8] {'row'}, dimensions={0} | all-to-all | bytes 131072 | tf_op jit(solution)/shard_map/all_to_all | solution.py:421
  89.0 2.3 %collective-permute-start.9 = (bf16[32,16,128]{2,1,0:T(8,128)(2,1)S(1)}, bf16[32,16,128]{2,1,0:T(8,128)(2,1)S(1)}, u32[]{:S(2)}, u32[]{:S(2)}) collective-permute-start(bf16[32,16,128]{2,1,0:T(8,128)(2,1)S(1)} %get-tuple-element.22.refs_0_), channel_id=1, source_target_pairs={{0,7},{1,0},{2,1},{3,2},{4,3},{5,4},{6,5},{7,6},{8,15},{9,8},{10,9... | collective-permute-start | bytes 393224 | tf_op jit(solution)/shard_map/ppermute | solution.py:113
  91.3 2.4 %collective-permute-done.8.refs_1_ = bf16[32,16,128]{2,1,0:T(8,128)(2,1)S(1)} collective-permute-done((bf16[32,16,128]{2,1,0:T(8,128)(2,1)S(1)}, bf16[32,16,128]{2,1,0:T(8,128)(2,1)S(1)}, u32[]{:S(2)}, u32[]{:S(2)}) %collective-permute-start.8) | collective-permute-done | bytes 131104 | tf_op jit(solution)/shard_map/ppermute | solution.py:112
  93.7 2.7 %collective-permute-start.11 = (bf16[32,16,128]{2,1,0:T(8,128)(2,1)S(1)}, bf16[32,16,128]{2,1,0:T(8,128)(2,1)S(1)}, u32[]{:S(2)}, u32[]{:S(2)}) collective-permute-start(bf16[32,16,128]{2,1,0:T(8,128)(2,1)S(1)} %collective-permute-done.9.refs_2_), channel_id=1, source_target_pairs={{0,7},{1,0},{2,1},{3,2},{4,3},{5,4},{6,5},{7,6},{8,15},{9,8},{10,9... | collective-permute-start | bytes 393224 | tf_op jit(solution)/shard_map/ppermute | solution.py:113
  96.4 2.3 %collective-permute-done.10.refs_3_ = bf16[32,16,128]{2,1,0:T(8,128)(2,1)S(1)} collective-permute-done((bf16[32,16,128]{2,1,0:T(8,128)(2,1)S(1)}, bf16[32,16,128]{2,1,0:T(8,128)(2,1)S(1)}, u32[]{:S(2)}, u32[]{:S(2)}) %collective-permute-start.10) | collective-permute-done | bytes 131104 | tf_op jit(solution)/shard_map/ppermute | solution.py:112
  98.7 2.7 %collective-permute-start.13 = (bf16[32,16,128]{2,1,0:T(8,128)(2,1)S(1)}, bf16[32,16,128]{2,1,0:T(8,128)(2,1)S(1)}, u32[]{:S(2)}, u32[]{:S(2)}) collective-permute-start(bf16[32,16,128]{2,1,0:T(8,128)(2,1)S(1)} %collective-permute-done.11.refs_4_), channel_id=1, source_target_pairs={{0,7},{1,0},{2,1},{3,2},{4,3},{5,4},{6,5},{7,6},{8,15},{9,8},{10,9... | collective-permute-start | bytes 393224 | tf_op jit(solution)/shard_map/ppermute | solution.py:113
  101.4 2.3 %collective-permute-done.12.refs_5_ = bf16[32,16,128]{2,1,0:T(8,128)(2,1)S(1)} collective-permute-done((bf16[32,16,128]{2,1,0:T(8,128)(2,1)S(1)}, bf16[32,16,128]{2,1,0:T(8,128)(2,1)S(1)}, u32[]{:S(2)}, u32[]{:S(2)}) %collective-permute-start.12) | collective-permute-done | bytes 131104 | tf_op jit(solution)/shard_map/ppermute | solution.py:112
  103.8 2.7 %collective-permute-start.15 = (bf16[16,16,128]{2,1,0:T(8,128)(2,1)S(1)}, bf16[16,16,128]{2,1,0:T(8,128)(2,1)S(1)}, u32[]{:S(2)}, u32[]{:S(2)}) collective-permute-start(bf16[16,16,128]{2,1,0:T(8,128)(2,1)S(1)} %slice.19), channel_id=1, source_target_pairs={{0,7},{1,0},{2,1},{3,2},{4,3},{5,4},{6,5},{7,6},{8,15},{9,8},{10,9... | collective-permute-start | bytes 196616 | tf_op jit(solution)/shard_map/ppermute | solution.py:117
  106.5 2.5 %collective-permute-done.14.refs_7_ = bf16[16,16,128]{2,1,0:T(8,128)(2,1)S(1)} collective-permute-done((bf16[16,16,128]{2,1,0:T(8,128)(2,1)S(1)}, bf16[16,16,128]{2,1,0:T(8,128)(2,1)S(1)}, u32[]{:S(2)}, u32[]{:S(2)}) %collective-permute-start.14) | collective-permute-done | bytes 65568 | tf_op jit(solution)/shard_map/ppermute | solution.py:116
  109.0 1.1 shard_map.111
  111.1 9.8 %all-to-all-start.3 = ((bf16[256,16,128]{2,1,0:T(8,128)(2,1)}), bf16[256,16,128]{2,1,0:T(8,128)(2,1)S(1)}, u32[]{:S(2)}, u32[]{:S(2)}) async-start(bf16[256,16,128]{2,1,0:T(8,128)(2,1)} %copy-done.8), calls=%async_computation.3 | async-start | bytes 2097152 | tf_op jit(solution)/shard_map/all_to_all | solution.py:421
  120.8 4.1 %shard_map.112.own_ref = f32[33,16,128]{2,1,0:T(8,128)S(1)} custom-call(s32[3,264]{1,0:T(4,128)S(1)} %get-tuple-element.18.list_ref, s32[2]{0:T(128)S(1)} %get-tuple-element.16.count_ref, bf16[256,16,128]{2,1,0:T(8,128)(2,1)S(1)} %get-tuple-element.24.lookup_ref, bf16[256,128,128]{2,1,0:T(8,128)(2,1)} %coupling_ref.7), custom_call_target="tpu_custom_call" | custom-call | flops 134217728 | bytes 8000000 | tf_op jit(solution)/shard_map/pallas_call | solution.py:191
  125.0 12.8 %all-to-all-done.3.lookup_ref = bf16[256,16,128]{2,1,0:T(8,128)(2,1)S(1)} async-done(((bf16[256,16,128]{2,1,0:T(8,128)(2,1)}), bf16[256,16,128]{2,1,0:T(8,128)(2,1)S(1)}, u32[]{:S(2)}, u32[]{:S(2)}) %all-to-all-start.3) | async-done | bytes 1048608 | tf_op jit(solution)/shard_map/all_to_all | solution.py:421
  138.7 5.4 %shard_map.113 = (f32[16,4096]{1,0:T(8,128)S(1)}, f32[32,24,128]{2,1,0:T(8,128)S(1)}) custom-call(s32[3,264]{1,0:T(4,128)S(1)} %get-tuple-element.15.list_ref, s32[2]{0:T(128)S(1)} %get-tuple-element.16.count_ref, bf16[256,16,128]{2,1,0:T(8,128)(2,1)S(1)} %all-to-all-done.3.lookup_ref, bf16[256,128,128]{2,1,0:T(8,128)(2,1)} %coupling_ref.7, ...), custom_call_target="tpu_custom_call" | custom-call | flops 134217728 | bytes 10000000 | tf_op jit(solution)/shard_map/pallas_call | solution.py:343
  144.2 16.6 %all_to_all.32.taken_ref = f32[32,24,128]{2,1,0:T(8,128)S(1)} all-to-all(f32[32,24,128]{2,1,0:T(8,128)S(1)} %get-tuple-element.26), channel_id=1, replica_groups=mesh['dom'=32,'row'=8] {'dom'}, dimensions={0} | all-to-all | bytes 786432 | tf_op jit(solution)/shard_map/all_to_all | solution.py:421
  160.8 10.5 %all_to_all.33.taken_ref = f32[8,24,128]{2,1,0:T(8,128)S(1)} all-to-all(f32[8,24,128]{2,1,0:T(8,128)S(1)} %shard_map.114), channel_id=1, replica_groups=mesh['dom'=32,'row'=8] {'row'}, dimensions={0} | all-to-all | bytes 196608 | tf_op jit(solution)/shard_map/all_to_all | solution.py:421
  171.3 8.7 %shard_map.115 = (f32[16,4096]{1,0:T(8,128)}, f32[16,4096]{1,0:T(8,128)}) custom-call(f32[8,24,128]{2,1,0:T(8,128)S(1)} %all_to_all.33.taken_ref, f32[16,4096]{1,0:T(8,128)S(1)} %copy-done.1, f32[16,4096]{1,0:T(8,128)S(1)} %copy-done.6, f32[16,4096]{1,0:T(8,128)S(1)} %copy-done.2, f32[16,4096]{1,0:T(8,128)S(1)} %get-tuple-element.21.image_ref, ...), custom_call_target="tpu_custom_call" | custom-call | flops 1000000 | bytes 3000000 | tf_op jit(solution)/shard_map/pallas_call | solution.py:409
  (50 shorter events, 7.5 us)
Async XLA Ops:
  0.6 1.0 copy-start
  1.6 54.8 %copy-start.1 = (f32[16,4096]{1,0:T(8,128)S(1)}, f32[16,4096]{1,0:T(8,128)}, u32[]{:S(2)}) copy-start(f32[16,4096]{1,0:T(8,128)} %basis_ref.7) | copy-start | bytes 786436
  1.6 54.8 %copy-start.9 = (f32[4096]{0:T(1024)S(1)}, f32[4096]{0:T(1024)}, u32[]{:S(2)}) copy-start(f32[4096]{0:T(1024)} %param.12) | copy-start | bytes 49156
  1.6 9.7 %collective-permute-start = (bf16[32,16,128]{2,1,0:T(8,128)(2,1)S(1)}, bf16[32,16,128]{2,1,0:T(8,128)(2,1)S(1)}, u32[]{:S(2)}, u32[]{:S(2)}) collective-permute-start(bf16[32,16,128]{2,1,0:T(8,128)(2,1)S(1)} %shard_map.105.refs_0_), channel_id=1, source_target_pairs={{0,1},{1,2},{2,3},{3,4},{4,5},{5,6},{6,7},{7,0},{8,9},{9,10},{10,1... | collective-permute-start | bytes 393224 | tf_op jit(solution)/shard_map/ppermute | solution.py:112
  4.1 7.2 %collective-permute-start.1 = (bf16[32,16,128]{2,1,0:T(8,128)(2,1)S(1)}, bf16[32,16,128]{2,1,0:T(8,128)(2,1)S(1)}, u32[]{:S(2)}, u32[]{:S(2)}) collective-permute-start(bf16[32,16,128]{2,1,0:T(8,128)(2,1)S(1)} %shard_map.105.refs_0_), channel_id=1, source_target_pairs={{0,7},{1,0},{2,1},{3,2},{4,3},{5,4},{6,5},{7,6},{8,15},{9,8},{10,9... | collective-permute-start | bytes 393224 | tf_op jit(solution)/shard_map/ppermute | solution.py:113
  11.3 5.0 %collective-permute-start.2 = (bf16[32,16,128]{2,1,0:T(8,128)(2,1)S(1)}, bf16[32,16,128]{2,1,0:T(8,128)(2,1)S(1)}, u32[]{:S(2)}, u32[]{:S(2)}) collective-permute-start(bf16[32,16,128]{2,1,0:T(8,128)(2,1)S(1)} %collective-permute-done.refs_1_), channel_id=1, source_target_pairs={{0,1},{1,2},{2,3},{3,4},{4,5},{5,6},{6,7},{7,0},{8,9},{9,10},{10,1... | collective-permute-start | bytes 393224 | tf_op jit(solution)/shard_map/ppermute | solution.py:112
  11.3 5.0 %collective-permute-start.3 = (bf16[32,16,128]{2,1,0:T(8,128)(2,1)S(1)}, bf16[32,16,128]{2,1,0:T(8,128)(2,1)S(1)}, u32[]{:S(2)}, u32[]{:S(2)}) collective-permute-start(bf16[32,16,128]{2,1,0:T(8,128)(2,1)S(1)} %collective-permute-done.1.refs_2_), channel_id=1, source_target_pairs={{0,7},{1,0},{2,1},{3,2},{4,3},{5,4},{6,5},{7,6},{8,15},{9,8},{10,9... | collective-permute-start | bytes 393224 | tf_op jit(solution)/shard_map/ppermute | solution.py:113
  16.3 5.0 %collective-permute-start.4 = (bf16[32,16,128]{2,1,0:T(8,128)(2,1)S(1)}, bf16[32,16,128]{2,1,0:T(8,128)(2,1)S(1)}, u32[]{:S(2)}, u32[]{:S(2)}) collective-permute-start(bf16[32,16,128]{2,1,0:T(8,128)(2,1)S(1)} %collective-permute-done.2.refs_3_), channel_id=1, source_target_pairs={{0,1},{1,2},{2,3},{3,4},{4,5},{5,6},{6,7},{7,0},{8,9},{9,10},{10,1... | collective-permute-start | bytes 393224 | tf_op jit(solution)/shard_map/ppermute | solution.py:112
  16.3 5.0 %collective-permute-start.5 = (bf16[32,16,128]{2,1,0:T(8,128)(2,1)S(1)}, bf16[32,16,128]{2,1,0:T(8,128)(2,1)S(1)}, u32[]{:S(2)}, u32[]{:S(2)}) collective-permute-start(bf16[32,16,128]{2,1,0:T(8,128)(2,1)S(1)} %collective-permute-done.3.refs_4_), channel_id=1, source_target_pairs={{0,7},{1,0},{2,1},{3,2},{4,3},{5,4},{6,5},{7,6},{8,15},{9,8},{10,9... | collective-permute-start | bytes 393224 | tf_op jit(solution)/shard_map/ppermute | solution.py:113
  21.4 4.3 %collective-permute-start.6 = (bf16[16,16,128]{2,1,0:T(8,128)(2,1)S(1)}, bf16[16,16,128]{2,1,0:T(8,128)(2,1)S(1)}, u32[]{:S(2)}, u32[]{:S(2)}) collective-permute-start(bf16[16,16,128]{2,1,0:T(8,128)(2,1)S(1)} %slice.16), channel_id=1, source_target_pairs={{0,1},{1,2},{2,3},{3,4},{4,5},{5,6},{6,7},{7,0},{8,9},{9,10},{10,1... | collective-permute-start | bytes 196616 | tf_op jit(solution)/shard_map/ppermute | solution.py:116
  21.4 4.3 %collective-permute-start.7 = (bf16[16,16,128]{2,1,0:T(8,128)(2,1)S(1)}, bf16[16,16,128]{2,1,0:T(8,128)(2,1)S(1)}, u32[]{:S(2)}, u32[]{:S(2)}) collective-permute-start(bf16[16,16,128]{2,1,0:T(8,128)(2,1)S(1)} %slice.17), channel_id=1, source_target_pairs={{0,7},{1,0},{2,1},{3,2},{4,3},{5,4},{6,5},{7,6},{8,15},{9,8},{10,9... | collective-permute-start | bytes 196616 | tf_op jit(solution)/shard_map/ppermute | solution.py:117
  26.8 1.0 copy-start.7
  27.7 28.7 %all-to-all-start = ((bf16[256,16,128]{2,1,0:T(8,128)(2,1)}), bf16[256,16,128]{2,1,0:T(8,128)(2,1)S(1)}, u32[]{:S(2)}, u32[]{:S(2)}) async-start(bf16[256,16,128]{2,1,0:T(8,128)(2,1)} %copy-done.7), calls=%async_computation | async-start | bytes 2097152 | tf_op jit(solution)/shard_map/all_to_all | solution.py:421
  40.2 0.7 copy-start.10
  40.8 0.7 copy-start.11
  60.5 77.3 %copy-start.2 = (f32[16,4096]{1,0:T(8,128)S(1)}, f32[16,4096]{1,0:T(8,128)}, u32[]{:S(2)}) copy-start(f32[16,4096]{1,0:T(8,128)} %previous_ref.3) | copy-start | bytes 786436
  60.5 77.3 %copy-start.3 = (f32[16,4096]{1,0:T(8,128)S(1)}, f32[16,4096]{1,0:T(8,128)}, u32[]{:S(2)}) copy-start(f32[16,4096]{1,0:T(8,128)} %previous_image_ref.3) | copy-start | bytes 786436
  88.6 20.5 %copy-start.4 = (f32[16,4096]{1,0:T(8,128)}, f32[16,4096]{1,0:T(8,128)S(1)}, u32[]{:S(2)}) copy-start(f32[16,4096]{1,0:T(8,128)S(1)} %get-tuple-element.25.residual_ref) | copy-start | bytes 786436
  88.6 5.1 %collective-permute-start.8 = (bf16[32,16,128]{2,1,0:T(8,128)(2,1)S(1)}, bf16[32,16,128]{2,1,0:T(8,128)(2,1)S(1)}, u32[]{:S(2)}, u32[]{:S(2)}) collective-permute-start(bf16[32,16,128]{2,1,0:T(8,128)(2,1)S(1)} %get-tuple-element.22.refs_0_), channel_id=1, source_target_pairs={{0,1},{1,2},{2,3},{3,4},{4,5},{5,6},{6,7},{7,0},{8,9},{9,10},{10,1... | collective-permute-start | bytes 393224 | tf_op jit(solution)/shard_map/ppermute | solution.py:112
  89.0 4.7 %collective-permute-start.9 = (bf16[32,16,128]{2,1,0:T(8,128)(2,1)S(1)}, bf16[32,16,128]{2,1,0:T(8,128)(2,1)S(1)}, u32[]{:S(2)}, u32[]{:S(2)}) collective-permute-start(bf16[32,16,128]{2,1,0:T(8,128)(2,1)S(1)} %get-tuple-element.22.refs_0_), channel_id=1, source_target_pairs={{0,7},{1,0},{2,1},{3,2},{4,3},{5,4},{6,5},{7,6},{8,15},{9,8},{10,9... | collective-permute-start | bytes 393224 | tf_op jit(solution)/shard_map/ppermute | solution.py:113
  93.7 5.0 %collective-permute-start.10 = (bf16[32,16,128]{2,1,0:T(8,128)(2,1)S(1)}, bf16[32,16,128]{2,1,0:T(8,128)(2,1)S(1)}, u32[]{:S(2)}, u32[]{:S(2)}) collective-permute-start(bf16[32,16,128]{2,1,0:T(8,128)(2,1)S(1)} %collective-permute-done.8.refs_1_), channel_id=1, source_target_pairs={{0,1},{1,2},{2,3},{3,4},{4,5},{5,6},{6,7},{7,0},{8,9},{9,10},{10,1... | collective-permute-start | bytes 393224 | tf_op jit(solution)/shard_map/ppermute | solution.py:112
  93.7 5.0 %collective-permute-start.11 = (bf16[32,16,128]{2,1,0:T(8,128)(2,1)S(1)}, bf16[32,16,128]{2,1,0:T(8,128)(2,1)S(1)}, u32[]{:S(2)}, u32[]{:S(2)}) collective-permute-start(bf16[32,16,128]{2,1,0:T(8,128)(2,1)S(1)} %collective-permute-done.9.refs_2_), channel_id=1, source_target_pairs={{0,7},{1,0},{2,1},{3,2},{4,3},{5,4},{6,5},{7,6},{8,15},{9,8},{10,9... | collective-permute-start | bytes 393224 | tf_op jit(solution)/shard_map/ppermute | solution.py:113
  98.7 5.0 %collective-permute-start.12 = (bf16[32,16,128]{2,1,0:T(8,128)(2,1)S(1)}, bf16[32,16,128]{2,1,0:T(8,128)(2,1)S(1)}, u32[]{:S(2)}, u32[]{:S(2)}) collective-permute-start(bf16[32,16,128]{2,1,0:T(8,128)(2,1)S(1)} %collective-permute-done.10.refs_3_), channel_id=1, source_target_pairs={{0,1},{1,2},{2,3},{3,4},{4,5},{5,6},{6,7},{7,0},{8,9},{9,10},{10,1... | collective-permute-start | bytes 393224 | tf_op jit(solution)/shard_map/ppermute | solution.py:112
  98.7 5.0 %collective-permute-start.13 = (bf16[32,16,128]{2,1,0:T(8,128)(2,1)S(1)}, bf16[32,16,128]{2,1,0:T(8,128)(2,1)S(1)}, u32[]{:S(2)}, u32[]{:S(2)}) collective-permute-start(bf16[32,16,128]{2,1,0:T(8,128)(2,1)S(1)} %collective-permute-done.11.refs_4_), channel_id=1, source_target_pairs={{0,7},{1,0},{2,1},{3,2},{4,3},{5,4},{6,5},{7,6},{8,15},{9,8},{10,9... | collective-permute-start | bytes 393224 | tf_op jit(solution)/shard_map/ppermute | solution.py:113
  103.7 5.3 %collective-permute-start.14 = (bf16[16,16,128]{2,1,0:T(8,128)(2,1)S(1)}, bf16[16,16,128]{2,1,0:T(8,128)(2,1)S(1)}, u32[]{:S(2)}, u32[]{:S(2)}) collective-permute-start(bf16[16,16,128]{2,1,0:T(8,128)(2,1)S(1)} %slice.18), channel_id=1, source_target_pairs={{0,1},{1,2},{2,3},{3,4},{4,5},{5,6},{6,7},{7,0},{8,9},{9,10},{10,1... | collective-permute-start | bytes 196616 | tf_op jit(solution)/shard_map/ppermute | solution.py:116
  103.8 5.2 %collective-permute-start.15 = (bf16[16,16,128]{2,1,0:T(8,128)(2,1)S(1)}, bf16[16,16,128]{2,1,0:T(8,128)(2,1)S(1)}, u32[]{:S(2)}, u32[]{:S(2)}) collective-permute-start(bf16[16,16,128]{2,1,0:T(8,128)(2,1)S(1)} %slice.19), channel_id=1, source_target_pairs={{0,7},{1,0},{2,1},{3,2},{4,3},{5,4},{6,5},{7,6},{8,15},{9,8},{10,9... | collective-permute-start | bytes 196616 | tf_op jit(solution)/shard_map/ppermute | solution.py:117
  110.1 1.0 copy-start.8
  111.1 26.7 %all-to-all-start.3 = ((bf16[256,16,128]{2,1,0:T(8,128)(2,1)}), bf16[256,16,128]{2,1,0:T(8,128)(2,1)S(1)}, u32[]{:S(2)}, u32[]{:S(2)}) async-start(bf16[256,16,128]{2,1,0:T(8,128)(2,1)} %copy-done.8), calls=%async_computation.3 | async-start | bytes 2097152 | tf_op jit(solution)/shard_map/all_to_all | solution.py:421
  137.7 1.0 copy-start.5
  138.7 32.6 %copy-start.6 = (f32[16,4096]{1,0:T(8,128)S(1)}, f32[16,4096]{1,0:T(8,128)}, u32[]{:S(2)}) copy-start(f32[16,4096]{1,0:T(8,128)} %copy-done.4) | copy-start | bytes 786436

commit v2 on v1

--- a/solution.py
+++ b/solution.py
@@ -13,6 +13,8 @@
 RB = 32
 SLOTS = 256
 SEND = 8
+HALF = RB // 2
+EXTRA = SEND + 1
 LEN = SLOTS + 8
 F32 = jnp.float32
 BF16 = jnp.bfloat16
@@ -55,6 +57,10 @@
     return slice(block * BS, (block + 1) * BS)
 
 
+def iota2(shape, axis):
+    return lax.broadcasted_iota(jnp.int32, shape, axis)
+
+
 def list_kernel(part, row_ref, column_ref, live_ref, own_ref, halo_ref, count_ref):
     live = live_ref[0]
 
@@ -62,15 +68,17 @@
         n_own, n_halo = counts
         column = column_ref[slot]
         row = row_ref[slot]
+        received = jnp.maximum(column - part, 0)
         own_ref[0, n_own] = slot
-        own_ref[1, n_own] = column
+        own_ref[1, n_own] = jnp.minimum(column, part - 1)
         own_ref[2, n_own] = row
+        own_ref[3, n_own] = jnp.minimum(column, part - 1) >> 5
         halo_ref[0, n_halo] = slot
-        halo_ref[1, n_halo] = column - part
+        halo_ref[1, n_halo] = received + (received >> 3)
         halo_ref[2, n_halo] = row
+        halo_ref[3, n_halo] = received
         used = slot < live
-        is_own = column < part
-        n_own = n_own + jnp.where(used & is_own, 1, 0)
+        n_own = n_own + jnp.where(used & (column < part), 1, 0)
         n_halo = n_halo + jnp.where(used & (column >= part), 1, 0)
         return n_own, n_halo
 
@@ -80,6 +88,7 @@
             ref[0, count + extra] = 0
             ref[1, count + extra] = 0
             ref[2, count + extra] = RB
+            ref[3, count + extra] = 0
     count_ref[0] = n_own
     count_ref[1] = n_halo
 
@@ -87,23 +96,38 @@
 def make_lists(slot_row, slot_column, live_slots, part):
     return call(
         functools.partial(list_kernel, part),
-        (shaped((3, LEN), jnp.int32), shaped((3, LEN), jnp.int32), shaped((2,), jnp.int32)),
+        (shaped((4, LEN), jnp.int32), shaped((4, LEN), jnp.int32), shaped((2,), jnp.int32)),
         [SMEM, SMEM, SMEM],
         (SMEM, SMEM, SMEM),
         moved=20000,
     )(slot_row, slot_column, live_slots)
 
 
-def cast_kernel(field_ref, tiles_ref):
+def split3(value):
+    high = value.astype(BF16).astype(F32)
+    rest = value - high
+    middle = rest.astype(BF16).astype(F32)
+    return high, middle, (rest - middle).astype(BF16).astype(F32)
+
+
+def cast_kernel(field_ref, degree_ref, tiles_ref):
     for block in range(RB):
-        tiles_ref[block] = field_ref[:, columns(block)].astype(BF16)
-
-
-def cast_tiles(field):
-    return call(cast_kernel, shaped((RB, K, BS), BF16), [VMEM], VMEM, moved=400000)(field)
-
-
-def gather_row(tiles, n_row):
+        tiles_ref[block + 2 * (block // HALF)] = field_ref[:, columns(block)].astype(BF16)
+    for half in range(2):
+        inverse = 1.0 / degree_ref[half * HALF : (half + 1) * HALF]
+        high = inverse.astype(BF16)
+        at = half * (HALF + 2) + HALF
+        tiles_ref[at] = high
+        tiles_ref[at + 1] = (inverse - high.astype(F32)).astype(BF16)
+
+
+def cast_tiles(field, degree):
+    return call(
+        cast_kernel, shaped((RB + 4, K, BS), BF16), [VMEM, VMEM], VMEM, moved=400000
+    )(field, degree)
+
+
+def gather_row(tiles, n_row, half):
     up = [(i, (i + 1) % n_row) for i in range(n_row)]
     down = [(i, (i - 1) % n_row) for i in range(n_row)]
     pieces = [(0, tiles)]
@@ -112,48 +136,108 @@
         from_below = lax.ppermute(from_below, "row", up)
         from_above = lax.ppermute(from_above, "row", down)
         pieces += [(-step, from_below), (step, from_above)]
-    half = RB // 2
     far_low = lax.ppermute(from_below[:half], "row", up)
     far_high = lax.ppermute(from_above[half:], "row", down)
     return pieces, far_low, far_high
 
 
-def select_kernel(offsets, n_row, place_ref, send_ref, *refs):
-    pieces, (far_low, far_high, part_ref, chosen_ref) = refs[: len(offsets)], refs[len(offsets) :]
-    place = place_ref[0]
-    half = RB // 2
+def halves(offsets, pieces, half, n_row, place):
+    parts = []
     for offset, piece in zip(offsets, pieces):
         owner = lax.rem(place + offset + n_row, n_row)
-        part_ref[pl.ds(owner * RB, RB)] = piece[...]
+        parts += [(owner, 0, piece, 0), (owner, 1, piece, half)]
     owner = lax.rem(place + n_row // 2, n_row)
-    part_ref[pl.ds(owner * RB, half)] = far_low[...]
-    part_ref[pl.ds(owner * RB + half, half)] = far_high[...]
-
-    def step(group, carry):
-        for j in range(8):
-            chosen_ref[group * 8 + j] = part_ref[send_ref[group * 8 + j]]
+    return parts + [(owner, 0, pieces[-2], 0), (owner, 1, pieces[-1], 0)]
+
+
+def first_select_kernel(offsets, n_row, place_ref, send_ref, *refs):
+    pieces, (part_ref, inverse_ref, chosen_ref, rows_ref) = refs[:-4], refs[-4:]
+    for owner, half, piece, start in halves(offsets, pieces, HALF + 2, n_row, place_ref[0]):
+        at = owner * RB + half * HALF
+        part_ref[pl.ds(at, HALF)] = piece[start : start + HALF]
+        inverse_ref[pl.ds(pl.multiple_of(at, HALF), HALF), :] = (
+            piece[start + HALF].astype(F32) + piece[start + HALF + 1].astype(F32)
+        )
+
+    def step(peer, carry):
+        for j in range(SEND):
+            block = send_ref[peer * SEND + j]
+            chosen_ref[peer * EXTRA + j] = part_ref[block]
+            rows_ref[j : j + 1, :] = inverse_ref[pl.ds(block, 1), :]
+        rows = rows_ref[...]
+        high = rows.astype(BF16).astype(F32)
+        chosen_ref[peer * EXTRA + SEND] = jnp.concatenate([high, rows - high], axis=0).astype(BF16)
         return carry
 
-    lax.fori_loop(0, chosen_ref.shape[0] // 8, step, 0)
-
-
-def select(gathered, place, send_list, n_row):
+    lax.fori_loop(0, chosen_ref.shape[0] // EXTRA, step, 0)
+
+
+def first_select(gathered, place, send_list, n_row):
     pieces, far_low, far_high = gathered
-    offsets = [offset for offset, _ in pieces]
-    count = send_list.shape[0]
-    return call(
-        functools.partial(select_kernel, offsets, n_row),
-        (shaped((n_row * RB, K, BS), BF16), shaped((count, K, BS), BF16)),
+    part = n_row * RB
+    peers = send_list.shape[0] // SEND
+    return call(
+        functools.partial(first_select_kernel, [offset for offset, _ in pieces], n_row),
+        (shaped((part, K, BS), BF16), shaped((part, BS), F32), shaped((peers * EXTRA, K, BS), BF16)),
         [SMEM, SMEM] + [VMEM] * (len(pieces) + 2),
-        (VMEM, VMEM),
+        (VMEM, VMEM, VMEM),
+        (pltpu.VMEM((SEND, BS), F32),),
         moved=3000000,
     )(place, send_list, *[piece for _, piece in pieces], far_low, far_high)
 
 
-def apply_list(count, list_ref, lookup_ref, coupling_ref, held, sems, acc_ref):
-    groups = lax.div(count + 7, 8)
-
-    def issue(group, carry):
+def second_select_kernel(offsets, n_row, place_ref, send_ref, pick_ref, *refs):
+    pieces, (part_ref, chosen_ref, table_ref) = refs[:-3], refs[-3:]
+    lane = iota2((K, BS), 1)
+    table = jnp.zeros((K, BS), F32)
+    side_sum = jnp.zeros((K, BS), F32)
+    for owner, half, piece, start in halves(offsets, pieces, HALF, n_row, place_ref[0]):
+        part_ref[pl.ds(owner * RB + half * HALF, HALF)] = piece[start : start + HALF]
+        if half == 1:
+            side = piece[start + HALF].astype(F32)
+            table = jnp.where(lane == owner, side[:, 0:1], table)
+            side_sum = side_sum + side
+    top = jnp.sum(jnp.where((lane >= 1) & (lane <= 3), side_sum, 0.0), axis=1, keepdims=True)
+    bottom = jnp.sum(jnp.where((lane >= 4) & (lane <= 6), side_sum, 0.0), axis=1, keepdims=True)
+    for at, value in enumerate(split3(top) + split3(bottom)):
+        table = jnp.where(lane == 8 + at, value, table)
+    table = table.astype(BF16)
+    table_ref[...] = table
+    sides = dot_nn(table, pick_ref[...])
+    for peer in range(chosen_ref.shape[0] // EXTRA):
+        chosen_ref[peer * EXTRA + SEND] = sides[:, columns(peer)].astype(BF16)
+
+    def step(peer, carry):
+        for j in range(SEND):
+            chosen_ref[peer * EXTRA + j] = part_ref[send_ref[peer * SEND + j]]
+        return carry
+
+    lax.fori_loop(0, chosen_ref.shape[0] // EXTRA, step, 0)
+
+
+def second_select(gathered, place, send_list, pick, n_row):
+    pieces, far_low, far_high = gathered
+    peers = send_list.shape[0] // SEND
+    return call(
+        functools.partial(second_select_kernel, [offset for offset, _ in pieces], n_row),
+        (shaped((n_row * RB, K, BS), BF16), shaped((peers * EXTRA, K, BS), BF16), shaped((K, BS), BF16)),
+        [SMEM, SMEM] + [VMEM] * (len(pieces) + 3),
+        (VMEM, VMEM, VMEM),
+        moved=3000000,
+    )(place, send_list, pick, *[piece for _, piece in pieces], far_low, far_high)
+
+
+def picks(send_list):
+    peers = send_list.shape[0] // SEND
+    owner = (send_list >> 5).reshape(peers, SEND)
+    lane = jnp.broadcast_to(jnp.arange(BS, dtype=jnp.int32)[None, :], (peers, BS))
+    target = jnp.where(lane < 14, lane, -1)
+    target = jnp.concatenate([owner, target[:, SEND:]], axis=1).reshape(-1)
+    return (jnp.arange(BS, dtype=jnp.int32)[:, None] == target[None, :]).astype(BF16)
+
+
+def issue(count, list_ref, coupling_ref, held, sems):
+    def step(group, carry):
         for j in range(8):
             at = group * 8 + j
             pltpu.make_async_copy(
@@ -161,71 +245,108 @@
             ).start()
         return carry
 
-    lax.fori_loop(0, groups, issue, 0)
-
-    def work(group, carry):
+    lax.fori_loop(0, lax.div(count + 7, 8), step, 0)
+
+
+def work(count, list_ref, coupling_ref, held, sems, multiply, add):
+    def step(group, carry):
         base = group * 8
         pltpu.make_async_copy(
             coupling_ref.at[pl.ds(0, 8)], held.at[pl.ds(base, 8)], sems.at[group]
         ).wait()
         products = [
-            dot_nt(lookup_ref[list_ref[1, base + j]], held[base + j]) for j in range(8)
+            multiply(list_ref[1, base + j], list_ref[3, base + j], held[base + j]) for j in range(8)
         ]
         for j in range(8):
-            row = list_ref[2, base + j]
-            acc_ref[row] = acc_ref[row] + products[j]
+            add(base + j, list_ref[2, base + j], list_ref[3, base + j], products[j])
         return carry
 
-    lax.fori_loop(0, groups, work, 0)
+    lax.fori_loop(0, lax.div(count + 7, 8), step, 0)
 
 
 HELD = (pltpu.VMEM((SLOTS, BS, BS), BF16), pltpu.SemaphoreType.DMA((SLOTS // 8,)))
-
-
-def own_kernel(list_ref, count_ref, lookup_ref, coupling_ref, acc_ref, held, sems):
+ROWS = shaped((RB + 1, K, BS), F32)
+PRODUCTS = shaped((SLOTS, K, BS), F32)
+
+
+def scale_block(block, inverse):
+    return (block.astype(F32) * inverse).astype(BF16)
+
+
+def first_own_kernel(
+    list_ref, count_ref, part_ref, inverse_ref, coupling_ref, acc_ref, scaled_ref, kept_ref, held, sems
+):
+    issue(count_ref[0], list_ref, coupling_ref, held, sems)
     acc_ref[...] = jnp.zeros_like(acc_ref)
-    apply_list(count_ref[0], list_ref, lookup_ref, coupling_ref, held, sems, acc_ref)
-
-
-def couple_own(own_list, counts, part_tiles, coupling):
-    return call(
-        own_kernel,
-        shaped((RB + 1, K, BS), F32),
-        [SMEM, SMEM, VMEM, HBM],
-        VMEM,
+    scaled_ref[...] = jnp.zeros_like(scaled_ref)
+
+    def multiply(tile, side, weights):
+        block = part_ref[tile]
+        scaled = scale_block(block, inverse_ref[pl.ds(tile, 1), :])
+        return dot_nt(jnp.concatenate([block, scaled], axis=0), weights)
+
+    def add(at, row, side, product):
+        acc_ref[row] = acc_ref[row] + product[0:K]
+        scaled_ref[row] = scaled_ref[row] + product[K:]
+        kept_ref[at] = product[K:]
+
+    work(count_ref[0], list_ref, coupling_ref, held, sems, multiply, add)
+
+
+def first_own(own_list, counts, part_tiles, inverse, coupling):
+    return call(
+        first_own_kernel,
+        (ROWS, ROWS, PRODUCTS),
+        [SMEM, SMEM, VMEM, VMEM, HBM],
+        (VMEM, VMEM, VMEM),
         HELD,
         flops=2 * SLOTS * K * BS * BS,
-        moved=8000000,
-    )(own_list, counts, part_tiles, coupling)
+        moved=10000000,
+    )(own_list, counts, part_tiles, inverse, coupling)
 
 
 def image_kernel(
-    list_ref, count_ref, lookup_ref, coupling_ref, own_ref, basis_ref, degree_ref,
-    image_ref, sums_ref, acc_ref, held, sems,
-):
+    list_ref, count_ref, halo_ref, coupling_ref, own_ref, basis_ref, degree_ref, image_ref, tiles_ref, acc_ref, held,
+    sems,
+):
+    issue(count_ref[1], list_ref, coupling_ref, held, sems)
     acc_ref[...] = own_ref[...]
-    apply_list(count_ref[1], list_ref, lookup_ref, coupling_ref, held, sems, acc_ref)
+
+    def multiply(tile, side, weights):
+        return dot_nt(halo_ref[tile], weights)
+
+    def add(at, row, side, product):
+        acc_ref[row] = acc_ref[row] + product
+
+    work(count_ref[1], list_ref, coupling_ref, held, sems, multiply, add)
     top = jnp.zeros((K, BS), F32)
     bottom = jnp.zeros((K, BS), F32)
     for block in range(RB):
         at = columns(block)
         basis = basis_ref[:, at]
-        image = degree_ref[:, at] * basis - acc_ref[block]
+        image = degree_ref[block : block + 1, :] * basis - acc_ref[block]
         image_ref[:, at] = image
         top = top + basis * image
         bottom = bottom + basis * basis
-    lane = lax.broadcasted_iota(jnp.int32, (K, BS), 1)
-    sums = jnp.where(
-        lane == 0, jnp.sum(top, axis=1, keepdims=True), jnp.sum(bottom, axis=1, keepdims=True)
-    )
-    for peer in range(sums_ref.shape[0]):
-        sums_ref[peer] = sums
-
-
-def make_image(halo_list, counts, halo_tiles, coupling, own, basis, degree, n_dom):
+    top = jnp.sum(top, axis=1, keepdims=True)
+    bottom = jnp.sum(bottom, axis=1, keepdims=True)
+    usable = bottom > 1e-30
+    quotient = jnp.where(usable, top / jnp.where(usable, bottom, 1.0), 0.0).astype(BF16).astype(F32)
+    for block in range(RB):
+        at = columns(block)
+        residual = (image_ref[:, at] - quotient * basis_ref[:, at]) / degree_ref[block : block + 1, :]
+        tiles_ref[block] = residual.astype(BF16)
+    lane = iota2((K, BS), 1)
+    side = jnp.where(lane == 0, quotient, 0.0)
+    for at, value in enumerate(split3(top) + split3(bottom)):
+        side = jnp.where(lane == 1 + at, value, side)
+    tiles_ref[RB] = side.astype(BF16)
+
+
+def make_image(halo_list, counts, halo_tiles, coupling, own, basis, degree):
     return call(
         image_kernel,
-        (shaped(basis.shape, F32), shaped((n_dom, K, BS), F32)),
+        (shaped(basis.shape, F32), shaped((RB + 1, K, BS), BF16)),
         [SMEM, SMEM, VMEM, HBM, VMEM, VMEM, VMEM],
         (VMEM, VMEM),
         (pltpu.VMEM((RB + 1, K, BS), F32),) + HELD,
@@ -234,6 +355,56 @@
     )(halo_list, counts, halo_tiles, coupling, own, basis, degree)
 
 
+def second_own_kernel(
+    own_list, halo_list, count_ref, part_ref, table_ref, own_kept_ref, own_scaled_ref, halo_ref, coupling_ref,
+    acc_ref, scaled_ref, kept_ref, held, sems, halo_held, halo_sems, quotient_ref, inverse_ref,
+):
+    issue(count_ref[0], own_list, coupling_ref, held, sems)
+    issue(count_ref[1], halo_list, coupling_ref, halo_held, halo_sems)
+    acc_ref[...] = jnp.zeros_like(acc_ref)
+    scaled_ref[...] = own_scaled_ref[...]
+    table = table_ref[...].astype(F32)
+    lane = iota2((K, BS), 1)
+    for owner in range(quotient_ref.shape[0]):
+        quotient_ref[owner] = jnp.broadcast_to(table[:, owner : owner + 1], (K, BS))
+    for peer in range(halo_ref.shape[0] // EXTRA):
+        side = halo_ref[peer * EXTRA + SEND].astype(F32)
+        inverse_ref[peer * SEND : (peer + 1) * SEND, :] = side[0:SEND] + side[SEND:]
+
+    def multiply(tile, side, weights):
+        return dot_nt(part_ref[tile], weights)
+
+    def add(at, row, side, product):
+        acc_ref[row] = acc_ref[row] + (product + quotient_ref[side] * own_kept_ref[at])
+
+    work(count_ref[0], own_list, coupling_ref, held, sems, multiply, add)
+
+    def multiply_halo(tile, side, weights):
+        return dot_nt(scale_block(halo_ref[tile], inverse_ref[pl.ds(side, 1), :]), weights)
+
+    def add_halo(at, row, side, product):
+        scaled_ref[row] = scaled_ref[row] + product
+        kept_ref[at] = product
+
+    work(count_ref[1], halo_list, coupling_ref, halo_held, halo_sems, multiply_halo, add_halo)
+
+
+def second_own(
+    own_list, halo_list, counts, part_tiles, table, own_kept, own_scaled, halo_tiles, coupling, n_row
+):
+    return call(
+        second_own_kernel,
+        (ROWS, ROWS, PRODUCTS),
+        [SMEM, SMEM, SMEM] + [VMEM] * 5 + [HBM],
+        (VMEM, VMEM, VMEM),
+        HELD
+        + HELD
+        + (pltpu.VMEM((n_row, K, BS), F32), pltpu.VMEM((halo_tiles.shape[0] // EXTRA * SEND, BS), F32)),
+        flops=4 * SLOTS * K * BS * BS,
+        moved=10000000,
+    )(own_list, halo_list, counts, part_tiles, table, own_kept, own_scaled, halo_tiles, coupling)
+
+
 def spread_kernel(taken_ref, given_ref):
     total = taken_ref[0]
     for peer in range(1, taken_ref.shape[0]):
@@ -246,32 +417,6 @@
     return call(
         spread_kernel, shaped((peers,) + taken.shape[1:], F32), [VMEM], VMEM, moved=400000
     )(taken)
-
-
-def residual_kernel(sums_ref, basis_ref, image_ref, degree_ref, residual_ref, tiles_ref):
-    sums = sums_ref[0]
-    for peer in range(1, sums_ref.shape[0]):
-        sums = sums + sums_ref[peer]
-    theta = sums[:, 0:1] / sums[:, 1:2]
-    for block in range(RB):
-        at = columns(block)
-        residual = (image_ref[:, at] - theta * basis_ref[:, at]) / degree_ref[:, at]
-        residual_ref[:, at] = residual
-        tiles_ref[block] = residual.astype(BF16)
-
-
-def make_residual(sums, basis, image, degree):
-    return call(
-        residual_kernel,
-        (shaped(basis.shape, F32), shaped((RB, K, BS), BF16)),
-        [VMEM] * 4,
-        (VMEM, VMEM),
-        moved=1000000,
-    )(sums, basis, image, degree)
-
-
-def iota2(shape, axis):
-    return lax.broadcasted_iota(jnp.int32, shape, axis)
 
 
 def square(value, wide_ref):
@@ -313,20 +458,45 @@
 
 
 def gram_kernel(
-    list_ref, count_ref, lookup_ref, coupling_ref, own_ref, basis_ref, image_ref, residual_ref, degree_ref,
-    previous_ref, previous_image_ref, residual_image_ref, packed_ref, acc_ref, held, sems, stacked, stacked_image,
-    wide_ref,
-):
+    list_ref, count_ref, halo_ref, coupling_ref, own_ref, scaled_ref, kept_ref, basis_ref, image_ref, degree_ref,
+    previous_ref, previous_image_ref, residual_ref, residual_image_ref, packed_ref, acc_ref, held, sems, side_ref,
+    quotient_ref, stacked, stacked_image, wide_ref,
+):
+    issue(count_ref[1], list_ref, coupling_ref, held, sems)
     acc_ref[...] = own_ref[...]
-    apply_list(count_ref[1], list_ref, lookup_ref, coupling_ref, held, sems, acc_ref)
+    peers = halo_ref.shape[0] // EXTRA
+    total = jnp.zeros((K, BS), F32)
+    for peer in range(peers):
+        side = halo_ref[peer * EXTRA + SEND]
+        side_ref[peer * K : (peer + 1) * K, :] = side
+        total = total + side.astype(F32)
+    side = side_ref[...]
+    for j in range(SEND):
+        spread = (iota2((BS, BS), 0) == j).astype(F32).astype(BF16)
+        quotient_ref[j] = dot_nn(side, spread).reshape(peers, K, BS)
+    lane = iota2((K, BS), 1)
+    top = jnp.sum(jnp.where((lane >= 8) & (lane <= 10), total, 0.0), axis=1, keepdims=True)
+    bottom = jnp.sum(jnp.where((lane >= 11) & (lane <= 13), total, 0.0), axis=1, keepdims=True)
+    theta = top / bottom
+
+    def multiply(tile, side, weights):
+        return dot_nt(halo_ref[tile], weights)
+
+    def add(at, row, side, product):
+        acc_ref[row] = acc_ref[row] + (product + quotient_ref[side & 7, side >> 3] * kept_ref[at])
+
+    work(count_ref[1], list_ref, coupling_ref, held, sems, multiply, add)
     stacked[0:16] = basis_ref[...]
-    stacked[16:32] = residual_ref[...]
     stacked[32:48] = previous_ref[...]
     stacked_image[0:16] = image_ref[...]
     stacked_image[32:48] = previous_image_ref[...]
     for block in range(RB):
         at = columns(block)
-        value = degree_ref[:, at] * residual_ref[:, at] - acc_ref[block]
+        degree = degree_ref[block : block + 1, :]
+        residual = (image_ref[:, at] - theta * basis_ref[:, at]) / degree
+        residual_ref[:, at] = residual
+        stacked[16:32, at] = residual
+        value = degree * residual - (acc_ref[block] - theta * scaled_ref[block])
         residual_image_ref[:, at] = value
         stacked_image[16:32, at] = value
     gram_b = dot_nt(stacked[...], stacked[...], HIGHEST)
@@ -337,20 +507,26 @@
 
 
 def make_grams(
-    halo_list, counts, halo_tiles, coupling, own, basis, image, residual, degree, previous, previous_image, n_dom
+    halo_list, counts, halo_tiles, coupling, own, scaled, kept, basis, image, degree, previous, previous_image, n_dom
 ):
     width = basis.shape[1]
     return call(
         gram_kernel,
-        (shaped(basis.shape, F32), shaped((n_dom, 24, BS), F32)),
-        [SMEM, SMEM, VMEM, HBM] + [VMEM] * 7,
-        (VMEM, VMEM),
+        (shaped(basis.shape, F32), shaped(basis.shape, F32), shaped((n_dom, 24, BS), F32)),
+        [SMEM, SMEM, VMEM, HBM] + [VMEM] * 8,
+        (VMEM, VMEM, VMEM),
         (pltpu.VMEM((RB + 1, K, BS), F32),)
         + HELD
-        + (pltpu.VMEM((48, width), F32), pltpu.VMEM((48, width), F32), pltpu.VMEM((BS, BS), F32)),
+        + (
+            pltpu.VMEM((n_dom * K, BS), BF16),
+            pltpu.VMEM((SEND, n_dom, K, BS), F32),
+            pltpu.VMEM((48, width), F32),
+            pltpu.VMEM((48, width), F32),
+            pltpu.VMEM((BS, BS), F32),
+        ),
         flops=2 * SLOTS * K * BS * BS,
         moved=10000000,
-    )(halo_list, counts, halo_tiles, coupling, own, basis, image, residual, degree, previous, previous_image)
+    )(halo_list, counts, halo_tiles, coupling, own, scaled, kept, basis, image, degree, previous, previous_image)
 
 
 def inverse_factor(gram, n):
@@ -428,21 +604,23 @@
     part = n_row * RB
     place = lax.axis_index("row").astype(jnp.int32).reshape(1)
     send_list = send_lists.reshape(n_dom * SEND)
-    degree = degree.reshape(1, -1)
+    degree = degree.reshape(RB, BS)
     own_list, halo_list, counts = make_lists(slot_row, slot_column, live_slots, part)
 
-    part_tiles, chosen = select(gather_row(cast_tiles(basis), n_row), place, send_list, n_row)
+    gathered = gather_row(cast_tiles(basis, degree), n_row, HALF + 2)
+    part_tiles, inverse, chosen = first_select(gathered, place, send_list, n_row)
     halo_tiles = to_all(chosen, "dom")
-    own = couple_own(own_list, counts, part_tiles, coupling)
-    image, sums = make_image(halo_list, counts, halo_tiles, coupling, own, basis, degree, n_dom)
-    sums = to_all(add_and_repeat(to_all(sums, "dom"), n_row), "row")
-    residual, tiles = make_residual(sums, basis, image, degree)
-
-    part_tiles, chosen = select(gather_row(tiles, n_row), place, send_list, n_row)
-    halo_tiles = to_all(chosen, "dom")
-    own = couple_own(own_list, counts, part_tiles, coupling)
-    residual_image, packed = make_grams(
-        halo_list, counts, halo_tiles, coupling, own, basis, image, residual, degree, previous, previous_image, n_dom
+    own, own_scaled, own_kept = first_own(own_list, counts, part_tiles, inverse, coupling)
+    image, tiles = make_image(halo_list, counts, halo_tiles, coupling, own, basis, degree)
+
+    gathered = gather_row(tiles, n_row, HALF)
+    part_tiles, chosen, table = second_select(gathered, place, send_list, picks(send_list), n_row)
+    far_tiles = to_all(chosen, "dom")
+    own, scaled, kept = second_own(
+        own_list, halo_list, counts, part_tiles, table, own_kept, own_scaled, halo_tiles, coupling, n_row
+    )
+    residual, residual_image, packed = make_grams(
+        halo_list, counts, far_tiles, coupling, own, scaled, kept, basis, image, degree, previous, previous_image, n_dom
     )
     packed = to_all(add_and_repeat(to_all(packed, "dom"), n_row), "row")
     root_rows = math.sqrt(basis.shape[1] * n_dom * n_row)

time: 182 us -> 168 us (0.923)
  blocking collectives: 54.9 us -> 29.5 us
  local copies, waits for them, and re-layouts: 6.08 us -> 15.1 us
  waiting for transfers between devices: 36.9 us -> 39 us
    all_to_all x4 -> x2, blocking collectives: 54.9 us -> 29.5 us  [to_all(): return lax.all_to_all(value, axis, split_axis=0, concat_axis=0, tiled=True)]
    ppermute x6, waiting for transfers between devices: 0.02 us -> 15.9 us  [gather_row(): from_above = lax.ppermute(from_above, 'row', down)]
    ppermute x6, waiting for transfers between devices: 14.9 us -> 0.02 us  [gather_row(): from_below = lax.ppermute(from_below, 'row', up)]
    unnamed x25 -> x43, local copies, waits for them, and re-layouts: 5.97 us -> 14.9 us
    ppermute x2, waiting for transfers between devices: 3.21 us -> 7.19 us  [gather_row(): far_low = lax.ppermute(from_below[:half], 'row', up)]
    all_to_all x2, waiting for transfers between devices: 18.8 us -> 15.4 us  [to_all(): return lax.all_to_all(value, axis, split_axis=0, concat_axis=0, tiled=True)]
    pallas_call x9 -> x8, Pallas kernels: 24.8 us -> 25.8 us  [the longest x1 5.56 us: make_lists(): call(functools.partial(list_kernel, part), (shaped((4, LEN), jnp.int32),...]
  transfers between devices with their start and end apart: 18 -> 18, of which waited for: 10 -> 11; matrix products, arithmetic and copies ran while one was open for 0% -> 1% of each run, Pallas kernels for 7% -> 8%
where the time goes in v2:
time: 168 us; the launch traced here: 167 us
  starting transfers between devices  47 us (28%)
  waiting for transfers between devices  39 us (23%)
  Pallas kernels  34.5 us (21%)
  blocking collectives  29.5 us (18%)
  local copies, waits for them, and re-layouts  15.1 us (9%)
    all_to_all x2, blocking collectives, to_all(): return lax.all_to_all(value, axis, split_axis=0, concat_axis=0, tiled=True)  29.5 us
    all_to_all x2, starting transfers between devices, to_all(): return lax.all_to_all(value, axis, split_axis=0, concat_axis=0, tiled=True)  22.2 us
    ppermute x6, starting transfers between devices, gather_row(): from_above = lax.ppermute(from_above, 'row', down)  16.9 us
    ppermute x6, waiting for transfers between devices, gather_row(): from_above = lax.ppermute(from_above, 'row', down)  15.9 us
    all_to_all x2, waiting for transfers between devices, to_all(): return lax.all_to_all(value, axis, split_axis=0, concat_axis=0, tiled=True)  15.4 us
    unnamed x43, local copies, waits for them, and re-layouts  14.9 us
    pallas_call x1, Pallas kernels, finish(): call(functools.partial(final_kernel, root_rows), (shaped(basis.shape, F32...  8.67 us
    ppermute x2, waiting for transfers between devices, gather_row(): far_low = lax.ppermute(from_below[:half], 'row', up)  7.19 us
  transfers between devices with their start and end apart: 18, of which 11 were waited for; matrix products, arithmetic and copies ran while one was open for 1% of the time, Pallas kernels for 8%

profile of v2, /device:TPU:1, one launch (start us, length us, event | category | flops | bytes accessed | tf_op | source)
XLA Modules:
  0.0 166.9 jit_solution(17820471108751687339)
XLA Ops:
  2.3 6.5 %collective-permute-start.1 = (bf16[36,16,128]{2,1,0:T(8,128)(2,1)S(1)}, bf16[36,16,128]{2,1,0:T(8,128)(2,1)S(1)}, u32[]{:S(2)}, u32[]{:S(2)}) collective-permute-start(bf16[36,16,128]{2,1,0:T(8,128)(2,1)S(1)} %shard_map.105.refs_0_), channel_id=1, source_target_pairs={{0,7},{1,0},{2,1},{3,2},{4,3},{5,4},{6,5},{7,6},{8,15},{9,8},{10,9... | collective-permute-start | bytes 442376 | tf_op jit(solution)/shard_map/ppermute | solution.py:137
  8.8 2.5 %collective-permute-done.1.refs_2_ = bf16[36,16,128]{2,1,0:T(8,128)(2,1)S(1)} collective-permute-done((bf16[36,16,128]{2,1,0:T(8,128)(2,1)S(1)}, bf16[36,16,128]{2,1,0:T(8,128)(2,1)S(1)}, u32[]{:S(2)}, u32[]{:S(2)}) %collective-permute-start.1) | collective-permute-done | bytes 147488 | tf_op jit(solution)/shard_map/ppermute | solution.py:137
  11.3 3.4 %collective-permute-start.3 = (bf16[36,16,128]{2,1,0:T(8,128)(2,1)S(1)}, bf16[36,16,128]{2,1,0:T(8,128)(2,1)S(1)}, u32[]{:S(2)}, u32[]{:S(2)}) collective-permute-start(bf16[36,16,128]{2,1,0:T(8,128)(2,1)S(1)} %collective-permute-done.1.refs_2_), channel_id=1, source_target_pairs={{0,7},{1,0},{2,1},{3,2},{4,3},{5,4},{6,5},{7,6},{8,15},{9,8},{10,9... | collective-permute-start | bytes 442376 | tf_op jit(solution)/shard_map/ppermute | solution.py:137
  14.7 2.1 %collective-permute-done.3.refs_4_ = bf16[36,16,128]{2,1,0:T(8,128)(2,1)S(1)} collective-permute-done((bf16[36,16,128]{2,1,0:T(8,128)(2,1)S(1)}, bf16[36,16,128]{2,1,0:T(8,128)(2,1)S(1)}, u32[]{:S(2)}, u32[]{:S(2)}) %collective-permute-start.3) | collective-permute-done | bytes 147488 | tf_op jit(solution)/shard_map/ppermute | solution.py:137
  16.8 3.1 %collective-permute-start.5 = (bf16[36,16,128]{2,1,0:T(8,128)(2,1)S(1)}, bf16[36,16,128]{2,1,0:T(8,128)(2,1)S(1)}, u32[]{:S(2)}, u32[]{:S(2)}) collective-permute-start(bf16[36,16,128]{2,1,0:T(8,128)(2,1)S(1)} %collective-permute-done.3.refs_4_), channel_id=1, source_target_pairs={{0,7},{1,0},{2,1},{3,2},{4,3},{5,4},{6,5},{7,6},{8,15},{9,8},{10,9... | collective-permute-start | bytes 442376 | tf_op jit(solution)/shard_map/ppermute | solution.py:137
  19.9 2.1 %collective-permute-done.5.refs_6_ = bf16[36,16,128]{2,1,0:T(8,128)(2,1)S(1)} collective-permute-done((bf16[36,16,128]{2,1,0:T(8,128)(2,1)S(1)}, bf16[36,16,128]{2,1,0:T(8,128)(2,1)S(1)}, u32[]{:S(2)}, u32[]{:S(2)}) %collective-permute-start.5) | collective-permute-done | bytes 147488 | tf_op jit(solution)/shard_map/ppermute | solution.py:137
  22.1 3.1 %collective-permute-start.7 = (bf16[18,16,128]{2,1,0:T(8,128)(2,1)S(1)}, bf16[18,16,128]{2,1,0:T(8,128)(2,1)S(1)}, u32[]{:S(2)}, u32[]{:S(2)}) collective-permute-start(bf16[18,16,128]{2,1,0:T(8,128)(2,1)S(1)} %slice.22), channel_id=1, source_target_pairs={{0,7},{1,0},{2,1},{3,2},{4,3},{5,4},{6,5},{7,6},{8,15},{9,8},{10,9... | collective-permute-start | bytes 221192 | tf_op jit(solution)/shard_map/ppermute | solution.py:140
  26.6 3.1 %collective-permute-done.6.refs_7_ = bf16[18,16,128]{2,1,0:T(8,128)(2,1)S(1)} collective-permute-done((bf16[18,16,128]{2,1,0:T(8,128)(2,1)S(1)}, bf16[18,16,128]{2,1,0:T(8,128)(2,1)S(1)}, u32[]{:S(2)}, u32[]{:S(2)}) %collective-permute-start.6) | collective-permute-done | bytes 73760 | tf_op jit(solution)/shard_map/ppermute | solution.py:139
  29.7 2.3 %shard_map.106 = (bf16[256,16,128]{2,1,0:T(8,128)(2,1)S(1)}, f32[256,128]{1,0:T(8,128)S(1)}, bf16[288,16,128]{2,1,0:T(8,128)(2,1)}) custom-call(s32[1]{0:T(128)} %bitcast.place_ref, s32[256]{0:T(256)S(1)} %reshape.19.send_ref, bf16[36,16,128]{2,1,0:T(8,128)(2,1)S(1)} %shard_map.105.refs_0_, bf16[36,16,128]{2,1,0:T(8,128)(2,1)S(1)} %collective-permute-done.refs_1_, ...), custom_call_target="tpu_custom_call" | custom-call | bytes 3000000 | tf_op jit(solution)/shard_map/pallas_call | solution.py:179
  31.9 12.4 %all-to-all-start = ((bf16[288,16,128]{2,1,0:T(8,128)(2,1)}), bf16[288,16,128]{2,1,0:T(8,128)(2,1)S(1)}, u32[]{:S(2)}, u32[]{:S(2)}) async-start(bf16[288,16,128]{2,1,0:T(8,128)(2,1)} %get-tuple-element.24), calls=%async_computation | async-start | bytes 2359296 | tf_op jit(solution)/shard_map/all_to_all | solution.py:597
  45.0 5.6 %shard_map.104 = (s32[4,264]{1,0:T(4,128)S(1)}, s32[4,264]{1,0:T(4,128)S(1)}, s32[2]{0:T(128)S(1)}) custom-call(s32[256]{0:T(256)S(1)} %copy-done.18, s32[256]{0:T(256)S(1)} %copy-done.19, s32[1]{0:T(128)S(6)} %copy.14.live_ref), custom_call_target="tpu_custom_call" | custom-call | bytes 20000 | tf_op jit(solution)/shard_map/pallas_call | solution.py:97
  50.6 2.6 %shard_map.107 = (f32[33,16,128]{2,1,0:T(8,128)S(1)}, f32[33,16,128]{2,1,0:T(8,128)S(1)}, f32[256,16,128]{2,1,0:T(8,128)S(1)}) custom-call(s32[4,264]{1,0:T(4,128)S(1)} %get-tuple-element.25.list_ref.own_list, s32[2]{0:T(128)S(1)} %get-tuple-element.23.count_ref, bf16[256,16,128]{2,1,0:T(8,128)(2,1)S(1)} %get-tuple-element.26.part_ref, ...), custom_call_target="tpu_custom_call" | custom-call | flops 134217728 | bytes 10000000 | tf_op jit(solution)/shard_map/pallas_call | solution.py:297
  53.2 1.3 copy-done.2
  55.2 7.5 %all-to-all-done.halo_ref = bf16[288,16,128]{2,1,0:T(8,128)(2,1)S(1)} async-done(((bf16[288,16,128]{2,1,0:T(8,128)(2,1)}), bf16[288,16,128]{2,1,0:T(8,128)(2,1)S(1)}, u32[]{:S(2)}, u32[]{:S(2)}) %all-to-all-start) | async-done | bytes 1179680 | tf_op jit(solution)/shard_map/all_to_all | solution.py:597
  62.7 3.5 %shard_map.108 = (f32[16,4096]{1,0:T(8,128)S(1)}, bf16[33,16,128]{2,1,0:T(8,128)(2,1)S(1)}) custom-call(s32[4,264]{1,0:T(4,128)S(1)} %get-tuple-element.22.list_ref.halo_list, s32[2]{0:T(128)S(1)} %get-tuple-element.23.count_ref, bf16[288,16,128]{2,1,0:T(8,128)(2,1)S(1)} %all-to-all-done.halo_ref, bf16[256,128,128]{2,1,0:T(8,128)(2,1)} %coupling_ref.7, ...), custom_call_target="tpu_custom_call" | custom-call | flops 134217728 | bytes 8000000 | tf_op jit(solution)/shard_map/pallas_call | solution.py:347
  66.4 1.3 collective-permute-start.8
  67.9 4.0 %collective-permute-done.9.refs_2_ = bf16[33,16,128]{2,1,0:T(8,128)(2,1)S(1)} collective-permute-done((bf16[33,16,128]{2,1,0:T(8,128)(2,1)S(1)}, bf16[33,16,128]{2,1,0:T(8,128)(2,1)S(1)}, u32[]{:S(2)}, u32[]{:S(2)}) %collective-permute-start.9) | collective-permute-done | bytes 135200 | tf_op jit(solution)/shard_map/ppermute | solution.py:137
  73.3 3.4 %collective-permute-done.11.refs_4_ = bf16[33,16,128]{2,1,0:T(8,128)(2,1)S(1)} collective-permute-done((bf16[33,16,128]{2,1,0:T(8,128)(2,1)S(1)}, bf16[33,16,128]{2,1,0:T(8,128)(2,1)S(1)}, u32[]{:S(2)}, u32[]{:S(2)}) %collective-permute-start.11) | collective-permute-done | bytes 135200 | tf_op jit(solution)/shard_map/ppermute | solution.py:137
  76.7 2.4 %collective-permute-start.13 = (bf16[33,16,128]{2,1,0:T(8,128)(2,1)S(1)}, bf16[33,16,128]{2,1,0:T(8,128)(2,1)S(1)}, u32[]{:S(2)}, u32[]{:S(2)}) collective-permute-start(bf16[33,16,128]{2,1,0:T(8,128)(2,1)S(1)} %collective-permute-done.11.refs_4_), channel_id=1, source_target_pairs={{0,7},{1,0},{2,1},{3,2},{4,3},{5,4},{6,5},{7,6},{8,15},{9,8},{10,9... | collective-permute-start | bytes 405512 | tf_op jit(solution)/shard_map/ppermute | solution.py:137
  79.3 1.8 %collective-permute-done.13.refs_6_ = bf16[33,16,128]{2,1,0:T(8,128)(2,1)S(1)} collective-permute-done((bf16[33,16,128]{2,1,0:T(8,128)(2,1)S(1)}, bf16[33,16,128]{2,1,0:T(8,128)(2,1)S(1)}, u32[]{:S(2)}, u32[]{:S(2)}) %collective-permute-start.13) | collective-permute-done | bytes 135200 | tf_op jit(solution)/shard_map/ppermute | solution.py:137
  81.1 3.1 %collective-permute-start.15 = (bf16[17,16,128]{2,1,0:T(8,128)(2,1)S(1)}, bf16[17,16,128]{2,1,0:T(8,128)(2,1)S(1)}, u32[]{:S(2)}, u32[]{:S(2)}) collective-permute-start(bf16[17,16,128]{2,1,0:T(8,128)(2,1)S(1)} %slice.24), channel_id=1, source_target_pairs={{0,7},{1,0},{2,1},{3,2},{4,3},{5,4},{6,5},{7,6},{8,15},{9,8},{10,9... | collective-permute-start | bytes 208904 | tf_op jit(solution)/shard_map/ppermute | solution.py:140
  84.5 4.1 %collective-permute-done.14.refs_7_ = bf16[16,16,128]{2,1,0:T(8,128)(2,1)S(1)} collective-permute-done((bf16[16,16,128]{2,1,0:T(8,128)(2,1)S(1)}, bf16[16,16,128]{2,1,0:T(8,128)(2,1)S(1)}, u32[]{:S(2)}, u32[]{:S(2)}) %collective-permute-start.14) | collective-permute-done | bytes 65568 | tf_op jit(solution)/shard_map/ppermute | solution.py:139
  88.6 1.4 shard_map.109
  92.0 9.9 %all-to-all-start.1 = ((bf16[288,16,128]{2,1,0:T(8,128)(2,1)}), bf16[288,16,128]{2,1,0:T(8,128)(2,1)S(1)}, u32[]{:S(2)}, u32[]{:S(2)}) async-start(bf16[288,16,128]{2,1,0:T(8,128)(2,1)} %copy-done.5), calls=%async_computation.1 | async-start | bytes 2359296 | tf_op jit(solution)/shard_map/all_to_all | solution.py:597
  104.1 5.4 %shard_map.110 = (f32[33,16,128]{2,1,0:T(8,128)S(1)}, f32[33,16,128]{2,1,0:T(8,128)S(1)}, f32[256,16,128]{2,1,0:T(8,128)S(1)}) custom-call(s32[4,264]{1,0:T(4,128)S(1)} %get-tuple-element.25.list_ref.own_list, s32[4,264]{1,0:T(4,128)S(1)} %get-tuple-element.22.list_ref.halo_list, s32[2]{0:T(128)S(1)} %get-tuple-element.23.count_ref, ...), custom_call_target="tpu_custom_call" | custom-call | flops 268435456 | bytes 10000000 | tf_op jit(solution)/shard_map/pallas_call | solution.py:395
  109.5 1.3 copy-done.3
  112.2 8.0 %all-to-all-done.1.halo_ref = bf16[288,16,128]{2,1,0:T(8,128)(2,1)S(1)} async-done(((bf16[288,16,128]{2,1,0:T(8,128)(2,1)}), bf16[288,16,128]{2,1,0:T(8,128)(2,1)S(1)}, u32[]{:S(2)}, u32[]{:S(2)}) %all-to-all-start.1) | async-done | bytes 1179680 | tf_op jit(solution)/shard_map/all_to_all | solution.py:597
  120.2 1.6 copy-done.4
  123.7 5.0 %shard_map.111 = (f32[16,4096]{1,0:T(8,128)S(1)}, f32[16,4096]{1,0:T(8,128)S(1)}, f32[32,24,128]{2,1,0:T(8,128)S(1)}) custom-call(s32[4,264]{1,0:T(4,128)S(1)} %get-tuple-element.22.list_ref.halo_list, s32[2]{0:T(128)S(1)} %get-tuple-element.23.count_ref, bf16[288,16,128]{2,1,0:T(8,128)(2,1)S(1)} %all-to-all-done.1.halo_ref, ...), custom_call_target="tpu_custom_call" | custom-call | flops 134217728 | bytes 10000000 | tf_op jit(solution)/shard_map/pallas_call | solution.py:513
  128.7 19.1 %all_to_all.20.taken_ref = f32[32,24,128]{2,1,0:T(8,128)S(1)} all-to-all(f32[32,24,128]{2,1,0:T(8,128)S(1)} %get-tuple-element.39), channel_id=1, replica_groups=mesh['dom'=32,'row'=8] {'dom'}, dimensions={0} | all-to-all | bytes 786432 | tf_op jit(solution)/shard_map/all_to_all | solution.py:597
  147.8 10.4 %all_to_all.21.taken_ref = f32[8,24,128]{2,1,0:T(8,128)S(1)} all-to-all(f32[8,24,128]{2,1,0:T(8,128)S(1)} %shard_map.112), channel_id=1, replica_groups=mesh['dom'=32,'row'=8] {'row'}, dimensions={0} | all-to-all | bytes 196608 | tf_op jit(solution)/shard_map/all_to_all | solution.py:597
  158.3 8.7 %shard_map.113 = (f32[16,4096]{1,0:T(8,128)}, f32[16,4096]{1,0:T(8,128)}) custom-call(f32[8,24,128]{2,1,0:T(8,128)S(1)} %all_to_all.21.taken_ref, f32[16,4096]{1,0:T(8,128)S(1)} %copy-done.1, f32[16,4096]{1,0:T(8,128)S(1)} %get-tuple-element.40.residual_ref, f32[16,4096]{1,0:T(8,128)S(1)} %copy-done.8, f32[16,4096]{1,0:T(8,128)S(1)} %get-tuple-element.38.image_ref, ...), custom_call_target="tpu_custom_call" | custom-call | flops 1000000 | bytes 3000000 | tf_op jit(solution)/shard_map/pallas_call | solution.py:585
  (71 shorter events, 13.6 us)
Async XLA Ops:
  0.6 1.0 copy-start
  2.3 42.7 %copy-start.18 = (s32[256]{0:T(256)S(1)}, s32[256]{0:T(256)}, u32[]{:S(2)}) copy-start(s32[256]{0:T(256)} %row_ref.1) | copy-start | bytes 3076
  2.3 42.7 %copy-start.19 = (s32[256]{0:T(256)S(1)}, s32[256]{0:T(256)}, u32[]{:S(2)}) copy-start(s32[256]{0:T(256)} %column_ref.1) | copy-start | bytes 3076
  2.3 9.0 %collective-permute-start.1 = (bf16[36,16,128]{2,1,0:T(8,128)(2,1)S(1)}, bf16[36,16,128]{2,1,0:T(8,128)(2,1)S(1)}, u32[]{:S(2)}, u32[]{:S(2)}) collective-permute-start(bf16[36,16,128]{2,1,0:T(8,128)(2,1)S(1)} %shard_map.105.refs_0_), channel_id=1, source_target_pairs={{0,7},{1,0},{2,1},{3,2},{4,3},{5,4},{6,5},{7,6},{8,15},{9,8},{10,9... | collective-permute-start | bytes 442376 | tf_op jit(solution)/shard_map/ppermute | solution.py:137
  8.8 5.9 %collective-permute-start = (bf16[36,16,128]{2,1,0:T(8,128)(2,1)S(1)}, bf16[36,16,128]{2,1,0:T(8,128)(2,1)S(1)}, u32[]{:S(2)}, u32[]{:S(2)}) collective-permute-start(bf16[36,16,128]{2,1,0:T(8,128)(2,1)S(1)} %shard_map.105.refs_0_), channel_id=1, source_target_pairs={{0,1},{1,2},{2,3},{3,4},{4,5},{5,6},{6,7},{7,0},{8,9},{9,10},{10,1... | collective-permute-start | bytes 442376 | tf_op jit(solution)/shard_map/ppermute | solution.py:136
  11.3 5.5 %collective-permute-start.3 = (bf16[36,16,128]{2,1,0:T(8,128)(2,1)S(1)}, bf16[36,16,128]{2,1,0:T(8,128)(2,1)S(1)}, u32[]{:S(2)}, u32[]{:S(2)}) collective-permute-start(bf16[36,16,128]{2,1,0:T(8,128)(2,1)S(1)} %collective-permute-done.1.refs_2_), channel_id=1, source_target_pairs={{0,7},{1,0},{2,1},{3,2},{4,3},{5,4},{6,5},{7,6},{8,15},{9,8},{10,9... | collective-permute-start | bytes 442376 | tf_op jit(solution)/shard_map/ppermute | solution.py:137
  14.7 5.2 %collective-permute-start.2 = (bf16[36,16,128]{2,1,0:T(8,128)(2,1)S(1)}, bf16[36,16,128]{2,1,0:T(8,128)(2,1)S(1)}, u32[]{:S(2)}, u32[]{:S(2)}) collective-permute-start(bf16[36,16,128]{2,1,0:T(8,128)(2,1)S(1)} %collective-permute-done.refs_1_), channel_id=1, source_target_pairs={{0,1},{1,2},{2,3},{3,4},{4,5},{5,6},{6,7},{7,0},{8,9},{9,10},{10,1... | collective-permute-start | bytes 442376 | tf_op jit(solution)/shard_map/ppermute | solution.py:136
  16.8 5.2 %collective-permute-start.5 = (bf16[36,16,128]{2,1,0:T(8,128)(2,1)S(1)}, bf16[36,16,128]{2,1,0:T(8,128)(2,1)S(1)}, u32[]{:S(2)}, u32[]{:S(2)}) collective-permute-start(bf16[36,16,128]{2,1,0:T(8,128)(2,1)S(1)} %collective-permute-done.3.refs_4_), channel_id=1, source_target_pairs={{0,7},{1,0},{2,1},{3,2},{4,3},{5,4},{6,5},{7,6},{8,15},{9,8},{10,9... | collective-permute-start | bytes 442376 | tf_op jit(solution)/shard_map/ppermute | solution.py:137
  19.9 5.2 %collective-permute-start.4 = (bf16[36,16,128]{2,1,0:T(8,128)(2,1)S(1)}, bf16[36,16,128]{2,1,0:T(8,128)(2,1)S(1)}, u32[]{:S(2)}, u32[]{:S(2)}) collective-permute-start(bf16[36,16,128]{2,1,0:T(8,128)(2,1)S(1)} %collective-permute-done.2.refs_3_), channel_id=1, source_target_pairs={{0,1},{1,2},{2,3},{3,4},{4,5},{5,6},{6,7},{7,0},{8,9},{9,10},{10,1... | collective-permute-start | bytes 442376 | tf_op jit(solution)/shard_map/ppermute | solution.py:136
  22.1 4.5 %collective-permute-start.7 = (bf16[18,16,128]{2,1,0:T(8,128)(2,1)S(1)}, bf16[18,16,128]{2,1,0:T(8,128)(2,1)S(1)}, u32[]{:S(2)}, u32[]{:S(2)}) collective-permute-start(bf16[18,16,128]{2,1,0:T(8,128)(2,1)S(1)} %slice.22), channel_id=1, source_target_pairs={{0,7},{1,0},{2,1},{3,2},{4,3},{5,4},{6,5},{7,6},{8,15},{9,8},{10,9... | collective-permute-start | bytes 221192 | tf_op jit(solution)/shard_map/ppermute | solution.py:140
  25.2 4.5 %collective-permute-start.6 = (bf16[18,16,128]{2,1,0:T(8,128)(2,1)S(1)}, bf16[18,16,128]{2,1,0:T(8,128)(2,1)S(1)}, u32[]{:S(2)}, u32[]{:S(2)}) collective-permute-start(bf16[18,16,128]{2,1,0:T(8,128)(2,1)S(1)} %slice.21), channel_id=1, source_target_pairs={{0,1},{1,2},{2,3},{3,4},{4,5},{5,6},{6,7},{7,0},{8,9},{9,10},{10,1... | collective-permute-start | bytes 221192 | tf_op jit(solution)/shard_map/ppermute | solution.py:139
  31.9 30.7 %all-to-all-start = ((bf16[288,16,128]{2,1,0:T(8,128)(2,1)}), bf16[288,16,128]{2,1,0:T(8,128)(2,1)S(1)}, u32[]{:S(2)}, u32[]{:S(2)}) async-start(bf16[288,16,128]{2,1,0:T(8,128)(2,1)} %get-tuple-element.24), calls=%async_computation | async-start | bytes 2359296 | tf_op jit(solution)/shard_map/all_to_all | solution.py:597
  50.5 12.1 %copy-start.1 = (f32[16,4096]{1,0:T(8,128)S(1)}, f32[16,4096]{1,0:T(8,128)}, u32[]{:S(2)}) copy-start(f32[16,4096]{1,0:T(8,128)} %basis_ref.5) | copy-start | bytes 786436
  50.6 12.1 %copy-start.17 = (f32[4096]{0:T(1024)S(1)}, f32[4096]{0:T(1024)}, u32[]{:S(2)}) copy-start(f32[4096]{0:T(1024)} %param.12) | copy-start | bytes 49156
  53.2 1.3 copy-start.2
  62.7 16.5 %copy-start.20 = (s32[1,32,8]{1,2,0:T(8,128)S(1)}, s32[1,32,8]{1,2,0:T(8,128)}, u32[]{:S(2)}) copy-start(s32[1,32,8]{1,2,0:T(8,128)} %param.16) | copy-start | bytes 3076
  66.2 5.6 %collective-permute-start.9 = (bf16[33,16,128]{2,1,0:T(8,128)(2,1)S(1)}, bf16[33,16,128]{2,1,0:T(8,128)(2,1)S(1)}, u32[]{:S(2)}, u32[]{:S(2)}) collective-permute-start(bf16[33,16,128]{2,1,0:T(8,128)(2,1)S(1)} %get-tuple-element.29.refs_0_), channel_id=1, source_target_pairs={{0,7},{1,0},{2,1},{3,2},{4,3},{5,4},{6,5},{7,6},{8,15},{9,8},{10,9... | collective-permute-start | bytes 405512 | tf_op jit(solution)/shard_map/ppermute | solution.py:137
  66.4 6.7 %collective-permute-start.8 = (bf16[33,16,128]{2,1,0:T(8,128)(2,1)S(1)}, bf16[33,16,128]{2,1,0:T(8,128)(2,1)S(1)}, u32[]{:S(2)}, u32[]{:S(2)}) collective-permute-start(bf16[33,16,128]{2,1,0:T(8,128)(2,1)S(1)} %get-tuple-element.29.refs_0_), channel_id=1, source_target_pairs={{0,1},{1,2},{2,3},{3,4},{4,5},{5,6},{6,7},{7,0},{8,9},{9,10},{10,1... | collective-permute-start | bytes 405512 | tf_op jit(solution)/shard_map/ppermute | solution.py:136
  71.9 4.8 %collective-permute-start.11 = (bf16[33,16,128]{2,1,0:T(8,128)(2,1)S(1)}, bf16[33,16,128]{2,1,0:T(8,128)(2,1)S(1)}, u32[]{:S(2)}, u32[]{:S(2)}) collective-permute-start(bf16[33,16,128]{2,1,0:T(8,128)(2,1)S(1)} %collective-permute-done.9.refs_2_), channel_id=1, source_target_pairs={{0,7},{1,0},{2,1},{3,2},{4,3},{5,4},{6,5},{7,6},{8,15},{9,8},{10,9... | collective-permute-start | bytes 405512 | tf_op jit(solution)/shard_map/ppermute | solution.py:137
  73.2 6.0 %collective-permute-start.10 = (bf16[33,16,128]{2,1,0:T(8,128)(2,1)S(1)}, bf16[33,16,128]{2,1,0:T(8,128)(2,1)S(1)}, u32[]{:S(2)}, u32[]{:S(2)}) collective-permute-start(bf16[33,16,128]{2,1,0:T(8,128)(2,1)S(1)} %collective-permute-done.8.refs_1_), channel_id=1, source_target_pairs={{0,1},{1,2},{2,3},{3,4},{4,5},{5,6},{6,7},{7,0},{8,9},{9,10},{10,1... | collective-permute-start | bytes 405512 | tf_op jit(solution)/shard_map/ppermute | solution.py:136
  76.7 4.4 %collective-permute-start.13 = (bf16[33,16,128]{2,1,0:T(8,128)(2,1)S(1)}, bf16[33,16,128]{2,1,0:T(8,128)(2,1)S(1)}, u32[]{:S(2)}, u32[]{:S(2)}) collective-permute-start(bf16[33,16,128]{2,1,0:T(8,128)(2,1)S(1)} %collective-permute-done.11.refs_4_), channel_id=1, source_target_pairs={{0,7},{1,0},{2,1},{3,2},{4,3},{5,4},{6,5},{7,6},{8,15},{9,8},{10,9... | collective-permute-start | bytes 405512 | tf_op jit(solution)/shard_map/ppermute | solution.py:137
  79.1 5.1 %collective-permute-start.12 = (bf16[33,16,128]{2,1,0:T(8,128)(2,1)S(1)}, bf16[33,16,128]{2,1,0:T(8,128)(2,1)S(1)}, u32[]{:S(2)}, u32[]{:S(2)}) collective-permute-start(bf16[33,16,128]{2,1,0:T(8,128)(2,1)S(1)} %collective-permute-done.10.refs_3_), channel_id=1, source_target_pairs={{0,1},{1,2},{2,3},{3,4},{4,5},{5,6},{6,7},{7,0},{8,9},{9,10},{10,1... | collective-permute-start | bytes 405512 | tf_op jit(solution)/shard_map/ppermute | solution.py:136
  81.1 7.5 %collective-permute-start.15 = (bf16[17,16,128]{2,1,0:T(8,128)(2,1)S(1)}, bf16[17,16,128]{2,1,0:T(8,128)(2,1)S(1)}, u32[]{:S(2)}, u32[]{:S(2)}) collective-permute-start(bf16[17,16,128]{2,1,0:T(8,128)(2,1)S(1)} %slice.24), channel_id=1, source_target_pairs={{0,7},{1,0},{2,1},{3,2},{4,3},{5,4},{6,5},{7,6},{8,15},{9,8},{10,9... | collective-permute-start | bytes 208904 | tf_op jit(solution)/shard_map/ppermute | solution.py:140
  84.2 4.4 %collective-permute-start.14 = (bf16[16,16,128]{2,1,0:T(8,128)(2,1)S(1)}, bf16[16,16,128]{2,1,0:T(8,128)(2,1)S(1)}, u32[]{:S(2)}, u32[]{:S(2)}) collective-permute-start(bf16[16,16,128]{2,1,0:T(8,128)(2,1)S(1)} %slice.23), channel_id=1, source_target_pairs={{0,1},{1,2},{2,3},{3,4},{4,5},{5,6},{6,7},{7,0},{8,9},{9,10},{10,1... | collective-permute-start | bytes 196616 | tf_op jit(solution)/shard_map/ppermute | solution.py:139
  90.0 1.0 copy-start.5
  91.0 1.0 copy-start.6
  92.0 28.2 %all-to-all-start.1 = ((bf16[288,16,128]{2,1,0:T(8,128)(2,1)}), bf16[288,16,128]{2,1,0:T(8,128)(2,1)S(1)}, u32[]{:S(2)}, u32[]{:S(2)}) async-start(bf16[288,16,128]{2,1,0:T(8,128)(2,1)} %copy-done.5), calls=%async_computation.1 | async-start | bytes 2359296 | tf_op jit(solution)/shard_map/all_to_all | solution.py:597
  101.9 1.2 copy-start.7
  104.1 16.2 %copy-start.8 = (f32[16,4096]{1,0:T(8,128)S(1)}, f32[16,4096]{1,0:T(8,128)}, u32[]{:S(2)}) copy-start(f32[16,4096]{1,0:T(8,128)} %previous_ref.3) | copy-start | bytes 786436
  104.1 16.2 %copy-start.9 = (f32[16,4096]{1,0:T(8,128)S(1)}, f32[16,4096]{1,0:T(8,128)}, u32[]{:S(2)}) copy-start(f32[16,4096]{1,0:T(8,128)} %previous_image_ref.3) | copy-start | bytes 786436
  109.5 1.3 copy-start.3
  120.2 1.6 copy-start.4
  (7 other events, 5.7 us)

commit v3 on v2

--- a/solution.py
+++ b/solution.py
@@ -15,26 +15,35 @@
 SEND = 8
 HALF = RB // 2
 EXTRA = SEND + 1
-LEN = SLOTS + 8
+GROUP = 32
+LEN = SLOTS + GROUP
 F32 = jnp.float32
 BF16 = jnp.bfloat16
 HIGHEST = lax.Precision.HIGHEST
-VMEM_LIMIT = 48 * 1024 * 1024
+MARGIN = 6 * 1024 * 1024
 SMEM = pl.BlockSpec(memory_space=pltpu.SMEM)
-HBM = pl.BlockSpec(memory_space=pl.ANY)
+HBM = pl.BlockSpec(memory_space=pltpu.HBM)
 VMEM = pl.BlockSpec(memory_space=pltpu.VMEM)
 
 
+def size(array):
+    return math.prod(array.shape) * jnp.dtype(array.dtype).itemsize
+
+
 def call(kernel, out_shape, in_specs, out_specs, scratch=(), flops=0, moved=0):
-    return pl.pallas_call(
-        kernel,
-        out_shape=out_shape,
-        in_specs=in_specs,
-        out_specs=out_specs,
-        scratch_shapes=scratch,
-        compiler_params=pltpu.CompilerParams(vmem_limit_bytes=VMEM_LIMIT),
-        cost_estimate=pl.CostEstimate(flops=flops, bytes_accessed=moved, transcendentals=0),
-    )
+    def run(*args):
+        arrays = list(args) + jax.tree.leaves(out_shape) + [held for held in scratch if jnp.issubdtype(held.dtype, jnp.floating)]
+        return pl.pallas_call(
+            kernel,
+            out_shape=out_shape,
+            in_specs=in_specs,
+            out_specs=out_specs,
+            scratch_shapes=scratch,
+            compiler_params=pltpu.CompilerParams(vmem_limit_bytes=MARGIN + sum(map(size, arrays))),
+            cost_estimate=pl.CostEstimate(flops=flops, bytes_accessed=moved, transcendentals=0),
+        )(*args)
+
+    return run
 
 
 def shaped(shape, dtype):
@@ -84,7 +93,7 @@
 
     n_own, n_halo = lax.fori_loop(0, SLOTS, step, (jnp.int32(0), jnp.int32(0)))
     for ref, count in ((own_ref, n_own), (halo_ref, n_halo)):
-        for extra in range(8):
+        for extra in range(GROUP):
             ref[0, count + extra] = 0
             ref[1, count + extra] = 0
             ref[2, count + extra] = RB
@@ -110,7 +119,15 @@
     return high, middle, (rest - middle).astype(BF16).astype(F32)
 
 
-def cast_kernel(field_ref, degree_ref, tiles_ref):
+def cast_kernel(field_hbm, degree_hbm, tiles_ref, field_ref, degree_ref, sems):
+    copies = [
+        pltpu.make_async_copy(field_hbm, field_ref, sems.at[0]),
+        pltpu.make_async_copy(degree_hbm, degree_ref, sems.at[1]),
+    ]
+    for copy in copies:
+        copy.start()
+    for copy in copies:
+        copy.wait()
     for block in range(RB):
         tiles_ref[block + 2 * (block // HALF)] = field_ref[:, columns(block)].astype(BF16)
     for half in range(2):
@@ -123,7 +140,12 @@
 
 def cast_tiles(field, degree):
     return call(
-        cast_kernel, shaped((RB + 4, K, BS), BF16), [VMEM, VMEM], VMEM, moved=400000
+        cast_kernel,
+        shaped((RB + 4, K, BS), BF16),
+        [HBM, HBM],
+        VMEM,
+        (pltpu.VMEM(field.shape, F32), pltpu.VMEM(degree.shape, F32), pltpu.SemaphoreType.DMA((2,))),
+        moved=400000,
     )(field, degree)
 
 
@@ -150,8 +172,26 @@
     return parts + [(owner, 0, pieces[-2], 0), (owner, 1, pieces[-1], 0)]
 
 
+def fill_and_send(fill, chosen_ref, chosen_hbm, sems):
+    peers = chosen_ref.shape[0] // EXTRA
+    quarter = max(1, peers // 4)
+    copies = []
+    for at in range(peers // quarter):
+
+        def step(peer, carry):
+            fill(peer)
+            return carry
+
+        lax.fori_loop(at * quarter, (at + 1) * quarter, step, 0)
+        span = pl.ds(at * quarter * EXTRA, quarter * EXTRA)
+        copies.append(pltpu.make_async_copy(chosen_ref.at[span], chosen_hbm.at[span], sems.at[at]))
+        copies[-1].start()
+    for copy in copies:
+        copy.wait()
+
+
 def first_select_kernel(offsets, n_row, place_ref, send_ref, *refs):
-    pieces, (part_ref, inverse_ref, chosen_ref, rows_ref) = refs[:-4], refs[-4:]
+    pieces, (part_ref, inverse_ref, chosen_hbm, rows_ref, chosen_ref, sems) = refs[:-6], refs[-6:]
     for owner, half, piece, start in halves(offsets, pieces, HALF + 2, n_row, place_ref[0]):
         at = owner * RB + half * HALF
         part_ref[pl.ds(at, HALF)] = piece[start : start + HALF]
@@ -159,7 +199,7 @@
             piece[start + HALF].astype(F32) + piece[start + HALF + 1].astype(F32)
         )
 
-    def step(peer, carry):
+    def fill(peer):
         for j in range(SEND):
             block = send_ref[peer * SEND + j]
             chosen_ref[peer * EXTRA + j] = part_ref[block]
@@ -167,9 +207,8 @@
         rows = rows_ref[...]
         high = rows.astype(BF16).astype(F32)
         chosen_ref[peer * EXTRA + SEND] = jnp.concatenate([high, rows - high], axis=0).astype(BF16)
-        return carry
-
-    lax.fori_loop(0, chosen_ref.shape[0] // EXTRA, step, 0)
+
+    fill_and_send(fill, chosen_ref, chosen_hbm, sems)
 
 
 def first_select(gathered, place, send_list, n_row):
@@ -180,14 +219,14 @@
         functools.partial(first_select_kernel, [offset for offset, _ in pieces], n_row),
         (shaped((part, K, BS), BF16), shaped((part, BS), F32), shaped((peers * EXTRA, K, BS), BF16)),
         [SMEM, SMEM] + [VMEM] * (len(pieces) + 2),
-        (VMEM, VMEM, VMEM),
-        (pltpu.VMEM((SEND, BS), F32),),
+        (VMEM, VMEM, HBM),
+        (pltpu.VMEM((SEND, BS), F32), pltpu.VMEM((peers * EXTRA, K, BS), BF16), pltpu.SemaphoreType.DMA((4,))),
         moved=3000000,
     )(place, send_list, *[piece for _, piece in pieces], far_low, far_high)
 
 
 def second_select_kernel(offsets, n_row, place_ref, send_ref, pick_ref, *refs):
-    pieces, (part_ref, chosen_ref, table_ref) = refs[:-3], refs[-3:]
+    pieces, (part_ref, chosen_hbm, table_ref, chosen_ref, sems) = refs[:-5], refs[-5:]
     lane = iota2((K, BS), 1)
     table = jnp.zeros((K, BS), F32)
     side_sum = jnp.zeros((K, BS), F32)
@@ -207,12 +246,11 @@
     for peer in range(chosen_ref.shape[0] // EXTRA):
         chosen_ref[peer * EXTRA + SEND] = sides[:, columns(peer)].astype(BF16)
 
-    def step(peer, carry):
+    def fill(peer):
         for j in range(SEND):
             chosen_ref[peer * EXTRA + j] = part_ref[send_ref[peer * SEND + j]]
-        return carry
-
-    lax.fori_loop(0, chosen_ref.shape[0] // EXTRA, step, 0)
+
+    fill_and_send(fill, chosen_ref, chosen_hbm, sems)
 
 
 def second_select(gathered, place, send_list, pick, n_row):
@@ -222,7 +260,8 @@
         functools.partial(second_select_kernel, [offset for offset, _ in pieces], n_row),
         (shaped((n_row * RB, K, BS), BF16), shaped((peers * EXTRA, K, BS), BF16), shaped((K, BS), BF16)),
         [SMEM, SMEM] + [VMEM] * (len(pieces) + 3),
-        (VMEM, VMEM, VMEM),
+        (VMEM, HBM, VMEM),
+        (pltpu.VMEM((peers * EXTRA, K, BS), BF16), pltpu.SemaphoreType.DMA((4,))),
         moved=3000000,
     )(place, send_list, pick, *[piece for _, piece in pieces], far_low, far_high)
 
@@ -236,35 +275,20 @@
     return (jnp.arange(BS, dtype=jnp.int32)[:, None] == target[None, :]).astype(BF16)
 
 
-def issue(count, list_ref, coupling_ref, held, sems):
+def work(count, list_ref, coupling_ref, multiply, add):
     def step(group, carry):
-        for j in range(8):
-            at = group * 8 + j
-            pltpu.make_async_copy(
-                coupling_ref.at[list_ref[0, at]], held.at[at], sems.at[group]
-            ).start()
-        return carry
-
-    lax.fori_loop(0, lax.div(count + 7, 8), step, 0)
-
-
-def work(count, list_ref, coupling_ref, held, sems, multiply, add):
-    def step(group, carry):
-        base = group * 8
-        pltpu.make_async_copy(
-            coupling_ref.at[pl.ds(0, 8)], held.at[pl.ds(base, 8)], sems.at[group]
-        ).wait()
+        base = group * GROUP
         products = [
-            multiply(list_ref[1, base + j], list_ref[3, base + j], held[base + j]) for j in range(8)
+            multiply(list_ref[1, base + j], list_ref[3, base + j], coupling_ref[list_ref[0, base + j]])
+            for j in range(GROUP)
         ]
-        for j in range(8):
+        for j in range(GROUP):
             add(base + j, list_ref[2, base + j], list_ref[3, base + j], products[j])
         return carry
 
-    lax.fori_loop(0, lax.div(count + 7, 8), step, 0)
-
-
-HELD = (pltpu.VMEM((SLOTS, BS, BS), BF16), pltpu.SemaphoreType.DMA((SLOTS // 8,)))
+    lax.fori_loop(0, lax.div(count + GROUP - 1, GROUP), step, 0)
+
+
 ROWS = shaped((RB + 1, K, BS), F32)
 PRODUCTS = shaped((SLOTS, K, BS), F32)
 
@@ -274,9 +298,8 @@
 
 
 def first_own_kernel(
-    list_ref, count_ref, part_ref, inverse_ref, coupling_ref, acc_ref, scaled_ref, kept_ref, held, sems
-):
-    issue(count_ref[0], list_ref, coupling_ref, held, sems)
+    list_ref, count_ref, part_ref, inverse_ref, coupling_ref, acc_ref, scaled_ref, kept_ref
+):
     acc_ref[...] = jnp.zeros_like(acc_ref)
     scaled_ref[...] = jnp.zeros_like(scaled_ref)
 
@@ -290,26 +313,23 @@
         scaled_ref[row] = scaled_ref[row] + product[K:]
         kept_ref[at] = product[K:]
 
-    work(count_ref[0], list_ref, coupling_ref, held, sems, multiply, add)
+    work(count_ref[0], list_ref, coupling_ref, multiply, add)
 
 
 def first_own(own_list, counts, part_tiles, inverse, coupling):
     return call(
         first_own_kernel,
         (ROWS, ROWS, PRODUCTS),
-        [SMEM, SMEM, VMEM, VMEM, HBM],
+        [SMEM, SMEM, VMEM, VMEM, VMEM],
         (VMEM, VMEM, VMEM),
-        HELD,
         flops=2 * SLOTS * K * BS * BS,
         moved=10000000,
     )(own_list, counts, part_tiles, inverse, coupling)
 
 
 def image_kernel(
-    list_ref, count_ref, halo_ref, coupling_ref, own_ref, basis_ref, degree_ref, image_ref, tiles_ref, acc_ref, held,
-    sems,
-):
-    issue(count_ref[1], list_ref, coupling_ref, held, sems)
+    list_ref, count_ref, halo_ref, coupling_ref, own_ref, basis_ref, degree_ref, image_ref, tiles_ref, acc_ref,
+):
     acc_ref[...] = own_ref[...]
 
     def multiply(tile, side, weights):
@@ -318,7 +338,7 @@
     def add(at, row, side, product):
         acc_ref[row] = acc_ref[row] + product
 
-    work(count_ref[1], list_ref, coupling_ref, held, sems, multiply, add)
+    work(count_ref[1], list_ref, coupling_ref, multiply, add)
     top = jnp.zeros((K, BS), F32)
     bottom = jnp.zeros((K, BS), F32)
     for block in range(RB):
@@ -347,9 +367,9 @@
     return call(
         image_kernel,
         (shaped(basis.shape, F32), shaped((RB + 1, K, BS), BF16)),
-        [SMEM, SMEM, VMEM, HBM, VMEM, VMEM, VMEM],
+        [SMEM, SMEM] + [VMEM] * 5,
         (VMEM, VMEM),
-        (pltpu.VMEM((RB + 1, K, BS), F32),) + HELD,
+        (pltpu.VMEM((RB + 1, K, BS), F32),),
         flops=2 * SLOTS * K * BS * BS,
         moved=8000000,
     )(halo_list, counts, halo_tiles, coupling, own, basis, degree)
@@ -357,10 +377,8 @@
 
 def second_own_kernel(
     own_list, halo_list, count_ref, part_ref, table_ref, own_kept_ref, own_scaled_ref, halo_ref, coupling_ref,
-    acc_ref, scaled_ref, kept_ref, held, sems, halo_held, halo_sems, quotient_ref, inverse_ref,
-):
-    issue(count_ref[0], own_list, coupling_ref, held, sems)
-    issue(count_ref[1], halo_list, coupling_ref, halo_held, halo_sems)
+    acc_ref, scaled_ref, kept_ref, quotient_ref, inverse_ref,
+):
     acc_ref[...] = jnp.zeros_like(acc_ref)
     scaled_ref[...] = own_scaled_ref[...]
     table = table_ref[...].astype(F32)
@@ -377,7 +395,7 @@
     def add(at, row, side, product):
         acc_ref[row] = acc_ref[row] + (product + quotient_ref[side] * own_kept_ref[at])
 
-    work(count_ref[0], own_list, coupling_ref, held, sems, multiply, add)
+    work(count_ref[0], own_list, coupling_ref, multiply, add)
 
     def multiply_halo(tile, side, weights):
         return dot_nt(scale_block(halo_ref[tile], inverse_ref[pl.ds(side, 1), :]), weights)
@@ -386,7 +404,7 @@
         scaled_ref[row] = scaled_ref[row] + product
         kept_ref[at] = product
 
-    work(count_ref[1], halo_list, coupling_ref, halo_held, halo_sems, multiply_halo, add_halo)
+    work(count_ref[1], halo_list, coupling_ref, multiply_halo, add_halo)
 
 
 def second_own(
@@ -395,11 +413,9 @@
     return call(
         second_own_kernel,
         (ROWS, ROWS, PRODUCTS),
-        [SMEM, SMEM, SMEM] + [VMEM] * 5 + [HBM],
+        [SMEM, SMEM, SMEM] + [VMEM] * 6,
         (VMEM, VMEM, VMEM),
-        HELD
-        + HELD
-        + (pltpu.VMEM((n_row, K, BS), F32), pltpu.VMEM((halo_tiles.shape[0] // EXTRA * SEND, BS), F32)),
+        (pltpu.VMEM((n_row, K, BS), F32), pltpu.VMEM((halo_tiles.shape[0] // EXTRA * SEND, BS), F32)),
         flops=4 * SLOTS * K * BS * BS,
         moved=10000000,
     )(own_list, halo_list, counts, part_tiles, table, own_kept, own_scaled, halo_tiles, coupling)
@@ -459,10 +475,9 @@
 
 def gram_kernel(
     list_ref, count_ref, halo_ref, coupling_ref, own_ref, scaled_ref, kept_ref, basis_ref, image_ref, degree_ref,
-    previous_ref, previous_image_ref, residual_ref, residual_image_ref, packed_ref, acc_ref, held, sems, side_ref,
+    previous_ref, previous_image_ref, residual_ref, residual_image_ref, packed_ref, acc_ref, side_ref,
     quotient_ref, stacked, stacked_image, wide_ref,
 ):
-    issue(count_ref[1], list_ref, coupling_ref, held, sems)
     acc_ref[...] = own_ref[...]
     peers = halo_ref.shape[0] // EXTRA
     total = jnp.zeros((K, BS), F32)
@@ -485,7 +500,7 @@
     def add(at, row, side, product):
         acc_ref[row] = acc_ref[row] + (product + quotient_ref[side & 7, side >> 3] * kept_ref[at])
 
-    work(count_ref[1], list_ref, coupling_ref, held, sems, multiply, add)
+    work(count_ref[1], list_ref, coupling_ref, multiply, add)
     stacked[0:16] = basis_ref[...]
     stacked[32:48] = previous_ref[...]
     stacked_image[0:16] = image_ref[...]
@@ -513,11 +528,10 @@
     return call(
         gram_kernel,
         (shaped(basis.shape, F32), shaped(basis.shape, F32), shaped((n_dom, 24, BS), F32)),
-        [SMEM, SMEM, VMEM, HBM] + [VMEM] * 8,
+        [SMEM, SMEM] + [VMEM] * 10,
         (VMEM, VMEM, VMEM),
-        (pltpu.VMEM((RB + 1, K, BS), F32),)
-        + HELD
-        + (
+        (
+            pltpu.VMEM((RB + 1, K, BS), F32),
             pltpu.VMEM((n_dom * K, BS), BF16),
             pltpu.VMEM((SEND, n_dom, K, BS), F32),
             pltpu.VMEM((48, width), F32),
@@ -533,13 +547,19 @@
     row = iota2((n, BS), 0)
     lane = iota2((n, BS), 1)
     work = jnp.where(lane < n, gram, jnp.where(lane == row + n, 1.0, 0.0))
-    for j in range(n):
-        column = work[:, j : j + 1]
-        pivot = work[j : j + 1, :]
-        scale = lax.rsqrt(work[j : j + 1, j : j + 1])
-        scaled = pivot * scale
-        below = jnp.where(row[:, 0:1] > j, column * scale, 0.0)
-        work = jnp.where(row == j, scaled, work - below * scaled)
+    for first in range(0, n, 8):
+        left = [jnp.broadcast_to(work[:, first + j : first + j + 1], (n, BS)) for j in range(8)]
+        rows = [work[first + j : first + j + 1, :] for j in range(8)]
+        for j in range(8):
+            scale = lax.rsqrt(left[j][first + j : first + j + 1, :])
+            rows[j] = rows[j] * scale
+            left[j] = jnp.where(row > first + j, left[j] * scale, 0.0)
+            for k in range(j + 1, 8):
+                entry = left[j][first + k : first + k + 1, :]
+                rows[k] = rows[k] - entry * rows[j]
+                left[k] = left[k] - left[j] * entry
+        for j in range(8):
+            work = jnp.where(row == first + j, rows[j], work - left[j] * rows[j])
     return pltpu.roll(work, BS - n, 1)
 
 
@@ -560,12 +580,9 @@
     row = iota2((48, 48), 0)
     lane = iota2((48, 48), 1)
     filter_mat = (jnp.where(row == lane, spread, 0.0) - reduced) / (2.0 * spread)
-    subspace = filter_mat[:, 0:16]
+    turned = filter_mat[0:16, :]
     for repeat in range(3):
-        subspace = dot_nn(filter_mat, subspace, HIGHEST)
-    wide_ref[...] = jnp.zeros_like(wide_ref)
-    wide_ref[0:48, 0:16] = subspace
-    turned = wide_ref[...].T[0:16, 0:48]
+        turned = dot_nn(turned, filter_mat, HIGHEST)
     inner = dot_nt(turned, turned, HIGHEST)
     wide_ref[...] = jnp.zeros_like(wide_ref)
     wide_ref[0:16, 0:16] = inner

time: 168 us -> 166 us (0.988)
  local copies, waits for them, and re-layouts: 15.1 us -> 30.3 us
  waiting for transfers between devices: 39 us -> 26.8 us
  blocking collectives: 29.5 us -> 25.6 us
    unnamed x43 -> x53, local copies, waits for them, and re-layouts: 14.9 us -> 30 us
    all_to_all x2, waiting for transfers between devices: 15.4 us -> 4.97 us  [to_all(): return lax.all_to_all(value, axis, split_axis=0, concat_axis=0, tiled=True)]
    all_to_all x2, blocking collectives: 29.5 us -> 25.6 us  [to_all(): return lax.all_to_all(value, axis, split_axis=0, concat_axis=0, tiled=True)]
    all_to_all x2, starting transfers between devices: 22.2 us -> 20.2 us  [to_all(): return lax.all_to_all(value, axis, split_axis=0, concat_axis=0, tiled=True)]
  transfers between devices with their start and end apart: 18 -> 18, of which waited for: 11 -> 11; matrix products, arithmetic and copies ran while one was open for 1% -> 1% of each run, Pallas kernels for 8% -> 10%
where the time goes in v3:
time: 166 us; the launch traced here: 165 us
  starting transfers between devices  45.9 us (28%)
  Pallas kernels  34.6 us (21%)
  local copies, waits for them, and re-layouts  30.3 us (18%)
  waiting for transfers between devices  26.8 us (16%)
  blocking collectives  25.6 us (15%)
    pallas_call x10, Pallas kernels, run(): pl.pallas_call(kernel, out_shape=out_shape, in_specs=in_specs, out_specs=...  34.6 us
    unnamed x53, local copies, waits for them, and re-layouts  30 us
    all_to_all x2, blocking collectives, to_all(): return lax.all_to_all(value, axis, split_axis=0, concat_axis=0, tiled=True)  25.6 us
    all_to_all x2, starting transfers between devices, to_all(): return lax.all_to_all(value, axis, split_axis=0, concat_axis=0, tiled=True)  20.2 us
    ppermute x6, starting transfers between devices, gather_row(): from_above = lax.ppermute(from_above, 'row', down)  17.9 us
    ppermute x6, waiting for transfers between devices, gather_row(): from_above = lax.ppermute(from_above, 'row', down)  14.2 us
    ppermute x2, waiting for transfers between devices, gather_row(): far_low = lax.ppermute(from_below[:half], 'row', up)  7.19 us
    ppermute x2, starting transfers between devices, gather_row(): far_high = lax.ppermute(from_above[half:], 'row', down)  6.19 us
  transfers between devices with their start and end apart: 18, of which 11 were waited for; matrix products, arithmetic and copies ran while one was open for 1% of the time, Pallas kernels for 10%

profile of v3, /device:TPU:1, one launch (start us, length us, event | category | flops | bytes accessed | tf_op | source)
XLA Modules:
  0.0 165.0 jit_solution(11944813214454470478)
XLA Ops:
  2.4 6.5 %collective-permute-start.1 = (bf16[36,16,128]{2,1,0:T(8,128)(2,1)S(1)}, bf16[36,16,128]{2,1,0:T(8,128)(2,1)S(1)}, u32[]{:S(2)}, u32[]{:S(2)}) collective-permute-start(bf16[36,16,128]{2,1,0:T(8,128)(2,1)S(1)} %shard_map.105.refs_0_), channel_id=1, source_target_pairs={{0,7},{1,0},{2,1},{3,2},{4,3},{5,4},{6,5},{7,6},{8,15},{9,8},{10,9... | collective-permute-start | bytes 442376 | tf_op jit(solution)/shard_map/ppermute | solution.py:159
  8.9 2.5 %collective-permute-done.1.refs_2_ = bf16[36,16,128]{2,1,0:T(8,128)(2,1)S(1)} collective-permute-done((bf16[36,16,128]{2,1,0:T(8,128)(2,1)S(1)}, bf16[36,16,128]{2,1,0:T(8,128)(2,1)S(1)}, u32[]{:S(2)}, u32[]{:S(2)}) %collective-permute-start.1) | collective-permute-done | bytes 147488 | tf_op jit(solution)/shard_map/ppermute | solution.py:159
  11.4 3.4 %collective-permute-start.3 = (bf16[36,16,128]{2,1,0:T(8,128)(2,1)S(1)}, bf16[36,16,128]{2,1,0:T(8,128)(2,1)S(1)}, u32[]{:S(2)}, u32[]{:S(2)}) collective-permute-start(bf16[36,16,128]{2,1,0:T(8,128)(2,1)S(1)} %collective-permute-done.1.refs_2_), channel_id=1, source_target_pairs={{0,7},{1,0},{2,1},{3,2},{4,3},{5,4},{6,5},{7,6},{8,15},{9,8},{10,9... | collective-permute-start | bytes 442376 | tf_op jit(solution)/shard_map/ppermute | solution.py:159
  14.8 2.1 %collective-permute-done.3.refs_4_ = bf16[36,16,128]{2,1,0:T(8,128)(2,1)S(1)} collective-permute-done((bf16[36,16,128]{2,1,0:T(8,128)(2,1)S(1)}, bf16[36,16,128]{2,1,0:T(8,128)(2,1)S(1)}, u32[]{:S(2)}, u32[]{:S(2)}) %collective-permute-start.3) | collective-permute-done | bytes 147488 | tf_op jit(solution)/shard_map/ppermute | solution.py:159
  16.9 3.1 %collective-permute-start.5 = (bf16[36,16,128]{2,1,0:T(8,128)(2,1)S(1)}, bf16[36,16,128]{2,1,0:T(8,128)(2,1)S(1)}, u32[]{:S(2)}, u32[]{:S(2)}) collective-permute-start(bf16[36,16,128]{2,1,0:T(8,128)(2,1)S(1)} %collective-permute-done.3.refs_4_), channel_id=1, source_target_pairs={{0,7},{1,0},{2,1},{3,2},{4,3},{5,4},{6,5},{7,6},{8,15},{9,8},{10,9... | collective-permute-start | bytes 442376 | tf_op jit(solution)/shard_map/ppermute | solution.py:159
  20.0 2.1 %collective-permute-done.5.refs_6_ = bf16[36,16,128]{2,1,0:T(8,128)(2,1)S(1)} collective-permute-done((bf16[36,16,128]{2,1,0:T(8,128)(2,1)S(1)}, bf16[36,16,128]{2,1,0:T(8,128)(2,1)S(1)}, u32[]{:S(2)}, u32[]{:S(2)}) %collective-permute-start.5) | collective-permute-done | bytes 147488 | tf_op jit(solution)/shard_map/ppermute | solution.py:159
  22.1 3.1 %collective-permute-start.7 = (bf16[18,16,128]{2,1,0:T(8,128)(2,1)S(1)}, bf16[18,16,128]{2,1,0:T(8,128)(2,1)S(1)}, u32[]{:S(2)}, u32[]{:S(2)}) collective-permute-start(bf16[18,16,128]{2,1,0:T(8,128)(2,1)S(1)} %slice.22), channel_id=1, source_target_pairs={{0,7},{1,0},{2,1},{3,2},{4,3},{5,4},{6,5},{7,6},{8,15},{9,8},{10,9... | collective-permute-start | bytes 221192 | tf_op jit(solution)/shard_map/ppermute | solution.py:162
  26.6 3.1 %collective-permute-done.6.refs_7_ = bf16[18,16,128]{2,1,0:T(8,128)(2,1)S(1)} collective-permute-done((bf16[18,16,128]{2,1,0:T(8,128)(2,1)S(1)}, bf16[18,16,128]{2,1,0:T(8,128)(2,1)S(1)}, u32[]{:S(2)}, u32[]{:S(2)}) %collective-permute-start.6) | collective-permute-done | bytes 73760 | tf_op jit(solution)/shard_map/ppermute | solution.py:161
  29.7 2.0 %shard_map.106 = (bf16[256,16,128]{2,1,0:T(8,128)(2,1)S(1)}, f32[256,128]{1,0:T(8,128)S(1)}, bf16[288,16,128]{2,1,0:T(8,128)(2,1)}) custom-call(s32[1]{0:T(128)} %bitcast.place_ref, s32[256]{0:T(256)S(1)} %reshape.19.send_ref, bf16[36,16,128]{2,1,0:T(8,128)(2,1)S(1)} %shard_map.105.refs_0_, bf16[36,16,128]{2,1,0:T(8,128)(2,1)S(1)} %collective-permute-done.refs_1_, ...), custom_call_target="tpu_custom_call" | custom-call | bytes 3000000 | tf_op jit(solution)/shard_map/pallas_call | solution.py:36
  31.8 12.4 %all-to-all-start = ((bf16[288,16,128]{2,1,0:T(8,128)(2,1)}), bf16[288,16,128]{2,1,0:T(8,128)(2,1)S(1)}, u32[]{:S(2)}, u32[]{:S(2)}) async-start(bf16[288,16,128]{2,1,0:T(8,128)(2,1)} %get-tuple-element.24), calls=%async_computation | async-start | bytes 2359296 | tf_op jit(solution)/shard_map/all_to_all | solution.py:614
  44.8 5.7 %shard_map.104 = (s32[4,288]{1,0:T(4,128)S(1)}, s32[4,288]{1,0:T(4,128)S(1)}, s32[2]{0:T(128)S(1)}) custom-call(s32[256]{0:T(256)S(1)} %copy-done.23, s32[256]{0:T(256)S(1)} %copy-done.24, s32[1]{0:T(128)S(6)} %copy.14.live_ref), custom_call_target="tpu_custom_call" | custom-call | bytes 20000 | tf_op jit(solution)/shard_map/pallas_call | solution.py:36
  50.5 3.4 %copy-done = bf16[256,128,128]{2,1,0:T(8,128)(2,1)S(1)} copy-done((bf16[256,128,128]{2,1,0:T(8,128)(2,1)S(1)}, bf16[256,128,128]{2,1,0:T(8,128)(2,1)}, u32[]{:S(2)}) %copy-start) | copy-done | bytes 8388632
  53.9 3.3 %shard_map.107 = (f32[33,16,128]{2,1,0:T(8,128)S(1)}, f32[33,16,128]{2,1,0:T(8,128)S(1)}, f32[256,16,128]{2,1,0:T(8,128)S(1)}) custom-call(s32[4,288]{1,0:T(4,128)S(1)} %get-tuple-element.25.list_ref.own_list, s32[2]{0:T(128)S(1)} %get-tuple-element.23.count_ref, bf16[256,16,128]{2,1,0:T(8,128)(2,1)S(1)} %get-tuple-element.26.part_ref, ...), custom_call_target="tpu_custom_call" | custom-call | flops 134217728 | bytes 10000000 | tf_op jit(solution)/shard_map/pallas_call | solution.py:36
  59.3 3.2 %all-to-all-done.halo_ref = bf16[288,16,128]{2,1,0:T(8,128)(2,1)S(1)} async-done(((bf16[288,16,128]{2,1,0:T(8,128)(2,1)}), bf16[288,16,128]{2,1,0:T(8,128)(2,1)S(1)}, u32[]{:S(2)}, u32[]{:S(2)}) %all-to-all-start) | async-done | bytes 1179680 | tf_op jit(solution)/shard_map/all_to_all | solution.py:614
  62.5 3.4 %copy-done.1 = bf16[256,128,128]{2,1,0:T(8,128)(2,1)S(1)} copy-done((bf16[256,128,128]{2,1,0:T(8,128)(2,1)S(1)}, bf16[256,128,128]{2,1,0:T(8,128)(2,1)}, u32[]{:S(2)}) %copy-start.1) | copy-done | bytes 8388632
  65.9 4.2 %shard_map.108 = (f32[16,4096]{1,0:T(8,128)S(1)}, bf16[33,16,128]{2,1,0:T(8,128)(2,1)S(1)}) custom-call(s32[4,288]{1,0:T(4,128)S(1)} %get-tuple-element.22.list_ref.halo_list, s32[2]{0:T(128)S(1)} %get-tuple-element.23.count_ref, bf16[288,16,128]{2,1,0:T(8,128)(2,1)S(1)} %all-to-all-done.halo_ref, bf16[256,128,128]{2,1,0:T(8,128)(2,1)S(1)} %copy-done.1, ...), custom_call_target="tpu_custom_call" | custom-call | flops 134217728 | bytes 8000000 | tf_op jit(solution)/shard_map/pallas_call | solution.py:36
  71.7 3.4 %collective-permute-done.9.refs_2_ = bf16[33,16,128]{2,1,0:T(8,128)(2,1)S(1)} collective-permute-done((bf16[33,16,128]{2,1,0:T(8,128)(2,1)S(1)}, bf16[33,16,128]{2,1,0:T(8,128)(2,1)S(1)}, u32[]{:S(2)}, u32[]{:S(2)}) %collective-permute-start.9) | collective-permute-done | bytes 135200 | tf_op jit(solution)/shard_map/ppermute | solution.py:159
  76.7 2.3 %collective-permute-done.11.refs_4_ = bf16[33,16,128]{2,1,0:T(8,128)(2,1)S(1)} collective-permute-done((bf16[33,16,128]{2,1,0:T(8,128)(2,1)S(1)}, bf16[33,16,128]{2,1,0:T(8,128)(2,1)S(1)}, u32[]{:S(2)}, u32[]{:S(2)}) %collective-permute-start.11) | collective-permute-done | bytes 135200 | tf_op jit(solution)/shard_map/ppermute | solution.py:159
  79.0 3.2 %collective-permute-start.13 = (bf16[33,16,128]{2,1,0:T(8,128)(2,1)S(1)}, bf16[33,16,128]{2,1,0:T(8,128)(2,1)S(1)}, u32[]{:S(2)}, u32[]{:S(2)}) collective-permute-start(bf16[33,16,128]{2,1,0:T(8,128)(2,1)S(1)} %collective-permute-done.11.refs_4_), channel_id=1, source_target_pairs={{0,7},{1,0},{2,1},{3,2},{4,3},{5,4},{6,5},{7,6},{8,15},{9,8},{10,9... | collective-permute-start | bytes 405512 | tf_op jit(solution)/shard_map/ppermute | solution.py:159
  82.4 1.8 %collective-permute-done.13.refs_6_ = bf16[33,16,128]{2,1,0:T(8,128)(2,1)S(1)} collective-permute-done((bf16[33,16,128]{2,1,0:T(8,128)(2,1)S(1)}, bf16[33,16,128]{2,1,0:T(8,128)(2,1)S(1)}, u32[]{:S(2)}, u32[]{:S(2)}) %collective-permute-start.13) | collective-permute-done | bytes 135200 | tf_op jit(solution)/shard_map/ppermute | solution.py:159
  84.2 3.1 %collective-permute-start.15 = (bf16[17,16,128]{2,1,0:T(8,128)(2,1)S(1)}, bf16[17,16,128]{2,1,0:T(8,128)(2,1)S(1)}, u32[]{:S(2)}, u32[]{:S(2)}) collective-permute-start(bf16[17,16,128]{2,1,0:T(8,128)(2,1)S(1)} %slice.24), channel_id=1, source_target_pairs={{0,7},{1,0},{2,1},{3,2},{4,3},{5,4},{6,5},{7,6},{8,15},{9,8},{10,9... | collective-permute-start | bytes 208904 | tf_op jit(solution)/shard_map/ppermute | solution.py:162
  87.6 4.1 %collective-permute-done.14.refs_7_ = bf16[16,16,128]{2,1,0:T(8,128)(2,1)S(1)} collective-permute-done((bf16[16,16,128]{2,1,0:T(8,128)(2,1)S(1)}, bf16[16,16,128]{2,1,0:T(8,128)(2,1)S(1)}, u32[]{:S(2)}, u32[]{:S(2)}) %collective-permute-start.14) | collective-permute-done | bytes 65568 | tf_op jit(solution)/shard_map/ppermute | solution.py:161
  91.7 1.7 %shard_map.109 = (bf16[256,16,128]{2,1,0:T(8,128)(2,1)S(1)}, bf16[288,16,128]{2,1,0:T(8,128)(2,1)S(1)}, bf16[16,128]{1,0:T(8,128)(2,1)S(1)}) custom-call(s32[1]{0:T(128)} %bitcast.place_ref, s32[256]{0:T(256)S(1)} %reshape.19.send_ref, bf16[128,4096]{1,0:T(8,128)(2,1)S(1)} %fusion.pick_ref, bf16[33,16,128]{2,1,0:T(8,128)(2,1)S(1)} %get-tuple-element.29.refs_0_, ...), custom_call_target="tpu_custom_call" | custom-call | bytes 3000000 | tf_op jit(solution)/shard_map/pallas_call | solution.py:36
  95.4 7.8 %all-to-all-start.1 = ((bf16[288,16,128]{2,1,0:T(8,128)(2,1)}), bf16[288,16,128]{2,1,0:T(8,128)(2,1)S(1)}, u32[]{:S(2)}, u32[]{:S(2)}) async-start(bf16[288,16,128]{2,1,0:T(8,128)(2,1)} %copy-done.10), calls=%async_computation.1 | async-start | bytes 2359296 | tf_op jit(solution)/shard_map/all_to_all | solution.py:614
  103.2 3.4 %copy-done.2 = bf16[256,128,128]{2,1,0:T(8,128)(2,1)S(1)} copy-done((bf16[256,128,128]{2,1,0:T(8,128)(2,1)S(1)}, bf16[256,128,128]{2,1,0:T(8,128)(2,1)}, u32[]{:S(2)}) %copy-start.2) | copy-done | bytes 8388632
  110.4 6.8 %shard_map.110 = (f32[33,16,128]{2,1,0:T(8,128)S(1)}, f32[33,16,128]{2,1,0:T(8,128)S(1)}, f32[256,16,128]{2,1,0:T(8,128)S(1)}) custom-call(s32[4,288]{1,0:T(4,128)S(1)} %get-tuple-element.25.list_ref.own_list, s32[4,288]{1,0:T(4,128)S(1)} %get-tuple-element.22.list_ref.halo_list, s32[2]{0:T(128)S(1)} %get-tuple-element.23.count_ref, ...), custom_call_target="tpu_custom_call" | custom-call | flops 268435456 | bytes 10000000 | tf_op jit(solution)/shard_map/pallas_call | solution.py:36
  119.9 1.7 %all-to-all-done.1.halo_ref = bf16[288,16,128]{2,1,0:T(8,128)(2,1)S(1)} async-done(((bf16[288,16,128]{2,1,0:T(8,128)(2,1)}), bf16[288,16,128]{2,1,0:T(8,128)(2,1)S(1)}, u32[]{:S(2)}, u32[]{:S(2)}) %all-to-all-start.1) | async-done | bytes 1179680 | tf_op jit(solution)/shard_map/all_to_all | solution.py:614
  121.7 3.4 %copy-done.3 = bf16[256,128,128]{2,1,0:T(8,128)(2,1)S(1)} copy-done((bf16[256,128,128]{2,1,0:T(8,128)(2,1)S(1)}, bf16[256,128,128]{2,1,0:T(8,128)(2,1)}, u32[]{:S(2)}) %copy-start.3) | copy-done | bytes 8388632
  128.6 6.0 %shard_map.111 = (f32[16,4096]{1,0:T(8,128)S(1)}, f32[16,4096]{1,0:T(8,128)S(1)}, f32[32,24,128]{2,1,0:T(8,128)S(1)}) custom-call(s32[4,288]{1,0:T(4,128)S(1)} %get-tuple-element.22.list_ref.halo_list, s32[2]{0:T(128)S(1)} %get-tuple-element.23.count_ref, bf16[288,16,128]{2,1,0:T(8,128)(2,1)S(1)} %all-to-all-done.1.halo_ref, ...), custom_call_target="tpu_custom_call" | custom-call | flops 134217728 | bytes 10000000 | tf_op jit(solution)/shard_map/pallas_call | solution.py:36
  134.6 14.7 %all_to_all.20.taken_ref = f32[32,24,128]{2,1,0:T(8,128)S(1)} all-to-all(f32[32,24,128]{2,1,0:T(8,128)S(1)} %get-tuple-element.39), channel_id=1, replica_groups=mesh['dom'=32,'row'=8] {'dom'}, dimensions={0} | all-to-all | bytes 786432 | tf_op jit(solution)/shard_map/all_to_all | solution.py:614
  149.3 11.0 %all_to_all.21.taken_ref = f32[8,24,128]{2,1,0:T(8,128)S(1)} all-to-all(f32[8,24,128]{2,1,0:T(8,128)S(1)} %shard_map.112), channel_id=1, replica_groups=mesh['dom'=32,'row'=8] {'row'}, dimensions={0} | all-to-all | bytes 196608 | tf_op jit(solution)/shard_map/all_to_all | solution.py:614
  160.3 4.7 %shard_map.113 = (f32[16,4096]{1,0:T(8,128)}, f32[16,4096]{1,0:T(8,128)}) custom-call(f32[8,24,128]{2,1,0:T(8,128)S(1)} %all_to_all.21.taken_ref, f32[16,4096]{1,0:T(8,128)S(1)} %copy-done.5, f32[16,4096]{1,0:T(8,128)S(1)} %get-tuple-element.40.residual_ref, f32[16,4096]{1,0:T(8,128)S(1)} %copy-done.13, f32[16,4096]{1,0:T(8,128)S(1)} %get-tuple-element.38.image_ref, ...), custom_call_target="tpu_custom_call" | custom-call | flops 1000000 | bytes 3000000 | tf_op jit(solution)/shard_map/pallas_call | solution.py:36
  (81 shorter events, 20.9 us)
Async XLA Ops:
  2.3 42.5 %copy-start.23 = (s32[256]{0:T(256)S(1)}, s32[256]{0:T(256)}, u32[]{:S(2)}) copy-start(s32[256]{0:T(256)} %row_ref.1) | copy-start | bytes 3076
  2.3 42.5 %copy-start.24 = (s32[256]{0:T(256)S(1)}, s32[256]{0:T(256)}, u32[]{:S(2)}) copy-start(s32[256]{0:T(256)} %column_ref.1) | copy-start | bytes 3076
  2.4 9.0 %collective-permute-start.1 = (bf16[36,16,128]{2,1,0:T(8,128)(2,1)S(1)}, bf16[36,16,128]{2,1,0:T(8,128)(2,1)S(1)}, u32[]{:S(2)}, u32[]{:S(2)}) collective-permute-start(bf16[36,16,128]{2,1,0:T(8,128)(2,1)S(1)} %shard_map.105.refs_0_), channel_id=1, source_target_pairs={{0,7},{1,0},{2,1},{3,2},{4,3},{5,4},{6,5},{7,6},{8,15},{9,8},{10,9... | collective-permute-start | bytes 442376 | tf_op jit(solution)/shard_map/ppermute | solution.py:159
  8.9 5.9 %collective-permute-start = (bf16[36,16,128]{2,1,0:T(8,128)(2,1)S(1)}, bf16[36,16,128]{2,1,0:T(8,128)(2,1)S(1)}, u32[]{:S(2)}, u32[]{:S(2)}) collective-permute-start(bf16[36,16,128]{2,1,0:T(8,128)(2,1)S(1)} %shard_map.105.refs_0_), channel_id=1, source_target_pairs={{0,1},{1,2},{2,3},{3,4},{4,5},{5,6},{6,7},{7,0},{8,9},{9,10},{10,1... | collective-permute-start | bytes 442376 | tf_op jit(solution)/shard_map/ppermute | solution.py:158
  11.4 5.5 %collective-permute-start.3 = (bf16[36,16,128]{2,1,0:T(8,128)(2,1)S(1)}, bf16[36,16,128]{2,1,0:T(8,128)(2,1)S(1)}, u32[]{:S(2)}, u32[]{:S(2)}) collective-permute-start(bf16[36,16,128]{2,1,0:T(8,128)(2,1)S(1)} %collective-permute-done.1.refs_2_), channel_id=1, source_target_pairs={{0,7},{1,0},{2,1},{3,2},{4,3},{5,4},{6,5},{7,6},{8,15},{9,8},{10,9... | collective-permute-start | bytes 442376 | tf_op jit(solution)/shard_map/ppermute | solution.py:159
  14.8 5.2 %collective-permute-start.2 = (bf16[36,16,128]{2,1,0:T(8,128)(2,1)S(1)}, bf16[36,16,128]{2,1,0:T(8,128)(2,1)S(1)}, u32[]{:S(2)}, u32[]{:S(2)}) collective-permute-start(bf16[36,16,128]{2,1,0:T(8,128)(2,1)S(1)} %collective-permute-done.refs_1_), channel_id=1, source_target_pairs={{0,1},{1,2},{2,3},{3,4},{4,5},{5,6},{6,7},{7,0},{8,9},{9,10},{10,1... | collective-permute-start | bytes 442376 | tf_op jit(solution)/shard_map/ppermute | solution.py:158
  16.9 5.2 %collective-permute-start.5 = (bf16[36,16,128]{2,1,0:T(8,128)(2,1)S(1)}, bf16[36,16,128]{2,1,0:T(8,128)(2,1)S(1)}, u32[]{:S(2)}, u32[]{:S(2)}) collective-permute-start(bf16[36,16,128]{2,1,0:T(8,128)(2,1)S(1)} %collective-permute-done.3.refs_4_), channel_id=1, source_target_pairs={{0,7},{1,0},{2,1},{3,2},{4,3},{5,4},{6,5},{7,6},{8,15},{9,8},{10,9... | collective-permute-start | bytes 442376 | tf_op jit(solution)/shard_map/ppermute | solution.py:159
  20.0 5.2 %collective-permute-start.4 = (bf16[36,16,128]{2,1,0:T(8,128)(2,1)S(1)}, bf16[36,16,128]{2,1,0:T(8,128)(2,1)S(1)}, u32[]{:S(2)}, u32[]{:S(2)}) collective-permute-start(bf16[36,16,128]{2,1,0:T(8,128)(2,1)S(1)} %collective-permute-done.2.refs_3_), channel_id=1, source_target_pairs={{0,1},{1,2},{2,3},{3,4},{4,5},{5,6},{6,7},{7,0},{8,9},{9,10},{10,1... | collective-permute-start | bytes 442376 | tf_op jit(solution)/shard_map/ppermute | solution.py:158
  22.1 4.5 %collective-permute-start.7 = (bf16[18,16,128]{2,1,0:T(8,128)(2,1)S(1)}, bf16[18,16,128]{2,1,0:T(8,128)(2,1)S(1)}, u32[]{:S(2)}, u32[]{:S(2)}) collective-permute-start(bf16[18,16,128]{2,1,0:T(8,128)(2,1)S(1)} %slice.22), channel_id=1, source_target_pairs={{0,7},{1,0},{2,1},{3,2},{4,3},{5,4},{6,5},{7,6},{8,15},{9,8},{10,9... | collective-permute-start | bytes 221192 | tf_op jit(solution)/shard_map/ppermute | solution.py:162
  25.2 4.5 %collective-permute-start.6 = (bf16[18,16,128]{2,1,0:T(8,128)(2,1)S(1)}, bf16[18,16,128]{2,1,0:T(8,128)(2,1)S(1)}, u32[]{:S(2)}, u32[]{:S(2)}) collective-permute-start(bf16[18,16,128]{2,1,0:T(8,128)(2,1)S(1)} %slice.21), channel_id=1, source_target_pairs={{0,1},{1,2},{2,3},{3,4},{4,5},{5,6},{6,7},{7,0},{8,9},{9,10},{10,1... | collective-permute-start | bytes 221192 | tf_op jit(solution)/shard_map/ppermute | solution.py:161
  31.8 30.7 %all-to-all-start = ((bf16[288,16,128]{2,1,0:T(8,128)(2,1)}), bf16[288,16,128]{2,1,0:T(8,128)(2,1)S(1)}, u32[]{:S(2)}, u32[]{:S(2)}) async-start(bf16[288,16,128]{2,1,0:T(8,128)(2,1)} %get-tuple-element.24), calls=%async_computation | async-start | bytes 2359296 | tf_op jit(solution)/shard_map/all_to_all | solution.py:614
  50.5 3.4 %copy-start = (bf16[256,128,128]{2,1,0:T(8,128)(2,1)S(1)}, bf16[256,128,128]{2,1,0:T(8,128)(2,1)}, u32[]{:S(2)}) copy-start(bf16[256,128,128]{2,1,0:T(8,128)(2,1)} %coupling_ref.7) | copy-start | bytes 25165828
  53.9 8.6 %copy-start.5 = (f32[16,4096]{1,0:T(8,128)S(1)}, f32[16,4096]{1,0:T(8,128)}, u32[]{:S(2)}) copy-start(f32[16,4096]{1,0:T(8,128)} %basis_ref.5) | copy-start | bytes 786436
  53.9 8.6 %copy-start.22 = (f32[4096]{0:T(1024)S(1)}, f32[4096]{0:T(1024)}, u32[]{:S(2)}) copy-start(f32[4096]{0:T(1024)} %param.12) | copy-start | bytes 49156
  62.5 3.4 %copy-start.1 = (bf16[256,128,128]{2,1,0:T(8,128)(2,1)S(1)}, bf16[256,128,128]{2,1,0:T(8,128)(2,1)}, u32[]{:S(2)}) copy-start(bf16[256,128,128]{2,1,0:T(8,128)(2,1)} %coupling_ref.7) | copy-start | bytes 25165828
  65.9 16.3 %copy-start.25 = (s32[1,32,8]{1,2,0:T(8,128)S(1)}, s32[1,32,8]{1,2,0:T(8,128)}, u32[]{:S(2)}) copy-start(s32[1,32,8]{1,2,0:T(8,128)} %param.16) | copy-start | bytes 3076
  70.1 5.0 %collective-permute-start.9 = (bf16[33,16,128]{2,1,0:T(8,128)(2,1)S(1)}, bf16[33,16,128]{2,1,0:T(8,128)(2,1)S(1)}, u32[]{:S(2)}, u32[]{:S(2)}) collective-permute-start(bf16[33,16,128]{2,1,0:T(8,128)(2,1)S(1)} %get-tuple-element.29.refs_0_), channel_id=1, source_target_pairs={{0,7},{1,0},{2,1},{3,2},{4,3},{5,4},{6,5},{7,6},{8,15},{9,8},{10,9... | collective-permute-start | bytes 405512 | tf_op jit(solution)/shard_map/ppermute | solution.py:159
  70.2 6.5 %collective-permute-start.8 = (bf16[33,16,128]{2,1,0:T(8,128)(2,1)S(1)}, bf16[33,16,128]{2,1,0:T(8,128)(2,1)S(1)}, u32[]{:S(2)}, u32[]{:S(2)}) collective-permute-start(bf16[33,16,128]{2,1,0:T(8,128)(2,1)S(1)} %get-tuple-element.29.refs_0_), channel_id=1, source_target_pairs={{0,1},{1,2},{2,3},{3,4},{4,5},{5,6},{6,7},{7,0},{8,9},{9,10},{10,1... | collective-permute-start | bytes 405512 | tf_op jit(solution)/shard_map/ppermute | solution.py:158
  75.1 3.9 %collective-permute-start.11 = (bf16[33,16,128]{2,1,0:T(8,128)(2,1)S(1)}, bf16[33,16,128]{2,1,0:T(8,128)(2,1)S(1)}, u32[]{:S(2)}, u32[]{:S(2)}) collective-permute-start(bf16[33,16,128]{2,1,0:T(8,128)(2,1)S(1)} %collective-permute-done.9.refs_2_), channel_id=1, source_target_pairs={{0,7},{1,0},{2,1},{3,2},{4,3},{5,4},{6,5},{7,6},{8,15},{9,8},{10,9... | collective-permute-start | bytes 405512 | tf_op jit(solution)/shard_map/ppermute | solution.py:159
  76.6 5.6 %collective-permute-start.10 = (bf16[33,16,128]{2,1,0:T(8,128)(2,1)S(1)}, bf16[33,16,128]{2,1,0:T(8,128)(2,1)S(1)}, u32[]{:S(2)}, u32[]{:S(2)}) collective-permute-start(bf16[33,16,128]{2,1,0:T(8,128)(2,1)S(1)} %collective-permute-done.8.refs_1_), channel_id=1, source_target_pairs={{0,1},{1,2},{2,3},{3,4},{4,5},{5,6},{6,7},{7,0},{8,9},{9,10},{10,1... | collective-permute-start | bytes 405512 | tf_op jit(solution)/shard_map/ppermute | solution.py:158
  79.0 5.2 %collective-permute-start.13 = (bf16[33,16,128]{2,1,0:T(8,128)(2,1)S(1)}, bf16[33,16,128]{2,1,0:T(8,128)(2,1)S(1)}, u32[]{:S(2)}, u32[]{:S(2)}) collective-permute-start(bf16[33,16,128]{2,1,0:T(8,128)(2,1)S(1)} %collective-permute-done.11.refs_4_), channel_id=1, source_target_pairs={{0,7},{1,0},{2,1},{3,2},{4,3},{5,4},{6,5},{7,6},{8,15},{9,8},{10,9... | collective-permute-start | bytes 405512 | tf_op jit(solution)/shard_map/ppermute | solution.py:159
  82.2 5.1 %collective-permute-start.12 = (bf16[33,16,128]{2,1,0:T(8,128)(2,1)S(1)}, bf16[33,16,128]{2,1,0:T(8,128)(2,1)S(1)}, u32[]{:S(2)}, u32[]{:S(2)}) collective-permute-start(bf16[33,16,128]{2,1,0:T(8,128)(2,1)S(1)} %collective-permute-done.10.refs_3_), channel_id=1, source_target_pairs={{0,1},{1,2},{2,3},{3,4},{4,5},{5,6},{6,7},{7,0},{8,9},{9,10},{10,1... | collective-permute-start | bytes 405512 | tf_op jit(solution)/shard_map/ppermute | solution.py:158
  84.2 7.5 %collective-permute-start.15 = (bf16[17,16,128]{2,1,0:T(8,128)(2,1)S(1)}, bf16[17,16,128]{2,1,0:T(8,128)(2,1)S(1)}, u32[]{:S(2)}, u32[]{:S(2)}) collective-permute-start(bf16[17,16,128]{2,1,0:T(8,128)(2,1)S(1)} %slice.24), channel_id=1, source_target_pairs={{0,7},{1,0},{2,1},{3,2},{4,3},{5,4},{6,5},{7,6},{8,15},{9,8},{10,9... | collective-permute-start | bytes 208904 | tf_op jit(solution)/shard_map/ppermute | solution.py:162
  87.3 4.4 %collective-permute-start.14 = (bf16[16,16,128]{2,1,0:T(8,128)(2,1)S(1)}, bf16[16,16,128]{2,1,0:T(8,128)(2,1)S(1)}, u32[]{:S(2)}, u32[]{:S(2)}) collective-permute-start(bf16[16,16,128]{2,1,0:T(8,128)(2,1)S(1)} %slice.23), channel_id=1, source_target_pairs={{0,1},{1,2},{2,3},{3,4},{4,5},{5,6},{6,7},{7,0},{8,9},{9,10},{10,1... | collective-permute-start | bytes 196616 | tf_op jit(solution)/shard_map/ppermute | solution.py:161
  95.4 26.3 %all-to-all-start.1 = ((bf16[288,16,128]{2,1,0:T(8,128)(2,1)}), bf16[288,16,128]{2,1,0:T(8,128)(2,1)S(1)}, u32[]{:S(2)}, u32[]{:S(2)}) async-start(bf16[288,16,128]{2,1,0:T(8,128)(2,1)} %copy-done.10), calls=%async_computation.1 | async-start | bytes 2359296 | tf_op jit(solution)/shard_map/all_to_all | solution.py:614
  103.2 3.4 %copy-start.2 = (bf16[256,128,128]{2,1,0:T(8,128)(2,1)S(1)}, bf16[256,128,128]{2,1,0:T(8,128)(2,1)}, u32[]{:S(2)}) copy-start(bf16[256,128,128]{2,1,0:T(8,128)(2,1)} %coupling_ref.7) | copy-start | bytes 25165828
  106.6 1.6 copy-start.7
  110.4 11.3 %copy-start.13 = (f32[16,4096]{1,0:T(8,128)S(1)}, f32[16,4096]{1,0:T(8,128)}, u32[]{:S(2)}) copy-start(f32[16,4096]{1,0:T(8,128)} %previous_ref.3) | copy-start | bytes 786436
  110.4 11.3 %copy-start.14 = (f32[16,4096]{1,0:T(8,128)S(1)}, f32[16,4096]{1,0:T(8,128)}, u32[]{:S(2)}) copy-start(f32[16,4096]{1,0:T(8,128)} %previous_image_ref.3) | copy-start | bytes 786436
  117.2 1.4 copy-start.8
  121.7 3.4 %copy-start.3 = (bf16[256,128,128]{2,1,0:T(8,128)(2,1)S(1)}, bf16[256,128,128]{2,1,0:T(8,128)(2,1)}, u32[]{:S(2)}) copy-start(bf16[256,128,128]{2,1,0:T(8,128)(2,1)} %coupling_ref.7) | copy-start | bytes 25165828
  125.1 1.6 copy-start.9
  (12 other events, 11.2 us)

commit v4 on v3

--- a/solution.py
+++ b/solution.py
@@ -15,6 +15,7 @@
 SEND = 8
 HALF = RB // 2
 EXTRA = SEND + 1
+CHUNK = 32
 GROUP = 32
 LEN = SLOTS + GROUP
 F32 = jnp.float32
@@ -22,7 +23,7 @@
 HIGHEST = lax.Precision.HIGHEST
 MARGIN = 6 * 1024 * 1024
 SMEM = pl.BlockSpec(memory_space=pltpu.SMEM)
-HBM = pl.BlockSpec(memory_space=pltpu.HBM)
+HBM = pl.BlockSpec(memory_space=pl.ANY)
 VMEM = pl.BlockSpec(memory_space=pltpu.VMEM)
 
 
@@ -73,39 +74,34 @@
 def list_kernel(part, row_ref, column_ref, live_ref, own_ref, halo_ref, count_ref):
     live = live_ref[0]
 
-    def step(slot, counts):
+    def step(quad, counts):
         n_own, n_halo = counts
-        column = column_ref[slot]
-        row = row_ref[slot]
-        received = jnp.maximum(column - part, 0)
-        own_ref[0, n_own] = slot
-        own_ref[1, n_own] = jnp.minimum(column, part - 1)
-        own_ref[2, n_own] = row
-        own_ref[3, n_own] = jnp.minimum(column, part - 1) >> 5
-        halo_ref[0, n_halo] = slot
-        halo_ref[1, n_halo] = received + (received >> 3)
-        halo_ref[2, n_halo] = row
-        halo_ref[3, n_halo] = received
-        used = slot < live
-        n_own = n_own + jnp.where(used & (column < part), 1, 0)
-        n_halo = n_halo + jnp.where(used & (column >= part), 1, 0)
+        for j in range(4):
+            slot = quad * 4 + j
+            column = column_ref[slot]
+            entry = slot + (row_ref[slot] << 16)
+            own_ref[n_own] = entry + (column << 8)
+            halo_ref[n_halo] = entry + ((column - part) << 8)
+            used = slot < live
+            is_own = used & (column < part)
+            is_halo = used & (column >= part)
+            n_own = n_own + is_own.astype(jnp.int32)
+            n_halo = n_halo + is_halo.astype(jnp.int32)
         return n_own, n_halo
 
-    n_own, n_halo = lax.fori_loop(0, SLOTS, step, (jnp.int32(0), jnp.int32(0)))
+    n_own, n_halo = lax.fori_loop(0, lax.div(live + 3, 4), step, (jnp.int32(0), jnp.int32(0)))
     for ref, count in ((own_ref, n_own), (halo_ref, n_halo)):
         for extra in range(GROUP):
-            ref[0, count + extra] = 0
-            ref[1, count + extra] = 0
-            ref[2, count + extra] = RB
-            ref[3, count + extra] = 0
+            ref[count + extra] = RB << 16
     count_ref[0] = n_own
     count_ref[1] = n_halo
+    count_ref[2] = live
 
 
 def make_lists(slot_row, slot_column, live_slots, part):
     return call(
         functools.partial(list_kernel, part),
-        (shaped((4, LEN), jnp.int32), shaped((4, LEN), jnp.int32), shaped((2,), jnp.int32)),
+        (shaped((LEN,), jnp.int32), shaped((LEN,), jnp.int32), shaped((3,), jnp.int32)),
         [SMEM, SMEM, SMEM],
         (SMEM, SMEM, SMEM),
         moved=20000,
@@ -217,7 +213,7 @@
     peers = send_list.shape[0] // SEND
     return call(
         functools.partial(first_select_kernel, [offset for offset, _ in pieces], n_row),
-        (shaped((part, K, BS), BF16), shaped((part, BS), F32), shaped((peers * EXTRA, K, BS), BF16)),
+        (shaped((part, K, BS), BF16), shaped((part, BS), F32), pltpu.HBM((peers * EXTRA, K, BS), BF16)),
         [SMEM, SMEM] + [VMEM] * (len(pieces) + 2),
         (VMEM, VMEM, HBM),
         (pltpu.VMEM((SEND, BS), F32), pltpu.VMEM((peers * EXTRA, K, BS), BF16), pltpu.SemaphoreType.DMA((4,))),
@@ -258,7 +254,7 @@
     peers = send_list.shape[0] // SEND
     return call(
         functools.partial(second_select_kernel, [offset for offset, _ in pieces], n_row),
-        (shaped((n_row * RB, K, BS), BF16), shaped((peers * EXTRA, K, BS), BF16), shaped((K, BS), BF16)),
+        (shaped((n_row * RB, K, BS), BF16), pltpu.HBM((peers * EXTRA, K, BS), BF16), shaped((K, BS), BF16)),
         [SMEM, SMEM] + [VMEM] * (len(pieces) + 3),
         (VMEM, HBM, VMEM),
         (pltpu.VMEM((peers * EXTRA, K, BS), BF16), pltpu.SemaphoreType.DMA((4,))),
@@ -275,70 +271,83 @@
     return (jnp.arange(BS, dtype=jnp.int32)[:, None] == target[None, :]).astype(BF16)
 
 
-def work(count, list_ref, coupling_ref, multiply, add):
-    def step(group, carry):
+def fetch(live, coupling_ref, held, sems):
+    def start(chunk, carry):
+        span = pl.ds(chunk * CHUNK, CHUNK)
+        pltpu.make_async_copy(coupling_ref.at[span], held.at[span], sems.at[chunk]).start()
+        return carry
+
+    lax.fori_loop(0, lax.div(live + CHUNK - 1, CHUNK), start, 0)
+
+
+def work(count, live, list_ref, coupling_ref, held, sems, multiply, add):
+    def wait(chunk, carry):
+        span = pl.ds(chunk * CHUNK, CHUNK)
+        pltpu.make_async_copy(coupling_ref.at[span], held.at[span], sems.at[chunk]).wait()
+        return carry
+
+    def step(group, waited):
         base = group * GROUP
-        products = [
-            multiply(list_ref[1, base + j], list_ref[3, base + j], coupling_ref[list_ref[0, base + j]])
-            for j in range(GROUP)
-        ]
-        for j in range(GROUP):
-            add(base + j, list_ref[2, base + j], list_ref[3, base + j], products[j])
-        return carry
-
-    lax.fori_loop(0, lax.div(count + GROUP - 1, GROUP), step, 0)
-
-
+        last = list_ref[jnp.minimum(base + GROUP, count) - 1] & 255
+        needed = lax.div(last, CHUNK) + 1
+        lax.fori_loop(waited, needed, wait, 0)
+        entries = [list_ref[base + j] for j in range(GROUP)]
+        products = [multiply((entry >> 8) & 255, held[entry & 255]) for entry in entries]
+        for entry, product in zip(entries, products):
+            add(entry >> 16, (entry >> 8) & 255, product)
+        return jnp.maximum(waited, needed)
+
+    waited = lax.fori_loop(0, lax.div(count + GROUP - 1, GROUP), step, jnp.int32(0))
+    lax.fori_loop(waited, lax.div(live + CHUNK - 1, CHUNK), wait, 0)
+
+
+HELD = (pltpu.VMEM((SLOTS, BS, BS), BF16), pltpu.SemaphoreType.DMA((SLOTS // CHUNK,)))
 ROWS = shaped((RB + 1, K, BS), F32)
-PRODUCTS = shaped((SLOTS, K, BS), F32)
 
 
 def scale_block(block, inverse):
     return (block.astype(F32) * inverse).astype(BF16)
 
 
-def first_own_kernel(
-    list_ref, count_ref, part_ref, inverse_ref, coupling_ref, acc_ref, scaled_ref, kept_ref
-):
+def first_own_kernel(list_ref, count_ref, part_ref, coupling_ref, acc_ref, held, sems):
+    fetch(count_ref[2], coupling_ref, held, sems)
     acc_ref[...] = jnp.zeros_like(acc_ref)
-    scaled_ref[...] = jnp.zeros_like(scaled_ref)
-
-    def multiply(tile, side, weights):
-        block = part_ref[tile]
-        scaled = scale_block(block, inverse_ref[pl.ds(tile, 1), :])
-        return dot_nt(jnp.concatenate([block, scaled], axis=0), weights)
-
-    def add(at, row, side, product):
-        acc_ref[row] = acc_ref[row] + product[0:K]
-        scaled_ref[row] = scaled_ref[row] + product[K:]
-        kept_ref[at] = product[K:]
-
-    work(count_ref[0], list_ref, coupling_ref, multiply, add)
-
-
-def first_own(own_list, counts, part_tiles, inverse, coupling):
+
+    def multiply(block, weights):
+        return dot_nt(part_ref[block], weights)
+
+    def add(row, block, product):
+        acc_ref[row] = acc_ref[row] + product
+
+    work(count_ref[0], count_ref[2], list_ref, coupling_ref, held, sems, multiply, add)
+
+
+def first_own(own_list, counts, part_tiles, coupling):
     return call(
         first_own_kernel,
-        (ROWS, ROWS, PRODUCTS),
-        [SMEM, SMEM, VMEM, VMEM, VMEM],
-        (VMEM, VMEM, VMEM),
+        ROWS,
+        [SMEM, SMEM, VMEM, HBM],
+        VMEM,
+        HELD,
         flops=2 * SLOTS * K * BS * BS,
         moved=10000000,
-    )(own_list, counts, part_tiles, inverse, coupling)
+    )(own_list, counts, part_tiles, coupling)
 
 
 def image_kernel(
-    list_ref, count_ref, halo_ref, coupling_ref, own_ref, basis_ref, degree_ref, image_ref, tiles_ref, acc_ref,
+    list_ref, count_ref, halo_ref, coupling_ref, own_ref, basis_ref, degree_ref, image_ref, tiles_ref, acc_ref, held,
+    sems,
 ):
+    fetch(count_ref[2], coupling_ref, held, sems)
     acc_ref[...] = own_ref[...]
 
-    def multiply(tile, side, weights):
-        return dot_nt(halo_ref[tile], weights)
-
-    def add(at, row, side, product):
+    def multiply(block, weights):
+        return dot_nt(halo_ref[block + (block >> 3)], weights)
+
+    def add(row, block, product):
         acc_ref[row] = acc_ref[row] + product
 
-    work(count_ref[1], list_ref, coupling_ref, multiply, add)
+    work(count_ref[1], count_ref[2], list_ref, coupling_ref, held, sems, multiply, add)
     top = jnp.zeros((K, BS), F32)
     bottom = jnp.zeros((K, BS), F32)
     for block in range(RB):
@@ -367,58 +376,46 @@
     return call(
         image_kernel,
         (shaped(basis.shape, F32), shaped((RB + 1, K, BS), BF16)),
-        [SMEM, SMEM] + [VMEM] * 5,
+        [SMEM, SMEM, VMEM, HBM, VMEM, VMEM, VMEM],
         (VMEM, VMEM),
-        (pltpu.VMEM((RB + 1, K, BS), F32),),
+        (pltpu.VMEM((RB + 1, K, BS), F32),) + HELD,
         flops=2 * SLOTS * K * BS * BS,
         moved=8000000,
     )(halo_list, counts, halo_tiles, coupling, own, basis, degree)
 
 
 def second_own_kernel(
-    own_list, halo_list, count_ref, part_ref, table_ref, own_kept_ref, own_scaled_ref, halo_ref, coupling_ref,
-    acc_ref, scaled_ref, kept_ref, quotient_ref, inverse_ref,
+    list_ref, count_ref, part_ref, table_ref, basis_part_ref, inverse_ref, coupling_ref, acc_ref, scaled_ref, held,
+    sems, quotient_ref,
 ):
+    fetch(count_ref[2], coupling_ref, held, sems)
     acc_ref[...] = jnp.zeros_like(acc_ref)
-    scaled_ref[...] = own_scaled_ref[...]
+    scaled_ref[...] = jnp.zeros_like(scaled_ref)
     table = table_ref[...].astype(F32)
-    lane = iota2((K, BS), 1)
     for owner in range(quotient_ref.shape[0]):
         quotient_ref[owner] = jnp.broadcast_to(table[:, owner : owner + 1], (K, BS))
-    for peer in range(halo_ref.shape[0] // EXTRA):
-        side = halo_ref[peer * EXTRA + SEND].astype(F32)
-        inverse_ref[peer * SEND : (peer + 1) * SEND, :] = side[0:SEND] + side[SEND:]
-
-    def multiply(tile, side, weights):
-        return dot_nt(part_ref[tile], weights)
-
-    def add(at, row, side, product):
-        acc_ref[row] = acc_ref[row] + (product + quotient_ref[side] * own_kept_ref[at])
-
-    work(count_ref[0], own_list, coupling_ref, multiply, add)
-
-    def multiply_halo(tile, side, weights):
-        return dot_nt(scale_block(halo_ref[tile], inverse_ref[pl.ds(side, 1), :]), weights)
-
-    def add_halo(at, row, side, product):
-        scaled_ref[row] = scaled_ref[row] + product
-        kept_ref[at] = product
-
-    work(count_ref[1], halo_list, coupling_ref, multiply_halo, add_halo)
-
-
-def second_own(
-    own_list, halo_list, counts, part_tiles, table, own_kept, own_scaled, halo_tiles, coupling, n_row
-):
+
+    def multiply(block, weights):
+        scaled = scale_block(basis_part_ref[block], inverse_ref[pl.ds(block, 1), :])
+        return dot_nt(jnp.concatenate([part_ref[block], scaled], axis=0), weights)
+
+    def add(row, block, product):
+        acc_ref[row] = acc_ref[row] + (product[0:K] + quotient_ref[block >> 5] * product[K:])
+        scaled_ref[row] = scaled_ref[row] + product[K:]
+
+    work(count_ref[0], count_ref[2], list_ref, coupling_ref, held, sems, multiply, add)
+
+
+def second_own(own_list, counts, part_tiles, table, basis_part, inverse, coupling, n_row):
     return call(
         second_own_kernel,
-        (ROWS, ROWS, PRODUCTS),
-        [SMEM, SMEM, SMEM] + [VMEM] * 6,
-        (VMEM, VMEM, VMEM),
-        (pltpu.VMEM((n_row, K, BS), F32), pltpu.VMEM((halo_tiles.shape[0] // EXTRA * SEND, BS), F32)),
+        (ROWS, ROWS),
+        [SMEM, SMEM, VMEM, VMEM, VMEM, VMEM, HBM],
+        (VMEM, VMEM),
+        HELD + (pltpu.VMEM((n_row, K, BS), F32),),
         flops=4 * SLOTS * K * BS * BS,
         moved=10000000,
-    )(own_list, halo_list, counts, part_tiles, table, own_kept, own_scaled, halo_tiles, coupling)
+    )(own_list, counts, part_tiles, table, basis_part, inverse, coupling)
 
 
 def spread_kernel(taken_ref, given_ref):
@@ -474,17 +471,21 @@
 
 
 def gram_kernel(
-    list_ref, count_ref, halo_ref, coupling_ref, own_ref, scaled_ref, kept_ref, basis_ref, image_ref, degree_ref,
-    previous_ref, previous_image_ref, residual_ref, residual_image_ref, packed_ref, acc_ref, side_ref,
-    quotient_ref, stacked, stacked_image, wide_ref,
+    list_ref, count_ref, halo_ref, basis_halo_ref, coupling_ref, own_ref, own_scaled_ref, basis_ref, image_ref, degree_ref,
+    previous_ref, previous_image_ref, residual_ref, residual_image_ref, packed_ref, acc_ref, scaled_ref, held, sems,
+    side_ref, quotient_ref, inverse_ref, stacked, stacked_image, wide_ref,
 ):
+    fetch(count_ref[2], coupling_ref, held, sems)
     acc_ref[...] = own_ref[...]
+    scaled_ref[...] = own_scaled_ref[...]
     peers = halo_ref.shape[0] // EXTRA
     total = jnp.zeros((K, BS), F32)
     for peer in range(peers):
         side = halo_ref[peer * EXTRA + SEND]
         side_ref[peer * K : (peer + 1) * K, :] = side
         total = total + side.astype(F32)
+        inverse = basis_halo_ref[peer * EXTRA + SEND].astype(F32)
+        inverse_ref[peer * SEND : (peer + 1) * SEND, :] = inverse[0:SEND] + inverse[SEND:]
     side = side_ref[...]
     for j in range(SEND):
         spread = (iota2((BS, BS), 0) == j).astype(F32).astype(BF16)
@@ -494,13 +495,17 @@
     bottom = jnp.sum(jnp.where((lane >= 11) & (lane <= 13), total, 0.0), axis=1, keepdims=True)
     theta = top / bottom
 
-    def multiply(tile, side, weights):
-        return dot_nt(halo_ref[tile], weights)
-
-    def add(at, row, side, product):
-        acc_ref[row] = acc_ref[row] + (product + quotient_ref[side & 7, side >> 3] * kept_ref[at])
-
-    work(count_ref[1], list_ref, coupling_ref, multiply, add)
+    def multiply(block, weights):
+        tile = block + (block >> 3)
+        scaled = scale_block(basis_halo_ref[tile], inverse_ref[pl.ds(block, 1), :])
+        return dot_nt(jnp.concatenate([halo_ref[tile], scaled], axis=0), weights)
+
+    def add(row, block, product):
+        quotient = quotient_ref[block & 7, block >> 3]
+        acc_ref[row] = acc_ref[row] + (product[0:K] + quotient * product[K:])
+        scaled_ref[row] = scaled_ref[row] + product[K:]
+
+    work(count_ref[1], count_ref[2], list_ref, coupling_ref, held, sems, multiply, add)
     stacked[0:16] = basis_ref[...]
     stacked[32:48] = previous_ref[...]
     stacked_image[0:16] = image_ref[...]
@@ -522,25 +527,27 @@
 
 
 def make_grams(
-    halo_list, counts, halo_tiles, coupling, own, scaled, kept, basis, image, degree, previous, previous_image, n_dom
+    halo_list, counts, halo_tiles, basis_halo, coupling, own, scaled, basis, image, degree, previous, previous_image, n_dom
 ):
     width = basis.shape[1]
     return call(
         gram_kernel,
         (shaped(basis.shape, F32), shaped(basis.shape, F32), shaped((n_dom, 24, BS), F32)),
-        [SMEM, SMEM] + [VMEM] * 10,
+        [SMEM, SMEM, VMEM, VMEM, HBM] + [VMEM] * 7,
         (VMEM, VMEM, VMEM),
-        (
-            pltpu.VMEM((RB + 1, K, BS), F32),
+        (pltpu.VMEM((RB + 1, K, BS), F32), pltpu.VMEM((RB + 1, K, BS), F32))
+        + HELD
+        + (
             pltpu.VMEM((n_dom * K, BS), BF16),
             pltpu.VMEM((SEND, n_dom, K, BS), F32),
+            pltpu.VMEM((n_dom * SEND, BS), F32),
             pltpu.VMEM((48, width), F32),
             pltpu.VMEM((48, width), F32),
             pltpu.VMEM((BS, BS), F32),
         ),
         flops=2 * SLOTS * K * BS * BS,
         moved=10000000,
-    )(halo_list, counts, halo_tiles, coupling, own, scaled, kept, basis, image, degree, previous, previous_image)
+    )(halo_list, counts, halo_tiles, basis_halo, coupling, own, scaled, basis, image, degree, previous, previous_image)
 
 
 def inverse_factor(gram, n):
@@ -622,22 +629,23 @@
     place = lax.axis_index("row").astype(jnp.int32).reshape(1)
     send_list = send_lists.reshape(n_dom * SEND)
     degree = degree.reshape(RB, BS)
+    coupling = pltpu.with_memory_space_constraint(coupling, pltpu.HBM)
     own_list, halo_list, counts = make_lists(slot_row, slot_column, live_slots, part)
 
-    gathered = gather_row(cast_tiles(basis, degree), n_row, HALF + 2)
-    part_tiles, inverse, chosen = first_select(gathered, place, send_list, n_row)
-    halo_tiles = to_all(chosen, "dom")
-    own, own_scaled, own_kept = first_own(own_list, counts, part_tiles, inverse, coupling)
-    image, tiles = make_image(halo_list, counts, halo_tiles, coupling, own, basis, degree)
+    in_hbm = [pltpu.with_memory_space_constraint(value, pltpu.HBM) for value in (basis, degree)]
+    gathered = gather_row(cast_tiles(*in_hbm), n_row, HALF + 2)
+    basis_part, inverse, chosen = first_select(gathered, place, send_list, n_row)
+    basis_halo = to_all(chosen, "dom")
+    own = first_own(own_list, counts, basis_part, coupling)
+    image, tiles = make_image(halo_list, counts, basis_halo, coupling, own, basis, degree)
 
     gathered = gather_row(tiles, n_row, HALF)
     part_tiles, chosen, table = second_select(gathered, place, send_list, picks(send_list), n_row)
-    far_tiles = to_all(chosen, "dom")
-    own, scaled, kept = second_own(
-        own_list, halo_list, counts, part_tiles, table, own_kept, own_scaled, halo_tiles, coupling, n_row
-    )
+    halo_tiles = to_all(chosen, "dom")
+    own, scaled = second_own(own_list, counts, part_tiles, table, basis_part, inverse, coupling, n_row)
     residual, residual_image, packed = make_grams(
-        halo_list, counts, far_tiles, coupling, own, scaled, kept, basis, image, degree, previous, previous_image, n_dom
+        halo_list, counts, halo_tiles, basis_halo, coupling, own, scaled, basis, image, degree, previous, previous_image,
+        n_dom,
     )
     packed = to_all(add_and_repeat(to_all(packed, "dom"), n_row), "row")
     root_rows = math.sqrt(basis.shape[1] * n_dom * n_row)

time: 166 us -> 163 us (0.982)
  waiting for transfers between devices: 26.8 us -> 47.2 us
  local copies, waits for them, and re-layouts: 30.3 us -> 15.6 us
  Pallas kernels: 34.6 us -> 23.3 us
    all_to_all x2, waiting for transfers between devices: 4.97 us -> 24.2 us  [to_all(): return lax.all_to_all(value, axis, split_axis=0, concat_axis=0, tiled=True)]
    unnamed x53 -> x51, local copies, waits for them, and re-layouts: 30 us -> 15.3 us
    pallas_call x10, Pallas kernels: 34.6 us -> 23.3 us  [run(): pl.pallas_call(kernel, out_shape=out_shape, in_specs=in_specs, out_specs=...]
    all_to_all x2, starting transfers between devices: 20.2 us -> 23.8 us  [to_all(): return lax.all_to_all(value, axis, split_axis=0, concat_axis=0, tiled=True)]
  transfers between devices with their start and end apart: 18 -> 18, of which waited for: 11 -> 12; matrix products, arithmetic and copies ran while one was open for 1% -> 1% of each run, Pallas kernels for 10% -> 4%
where the time goes in v4:
time: 163 us; the launch traced here: 162 us
  starting transfers between devices  47.5 us (29%)
  waiting for transfers between devices  47.2 us (29%)
  blocking collectives  26.9 us (17%)
  Pallas kernels  23.3 us (14%)
  local copies, waits for them, and re-layouts  15.6 us (10%)
    all_to_all x2, blocking collectives, to_all(): return lax.all_to_all(value, axis, split_axis=0, concat_axis=0, tiled=True)  26.9 us
    all_to_all x2, waiting for transfers between devices, to_all(): return lax.all_to_all(value, axis, split_axis=0, concat_axis=0, tiled=True)  24.2 us
    all_to_all x2, starting transfers between devices, to_all(): return lax.all_to_all(value, axis, split_axis=0, concat_axis=0, tiled=True)  23.8 us
    pallas_call x10, Pallas kernels, run(): pl.pallas_call(kernel, out_shape=out_shape, in_specs=in_specs, out_specs=...  23.3 us
    ppermute x6, starting transfers between devices, gather_row(): from_above = lax.ppermute(from_above, 'row', down)  16.6 us
    unnamed x51, local copies, waits for them, and re-layouts  15.3 us
    ppermute x6, waiting for transfers between devices, gather_row(): from_above = lax.ppermute(from_above, 'row', down)  14.1 us
    ppermute x2, waiting for transfers between devices, gather_row(): far_low = lax.ppermute(from_below[:half], 'row', up)  8.15 us
  transfers between devices with their start and end apart: 18, of which 12 were waited for; matrix products, arithmetic and copies ran while one was open for 1% of the time, Pallas kernels for 4%

profile of v4, /device:TPU:1, one launch (start us, length us, event | category | flops | bytes accessed | tf_op | source)
XLA Modules:
  0.0 162.4 jit_solution(13570187634231594875)
XLA Ops:
  0.6 1.0 shard_map.105.refs_0_
  1.6 6.5 %collective-permute-start.1 = (bf16[36,16,128]{2,1,0:T(8,128)(2,1)S(1)}, bf16[36,16,128]{2,1,0:T(8,128)(2,1)S(1)}, u32[]{:S(2)}, u32[]{:S(2)}) collective-permute-start(bf16[36,16,128]{2,1,0:T(8,128)(2,1)S(1)} %shard_map.105.refs_0_), channel_id=1, source_target_pairs={{0,7},{1,0},{2,1},{3,2},{4,3},{5,4},{6,5},{7,6},{8,15},{9,8},{10,9... | collective-permute-start | bytes 442376 | tf_op jit(solution)/shard_map/ppermute | solution.py:155
  8.1 2.5 %collective-permute-done.1.refs_2_ = bf16[36,16,128]{2,1,0:T(8,128)(2,1)S(1)} collective-permute-done((bf16[36,16,128]{2,1,0:T(8,128)(2,1)S(1)}, bf16[36,16,128]{2,1,0:T(8,128)(2,1)S(1)}, u32[]{:S(2)}, u32[]{:S(2)}) %collective-permute-start.1) | collective-permute-done | bytes 147488 | tf_op jit(solution)/shard_map/ppermute | solution.py:155
  10.6 3.4 %collective-permute-start.3 = (bf16[36,16,128]{2,1,0:T(8,128)(2,1)S(1)}, bf16[36,16,128]{2,1,0:T(8,128)(2,1)S(1)}, u32[]{:S(2)}, u32[]{:S(2)}) collective-permute-start(bf16[36,16,128]{2,1,0:T(8,128)(2,1)S(1)} %collective-permute-done.1.refs_2_), channel_id=1, source_target_pairs={{0,7},{1,0},{2,1},{3,2},{4,3},{5,4},{6,5},{7,6},{8,15},{9,8},{10,9... | collective-permute-start | bytes 442376 | tf_op jit(solution)/shard_map/ppermute | solution.py:155
  14.0 2.1 %collective-permute-done.3.refs_4_ = bf16[36,16,128]{2,1,0:T(8,128)(2,1)S(1)} collective-permute-done((bf16[36,16,128]{2,1,0:T(8,128)(2,1)S(1)}, bf16[36,16,128]{2,1,0:T(8,128)(2,1)S(1)}, u32[]{:S(2)}, u32[]{:S(2)}) %collective-permute-start.3) | collective-permute-done | bytes 147488 | tf_op jit(solution)/shard_map/ppermute | solution.py:155
  16.1 3.1 %collective-permute-start.5 = (bf16[36,16,128]{2,1,0:T(8,128)(2,1)S(1)}, bf16[36,16,128]{2,1,0:T(8,128)(2,1)S(1)}, u32[]{:S(2)}, u32[]{:S(2)}) collective-permute-start(bf16[36,16,128]{2,1,0:T(8,128)(2,1)S(1)} %collective-permute-done.3.refs_4_), channel_id=1, source_target_pairs={{0,7},{1,0},{2,1},{3,2},{4,3},{5,4},{6,5},{7,6},{8,15},{9,8},{10,9... | collective-permute-start | bytes 442376 | tf_op jit(solution)/shard_map/ppermute | solution.py:155
  19.3 2.1 %collective-permute-done.5.refs_6_ = bf16[36,16,128]{2,1,0:T(8,128)(2,1)S(1)} collective-permute-done((bf16[36,16,128]{2,1,0:T(8,128)(2,1)S(1)}, bf16[36,16,128]{2,1,0:T(8,128)(2,1)S(1)}, u32[]{:S(2)}, u32[]{:S(2)}) %collective-permute-start.5) | collective-permute-done | bytes 147488 | tf_op jit(solution)/shard_map/ppermute | solution.py:155
  21.4 3.1 %collective-permute-start.7 = (bf16[18,16,128]{2,1,0:T(8,128)(2,1)S(1)}, bf16[18,16,128]{2,1,0:T(8,128)(2,1)S(1)}, u32[]{:S(2)}, u32[]{:S(2)}) collective-permute-start(bf16[18,16,128]{2,1,0:T(8,128)(2,1)S(1)} %slice.22), channel_id=1, source_target_pairs={{0,7},{1,0},{2,1},{3,2},{4,3},{5,4},{6,5},{7,6},{8,15},{9,8},{10,9... | collective-permute-start | bytes 221192 | tf_op jit(solution)/shard_map/ppermute | solution.py:158
  25.9 3.1 %collective-permute-done.6.refs_7_ = bf16[18,16,128]{2,1,0:T(8,128)(2,1)S(1)} collective-permute-done((bf16[18,16,128]{2,1,0:T(8,128)(2,1)S(1)}, bf16[18,16,128]{2,1,0:T(8,128)(2,1)S(1)}, u32[]{:S(2)}, u32[]{:S(2)}) %collective-permute-start.6) | collective-permute-done | bytes 73760 | tf_op jit(solution)/shard_map/ppermute | solution.py:157
  29.0 2.0 %shard_map.106 = (bf16[256,16,128]{2,1,0:T(8,128)(2,1)S(1)}, f32[256,128]{1,0:T(8,128)S(1)}, bf16[288,16,128]{2,1,0:T(8,128)(2,1)}) custom-call(s32[1]{0:T(128)} %bitcast.place_ref, s32[256]{0:T(256)S(1)} %reshape.19.send_ref, bf16[36,16,128]{2,1,0:T(8,128)(2,1)S(1)} %shard_map.105.refs_0_, bf16[36,16,128]{2,1,0:T(8,128)(2,1)S(1)} %collective-permute-done.refs_1_, ...), custom_call_target="tpu_custom_call" | custom-call | bytes 3000000 | tf_op jit(solution)/shard_map/pallas_call | solution.py:37
  31.0 12.4 %all-to-all-start = ((bf16[288,16,128]{2,1,0:T(8,128)(2,1)}), bf16[288,16,128]{2,1,0:T(8,128)(2,1)S(1)}, u32[]{:S(2)}, u32[]{:S(2)}) async-start(bf16[288,16,128]{2,1,0:T(8,128)(2,1)} %get-tuple-element.20), calls=%async_computation | async-start | bytes 2359296 | tf_op jit(solution)/shard_map/all_to_all | solution.py:621
  44.1 1.5 shard_map.104
  46.1 2.5 %shard_map.107.own_ref = f32[33,16,128]{2,1,0:T(8,128)S(1)} custom-call(s32[288]{0:T(512)S(1)} %get-tuple-element.21.list_ref, s32[3]{0:T(128)S(1)} %get-tuple-element.19.count_ref, bf16[256,16,128]{2,1,0:T(8,128)(2,1)S(1)} %get-tuple-element.22.part_ref.basis_part_ref, bf16[256,128,128]{2,1,0:T(8,128)(2,1)} %coupling_ref.7), custom_call_target="tpu_custom_call" | custom-call | flops 134217728 | bytes 10000000 | tf_op jit(solution)/shard_map/pallas_call | solution.py:37
  48.7 13.1 %all-to-all-done.halo_ref.basis_halo_ref = bf16[288,16,128]{2,1,0:T(8,128)(2,1)S(1)} async-done(((bf16[288,16,128]{2,1,0:T(8,128)(2,1)}), bf16[288,16,128]{2,1,0:T(8,128)(2,1)S(1)}, u32[]{:S(2)}, u32[]{:S(2)}) %all-to-all-start) | async-done | bytes 1179680 | tf_op jit(solution)/shard_map/all_to_all | solution.py:621
  61.8 2.7 %shard_map.108 = (f32[16,4096]{1,0:T(8,128)S(1)}, bf16[33,16,128]{2,1,0:T(8,128)(2,1)S(1)}) custom-call(s32[288]{0:T(512)S(1)} %get-tuple-element.18.list_ref, s32[3]{0:T(128)S(1)} %get-tuple-element.19.count_ref, bf16[288,16,128]{2,1,0:T(8,128)(2,1)S(1)} %all-to-all-done.halo_ref.basis_halo_ref, bf16[256,128,128]{2,1,0:T(8,128)(2,1)} %coupling_ref.7, ...), custom_call_target="tpu_custom_call" | custom-call | flops 134217728 | bytes 8000000 | tf_op jit(solution)/shard_map/pallas_call | solution.py:37
  65.2 1.5 collective-permute-start.8
  66.8 2.3 %collective-permute-done.9.refs_2_ = bf16[33,16,128]{2,1,0:T(8,128)(2,1)S(1)} collective-permute-done((bf16[33,16,128]{2,1,0:T(8,128)(2,1)S(1)}, bf16[33,16,128]{2,1,0:T(8,128)(2,1)S(1)}, u32[]{:S(2)}, u32[]{:S(2)}) %collective-permute-start.9) | collective-permute-done | bytes 135200 | tf_op jit(solution)/shard_map/ppermute | solution.py:155
  69.1 1.2 collective-permute-start.11
  70.6 2.4 %collective-permute-done.11.refs_4_ = bf16[33,16,128]{2,1,0:T(8,128)(2,1)S(1)} collective-permute-done((bf16[33,16,128]{2,1,0:T(8,128)(2,1)S(1)}, bf16[33,16,128]{2,1,0:T(8,128)(2,1)S(1)}, u32[]{:S(2)}, u32[]{:S(2)}) %collective-permute-start.11) | collective-permute-done | bytes 135200 | tf_op jit(solution)/shard_map/ppermute | solution.py:155
  73.0 2.4 %collective-permute-start.13 = (bf16[33,16,128]{2,1,0:T(8,128)(2,1)S(1)}, bf16[33,16,128]{2,1,0:T(8,128)(2,1)S(1)}, u32[]{:S(2)}, u32[]{:S(2)}) collective-permute-start(bf16[33,16,128]{2,1,0:T(8,128)(2,1)S(1)} %collective-permute-done.11.refs_4_), channel_id=1, source_target_pairs={{0,7},{1,0},{2,1},{3,2},{4,3},{5,4},{6,5},{7,6},{8,15},{9,8},{10,9... | collective-permute-start | bytes 405512 | tf_op jit(solution)/shard_map/ppermute | solution.py:155
  75.6 2.7 %collective-permute-done.13.refs_6_ = bf16[33,16,128]{2,1,0:T(8,128)(2,1)S(1)} collective-permute-done((bf16[33,16,128]{2,1,0:T(8,128)(2,1)S(1)}, bf16[33,16,128]{2,1,0:T(8,128)(2,1)S(1)}, u32[]{:S(2)}, u32[]{:S(2)}) %collective-permute-start.13) | collective-permute-done | bytes 135200 | tf_op jit(solution)/shard_map/ppermute | solution.py:155
  78.2 2.2 %collective-permute-start.15 = (bf16[17,16,128]{2,1,0:T(8,128)(2,1)S(1)}, bf16[17,16,128]{2,1,0:T(8,128)(2,1)S(1)}, u32[]{:S(2)}, u32[]{:S(2)}) collective-permute-start(bf16[17,16,128]{2,1,0:T(8,128)(2,1)S(1)} %slice.24), channel_id=1, source_target_pairs={{0,7},{1,0},{2,1},{3,2},{4,3},{5,4},{6,5},{7,6},{8,15},{9,8},{10,9... | collective-permute-start | bytes 208904 | tf_op jit(solution)/shard_map/ppermute | solution.py:158
  81.0 5.1 %collective-permute-done.14.refs_7_ = bf16[16,16,128]{2,1,0:T(8,128)(2,1)S(1)} collective-permute-done((bf16[16,16,128]{2,1,0:T(8,128)(2,1)S(1)}, bf16[16,16,128]{2,1,0:T(8,128)(2,1)S(1)}, u32[]{:S(2)}, u32[]{:S(2)}) %collective-permute-start.14) | collective-permute-done | bytes 65568 | tf_op jit(solution)/shard_map/ppermute | solution.py:157
  86.1 2.2 %shard_map.109 = (bf16[256,16,128]{2,1,0:T(8,128)(2,1)S(1)}, bf16[288,16,128]{2,1,0:T(8,128)(2,1)}, bf16[16,128]{1,0:T(8,128)(2,1)S(1)}) custom-call(s32[1]{0:T(128)} %bitcast.place_ref, s32[256]{0:T(256)S(1)} %reshape.19.send_ref, bf16[128,4096]{1,0:T(8,128)(2,1)S(1)} %fusion.pick_ref, bf16[33,16,128]{2,1,0:T(8,128)(2,1)S(1)} %get-tuple-element.23.refs_0_, ...), custom_call_target="tpu_custom_call" | custom-call | bytes 3000000 | tf_op jit(solution)/shard_map/pallas_call | solution.py:37
  89.8 11.4 %all-to-all-start.1 = ((bf16[288,16,128]{2,1,0:T(8,128)(2,1)}), bf16[288,16,128]{2,1,0:T(8,128)(2,1)S(1)}, u32[]{:S(2)}, u32[]{:S(2)}) async-start(bf16[288,16,128]{2,1,0:T(8,128)(2,1)} %get-tuple-element.24), calls=%async_computation.1 | async-start | bytes 2359296 | tf_op jit(solution)/shard_map/all_to_all | solution.py:621
  101.2 1.2 copy-done.3
  104.5 2.5 %shard_map.110 = (f32[33,16,128]{2,1,0:T(8,128)S(1)}, f32[33,16,128]{2,1,0:T(8,128)S(1)}) custom-call(s32[288]{0:T(512)S(1)} %copy-done.16, s32[3]{0:T(128)S(1)} %copy-done.18, bf16[256,16,128]{2,1,0:T(8,128)(2,1)S(1)} %copy-done.3, bf16[16,128]{1,0:T(8,128)(2,1)S(1)} %copy-done.21, bf16[256,16,128]{2,1,0:T(8,128)(2,1)S(1)} %get-tuple-element.22.part_ref.basis_part_ref, ...), custom_call_target="tpu_custom_call" | custom-call | flops 268435456 | bytes 10000000 | tf_op jit(solution)/shard_map/pallas_call | solution.py:37
  108.4 11.1 %all-to-all-done.1.halo_ref = bf16[288,16,128]{2,1,0:T(8,128)(2,1)S(1)} async-done(((bf16[288,16,128]{2,1,0:T(8,128)(2,1)}), bf16[288,16,128]{2,1,0:T(8,128)(2,1)S(1)}, u32[]{:S(2)}, u32[]{:S(2)}) %all-to-all-start.1) | async-done | bytes 1179680 | tf_op jit(solution)/shard_map/all_to_all | solution.py:621
  126.6 4.1 %shard_map.111 = (f32[16,4096]{1,0:T(8,128)S(1)}, f32[16,4096]{1,0:T(8,128)S(1)}, f32[32,24,128]{2,1,0:T(8,128)S(1)}) custom-call(s32[288]{0:T(512)S(1)} %copy-done.14, s32[3]{0:T(128)S(1)} %copy-done.19, bf16[288,16,128]{2,1,0:T(8,128)(2,1)S(1)} %all-to-all-done.1.halo_ref, bf16[288,16,128]{2,1,0:T(8,128)(2,1)S(1)} %all-to-all-done.halo_ref.basis_halo_ref, ...), custom_call_target="tpu_custom_call" | custom-call | flops 134217728 | bytes 10000000 | tf_op jit(solution)/shard_map/pallas_call | solution.py:37
  130.8 16.3 %all_to_all.20.taken_ref = f32[32,24,128]{2,1,0:T(8,128)S(1)} all-to-all(f32[32,24,128]{2,1,0:T(8,128)S(1)} %get-tuple-element.31), channel_id=1, replica_groups=mesh['dom'=32,'row'=8] {'dom'}, dimensions={0} | all-to-all | bytes 786432 | tf_op jit(solution)/shard_map/all_to_all | solution.py:621
  147.2 10.6 %all_to_all.21.taken_ref = f32[8,24,128]{2,1,0:T(8,128)S(1)} all-to-all(f32[8,24,128]{2,1,0:T(8,128)S(1)} %shard_map.112), channel_id=1, replica_groups=mesh['dom'=32,'row'=8] {'row'}, dimensions={0} | all-to-all | bytes 196608 | tf_op jit(solution)/shard_map/all_to_all | solution.py:621
  157.8 4.7 %shard_map.113 = (f32[16,4096]{1,0:T(8,128)}, f32[16,4096]{1,0:T(8,128)}) custom-call(f32[8,24,128]{2,1,0:T(8,128)S(1)} %all_to_all.21.taken_ref, f32[16,4096]{1,0:T(8,128)S(1)} %copy-done.1, f32[16,4096]{1,0:T(8,128)S(1)} %get-tuple-element.32.residual_ref, f32[16,4096]{1,0:T(8,128)S(1)} %copy-done.4, f32[16,4096]{1,0:T(8,128)S(1)} %copy-done.7, ...), custom_call_target="tpu_custom_call" | custom-call | flops 1000000 | bytes 3000000 | tf_op jit(solution)/shard_map/pallas_call | solution.py:37
  (79 shorter events, 15.8 us)
Async XLA Ops:
  1.6 9.0 %collective-permute-start.1 = (bf16[36,16,128]{2,1,0:T(8,128)(2,1)S(1)}, bf16[36,16,128]{2,1,0:T(8,128)(2,1)S(1)}, u32[]{:S(2)}, u32[]{:S(2)}) collective-permute-start(bf16[36,16,128]{2,1,0:T(8,128)(2,1)S(1)} %shard_map.105.refs_0_), channel_id=1, source_target_pairs={{0,7},{1,0},{2,1},{3,2},{4,3},{5,4},{6,5},{7,6},{8,15},{9,8},{10,9... | collective-permute-start | bytes 442376 | tf_op jit(solution)/shard_map/ppermute | solution.py:155
  8.1 5.9 %collective-permute-start = (bf16[36,16,128]{2,1,0:T(8,128)(2,1)S(1)}, bf16[36,16,128]{2,1,0:T(8,128)(2,1)S(1)}, u32[]{:S(2)}, u32[]{:S(2)}) collective-permute-start(bf16[36,16,128]{2,1,0:T(8,128)(2,1)S(1)} %shard_map.105.refs_0_), channel_id=1, source_target_pairs={{0,1},{1,2},{2,3},{3,4},{4,5},{5,6},{6,7},{7,0},{8,9},{9,10},{10,1... | collective-permute-start | bytes 442376 | tf_op jit(solution)/shard_map/ppermute | solution.py:154
  10.6 5.5 %collective-permute-start.3 = (bf16[36,16,128]{2,1,0:T(8,128)(2,1)S(1)}, bf16[36,16,128]{2,1,0:T(8,128)(2,1)S(1)}, u32[]{:S(2)}, u32[]{:S(2)}) collective-permute-start(bf16[36,16,128]{2,1,0:T(8,128)(2,1)S(1)} %collective-permute-done.1.refs_2_), channel_id=1, source_target_pairs={{0,7},{1,0},{2,1},{3,2},{4,3},{5,4},{6,5},{7,6},{8,15},{9,8},{10,9... | collective-permute-start | bytes 442376 | tf_op jit(solution)/shard_map/ppermute | solution.py:155
  14.0 5.2 %collective-permute-start.2 = (bf16[36,16,128]{2,1,0:T(8,128)(2,1)S(1)}, bf16[36,16,128]{2,1,0:T(8,128)(2,1)S(1)}, u32[]{:S(2)}, u32[]{:S(2)}) collective-permute-start(bf16[36,16,128]{2,1,0:T(8,128)(2,1)S(1)} %collective-permute-done.refs_1_), channel_id=1, source_target_pairs={{0,1},{1,2},{2,3},{3,4},{4,5},{5,6},{6,7},{7,0},{8,9},{9,10},{10,1... | collective-permute-start | bytes 442376 | tf_op jit(solution)/shard_map/ppermute | solution.py:154
  16.1 5.2 %collective-permute-start.5 = (bf16[36,16,128]{2,1,0:T(8,128)(2,1)S(1)}, bf16[36,16,128]{2,1,0:T(8,128)(2,1)S(1)}, u32[]{:S(2)}, u32[]{:S(2)}) collective-permute-start(bf16[36,16,128]{2,1,0:T(8,128)(2,1)S(1)} %collective-permute-done.3.refs_4_), channel_id=1, source_target_pairs={{0,7},{1,0},{2,1},{3,2},{4,3},{5,4},{6,5},{7,6},{8,15},{9,8},{10,9... | collective-permute-start | bytes 442376 | tf_op jit(solution)/shard_map/ppermute | solution.py:155
  19.3 5.2 %collective-permute-start.4 = (bf16[36,16,128]{2,1,0:T(8,128)(2,1)S(1)}, bf16[36,16,128]{2,1,0:T(8,128)(2,1)S(1)}, u32[]{:S(2)}, u32[]{:S(2)}) collective-permute-start(bf16[36,16,128]{2,1,0:T(8,128)(2,1)S(1)} %collective-permute-done.2.refs_3_), channel_id=1, source_target_pairs={{0,1},{1,2},{2,3},{3,4},{4,5},{5,6},{6,7},{7,0},{8,9},{9,10},{10,1... | collective-permute-start | bytes 442376 | tf_op jit(solution)/shard_map/ppermute | solution.py:154
  21.4 4.5 %collective-permute-start.7 = (bf16[18,16,128]{2,1,0:T(8,128)(2,1)S(1)}, bf16[18,16,128]{2,1,0:T(8,128)(2,1)S(1)}, u32[]{:S(2)}, u32[]{:S(2)}) collective-permute-start(bf16[18,16,128]{2,1,0:T(8,128)(2,1)S(1)} %slice.22), channel_id=1, source_target_pairs={{0,7},{1,0},{2,1},{3,2},{4,3},{5,4},{6,5},{7,6},{8,15},{9,8},{10,9... | collective-permute-start | bytes 221192 | tf_op jit(solution)/shard_map/ppermute | solution.py:158
  24.5 4.5 %collective-permute-start.6 = (bf16[18,16,128]{2,1,0:T(8,128)(2,1)S(1)}, bf16[18,16,128]{2,1,0:T(8,128)(2,1)S(1)}, u32[]{:S(2)}, u32[]{:S(2)}) collective-permute-start(bf16[18,16,128]{2,1,0:T(8,128)(2,1)S(1)} %slice.21), channel_id=1, source_target_pairs={{0,1},{1,2},{2,3},{3,4},{4,5},{5,6},{6,7},{7,0},{8,9},{9,10},{10,1... | collective-permute-start | bytes 221192 | tf_op jit(solution)/shard_map/ppermute | solution.py:157
  31.0 13.1 %copy-start.22 = (s32[256]{0:T(256)S(1)}, s32[256]{0:T(256)}, u32[]{:S(2)}) copy-start(s32[256]{0:T(256)} %row_ref.1) | copy-start | bytes 3076
  31.0 13.0 %copy-start.23 = (s32[256]{0:T(256)S(1)}, s32[256]{0:T(256)}, u32[]{:S(2)}) copy-start(s32[256]{0:T(256)} %column_ref.1) | copy-start | bytes 3076
  31.0 30.7 %all-to-all-start = ((bf16[288,16,128]{2,1,0:T(8,128)(2,1)}), bf16[288,16,128]{2,1,0:T(8,128)(2,1)S(1)}, u32[]{:S(2)}, u32[]{:S(2)}) async-start(bf16[288,16,128]{2,1,0:T(8,128)(2,1)} %get-tuple-element.20), calls=%async_computation | async-start | bytes 2359296 | tf_op jit(solution)/shard_map/all_to_all | solution.py:621
  45.6 16.2 %copy-start.13 = (s32[288]{0:T(512)}, s32[288]{0:T(512)S(1)}, u32[]{:S(2)}) copy-start(s32[288]{0:T(512)S(1)} %get-tuple-element.18.list_ref) | copy-start | bytes 3460
  45.6 16.2 %copy-start.17 = (s32[3]{0:T(128)}, s32[3]{0:T(128)S(1)}, u32[]{:S(2)}) copy-start(s32[3]{0:T(128)S(1)} %get-tuple-element.19.count_ref) | copy-start | bytes 40
  46.1 15.6 %copy-start = (f32[16,4096]{1,0:T(8,128)S(1)}, f32[16,4096]{1,0:T(8,128)}, u32[]{:S(2)}) copy-start(f32[16,4096]{1,0:T(8,128)} %basis_ref.5) | copy-start | bytes 786436
  46.1 15.6 %copy-start.12 = (f32[4096]{0:T(1024)S(1)}, f32[4096]{0:T(1024)}, u32[]{:S(2)}) copy-start(f32[4096]{0:T(1024)} %param.12) | copy-start | bytes 49156
  61.8 13.6 %copy-start.24 = (s32[1,32,8]{1,2,0:T(8,128)S(1)}, s32[1,32,8]{1,2,0:T(8,128)}, u32[]{:S(2)}) copy-start(s32[1,32,8]{1,2,0:T(8,128)} %param.16) | copy-start | bytes 3076
  65.2 3.9 %collective-permute-start.9 = (bf16[33,16,128]{2,1,0:T(8,128)(2,1)S(1)}, bf16[33,16,128]{2,1,0:T(8,128)(2,1)S(1)}, u32[]{:S(2)}, u32[]{:S(2)}) collective-permute-start(bf16[33,16,128]{2,1,0:T(8,128)(2,1)S(1)} %get-tuple-element.23.refs_0_), channel_id=1, source_target_pairs={{0,7},{1,0},{2,1},{3,2},{4,3},{5,4},{6,5},{7,6},{8,15},{9,8},{10,9... | collective-permute-start | bytes 405512 | tf_op jit(solution)/shard_map/ppermute | solution.py:155
  65.2 5.1 %collective-permute-start.8 = (bf16[33,16,128]{2,1,0:T(8,128)(2,1)S(1)}, bf16[33,16,128]{2,1,0:T(8,128)(2,1)S(1)}, u32[]{:S(2)}, u32[]{:S(2)}) collective-permute-start(bf16[33,16,128]{2,1,0:T(8,128)(2,1)S(1)} %get-tuple-element.23.refs_0_), channel_id=1, source_target_pairs={{0,1},{1,2},{2,3},{3,4},{4,5},{5,6},{6,7},{7,0},{8,9},{9,10},{10,1... | collective-permute-start | bytes 405512 | tf_op jit(solution)/shard_map/ppermute | solution.py:154
  69.1 3.9 %collective-permute-start.11 = (bf16[33,16,128]{2,1,0:T(8,128)(2,1)S(1)}, bf16[33,16,128]{2,1,0:T(8,128)(2,1)S(1)}, u32[]{:S(2)}, u32[]{:S(2)}) collective-permute-start(bf16[33,16,128]{2,1,0:T(8,128)(2,1)S(1)} %collective-permute-done.9.refs_2_), channel_id=1, source_target_pairs={{0,7},{1,0},{2,1},{3,2},{4,3},{5,4},{6,5},{7,6},{8,15},{9,8},{10,9... | collective-permute-start | bytes 405512 | tf_op jit(solution)/shard_map/ppermute | solution.py:155
  70.3 5.1 %collective-permute-start.10 = (bf16[33,16,128]{2,1,0:T(8,128)(2,1)S(1)}, bf16[33,16,128]{2,1,0:T(8,128)(2,1)S(1)}, u32[]{:S(2)}, u32[]{:S(2)}) collective-permute-start(bf16[33,16,128]{2,1,0:T(8,128)(2,1)S(1)} %collective-permute-done.8.refs_1_), channel_id=1, source_target_pairs={{0,1},{1,2},{2,3},{3,4},{4,5},{5,6},{6,7},{7,0},{8,9},{9,10},{10,1... | collective-permute-start | bytes 405512 | tf_op jit(solution)/shard_map/ppermute | solution.py:154
  73.0 5.2 %collective-permute-start.13 = (bf16[33,16,128]{2,1,0:T(8,128)(2,1)S(1)}, bf16[33,16,128]{2,1,0:T(8,128)(2,1)S(1)}, u32[]{:S(2)}, u32[]{:S(2)}) collective-permute-start(bf16[33,16,128]{2,1,0:T(8,128)(2,1)S(1)} %collective-permute-done.11.refs_4_), channel_id=1, source_target_pairs={{0,7},{1,0},{2,1},{3,2},{4,3},{5,4},{6,5},{7,6},{8,15},{9,8},{10,9... | collective-permute-start | bytes 405512 | tf_op jit(solution)/shard_map/ppermute | solution.py:155
  75.4 5.4 %collective-permute-start.12 = (bf16[33,16,128]{2,1,0:T(8,128)(2,1)S(1)}, bf16[33,16,128]{2,1,0:T(8,128)(2,1)S(1)}, u32[]{:S(2)}, u32[]{:S(2)}) collective-permute-start(bf16[33,16,128]{2,1,0:T(8,128)(2,1)S(1)} %collective-permute-done.10.refs_3_), channel_id=1, source_target_pairs={{0,1},{1,2},{2,3},{3,4},{4,5},{5,6},{6,7},{7,0},{8,9},{9,10},{10,1... | collective-permute-start | bytes 405512 | tf_op jit(solution)/shard_map/ppermute | solution.py:154
  78.2 7.8 %collective-permute-start.15 = (bf16[17,16,128]{2,1,0:T(8,128)(2,1)S(1)}, bf16[17,16,128]{2,1,0:T(8,128)(2,1)S(1)}, u32[]{:S(2)}, u32[]{:S(2)}) collective-permute-start(bf16[17,16,128]{2,1,0:T(8,128)(2,1)S(1)} %slice.24), channel_id=1, source_target_pairs={{0,7},{1,0},{2,1},{3,2},{4,3},{5,4},{6,5},{7,6},{8,15},{9,8},{10,9... | collective-permute-start | bytes 208904 | tf_op jit(solution)/shard_map/ppermute | solution.py:158
  80.8 5.3 %collective-permute-start.14 = (bf16[16,16,128]{2,1,0:T(8,128)(2,1)S(1)}, bf16[16,16,128]{2,1,0:T(8,128)(2,1)S(1)}, u32[]{:S(2)}, u32[]{:S(2)}) collective-permute-start(bf16[16,16,128]{2,1,0:T(8,128)(2,1)S(1)} %slice.23), channel_id=1, source_target_pairs={{0,1},{1,2},{2,3},{3,4},{4,5},{5,6},{6,7},{7,0},{8,9},{9,10},{10,1... | collective-permute-start | bytes 196616 | tf_op jit(solution)/shard_map/ppermute | solution.py:157
  88.2 1.0 copy-start.2
  89.8 29.7 %all-to-all-start.1 = ((bf16[288,16,128]{2,1,0:T(8,128)(2,1)}), bf16[288,16,128]{2,1,0:T(8,128)(2,1)S(1)}, u32[]{:S(2)}, u32[]{:S(2)}) async-start(bf16[288,16,128]{2,1,0:T(8,128)(2,1)} %get-tuple-element.24), calls=%async_computation.1 | async-start | bytes 2359296 | tf_op jit(solution)/shard_map/all_to_all | solution.py:621
  101.2 1.2 copy-start.3
  119.6 1.0 copy-start.1
  120.5 0.9 copy-start.4
  121.5 0.9 copy-start.5
  123.4 1.0 copy-start.9
  124.3 1.0 copy-start.11
  (11 other events, 7.6 us)

commit v5 on v4

--- a/solution.py
+++ b/solution.py
@@ -51,6 +51,22 @@
     return jax.ShapeDtypeStruct(shape, dtype)
 
 
+def in_hbm(value):
+    return pltpu.with_memory_space_constraint(value, pltpu.HBM)
+
+
+def start_copies(pairs, sems, first=0):
+    copies = [pltpu.make_async_copy(source, target, sems.at[first + i]) for i, (source, target) in enumerate(pairs)]
+    for copy in copies:
+        copy.start()
+    return copies
+
+
+def wait_all(copies):
+    for copy in copies:
+        copy.wait()
+
+
 def dot_nt(left, right, precision=None):
     return lax.dot_general(
         left, right, (((1,), (1,)), ((), ())), precision=precision, preferred_element_type=F32
@@ -116,14 +132,7 @@
 
 
 def cast_kernel(field_hbm, degree_hbm, tiles_ref, field_ref, degree_ref, sems):
-    copies = [
-        pltpu.make_async_copy(field_hbm, field_ref, sems.at[0]),
-        pltpu.make_async_copy(degree_hbm, degree_ref, sems.at[1]),
-    ]
-    for copy in copies:
-        copy.start()
-    for copy in copies:
-        copy.wait()
+    wait_all(start_copies([(field_hbm, field_ref), (degree_hbm, degree_ref)], sems))
     for block in range(RB):
         tiles_ref[block + 2 * (block // HALF)] = field_ref[:, columns(block)].astype(BF16)
     for half in range(2):
@@ -187,13 +196,16 @@
 
 
 def first_select_kernel(offsets, n_row, place_ref, send_ref, *refs):
-    pieces, (part_ref, inverse_ref, chosen_hbm, rows_ref, chosen_ref, sems) = refs[:-6], refs[-6:]
+    pieces, (part_hbm, inverse_hbm, chosen_hbm) = refs[:-8], refs[-8:-5]
+    part_ref, inverse_ref, rows_ref, chosen_ref, sems = refs[-5:]
     for owner, half, piece, start in halves(offsets, pieces, HALF + 2, n_row, place_ref[0]):
         at = owner * RB + half * HALF
         part_ref[pl.ds(at, HALF)] = piece[start : start + HALF]
         inverse_ref[pl.ds(pl.multiple_of(at, HALF), HALF), :] = (
             piece[start + HALF].astype(F32) + piece[start + HALF + 1].astype(F32)
         )
+
+    copies = start_copies([(part_ref, part_hbm), (inverse_ref, inverse_hbm)], sems, 4)
 
     def fill(peer):
         for j in range(SEND):
@@ -205,6 +217,7 @@
         chosen_ref[peer * EXTRA + SEND] = jnp.concatenate([high, rows - high], axis=0).astype(BF16)
 
     fill_and_send(fill, chosen_ref, chosen_hbm, sems)
+    wait_all(copies)
 
 
 def first_select(gathered, place, send_list, n_row):
@@ -213,16 +226,22 @@
     peers = send_list.shape[0] // SEND
     return call(
         functools.partial(first_select_kernel, [offset for offset, _ in pieces], n_row),
-        (shaped((part, K, BS), BF16), shaped((part, BS), F32), pltpu.HBM((peers * EXTRA, K, BS), BF16)),
+        (pltpu.HBM((part, K, BS), BF16), pltpu.HBM((part, BS), F32), pltpu.HBM((peers * EXTRA, K, BS), BF16)),
         [SMEM, SMEM] + [VMEM] * (len(pieces) + 2),
-        (VMEM, VMEM, HBM),
-        (pltpu.VMEM((SEND, BS), F32), pltpu.VMEM((peers * EXTRA, K, BS), BF16), pltpu.SemaphoreType.DMA((4,))),
+        (HBM, HBM, HBM),
+        (
+            pltpu.VMEM((part, K, BS), BF16),
+            pltpu.VMEM((part, BS), F32),
+            pltpu.VMEM((SEND, BS), F32),
+            pltpu.VMEM((peers * EXTRA, K, BS), BF16),
+            pltpu.SemaphoreType.DMA((6,)),
+        ),
         moved=3000000,
     )(place, send_list, *[piece for _, piece in pieces], far_low, far_high)
 
 
 def second_select_kernel(offsets, n_row, place_ref, send_ref, pick_ref, *refs):
-    pieces, (part_ref, chosen_hbm, table_ref, chosen_ref, sems) = refs[:-5], refs[-5:]
+    pieces, (part_hbm, chosen_hbm, table_hbm, part_ref, chosen_ref, table_ref, sems) = refs[:-7], refs[-7:]
     lane = iota2((K, BS), 1)
     table = jnp.zeros((K, BS), F32)
     side_sum = jnp.zeros((K, BS), F32)
@@ -238,6 +257,7 @@
         table = jnp.where(lane == 8 + at, value, table)
     table = table.astype(BF16)
     table_ref[...] = table
+    copies = start_copies([(part_ref, part_hbm), (table_ref, table_hbm)], sems, 4)
     sides = dot_nn(table, pick_ref[...])
     for peer in range(chosen_ref.shape[0] // EXTRA):
         chosen_ref[peer * EXTRA + SEND] = sides[:, columns(peer)].astype(BF16)
@@ -247,6 +267,7 @@
             chosen_ref[peer * EXTRA + j] = part_ref[send_ref[peer * SEND + j]]
 
     fill_and_send(fill, chosen_ref, chosen_hbm, sems)
+    wait_all(copies)
 
 
 def second_select(gathered, place, send_list, pick, n_row):
@@ -254,10 +275,15 @@
     peers = send_list.shape[0] // SEND
     return call(
         functools.partial(second_select_kernel, [offset for offset, _ in pieces], n_row),
-        (shaped((n_row * RB, K, BS), BF16), pltpu.HBM((peers * EXTRA, K, BS), BF16), shaped((K, BS), BF16)),
+        (pltpu.HBM((n_row * RB, K, BS), BF16), pltpu.HBM((peers * EXTRA, K, BS), BF16), pltpu.HBM((K, BS), BF16)),
         [SMEM, SMEM] + [VMEM] * (len(pieces) + 3),
-        (VMEM, HBM, VMEM),
-        (pltpu.VMEM((peers * EXTRA, K, BS), BF16), pltpu.SemaphoreType.DMA((4,))),
+        (HBM, HBM, HBM),
+        (
+            pltpu.VMEM((n_row * RB, K, BS), BF16),
+            pltpu.VMEM((peers * EXTRA, K, BS), BF16),
+            pltpu.VMEM((K, BS), BF16),
+            pltpu.SemaphoreType.DMA((6,)),
+        ),
         moved=3000000,
     )(place, send_list, pick, *[piece for _, piece in pieces], far_low, far_high)
 
@@ -331,13 +357,14 @@
         HELD,
         flops=2 * SLOTS * K * BS * BS,
         moved=10000000,
-    )(own_list, counts, part_tiles, coupling)
+    )(own_list, counts, in_hbm(part_tiles), in_hbm(coupling))
 
 
 def image_kernel(
-    list_ref, count_ref, halo_ref, coupling_ref, own_ref, basis_ref, degree_ref, image_ref, tiles_ref, acc_ref, held,
-    sems,
+    list_ref, count_ref, halo_ref, coupling_ref, own_ref, basis_ref, degree_ref, image_hbm, tiles_ref, halo_hbm, image_ref,
+    out_sems, acc_ref, held, sems,
 ):
+    copies = start_copies([(halo_ref, halo_hbm)], out_sems)
     fetch(count_ref[2], coupling_ref, held, sems)
     acc_ref[...] = own_ref[...]
 
@@ -357,6 +384,7 @@
         image_ref[:, at] = image
         top = top + basis * image
         bottom = bottom + basis * basis
+    copies += start_copies([(image_ref, image_hbm)], out_sems, 1)
     top = jnp.sum(top, axis=1, keepdims=True)
     bottom = jnp.sum(bottom, axis=1, keepdims=True)
     usable = bottom > 1e-30
@@ -370,18 +398,19 @@
     for at, value in enumerate(split3(top) + split3(bottom)):
         side = jnp.where(lane == 1 + at, value, side)
     tiles_ref[RB] = side.astype(BF16)
+    wait_all(copies)
 
 
 def make_image(halo_list, counts, halo_tiles, coupling, own, basis, degree):
     return call(
         image_kernel,
-        (shaped(basis.shape, F32), shaped((RB + 1, K, BS), BF16)),
+        (pltpu.HBM(basis.shape, F32), shaped((RB + 1, K, BS), BF16), pltpu.HBM(halo_tiles.shape, BF16)),
         [SMEM, SMEM, VMEM, HBM, VMEM, VMEM, VMEM],
-        (VMEM, VMEM),
-        (pltpu.VMEM((RB + 1, K, BS), F32),) + HELD,
+        (HBM, VMEM, HBM),
+        (pltpu.VMEM(basis.shape, F32), pltpu.SemaphoreType.DMA((2,)), pltpu.VMEM((RB + 1, K, BS), F32)) + HELD,
         flops=2 * SLOTS * K * BS * BS,
         moved=8000000,
-    )(halo_list, counts, halo_tiles, coupling, own, basis, degree)
+    )(halo_list, counts, halo_tiles, in_hbm(coupling), own, basis, degree)
 
 
 def second_own_kernel(
@@ -409,13 +438,13 @@
 def second_own(own_list, counts, part_tiles, table, basis_part, inverse, coupling, n_row):
     return call(
         second_own_kernel,
-        (ROWS, ROWS),
+        (pltpu.HBM(ROWS.shape, F32), pltpu.HBM(ROWS.shape, F32)),
         [SMEM, SMEM, VMEM, VMEM, VMEM, VMEM, HBM],
         (VMEM, VMEM),
         HELD + (pltpu.VMEM((n_row, K, BS), F32),),
         flops=4 * SLOTS * K * BS * BS,
         moved=10000000,
-    )(own_list, counts, part_tiles, table, basis_part, inverse, coupling)
+    )(own_list, counts, *map(in_hbm, (part_tiles, table, basis_part, inverse, coupling)))
 
 
 def spread_kernel(taken_ref, given_ref):
@@ -471,21 +500,27 @@
 
 
 def gram_kernel(
-    list_ref, count_ref, halo_ref, basis_halo_ref, coupling_ref, own_ref, own_scaled_ref, basis_ref, image_ref, degree_ref,
-    previous_ref, previous_image_ref, residual_ref, residual_image_ref, packed_ref, acc_ref, scaled_ref, held, sems,
-    side_ref, quotient_ref, inverse_ref, stacked, stacked_image, wide_ref,
+    list_ref, count_ref, halo_ref, basis_halo_hbm, coupling_ref, own_hbm, own_scaled_hbm, basis_hbm, image_hbm, degree_hbm,
+    previous_hbm, previous_image_hbm, stacked, stacked_image, packed_ref, basis_halo_ref, acc_ref, scaled_ref, degree_ref,
+    in_sems, held, sems, side_ref, quotient_ref, inverse_ref, wide_ref,
 ):
+    early = [(basis_halo_hbm, basis_halo_ref), (own_hbm, acc_ref), (own_scaled_hbm, scaled_ref)]
+    late = [
+        (basis_hbm, stacked.at[0:16]),
+        (previous_hbm, stacked.at[32:48]),
+        (image_hbm, stacked_image.at[0:16]),
+        (previous_image_hbm, stacked_image.at[32:48]),
+        (degree_hbm, degree_ref),
+    ]
+    early = start_copies(early, in_sems)
     fetch(count_ref[2], coupling_ref, held, sems)
-    acc_ref[...] = own_ref[...]
-    scaled_ref[...] = own_scaled_ref[...]
+    late = start_copies(late, in_sems, 3)
     peers = halo_ref.shape[0] // EXTRA
     total = jnp.zeros((K, BS), F32)
     for peer in range(peers):
         side = halo_ref[peer * EXTRA + SEND]
         side_ref[peer * K : (peer + 1) * K, :] = side
         total = total + side.astype(F32)
-        inverse = basis_halo_ref[peer * EXTRA + SEND].astype(F32)
-        inverse_ref[peer * SEND : (peer + 1) * SEND, :] = inverse[0:SEND] + inverse[SEND:]
     side = side_ref[...]
     for j in range(SEND):
         spread = (iota2((BS, BS), 0) == j).astype(F32).astype(BF16)
@@ -494,6 +529,10 @@
     top = jnp.sum(jnp.where((lane >= 8) & (lane <= 10), total, 0.0), axis=1, keepdims=True)
     bottom = jnp.sum(jnp.where((lane >= 11) & (lane <= 13), total, 0.0), axis=1, keepdims=True)
     theta = top / bottom
+    wait_all(early)
+    for peer in range(peers):
+        inverse = basis_halo_ref[peer * EXTRA + SEND].astype(F32)
+        inverse_ref[peer * SEND : (peer + 1) * SEND, :] = inverse[0:SEND] + inverse[SEND:]
 
     def multiply(block, weights):
         tile = block + (block >> 3)
@@ -506,19 +545,13 @@
         scaled_ref[row] = scaled_ref[row] + product[K:]
 
     work(count_ref[1], count_ref[2], list_ref, coupling_ref, held, sems, multiply, add)
-    stacked[0:16] = basis_ref[...]
-    stacked[32:48] = previous_ref[...]
-    stacked_image[0:16] = image_ref[...]
-    stacked_image[32:48] = previous_image_ref[...]
+    wait_all(late)
     for block in range(RB):
         at = columns(block)
         degree = degree_ref[block : block + 1, :]
-        residual = (image_ref[:, at] - theta * basis_ref[:, at]) / degree
-        residual_ref[:, at] = residual
+        residual = (stacked_image[0:16, at] - theta * stacked[0:16, at]) / degree
         stacked[16:32, at] = residual
-        value = degree * residual - (acc_ref[block] - theta * scaled_ref[block])
-        residual_image_ref[:, at] = value
-        stacked_image[16:32, at] = value
+        stacked_image[16:32, at] = degree * residual - (acc_ref[block] - theta * scaled_ref[block])
     gram_b = dot_nt(stacked[...], stacked[...], HIGHEST)
     gram_a = dot_nt(stacked[...], stacked_image[...], HIGHEST)
     packed = pack_grams(gram_b, gram_a, wide_ref)
@@ -529,25 +562,32 @@
 def make_grams(
     halo_list, counts, halo_tiles, basis_halo, coupling, own, scaled, basis, image, degree, previous, previous_image, n_dom
 ):
-    width = basis.shape[1]
+    stack = shaped((3 * K, basis.shape[1]), F32)
     return call(
         gram_kernel,
-        (shaped(basis.shape, F32), shaped(basis.shape, F32), shaped((n_dom, 24, BS), F32)),
-        [SMEM, SMEM, VMEM, VMEM, HBM] + [VMEM] * 7,
+        (stack, stack, shaped((n_dom, 24, BS), F32)),
+        [SMEM, SMEM, VMEM] + [HBM] * 9,
         (VMEM, VMEM, VMEM),
-        (pltpu.VMEM((RB + 1, K, BS), F32), pltpu.VMEM((RB + 1, K, BS), F32))
+        (
+            pltpu.VMEM(basis_halo.shape, BF16),
+            pltpu.VMEM((RB + 1, K, BS), F32),
+            pltpu.VMEM((RB + 1, K, BS), F32),
+            pltpu.VMEM(degree.shape, F32),
+            pltpu.SemaphoreType.DMA((8,)),
+        )
         + HELD
         + (
             pltpu.VMEM((n_dom * K, BS), BF16),
             pltpu.VMEM((SEND, n_dom, K, BS), F32),
             pltpu.VMEM((n_dom * SEND, BS), F32),
-            pltpu.VMEM((48, width), F32),
-            pltpu.VMEM((48, width), F32),
             pltpu.VMEM((BS, BS), F32),
         ),
         flops=2 * SLOTS * K * BS * BS,
         moved=10000000,
-    )(halo_list, counts, halo_tiles, basis_halo, coupling, own, scaled, basis, image, degree, previous, previous_image)
+    )(
+        halo_list, counts, halo_tiles,
+        *map(in_hbm, (basis_halo, coupling, own, scaled, basis, image, degree, previous, previous_image)),
+    )
 
 
 def inverse_factor(gram, n):
@@ -571,8 +611,7 @@
 
 
 def final_kernel(
-    root_rows, taken_ref, basis_ref, residual_ref, previous_ref, image_ref, residual_image_ref, previous_image_ref,
-    new_basis_ref, new_image_ref, wide_ref, stacked,
+    root_rows, taken_ref, stacked_ref, stacked_image_ref, new_basis_ref, new_image_ref, wide_ref
 ):
     packed = taken_ref[0]
     for peer in range(1, taken_ref.shape[0]):
@@ -595,26 +634,21 @@
     wide_ref[0:16, 0:16] = inner
     sub_inverse = inverse_factor(wide_ref[0:16, :], 16)[:, 0:16]
     coeff = dot_nn(dot_nn(sub_inverse, turned, HIGHEST), inverse, HIGHEST) * root_rows
-    stacked[0:16] = basis_ref[...]
-    stacked[16:32] = residual_ref[...]
-    stacked[32:48] = previous_ref[...]
-    new_basis_ref[...] = dot_nn(coeff, stacked[...], HIGHEST)
-    stacked[0:16] = image_ref[...]
-    stacked[16:32] = residual_image_ref[...]
-    stacked[32:48] = previous_image_ref[...]
-    new_image_ref[...] = dot_nn(coeff, stacked[...], HIGHEST)
-
-
-def finish(root_rows, packed, basis, residual, previous, image, residual_image, previous_image):
+    new_basis_ref[...] = dot_nn(coeff, stacked_ref[...], HIGHEST)
+    new_image_ref[...] = dot_nn(coeff, stacked_image_ref[...], HIGHEST)
+
+
+def finish(root_rows, packed, stacked, stacked_image):
+    shape = (K, stacked.shape[1])
     return call(
         functools.partial(final_kernel, root_rows),
-        (shaped(basis.shape, F32), shaped(basis.shape, F32)),
-        [VMEM] * 7,
+        (shaped(shape, F32), shaped(shape, F32)),
+        [VMEM] * 3,
         (VMEM, VMEM),
-        (pltpu.VMEM((BS, BS), F32), pltpu.VMEM((48, basis.shape[1]), F32)),
+        (pltpu.VMEM((BS, BS), F32),),
         flops=1000000,
         moved=3000000,
-    )(packed, basis, residual, previous, image, residual_image, previous_image)
+    )(packed, stacked, stacked_image)
 
 
 def to_all(value, axis):
@@ -629,27 +663,25 @@
     place = lax.axis_index("row").astype(jnp.int32).reshape(1)
     send_list = send_lists.reshape(n_dom * SEND)
     degree = degree.reshape(RB, BS)
-    coupling = pltpu.with_memory_space_constraint(coupling, pltpu.HBM)
     own_list, halo_list, counts = make_lists(slot_row, slot_column, live_slots, part)
 
-    in_hbm = [pltpu.with_memory_space_constraint(value, pltpu.HBM) for value in (basis, degree)]
-    gathered = gather_row(cast_tiles(*in_hbm), n_row, HALF + 2)
+    gathered = gather_row(cast_tiles(in_hbm(basis), in_hbm(degree)), n_row, HALF + 2)
     basis_part, inverse, chosen = first_select(gathered, place, send_list, n_row)
-    basis_halo = to_all(chosen, "dom")
+    halo_tiles = to_all(chosen, "dom")
     own = first_own(own_list, counts, basis_part, coupling)
-    image, tiles = make_image(halo_list, counts, basis_halo, coupling, own, basis, degree)
+    image, tiles, basis_halo = make_image(halo_list, counts, halo_tiles, coupling, own, basis, degree)
 
     gathered = gather_row(tiles, n_row, HALF)
     part_tiles, chosen, table = second_select(gathered, place, send_list, picks(send_list), n_row)
     halo_tiles = to_all(chosen, "dom")
     own, scaled = second_own(own_list, counts, part_tiles, table, basis_part, inverse, coupling, n_row)
-    residual, residual_image, packed = make_grams(
+    stacked, stacked_image, packed = make_grams(
         halo_list, counts, halo_tiles, basis_halo, coupling, own, scaled, basis, image, degree, previous, previous_image,
         n_dom,
     )
     packed = to_all(add_and_repeat(to_all(packed, "dom"), n_row), "row")
     root_rows = math.sqrt(basis.shape[1] * n_dom * n_row)
-    return finish(root_rows, packed, basis, residual, previous, image, residual_image, previous_image)
+    return finish(root_rows, packed, stacked, stacked_image)
 
 
 def solution(mesh):

time: 163 us -> 158 us (0.969)
  local copies, waits for them, and re-layouts: 15.6 us -> 1.06 us
  Pallas kernels: 23.3 us -> 32.9 us
  starting transfers between devices: 47.5 us -> 45.4 us
    unnamed x51 -> x11, local copies, waits for them, and re-layouts: 15.3 us -> 0.79 us
    pallas_call x10, Pallas kernels: 23.3 us -> 32.9 us  [run(): pl.pallas_call(kernel, out_shape=out_shape, in_specs=in_specs, out_specs=...]
  transfers between devices with their start and end apart: 18 -> 18, of which waited for: 12 -> 14; matrix products, arithmetic and copies ran while one was open for 1% -> 1% of each run, Pallas kernels for 4% -> 8%
where the time goes in v5:
time: 158 us; the launch traced here: 156 us
  waiting for transfers between devices  48 us (30%)
  starting transfers between devices  45.4 us (29%)
  Pallas kernels  32.9 us (21%)
  blocking collectives  27.2 us (17%)
    pallas_call x10, Pallas kernels, run(): pl.pallas_call(kernel, out_shape=out_shape, in_specs=in_specs, out_specs=...  32.9 us
    all_to_all x2, blocking collectives, to_all(): return lax.all_to_all(value, axis, split_axis=0, concat_axis=0, tiled=True)  27.2 us
    all_to_all x2, waiting for transfers between devices, to_all(): return lax.all_to_all(value, axis, split_axis=0, concat_axis=0, tiled=True)  23.7 us
    all_to_all x2, starting transfers between devices, to_all(): return lax.all_to_all(value, axis, split_axis=0, concat_axis=0, tiled=True)  22.7 us
    ppermute x6, starting transfers between devices, gather_row(): from_above = lax.ppermute(from_above, 'row', down)  16.1 us
    ppermute x6, waiting for transfers between devices, gather_row(): from_above = lax.ppermute(from_above, 'row', down)  15.2 us
    ppermute x2, waiting for transfers between devices, gather_row(): far_low = lax.ppermute(from_below[:half], 'row', up)  8.1 us
    ppermute x2, starting transfers between devices, gather_row(): far_high = lax.ppermute(from_above[half:], 'row', down)  4.88 us
  transfers between devices with their start and end apart: 18, of which 14 were waited for; matrix products, arithmetic and copies ran while one was open for 1% of the time, Pallas kernels for 8%

profile of v5, /device:TPU:1, one launch (start us, length us, event | category | flops | bytes accessed | tf_op | source)
XLA Modules:
  0.0 156.3 jit_solution(6177752558142958204)
XLA Ops:
  0.6 1.0 shard_map.105.refs_0_
  1.6 6.5 %collective-permute-start.1 = (bf16[36,16,128]{2,1,0:T(8,128)(2,1)S(1)}, bf16[36,16,128]{2,1,0:T(8,128)(2,1)S(1)}, u32[]{:S(2)}, u32[]{:S(2)}) collective-permute-start(bf16[36,16,128]{2,1,0:T(8,128)(2,1)S(1)} %shard_map.105.refs_0_), channel_id=1, source_target_pairs={{0,7},{1,0},{2,1},{3,2},{4,3},{5,4},{6,5},{7,6},{8,15},{9,8},{10,9... | collective-permute-start | bytes 442376 | tf_op jit(solution)/shard_map/ppermute | solution.py:164
  8.1 2.5 %collective-permute-done.1.refs_2_ = bf16[36,16,128]{2,1,0:T(8,128)(2,1)S(1)} collective-permute-done((bf16[36,16,128]{2,1,0:T(8,128)(2,1)S(1)}, bf16[36,16,128]{2,1,0:T(8,128)(2,1)S(1)}, u32[]{:S(2)}, u32[]{:S(2)}) %collective-permute-start.1) | collective-permute-done | bytes 147488 | tf_op jit(solution)/shard_map/ppermute | solution.py:164
  10.6 3.4 %collective-permute-start.3 = (bf16[36,16,128]{2,1,0:T(8,128)(2,1)S(1)}, bf16[36,16,128]{2,1,0:T(8,128)(2,1)S(1)}, u32[]{:S(2)}, u32[]{:S(2)}) collective-permute-start(bf16[36,16,128]{2,1,0:T(8,128)(2,1)S(1)} %collective-permute-done.1.refs_2_), channel_id=1, source_target_pairs={{0,7},{1,0},{2,1},{3,2},{4,3},{5,4},{6,5},{7,6},{8,15},{9,8},{10,9... | collective-permute-start | bytes 442376 | tf_op jit(solution)/shard_map/ppermute | solution.py:164
  14.0 2.1 %collective-permute-done.3.refs_4_ = bf16[36,16,128]{2,1,0:T(8,128)(2,1)S(1)} collective-permute-done((bf16[36,16,128]{2,1,0:T(8,128)(2,1)S(1)}, bf16[36,16,128]{2,1,0:T(8,128)(2,1)S(1)}, u32[]{:S(2)}, u32[]{:S(2)}) %collective-permute-start.3) | collective-permute-done | bytes 147488 | tf_op jit(solution)/shard_map/ppermute | solution.py:164
  16.1 3.1 %collective-permute-start.5 = (bf16[36,16,128]{2,1,0:T(8,128)(2,1)S(1)}, bf16[36,16,128]{2,1,0:T(8,128)(2,1)S(1)}, u32[]{:S(2)}, u32[]{:S(2)}) collective-permute-start(bf16[36,16,128]{2,1,0:T(8,128)(2,1)S(1)} %collective-permute-done.3.refs_4_), channel_id=1, source_target_pairs={{0,7},{1,0},{2,1},{3,2},{4,3},{5,4},{6,5},{7,6},{8,15},{9,8},{10,9... | collective-permute-start | bytes 442376 | tf_op jit(solution)/shard_map/ppermute | solution.py:164
  19.3 2.1 %collective-permute-done.5.refs_6_ = bf16[36,16,128]{2,1,0:T(8,128)(2,1)S(1)} collective-permute-done((bf16[36,16,128]{2,1,0:T(8,128)(2,1)S(1)}, bf16[36,16,128]{2,1,0:T(8,128)(2,1)S(1)}, u32[]{:S(2)}, u32[]{:S(2)}) %collective-permute-start.5) | collective-permute-done | bytes 147488 | tf_op jit(solution)/shard_map/ppermute | solution.py:164
  21.4 3.1 %collective-permute-start.7 = (bf16[18,16,128]{2,1,0:T(8,128)(2,1)S(1)}, bf16[18,16,128]{2,1,0:T(8,128)(2,1)S(1)}, u32[]{:S(2)}, u32[]{:S(2)}) collective-permute-start(bf16[18,16,128]{2,1,0:T(8,128)(2,1)S(1)} %slice.22), channel_id=1, source_target_pairs={{0,7},{1,0},{2,1},{3,2},{4,3},{5,4},{6,5},{7,6},{8,15},{9,8},{10,9... | collective-permute-start | bytes 221192 | tf_op jit(solution)/shard_map/ppermute | solution.py:167
  24.6 0.8 copy.12
  25.9 3.1 %collective-permute-done.6.refs_7_ = bf16[18,16,128]{2,1,0:T(8,128)(2,1)S(1)} collective-permute-done((bf16[18,16,128]{2,1,0:T(8,128)(2,1)S(1)}, bf16[18,16,128]{2,1,0:T(8,128)(2,1)S(1)}, u32[]{:S(2)}, u32[]{:S(2)}) %collective-permute-start.6) | collective-permute-done | bytes 73760 | tf_op jit(solution)/shard_map/ppermute | solution.py:166
  29.0 2.1 %shard_map.106 = (bf16[256,16,128]{2,1,0:T(8,128)(2,1)}, f32[256,128]{1,0:T(8,128)}, bf16[288,16,128]{2,1,0:T(8,128)(2,1)}) custom-call(s32[1]{0:T(128)} %bitcast.place_ref, s32[256]{0:T(256)S(1)} %reshape.19.send_ref, bf16[36,16,128]{2,1,0:T(8,128)(2,1)S(1)} %shard_map.105.refs_0_, bf16[36,16,128]{2,1,0:T(8,128)(2,1)S(1)} %collective-permute-done.refs_1_, ...), custom_call_target="tpu_custom_call" | custom-call | bytes 3000000 | tf_op jit(solution)/shard_map/pallas_call | solution.py:37
  31.1 12.4 %all-to-all-start = ((bf16[288,16,128]{2,1,0:T(8,128)(2,1)}), bf16[288,16,128]{2,1,0:T(8,128)(2,1)S(1)}, u32[]{:S(2)}, u32[]{:S(2)}) async-start(bf16[288,16,128]{2,1,0:T(8,128)(2,1)} %get-tuple-element.21), calls=%async_computation | async-start | bytes 2359296 | tf_op jit(solution)/shard_map/all_to_all | solution.py:655
  44.1 2.2 %shard_map.104 = (s32[288]{0:T(512)S(1)}, s32[288]{0:T(512)S(1)}, s32[3]{0:T(128)S(1)}) custom-call(s32[256]{0:T(256)S(1)} %copy-done.2, s32[256]{0:T(256)S(1)} %copy-done.3, s32[1]{0:T(128)S(6)} %copy.14.live_ref), custom_call_target="tpu_custom_call" | custom-call | bytes 20000 | tf_op jit(solution)/shard_map/pallas_call | solution.py:37
  46.3 4.5 %shard_map.107.own_ref = f32[33,16,128]{2,1,0:T(8,128)S(1)} custom-call(s32[288]{0:T(512)S(1)} %get-tuple-element.22.list_ref, s32[3]{0:T(128)S(1)} %get-tuple-element.20.count_ref, bf16[256,16,128]{2,1,0:T(8,128)(2,1)} %get-tuple-element.23.part_ref.basis_part_ref, bf16[256,128,128]{2,1,0:T(8,128)(2,1)} %coupling_ref.7), custom_call_target="tpu_custom_call" | custom-call | flops 134217728 | bytes 10000000 | tf_op jit(solution)/shard_map/pallas_call | solution.py:37
  50.9 10.9 %all-to-all-done.halo_ref = bf16[288,16,128]{2,1,0:T(8,128)(2,1)S(1)} async-done(((bf16[288,16,128]{2,1,0:T(8,128)(2,1)}), bf16[288,16,128]{2,1,0:T(8,128)(2,1)S(1)}, u32[]{:S(2)}, u32[]{:S(2)}) %all-to-all-start) | async-done | bytes 1179680 | tf_op jit(solution)/shard_map/all_to_all | solution.py:655
  61.8 4.7 %shard_map.108 = (f32[16,4096]{1,0:T(8,128)}, bf16[33,16,128]{2,1,0:T(8,128)(2,1)S(1)}, bf16[288,16,128]{2,1,0:T(8,128)(2,1)}) custom-call(s32[288]{0:T(512)S(1)} %get-tuple-element.19.list_ref, s32[3]{0:T(128)S(1)} %get-tuple-element.20.count_ref, bf16[288,16,128]{2,1,0:T(8,128)(2,1)S(1)} %all-to-all-done.halo_ref, bf16[256,128,128]{2,1,0:T(8,128)(2,1)} %coupling_ref.7, ...), custom_call_target="tpu_custom_call" | custom-call | flops 134217728 | bytes 8000000 | tf_op jit(solution)/shard_map/pallas_call | solution.py:37
  66.6 1.5 collective-permute-start.8
  68.2 2.3 %collective-permute-done.9.refs_2_ = bf16[33,16,128]{2,1,0:T(8,128)(2,1)S(1)} collective-permute-done((bf16[33,16,128]{2,1,0:T(8,128)(2,1)S(1)}, bf16[33,16,128]{2,1,0:T(8,128)(2,1)S(1)}, u32[]{:S(2)}, u32[]{:S(2)}) %collective-permute-start.9) | collective-permute-done | bytes 135200 | tf_op jit(solution)/shard_map/ppermute | solution.py:164
  70.5 1.2 collective-permute-start.11
  72.0 3.0 %collective-permute-done.11.refs_4_ = bf16[33,16,128]{2,1,0:T(8,128)(2,1)S(1)} collective-permute-done((bf16[33,16,128]{2,1,0:T(8,128)(2,1)S(1)}, bf16[33,16,128]{2,1,0:T(8,128)(2,1)S(1)}, u32[]{:S(2)}, u32[]{:S(2)}) %collective-permute-start.11) | collective-permute-done | bytes 135200 | tf_op jit(solution)/shard_map/ppermute | solution.py:164
  75.0 1.8 %collective-permute-start.13 = (bf16[33,16,128]{2,1,0:T(8,128)(2,1)S(1)}, bf16[33,16,128]{2,1,0:T(8,128)(2,1)S(1)}, u32[]{:S(2)}, u32[]{:S(2)}) collective-permute-start(bf16[33,16,128]{2,1,0:T(8,128)(2,1)S(1)} %collective-permute-done.11.refs_4_), channel_id=1, source_target_pairs={{0,7},{1,0},{2,1},{3,2},{4,3},{5,4},{6,5},{7,6},{8,15},{9,8},{10,9... | collective-permute-start | bytes 405512 | tf_op jit(solution)/shard_map/ppermute | solution.py:164
  77.0 3.2 %collective-permute-done.13.refs_6_ = bf16[33,16,128]{2,1,0:T(8,128)(2,1)S(1)} collective-permute-done((bf16[33,16,128]{2,1,0:T(8,128)(2,1)S(1)}, bf16[33,16,128]{2,1,0:T(8,128)(2,1)S(1)}, u32[]{:S(2)}, u32[]{:S(2)}) %collective-permute-start.13) | collective-permute-done | bytes 135200 | tf_op jit(solution)/shard_map/ppermute | solution.py:164
  80.3 1.8 %collective-permute-start.15 = (bf16[17,16,128]{2,1,0:T(8,128)(2,1)S(1)}, bf16[17,16,128]{2,1,0:T(8,128)(2,1)S(1)}, u32[]{:S(2)}, u32[]{:S(2)}) collective-permute-start(bf16[17,16,128]{2,1,0:T(8,128)(2,1)S(1)} %slice.24), channel_id=1, source_target_pairs={{0,7},{1,0},{2,1},{3,2},{4,3},{5,4},{6,5},{7,6},{8,15},{9,8},{10,9... | collective-permute-start | bytes 208904 | tf_op jit(solution)/shard_map/ppermute | solution.py:167
  82.6 5.0 %collective-permute-done.14.refs_7_ = bf16[16,16,128]{2,1,0:T(8,128)(2,1)S(1)} collective-permute-done((bf16[16,16,128]{2,1,0:T(8,128)(2,1)S(1)}, bf16[16,16,128]{2,1,0:T(8,128)(2,1)S(1)}, u32[]{:S(2)}, u32[]{:S(2)}) %collective-permute-start.14) | collective-permute-done | bytes 65568 | tf_op jit(solution)/shard_map/ppermute | solution.py:166
  87.6 2.3 %shard_map.109 = (bf16[256,16,128]{2,1,0:T(8,128)(2,1)}, bf16[288,16,128]{2,1,0:T(8,128)(2,1)}, bf16[16,128]{1,0:T(8,128)(2,1)}) custom-call(s32[1]{0:T(128)} %bitcast.place_ref, s32[256]{0:T(256)S(1)} %reshape.19.send_ref, bf16[128,4096]{1,0:T(8,128)(2,1)S(1)} %fusion.pick_ref, bf16[33,16,128]{2,1,0:T(8,128)(2,1)S(1)} %get-tuple-element.24.refs_0_, ...), custom_call_target="tpu_custom_call" | custom-call | bytes 3000000 | tf_op jit(solution)/shard_map/pallas_call | solution.py:37
  89.9 10.3 %all-to-all-start.1 = ((bf16[288,16,128]{2,1,0:T(8,128)(2,1)}), bf16[288,16,128]{2,1,0:T(8,128)(2,1)S(1)}, u32[]{:S(2)}, u32[]{:S(2)}) async-start(bf16[288,16,128]{2,1,0:T(8,128)(2,1)} %get-tuple-element.25), calls=%async_computation.1 | async-start | bytes 2359296 | tf_op jit(solution)/shard_map/all_to_all | solution.py:655
  100.3 5.7 %shard_map.110 = (f32[33,16,128]{2,1,0:T(8,128)}, f32[33,16,128]{2,1,0:T(8,128)}) custom-call(s32[288]{0:T(512)S(1)} %get-tuple-element.22.list_ref, s32[3]{0:T(128)S(1)} %get-tuple-element.20.count_ref, bf16[256,16,128]{2,1,0:T(8,128)(2,1)} %get-tuple-element.27.part_ref, bf16[16,128]{1,0:T(8,128)(2,1)} %get-tuple-element.28.table_ref, ...), custom_call_target="tpu_custom_call" | custom-call | flops 268435456 | bytes 10000000 | tf_op jit(solution)/shard_map/pallas_call | solution.py:37
  105.9 12.8 %all-to-all-done.1.halo_ref = bf16[288,16,128]{2,1,0:T(8,128)(2,1)S(1)} async-done(((bf16[288,16,128]{2,1,0:T(8,128)(2,1)}), bf16[288,16,128]{2,1,0:T(8,128)(2,1)S(1)}, u32[]{:S(2)}, u32[]{:S(2)}) %all-to-all-start.1) | async-done | bytes 1179680 | tf_op jit(solution)/shard_map/all_to_all | solution.py:655
  118.7 5.7 %shard_map.111 = (f32[48,4096]{1,0:T(8,128)S(1)}, f32[48,4096]{1,0:T(8,128)S(1)}, f32[32,24,128]{2,1,0:T(8,128)S(1)}) custom-call(s32[288]{0:T(512)S(1)} %get-tuple-element.19.list_ref, s32[3]{0:T(128)S(1)} %get-tuple-element.20.count_ref, bf16[288,16,128]{2,1,0:T(8,128)(2,1)S(1)} %all-to-all-done.1.halo_ref, ...), custom_call_target="tpu_custom_call" | custom-call | flops 134217728 | bytes 10000000 | tf_op jit(solution)/shard_map/pallas_call | solution.py:37
  124.4 16.0 %all_to_all.20.taken_ref = f32[32,24,128]{2,1,0:T(8,128)S(1)} all-to-all(f32[32,24,128]{2,1,0:T(8,128)S(1)} %get-tuple-element.33), channel_id=1, replica_groups=mesh['dom'=32,'row'=8] {'dom'}, dimensions={0} | all-to-all | bytes 786432 | tf_op jit(solution)/shard_map/all_to_all | solution.py:655
  140.4 11.2 %all_to_all.21.taken_ref = f32[8,24,128]{2,1,0:T(8,128)S(1)} all-to-all(f32[8,24,128]{2,1,0:T(8,128)S(1)} %shard_map.112), channel_id=1, replica_groups=mesh['dom'=32,'row'=8] {'row'}, dimensions={0} | all-to-all | bytes 196608 | tf_op jit(solution)/shard_map/all_to_all | solution.py:655
  151.6 4.7 %shard_map.113 = (f32[16,4096]{1,0:T(8,128)}, f32[16,4096]{1,0:T(8,128)}) custom-call(f32[8,24,128]{2,1,0:T(8,128)S(1)} %all_to_all.21.taken_ref, f32[48,4096]{1,0:T(8,128)S(1)} %get-tuple-element.34.stacked_ref, f32[48,4096]{1,0:T(8,128)S(1)} %get-tuple-element.35.stacked_image_ref), custom_call_target="tpu_custom_call" | custom-call | flops 1000000 | bytes 3000000 | tf_op jit(solution)/shard_map/pallas_call | solution.py:37
  (39 shorter events, 1.9 us)
Async XLA Ops:
  1.6 9.0 %collective-permute-start.1 = (bf16[36,16,128]{2,1,0:T(8,128)(2,1)S(1)}, bf16[36,16,128]{2,1,0:T(8,128)(2,1)S(1)}, u32[]{:S(2)}, u32[]{:S(2)}) collective-permute-start(bf16[36,16,128]{2,1,0:T(8,128)(2,1)S(1)} %shard_map.105.refs_0_), channel_id=1, source_target_pairs={{0,7},{1,0},{2,1},{3,2},{4,3},{5,4},{6,5},{7,6},{8,15},{9,8},{10,9... | collective-permute-start | bytes 442376 | tf_op jit(solution)/shard_map/ppermute | solution.py:164
  8.1 5.9 %collective-permute-start = (bf16[36,16,128]{2,1,0:T(8,128)(2,1)S(1)}, bf16[36,16,128]{2,1,0:T(8,128)(2,1)S(1)}, u32[]{:S(2)}, u32[]{:S(2)}) collective-permute-start(bf16[36,16,128]{2,1,0:T(8,128)(2,1)S(1)} %shard_map.105.refs_0_), channel_id=1, source_target_pairs={{0,1},{1,2},{2,3},{3,4},{4,5},{5,6},{6,7},{7,0},{8,9},{9,10},{10,1... | collective-permute-start | bytes 442376 | tf_op jit(solution)/shard_map/ppermute | solution.py:163
  10.6 5.5 %collective-permute-start.3 = (bf16[36,16,128]{2,1,0:T(8,128)(2,1)S(1)}, bf16[36,16,128]{2,1,0:T(8,128)(2,1)S(1)}, u32[]{:S(2)}, u32[]{:S(2)}) collective-permute-start(bf16[36,16,128]{2,1,0:T(8,128)(2,1)S(1)} %collective-permute-done.1.refs_2_), channel_id=1, source_target_pairs={{0,7},{1,0},{2,1},{3,2},{4,3},{5,4},{6,5},{7,6},{8,15},{9,8},{10,9... | collective-permute-start | bytes 442376 | tf_op jit(solution)/shard_map/ppermute | solution.py:164
  14.0 5.2 %collective-permute-start.2 = (bf16[36,16,128]{2,1,0:T(8,128)(2,1)S(1)}, bf16[36,16,128]{2,1,0:T(8,128)(2,1)S(1)}, u32[]{:S(2)}, u32[]{:S(2)}) collective-permute-start(bf16[36,16,128]{2,1,0:T(8,128)(2,1)S(1)} %collective-permute-done.refs_1_), channel_id=1, source_target_pairs={{0,1},{1,2},{2,3},{3,4},{4,5},{5,6},{6,7},{7,0},{8,9},{9,10},{10,1... | collective-permute-start | bytes 442376 | tf_op jit(solution)/shard_map/ppermute | solution.py:163
  16.1 5.2 %collective-permute-start.5 = (bf16[36,16,128]{2,1,0:T(8,128)(2,1)S(1)}, bf16[36,16,128]{2,1,0:T(8,128)(2,1)S(1)}, u32[]{:S(2)}, u32[]{:S(2)}) collective-permute-start(bf16[36,16,128]{2,1,0:T(8,128)(2,1)S(1)} %collective-permute-done.3.refs_4_), channel_id=1, source_target_pairs={{0,7},{1,0},{2,1},{3,2},{4,3},{5,4},{6,5},{7,6},{8,15},{9,8},{10,9... | collective-permute-start | bytes 442376 | tf_op jit(solution)/shard_map/ppermute | solution.py:164
  19.3 5.2 %collective-permute-start.4 = (bf16[36,16,128]{2,1,0:T(8,128)(2,1)S(1)}, bf16[36,16,128]{2,1,0:T(8,128)(2,1)S(1)}, u32[]{:S(2)}, u32[]{:S(2)}) collective-permute-start(bf16[36,16,128]{2,1,0:T(8,128)(2,1)S(1)} %collective-permute-done.2.refs_3_), channel_id=1, source_target_pairs={{0,1},{1,2},{2,3},{3,4},{4,5},{5,6},{6,7},{7,0},{8,9},{9,10},{10,1... | collective-permute-start | bytes 442376 | tf_op jit(solution)/shard_map/ppermute | solution.py:163
  21.4 4.5 %collective-permute-start.7 = (bf16[18,16,128]{2,1,0:T(8,128)(2,1)S(1)}, bf16[18,16,128]{2,1,0:T(8,128)(2,1)S(1)}, u32[]{:S(2)}, u32[]{:S(2)}) collective-permute-start(bf16[18,16,128]{2,1,0:T(8,128)(2,1)S(1)} %slice.22), channel_id=1, source_target_pairs={{0,7},{1,0},{2,1},{3,2},{4,3},{5,4},{6,5},{7,6},{8,15},{9,8},{10,9... | collective-permute-start | bytes 221192 | tf_op jit(solution)/shard_map/ppermute | solution.py:167
  24.5 4.5 %collective-permute-start.6 = (bf16[18,16,128]{2,1,0:T(8,128)(2,1)S(1)}, bf16[18,16,128]{2,1,0:T(8,128)(2,1)S(1)}, u32[]{:S(2)}, u32[]{:S(2)}) collective-permute-start(bf16[18,16,128]{2,1,0:T(8,128)(2,1)S(1)} %slice.21), channel_id=1, source_target_pairs={{0,1},{1,2},{2,3},{3,4},{4,5},{5,6},{6,7},{7,0},{8,9},{9,10},{10,1... | collective-permute-start | bytes 221192 | tf_op jit(solution)/shard_map/ppermute | solution.py:166
  31.1 13.1 %copy-start.2 = (s32[256]{0:T(256)S(1)}, s32[256]{0:T(256)}, u32[]{:S(2)}) copy-start(s32[256]{0:T(256)} %row_ref.1) | copy-start | bytes 3076
  31.1 13.0 %copy-start.3 = (s32[256]{0:T(256)S(1)}, s32[256]{0:T(256)}, u32[]{:S(2)}) copy-start(s32[256]{0:T(256)} %column_ref.1) | copy-start | bytes 3076
  31.1 30.7 %all-to-all-start = ((bf16[288,16,128]{2,1,0:T(8,128)(2,1)}), bf16[288,16,128]{2,1,0:T(8,128)(2,1)S(1)}, u32[]{:S(2)}, u32[]{:S(2)}) async-start(bf16[288,16,128]{2,1,0:T(8,128)(2,1)} %get-tuple-element.21), calls=%async_computation | async-start | bytes 2359296 | tf_op jit(solution)/shard_map/all_to_all | solution.py:655
  46.3 15.5 %copy-start = (f32[16,4096]{1,0:T(8,128)S(1)}, f32[16,4096]{1,0:T(8,128)}, u32[]{:S(2)}) copy-start(f32[16,4096]{1,0:T(8,128)} %basis_hbm.1) | copy-start | bytes 786436
  46.3 15.5 %copy-start.1 = (f32[4096]{0:T(1024)S(1)}, f32[4096]{0:T(1024)}, u32[]{:S(2)}) copy-start(f32[4096]{0:T(1024)} %param.12) | copy-start | bytes 49156
  61.8 15.1 %copy-start.4 = (s32[1,32,8]{1,2,0:T(8,128)S(1)}, s32[1,32,8]{1,2,0:T(8,128)}, u32[]{:S(2)}) copy-start(s32[1,32,8]{1,2,0:T(8,128)} %param.16) | copy-start | bytes 3076
  66.6 3.9 %collective-permute-start.9 = (bf16[33,16,128]{2,1,0:T(8,128)(2,1)S(1)}, bf16[33,16,128]{2,1,0:T(8,128)(2,1)S(1)}, u32[]{:S(2)}, u32[]{:S(2)}) collective-permute-start(bf16[33,16,128]{2,1,0:T(8,128)(2,1)S(1)} %get-tuple-element.24.refs_0_), channel_id=1, source_target_pairs={{0,7},{1,0},{2,1},{3,2},{4,3},{5,4},{6,5},{7,6},{8,15},{9,8},{10,9... | collective-permute-start | bytes 405512 | tf_op jit(solution)/shard_map/ppermute | solution.py:164
  66.6 5.2 %collective-permute-start.8 = (bf16[33,16,128]{2,1,0:T(8,128)(2,1)S(1)}, bf16[33,16,128]{2,1,0:T(8,128)(2,1)S(1)}, u32[]{:S(2)}, u32[]{:S(2)}) collective-permute-start(bf16[33,16,128]{2,1,0:T(8,128)(2,1)S(1)} %get-tuple-element.24.refs_0_), channel_id=1, source_target_pairs={{0,1},{1,2},{2,3},{3,4},{4,5},{5,6},{6,7},{7,0},{8,9},{9,10},{10,1... | collective-permute-start | bytes 405512 | tf_op jit(solution)/shard_map/ppermute | solution.py:163
  70.5 4.5 %collective-permute-start.11 = (bf16[33,16,128]{2,1,0:T(8,128)(2,1)S(1)}, bf16[33,16,128]{2,1,0:T(8,128)(2,1)S(1)}, u32[]{:S(2)}, u32[]{:S(2)}) collective-permute-start(bf16[33,16,128]{2,1,0:T(8,128)(2,1)S(1)} %collective-permute-done.9.refs_2_), channel_id=1, source_target_pairs={{0,7},{1,0},{2,1},{3,2},{4,3},{5,4},{6,5},{7,6},{8,15},{9,8},{10,9... | collective-permute-start | bytes 405512 | tf_op jit(solution)/shard_map/ppermute | solution.py:164
  71.8 5.1 %collective-permute-start.10 = (bf16[33,16,128]{2,1,0:T(8,128)(2,1)S(1)}, bf16[33,16,128]{2,1,0:T(8,128)(2,1)S(1)}, u32[]{:S(2)}, u32[]{:S(2)}) collective-permute-start(bf16[33,16,128]{2,1,0:T(8,128)(2,1)S(1)} %collective-permute-done.8.refs_1_), channel_id=1, source_target_pairs={{0,1},{1,2},{2,3},{3,4},{4,5},{5,6},{6,7},{7,0},{8,9},{9,10},{10,1... | collective-permute-start | bytes 405512 | tf_op jit(solution)/shard_map/ppermute | solution.py:163
  75.0 5.3 %collective-permute-start.13 = (bf16[33,16,128]{2,1,0:T(8,128)(2,1)S(1)}, bf16[33,16,128]{2,1,0:T(8,128)(2,1)S(1)}, u32[]{:S(2)}, u32[]{:S(2)}) collective-permute-start(bf16[33,16,128]{2,1,0:T(8,128)(2,1)S(1)} %collective-permute-done.11.refs_4_), channel_id=1, source_target_pairs={{0,7},{1,0},{2,1},{3,2},{4,3},{5,4},{6,5},{7,6},{8,15},{9,8},{10,9... | collective-permute-start | bytes 405512 | tf_op jit(solution)/shard_map/ppermute | solution.py:164
  76.9 5.5 %collective-permute-start.12 = (bf16[33,16,128]{2,1,0:T(8,128)(2,1)S(1)}, bf16[33,16,128]{2,1,0:T(8,128)(2,1)S(1)}, u32[]{:S(2)}, u32[]{:S(2)}) collective-permute-start(bf16[33,16,128]{2,1,0:T(8,128)(2,1)S(1)} %collective-permute-done.10.refs_3_), channel_id=1, source_target_pairs={{0,1},{1,2},{2,3},{3,4},{4,5},{5,6},{6,7},{7,0},{8,9},{9,10},{10,1... | collective-permute-start | bytes 405512 | tf_op jit(solution)/shard_map/ppermute | solution.py:163
  80.3 7.3 %collective-permute-start.15 = (bf16[17,16,128]{2,1,0:T(8,128)(2,1)S(1)}, bf16[17,16,128]{2,1,0:T(8,128)(2,1)S(1)}, u32[]{:S(2)}, u32[]{:S(2)}) collective-permute-start(bf16[17,16,128]{2,1,0:T(8,128)(2,1)S(1)} %slice.24), channel_id=1, source_target_pairs={{0,7},{1,0},{2,1},{3,2},{4,3},{5,4},{6,5},{7,6},{8,15},{9,8},{10,9... | collective-permute-start | bytes 208904 | tf_op jit(solution)/shard_map/ppermute | solution.py:167
  82.3 5.2 %collective-permute-start.14 = (bf16[16,16,128]{2,1,0:T(8,128)(2,1)S(1)}, bf16[16,16,128]{2,1,0:T(8,128)(2,1)S(1)}, u32[]{:S(2)}, u32[]{:S(2)}) collective-permute-start(bf16[16,16,128]{2,1,0:T(8,128)(2,1)S(1)} %slice.23), channel_id=1, source_target_pairs={{0,1},{1,2},{2,3},{3,4},{4,5},{5,6},{6,7},{7,0},{8,9},{9,10},{10,1... | collective-permute-start | bytes 196616 | tf_op jit(solution)/shard_map/ppermute | solution.py:166
  89.9 28.8 %all-to-all-start.1 = ((bf16[288,16,128]{2,1,0:T(8,128)(2,1)}), bf16[288,16,128]{2,1,0:T(8,128)(2,1)S(1)}, u32[]{:S(2)}, u32[]{:S(2)}) async-start(bf16[288,16,128]{2,1,0:T(8,128)(2,1)} %get-tuple-element.25), calls=%async_computation.1 | async-start | bytes 2359296 | tf_op jit(solution)/shard_map/all_to_all | solution.py:655

commit v6 on v5

--- a/solution.py
+++ b/solution.py
@@ -297,37 +297,24 @@
     return (jnp.arange(BS, dtype=jnp.int32)[:, None] == target[None, :]).astype(BF16)
 
 
-def fetch(live, coupling_ref, held, sems):
-    def start(chunk, carry):
-        span = pl.ds(chunk * CHUNK, CHUNK)
-        pltpu.make_async_copy(coupling_ref.at[span], held.at[span], sems.at[chunk]).start()
-        return carry
-
-    lax.fori_loop(0, lax.div(live + CHUNK - 1, CHUNK), start, 0)
-
-
-def work(count, live, list_ref, coupling_ref, held, sems, multiply, add):
-    def wait(chunk, carry):
-        span = pl.ds(chunk * CHUNK, CHUNK)
-        pltpu.make_async_copy(coupling_ref.at[span], held.at[span], sems.at[chunk]).wait()
-        return carry
-
-    def step(group, waited):
+def work(count, list_ref, weights_ref, load, add):
+    def step(group, carry):
         base = group * GROUP
-        last = list_ref[jnp.minimum(base + GROUP, count) - 1] & 255
-        needed = lax.div(last, CHUNK) + 1
-        lax.fori_loop(waited, needed, wait, 0)
         entries = [list_ref[base + j] for j in range(GROUP)]
-        products = [multiply((entry >> 8) & 255, held[entry & 255]) for entry in entries]
+        products = []
+        for one, two in zip(entries[0::2], entries[1::2]):
+            left = [load((entry >> 8) & 255) for entry in (one, two)]
+            right = [weights_ref[entry & 255] for entry in (one, two)]
+            product = dot_nn(jnp.concatenate(left, axis=0), jnp.concatenate(right, axis=1))
+            rows = left[0].shape[0]
+            products += [product[:rows, :BS], product[rows:, BS:]]
         for entry, product in zip(entries, products):
             add(entry >> 16, (entry >> 8) & 255, product)
-        return jnp.maximum(waited, needed)
-
-    waited = lax.fori_loop(0, lax.div(count + GROUP - 1, GROUP), step, jnp.int32(0))
-    lax.fori_loop(waited, lax.div(live + CHUNK - 1, CHUNK), wait, 0)
-
-
-HELD = (pltpu.VMEM((SLOTS, BS, BS), BF16), pltpu.SemaphoreType.DMA((SLOTS // CHUNK,)))
+        return carry
+
+    lax.fori_loop(0, lax.div(count + GROUP - 1, GROUP), step, 0)
+
+
 ROWS = shaped((RB + 1, K, BS), F32)
 
 
@@ -335,46 +322,62 @@
     return (block.astype(F32) * inverse).astype(BF16)
 
 
-def first_own_kernel(list_ref, count_ref, part_ref, coupling_ref, acc_ref, held, sems):
-    fetch(count_ref[2], coupling_ref, held, sems)
+def first_own_kernel(list_ref, count_ref, part_ref, coupling_ref, acc_ref, weights_ref, held, sems):
+    chunks = lax.div(count_ref[2] + CHUNK - 1, CHUNK)
+
+    def copy_of(chunk):
+        span = pl.ds(chunk * CHUNK, CHUNK)
+        return pltpu.make_async_copy(coupling_ref.at[span], held.at[span], sems.at[chunk])
+
+    def start(chunk, carry):
+        copy_of(chunk).start()
+        return carry
+
+    def turn(chunk, carry):
+        copy_of(chunk).wait()
+        for j in range(CHUNK):
+            weights_ref[chunk * CHUNK + j] = held[chunk * CHUNK + j].T
+        return carry
+
+    lax.fori_loop(0, chunks, start, 0)
+    lax.fori_loop(0, chunks, turn, 0)
     acc_ref[...] = jnp.zeros_like(acc_ref)
 
-    def multiply(block, weights):
-        return dot_nt(part_ref[block], weights)
+    def load(block):
+        return part_ref[block]
 
     def add(row, block, product):
         acc_ref[row] = acc_ref[row] + product
 
-    work(count_ref[0], count_ref[2], list_ref, coupling_ref, held, sems, multiply, add)
+    work(count_ref[0], list_ref, weights_ref, load, add)
 
 
 def first_own(own_list, counts, part_tiles, coupling):
     return call(
         first_own_kernel,
-        ROWS,
+        (ROWS, pltpu.VMEM((SLOTS, BS, BS), BF16)),
         [SMEM, SMEM, VMEM, HBM],
-        VMEM,
-        HELD,
+        (VMEM, VMEM),
+        (pltpu.VMEM((SLOTS, BS, BS), BF16), pltpu.SemaphoreType.DMA((SLOTS // CHUNK,))),
         flops=2 * SLOTS * K * BS * BS,
         moved=10000000,
     )(own_list, counts, in_hbm(part_tiles), in_hbm(coupling))
 
 
 def image_kernel(
-    list_ref, count_ref, halo_ref, coupling_ref, own_ref, basis_ref, degree_ref, image_hbm, tiles_ref, halo_hbm, image_ref,
-    out_sems, acc_ref, held, sems,
+    list_ref, count_ref, halo_ref, weights_ref, own_ref, basis_ref, degree_ref, image_hbm, tiles_ref, halo_hbm, image_ref,
+    out_sems, acc_ref,
 ):
     copies = start_copies([(halo_ref, halo_hbm)], out_sems)
-    fetch(count_ref[2], coupling_ref, held, sems)
     acc_ref[...] = own_ref[...]
 
-    def multiply(block, weights):
-        return dot_nt(halo_ref[block + (block >> 3)], weights)
+    def load(block):
+        return halo_ref[block + (block >> 3)]
 
     def add(row, block, product):
         acc_ref[row] = acc_ref[row] + product
 
-    work(count_ref[1], count_ref[2], list_ref, coupling_ref, held, sems, multiply, add)
+    work(count_ref[1], list_ref, weights_ref, load, add)
     top = jnp.zeros((K, BS), F32)
     bottom = jnp.zeros((K, BS), F32)
     for block in range(RB):
@@ -401,50 +404,48 @@
     wait_all(copies)
 
 
-def make_image(halo_list, counts, halo_tiles, coupling, own, basis, degree):
+def make_image(halo_list, counts, halo_tiles, weights, own, basis, degree):
     return call(
         image_kernel,
         (pltpu.HBM(basis.shape, F32), shaped((RB + 1, K, BS), BF16), pltpu.HBM(halo_tiles.shape, BF16)),
-        [SMEM, SMEM, VMEM, HBM, VMEM, VMEM, VMEM],
+        [SMEM, SMEM, VMEM, VMEM, VMEM, VMEM, VMEM],
         (HBM, VMEM, HBM),
-        (pltpu.VMEM(basis.shape, F32), pltpu.SemaphoreType.DMA((2,)), pltpu.VMEM((RB + 1, K, BS), F32)) + HELD,
+        (pltpu.VMEM(basis.shape, F32), pltpu.SemaphoreType.DMA((2,)), pltpu.VMEM((RB + 1, K, BS), F32)),
         flops=2 * SLOTS * K * BS * BS,
         moved=8000000,
-    )(halo_list, counts, halo_tiles, in_hbm(coupling), own, basis, degree)
+    )(halo_list, counts, halo_tiles, weights, own, basis, degree)
 
 
 def second_own_kernel(
-    list_ref, count_ref, part_ref, table_ref, basis_part_ref, inverse_ref, coupling_ref, acc_ref, scaled_ref, held,
-    sems, quotient_ref,
+    list_ref, count_ref, part_ref, table_ref, basis_part_ref, inverse_ref, weights_ref, acc_ref, scaled_ref, quotient_ref
 ):
-    fetch(count_ref[2], coupling_ref, held, sems)
     acc_ref[...] = jnp.zeros_like(acc_ref)
     scaled_ref[...] = jnp.zeros_like(scaled_ref)
     table = table_ref[...].astype(F32)
     for owner in range(quotient_ref.shape[0]):
         quotient_ref[owner] = jnp.broadcast_to(table[:, owner : owner + 1], (K, BS))
 
-    def multiply(block, weights):
+    def load(block):
         scaled = scale_block(basis_part_ref[block], inverse_ref[pl.ds(block, 1), :])
-        return dot_nt(jnp.concatenate([part_ref[block], scaled], axis=0), weights)
+        return jnp.concatenate([part_ref[block], scaled], axis=0)
 
     def add(row, block, product):
         acc_ref[row] = acc_ref[row] + (product[0:K] + quotient_ref[block >> 5] * product[K:])
         scaled_ref[row] = scaled_ref[row] + product[K:]
 
-    work(count_ref[0], count_ref[2], list_ref, coupling_ref, held, sems, multiply, add)
-
-
-def second_own(own_list, counts, part_tiles, table, basis_part, inverse, coupling, n_row):
+    work(count_ref[0], list_ref, weights_ref, load, add)
+
+
+def second_own(own_list, counts, part_tiles, table, basis_part, inverse, weights, n_row):
     return call(
         second_own_kernel,
         (pltpu.HBM(ROWS.shape, F32), pltpu.HBM(ROWS.shape, F32)),
-        [SMEM, SMEM, VMEM, VMEM, VMEM, VMEM, HBM],
+        [SMEM, SMEM, VMEM, VMEM, VMEM, VMEM, VMEM],
         (VMEM, VMEM),
-        HELD + (pltpu.VMEM((n_row, K, BS), F32),),
+        (pltpu.VMEM((n_row, K, BS), F32),),
         flops=4 * SLOTS * K * BS * BS,
         moved=10000000,
-    )(own_list, counts, *map(in_hbm, (part_tiles, table, basis_part, inverse, coupling)))
+    )(own_list, counts, *map(in_hbm, (part_tiles, table, basis_part, inverse)), weights)
 
 
 def spread_kernel(taken_ref, given_ref):
@@ -500,9 +501,9 @@
 
 
 def gram_kernel(
-    list_ref, count_ref, halo_ref, basis_halo_hbm, coupling_ref, own_hbm, own_scaled_hbm, basis_hbm, image_hbm, degree_hbm,
+    list_ref, count_ref, halo_ref, weights_ref, basis_halo_hbm, own_hbm, own_scaled_hbm, basis_hbm, image_hbm, degree_hbm,
     previous_hbm, previous_image_hbm, stacked, stacked_image, packed_ref, basis_halo_ref, acc_ref, scaled_ref, degree_ref,
-    in_sems, held, sems, side_ref, quotient_ref, inverse_ref, wide_ref,
+    in_sems, side_ref, quotient_ref, inverse_ref, wide_ref,
 ):
     early = [(basis_halo_hbm, basis_halo_ref), (own_hbm, acc_ref), (own_scaled_hbm, scaled_ref)]
     late = [
@@ -513,7 +514,6 @@
         (degree_hbm, degree_ref),
     ]
     early = start_copies(early, in_sems)
-    fetch(count_ref[2], coupling_ref, held, sems)
     late = start_copies(late, in_sems, 3)
     peers = halo_ref.shape[0] // EXTRA
     total = jnp.zeros((K, BS), F32)
@@ -534,17 +534,17 @@
         inverse = basis_halo_ref[peer * EXTRA + SEND].astype(F32)
         inverse_ref[peer * SEND : (peer + 1) * SEND, :] = inverse[0:SEND] + inverse[SEND:]
 
-    def multiply(block, weights):
+    def load(block):
         tile = block + (block >> 3)
         scaled = scale_block(basis_halo_ref[tile], inverse_ref[pl.ds(block, 1), :])
-        return dot_nt(jnp.concatenate([halo_ref[tile], scaled], axis=0), weights)
+        return jnp.concatenate([halo_ref[tile], scaled], axis=0)
 
     def add(row, block, product):
         quotient = quotient_ref[block & 7, block >> 3]
         acc_ref[row] = acc_ref[row] + (product[0:K] + quotient * product[K:])
         scaled_ref[row] = scaled_ref[row] + product[K:]
 
-    work(count_ref[1], count_ref[2], list_ref, coupling_ref, held, sems, multiply, add)
+    work(count_ref[1], list_ref, weights_ref, load, add)
     wait_all(late)
     for block in range(RB):
         at = columns(block)
@@ -560,13 +560,13 @@
 
 
 def make_grams(
-    halo_list, counts, halo_tiles, basis_halo, coupling, own, scaled, basis, image, degree, previous, previous_image, n_dom
+    halo_list, counts, halo_tiles, weights, basis_halo, own, scaled, basis, image, degree, previous, previous_image, n_dom
 ):
     stack = shaped((3 * K, basis.shape[1]), F32)
     return call(
         gram_kernel,
         (stack, stack, shaped((n_dom, 24, BS), F32)),
-        [SMEM, SMEM, VMEM] + [HBM] * 9,
+        [SMEM, SMEM, VMEM, VMEM] + [HBM] * 8,
         (VMEM, VMEM, VMEM),
         (
             pltpu.VMEM(basis_halo.shape, BF16),
@@ -574,9 +574,6 @@
             pltpu.VMEM((RB + 1, K, BS), F32),
             pltpu.VMEM(degree.shape, F32),
             pltpu.SemaphoreType.DMA((8,)),
-        )
-        + HELD
-        + (
             pltpu.VMEM((n_dom * K, BS), BF16),
             pltpu.VMEM((SEND, n_dom, K, BS), F32),
             pltpu.VMEM((n_dom * SEND, BS), F32),
@@ -585,8 +582,8 @@
         flops=2 * SLOTS * K * BS * BS,
         moved=10000000,
     )(
-        halo_list, counts, halo_tiles,
-        *map(in_hbm, (basis_halo, coupling, own, scaled, basis, image, degree, previous, previous_image)),
+        halo_list, counts, halo_tiles, weights,
+        *map(in_hbm, (basis_halo, own, scaled, basis, image, degree, previous, previous_image)),
     )
 
 
@@ -668,15 +665,15 @@
     gathered = gather_row(cast_tiles(in_hbm(basis), in_hbm(degree)), n_row, HALF + 2)
     basis_part, inverse, chosen = first_select(gathered, place, send_list, n_row)
     halo_tiles = to_all(chosen, "dom")
-    own = first_own(own_list, counts, basis_part, coupling)
-    image, tiles, basis_halo = make_image(halo_list, counts, halo_tiles, coupling, own, basis, degree)
+    own, weights = first_own(own_list, counts, basis_part, coupling)
+    image, tiles, basis_halo = make_image(halo_list, counts, halo_tiles, weights, own, basis, degree)
 
     gathered = gather_row(tiles, n_row, HALF)
     part_tiles, chosen, table = second_select(gathered, place, send_list, picks(send_list), n_row)
     halo_tiles = to_all(chosen, "dom")
-    own, scaled = second_own(own_list, counts, part_tiles, table, basis_part, inverse, coupling, n_row)
+    own, scaled = second_own(own_list, counts, part_tiles, table, basis_part, inverse, weights, n_row)
     stacked, stacked_image, packed = make_grams(
-        halo_list, counts, halo_tiles, basis_halo, coupling, own, scaled, basis, image, degree, previous, previous_image,
+        halo_list, counts, halo_tiles, weights, basis_halo, own, scaled, basis, image, degree, previous, previous_image,
         n_dom,
     )
     packed = to_all(add_and_repeat(to_all(packed, "dom"), n_row), "row")

time: 158 us -> 156 us (0.987); the launches traced: 156 us -> 156 us
  local copies, waits for them, and re-layouts: 1.06 us -> 14.5 us
  waiting for transfers between devices: 48 us -> 40.3 us
  blocking collectives: 27.2 us -> 24.4 us
  starting transfers between devices: 45.4 us -> 43.1 us
    unnamed x11 -> x19, local copies, waits for them, and re-layouts: 0.79 us -> 14.2 us
    all_to_all x2, waiting for transfers between devices: 23.7 us -> 16 us  [to_all(): return lax.all_to_all(value, axis, split_axis=0, concat_axis=0, tiled=True)]
    all_to_all x2, starting transfers between devices: 22.7 us -> 19.5 us  [to_all(): return lax.all_to_all(value, axis, split_axis=0, concat_axis=0, tiled=True)]
    all_to_all x2, blocking collectives: 27.2 us -> 24.4 us  [to_all(): return lax.all_to_all(value, axis, split_axis=0, concat_axis=0, tiled=True)]
  transfers between devices with their start and end apart: 18 -> 18, of which waited for: 14 -> 14; matrix products, arithmetic and copies ran while one was open for 1% -> 1% of each run, Pallas kernels for 8% -> 9%
where the time goes in v6:
time: 156 us
  starting transfers between devices  43.1 us (28%)
  waiting for transfers between devices  40.3 us (26%)
  Pallas kernels  31.9 us (20%)
  blocking collectives  24.4 us (16%)
  local copies, waits for them, and re-layouts  14.5 us (9%)
    pallas_call x10, Pallas kernels, run(): pl.pallas_call(kernel, out_shape=out_shape, in_specs=in_specs, out_specs=...  31.9 us
    all_to_all x2, blocking collectives, to_all(): return lax.all_to_all(value, axis, split_axis=0, concat_axis=0, tiled=True)  24.4 us
    all_to_all x2, starting transfers between devices, to_all(): return lax.all_to_all(value, axis, split_axis=0, concat_axis=0, tiled=True)  19.5 us
    all_to_all x2, waiting for transfers between devices, to_all(): return lax.all_to_all(value, axis, split_axis=0, concat_axis=0, tiled=True)  16 us
    ppermute x6, waiting for transfers between devices, gather_row(): from_above = lax.ppermute(from_above, 'row', down)  15.6 us
    ppermute x6, starting transfers between devices, gather_row(): from_above = lax.ppermute(from_above, 'row', down)  15.5 us
    unnamed x19, local copies, waits for them, and re-layouts  14.2 us
    ppermute x2, waiting for transfers between devices, gather_row(): far_low = lax.ppermute(from_below[:half], 'row', up)  7.19 us
  transfers between devices with their start and end apart: 18, of which 14 were waited for; matrix products, arithmetic and copies ran while one was open for 1% of the time, Pallas kernels for 9%

profile of v6, /device:TPU:1, one launch (start us, length us, event | category | flops | bytes accessed | tf_op | source)
XLA Modules:
  0.0 156.0 jit_solution(9794881052247077077)
XLA Ops:
  1.6 6.5 %collective-permute-start.1 = (bf16[36,16,128]{2,1,0:T(8,128)(2,1)S(1)}, bf16[36,16,128]{2,1,0:T(8,128)(2,1)S(1)}, u32[]{:S(2)}, u32[]{:S(2)}) collective-permute-start(bf16[36,16,128]{2,1,0:T(8,128)(2,1)S(1)} %shard_map.105.refs_0_), channel_id=1, source_target_pairs={{0,7},{1,0},{2,1},{3,2},{4,3},{5,4},{6,5},{7,6},{8,15},{9,8},{10,9... | collective-permute-start | bytes 442376 | tf_op jit(solution)/shard_map/ppermute | solution.py:164
  8.1 2.5 %collective-permute-done.1.refs_2_ = bf16[36,16,128]{2,1,0:T(8,128)(2,1)S(1)} collective-permute-done((bf16[36,16,128]{2,1,0:T(8,128)(2,1)S(1)}, bf16[36,16,128]{2,1,0:T(8,128)(2,1)S(1)}, u32[]{:S(2)}, u32[]{:S(2)}) %collective-permute-start.1) | collective-permute-done | bytes 147488 | tf_op jit(solution)/shard_map/ppermute | solution.py:164
  10.6 3.4 %collective-permute-start.3 = (bf16[36,16,128]{2,1,0:T(8,128)(2,1)S(1)}, bf16[36,16,128]{2,1,0:T(8,128)(2,1)S(1)}, u32[]{:S(2)}, u32[]{:S(2)}) collective-permute-start(bf16[36,16,128]{2,1,0:T(8,128)(2,1)S(1)} %collective-permute-done.1.refs_2_), channel_id=1, source_target_pairs={{0,7},{1,0},{2,1},{3,2},{4,3},{5,4},{6,5},{7,6},{8,15},{9,8},{10,9... | collective-permute-start | bytes 442376 | tf_op jit(solution)/shard_map/ppermute | solution.py:164
  14.0 2.1 %collective-permute-done.3.refs_4_ = bf16[36,16,128]{2,1,0:T(8,128)(2,1)S(1)} collective-permute-done((bf16[36,16,128]{2,1,0:T(8,128)(2,1)S(1)}, bf16[36,16,128]{2,1,0:T(8,128)(2,1)S(1)}, u32[]{:S(2)}, u32[]{:S(2)}) %collective-permute-start.3) | collective-permute-done | bytes 147488 | tf_op jit(solution)/shard_map/ppermute | solution.py:164
  16.1 3.1 %collective-permute-start.5 = (bf16[36,16,128]{2,1,0:T(8,128)(2,1)S(1)}, bf16[36,16,128]{2,1,0:T(8,128)(2,1)S(1)}, u32[]{:S(2)}, u32[]{:S(2)}) collective-permute-start(bf16[36,16,128]{2,1,0:T(8,128)(2,1)S(1)} %collective-permute-done.3.refs_4_), channel_id=1, source_target_pairs={{0,7},{1,0},{2,1},{3,2},{4,3},{5,4},{6,5},{7,6},{8,15},{9,8},{10,9... | collective-permute-start | bytes 442376 | tf_op jit(solution)/shard_map/ppermute | solution.py:164
  19.3 2.1 %collective-permute-done.5.refs_6_ = bf16[36,16,128]{2,1,0:T(8,128)(2,1)S(1)} collective-permute-done((bf16[36,16,128]{2,1,0:T(8,128)(2,1)S(1)}, bf16[36,16,128]{2,1,0:T(8,128)(2,1)S(1)}, u32[]{:S(2)}, u32[]{:S(2)}) %collective-permute-start.5) | collective-permute-done | bytes 147488 | tf_op jit(solution)/shard_map/ppermute | solution.py:164
  21.4 3.1 %collective-permute-start.7 = (bf16[18,16,128]{2,1,0:T(8,128)(2,1)S(1)}, bf16[18,16,128]{2,1,0:T(8,128)(2,1)S(1)}, u32[]{:S(2)}, u32[]{:S(2)}) collective-permute-start(bf16[18,16,128]{2,1,0:T(8,128)(2,1)S(1)} %slice.22), channel_id=1, source_target_pairs={{0,7},{1,0},{2,1},{3,2},{4,3},{5,4},{6,5},{7,6},{8,15},{9,8},{10,9... | collective-permute-start | bytes 221192 | tf_op jit(solution)/shard_map/ppermute | solution.py:167
  25.9 3.1 %collective-permute-done.6.refs_7_ = bf16[18,16,128]{2,1,0:T(8,128)(2,1)S(1)} collective-permute-done((bf16[18,16,128]{2,1,0:T(8,128)(2,1)S(1)}, bf16[18,16,128]{2,1,0:T(8,128)(2,1)S(1)}, u32[]{:S(2)}, u32[]{:S(2)}) %collective-permute-start.6) | collective-permute-done | bytes 73760 | tf_op jit(solution)/shard_map/ppermute | solution.py:166
  29.0 2.1 %shard_map.106 = (bf16[256,16,128]{2,1,0:T(8,128)(2,1)}, f32[256,128]{1,0:T(8,128)}, bf16[288,16,128]{2,1,0:T(8,128)(2,1)}) custom-call(s32[1]{0:T(128)} %bitcast.place_ref, s32[256]{0:T(256)S(1)} %reshape.19.send_ref, bf16[36,16,128]{2,1,0:T(8,128)(2,1)S(1)} %shard_map.105.refs_0_, bf16[36,16,128]{2,1,0:T(8,128)(2,1)S(1)} %collective-permute-done.refs_1_, ...), custom_call_target="tpu_custom_call" | custom-call | bytes 3000000 | tf_op jit(solution)/shard_map/pallas_call | solution.py:37
  31.1 12.4 %all-to-all-start = ((bf16[288,16,128]{2,1,0:T(8,128)(2,1)}), bf16[288,16,128]{2,1,0:T(8,128)(2,1)S(1)}, u32[]{:S(2)}, u32[]{:S(2)}) async-start(bf16[288,16,128]{2,1,0:T(8,128)(2,1)} %get-tuple-element.23), calls=%async_computation | async-start | bytes 2359296 | tf_op jit(solution)/shard_map/all_to_all | solution.py:652
  44.1 3.1 %shard_map.104 = (s32[288]{0:T(512)S(1)}, s32[288]{0:T(512)S(1)}, s32[3]{0:T(128)S(1)}) custom-call(s32[256]{0:T(256)S(1)} %copy-done.6, s32[256]{0:T(256)S(1)} %copy-done.7, s32[1]{0:T(128)S(6)} %copy.14.live_ref), custom_call_target="tpu_custom_call" | custom-call | bytes 20000 | tf_op jit(solution)/shard_map/pallas_call | solution.py:37
  47.3 6.5 %shard_map.107 = (f32[33,16,128]{2,1,0:T(8,128)S(1)}, bf16[256,128,128]{2,1,0:T(8,128)(2,1)S(1)}) custom-call(s32[288]{0:T(512)S(1)} %get-tuple-element.24.list_ref, s32[3]{0:T(128)S(1)} %get-tuple-element.22.count_ref, bf16[256,16,128]{2,1,0:T(8,128)(2,1)} %get-tuple-element.25.part_ref.basis_part_ref, bf16[256,128,128]{2,1,0:T(8,128)(2,1)} %coupling_ref.1), custom_call_target="tpu_custom_call" | custom-call | flops 134217728 | bytes 10000000 | tf_op jit(solution)/shard_map/pallas_call | solution.py:37
  53.8 3.3 %copy-done = bf16[256,128,128]{2,1,0:T(8,128)(2,1)} copy-done((bf16[256,128,128]{2,1,0:T(8,128)(2,1)}, bf16[256,128,128]{2,1,0:T(8,128)(2,1)S(1)}, u32[]{:S(2)}) %copy-start) | copy-done | bytes 8388632
  57.0 4.8 %all-to-all-done.halo_ref = bf16[288,16,128]{2,1,0:T(8,128)(2,1)S(1)} async-done(((bf16[288,16,128]{2,1,0:T(8,128)(2,1)}), bf16[288,16,128]{2,1,0:T(8,128)(2,1)S(1)}, u32[]{:S(2)}, u32[]{:S(2)}) %all-to-all-start) | async-done | bytes 1179680 | tf_op jit(solution)/shard_map/all_to_all | solution.py:652
  61.8 3.4 %copy-done.1 = bf16[256,128,128]{2,1,0:T(8,128)(2,1)S(1)} copy-done((bf16[256,128,128]{2,1,0:T(8,128)(2,1)S(1)}, bf16[256,128,128]{2,1,0:T(8,128)(2,1)}, u32[]{:S(2)}) %copy-start.1) | copy-done | bytes 8388632
  65.2 3.0 %shard_map.108 = (f32[16,4096]{1,0:T(8,128)}, bf16[33,16,128]{2,1,0:T(8,128)(2,1)S(1)}, bf16[288,16,128]{2,1,0:T(8,128)(2,1)}) custom-call(s32[288]{0:T(512)S(1)} %get-tuple-element.21.list_ref, s32[3]{0:T(128)S(1)} %get-tuple-element.22.count_ref, bf16[288,16,128]{2,1,0:T(8,128)(2,1)S(1)} %all-to-all-done.halo_ref, bf16[256,128,128]{2,1,0:T(8,128)(2,1)S(1)} %copy-done.1, ...), custom_call_target="tpu_custom_call" | custom-call | flops 134217728 | bytes 8000000 | tf_op jit(solution)/shard_map/pallas_call | solution.py:37
  69.8 3.8 %collective-permute-done.9.refs_2_ = bf16[33,16,128]{2,1,0:T(8,128)(2,1)S(1)} collective-permute-done((bf16[33,16,128]{2,1,0:T(8,128)(2,1)S(1)}, bf16[33,16,128]{2,1,0:T(8,128)(2,1)S(1)}, u32[]{:S(2)}, u32[]{:S(2)}) %collective-permute-start.9) | collective-permute-done | bytes 135200 | tf_op jit(solution)/shard_map/ppermute | solution.py:164
  75.2 3.4 %collective-permute-done.11.refs_4_ = bf16[33,16,128]{2,1,0:T(8,128)(2,1)S(1)} collective-permute-done((bf16[33,16,128]{2,1,0:T(8,128)(2,1)S(1)}, bf16[33,16,128]{2,1,0:T(8,128)(2,1)S(1)}, u32[]{:S(2)}, u32[]{:S(2)}) %collective-permute-start.11) | collective-permute-done | bytes 135200 | tf_op jit(solution)/shard_map/ppermute | solution.py:164
  78.7 1.7 %collective-permute-start.13 = (bf16[33,16,128]{2,1,0:T(8,128)(2,1)S(1)}, bf16[33,16,128]{2,1,0:T(8,128)(2,1)S(1)}, u32[]{:S(2)}, u32[]{:S(2)}) collective-permute-start(bf16[33,16,128]{2,1,0:T(8,128)(2,1)S(1)} %collective-permute-done.11.refs_4_), channel_id=1, source_target_pairs={{0,7},{1,0},{2,1},{3,2},{4,3},{5,4},{6,5},{7,6},{8,15},{9,8},{10,9... | collective-permute-start | bytes 405512 | tf_op jit(solution)/shard_map/ppermute | solution.py:164
  80.9 1.6 %collective-permute-done.13.refs_6_ = bf16[33,16,128]{2,1,0:T(8,128)(2,1)S(1)} collective-permute-done((bf16[33,16,128]{2,1,0:T(8,128)(2,1)S(1)}, bf16[33,16,128]{2,1,0:T(8,128)(2,1)S(1)}, u32[]{:S(2)}, u32[]{:S(2)}) %collective-permute-start.13) | collective-permute-done | bytes 135200 | tf_op jit(solution)/shard_map/ppermute | solution.py:164
  82.5 3.0 %collective-permute-start.15 = (bf16[17,16,128]{2,1,0:T(8,128)(2,1)S(1)}, bf16[17,16,128]{2,1,0:T(8,128)(2,1)S(1)}, u32[]{:S(2)}, u32[]{:S(2)}) collective-permute-start(bf16[17,16,128]{2,1,0:T(8,128)(2,1)S(1)} %slice.24), channel_id=1, source_target_pairs={{0,7},{1,0},{2,1},{3,2},{4,3},{5,4},{6,5},{7,6},{8,15},{9,8},{10,9... | collective-permute-start | bytes 208904 | tf_op jit(solution)/shard_map/ppermute | solution.py:167
  86.0 4.1 %collective-permute-done.14.refs_7_ = bf16[16,16,128]{2,1,0:T(8,128)(2,1)S(1)} collective-permute-done((bf16[16,16,128]{2,1,0:T(8,128)(2,1)S(1)}, bf16[16,16,128]{2,1,0:T(8,128)(2,1)S(1)}, u32[]{:S(2)}, u32[]{:S(2)}) %collective-permute-start.14) | collective-permute-done | bytes 65568 | tf_op jit(solution)/shard_map/ppermute | solution.py:166
  90.1 2.3 %shard_map.109 = (bf16[256,16,128]{2,1,0:T(8,128)(2,1)}, bf16[288,16,128]{2,1,0:T(8,128)(2,1)}, bf16[16,128]{1,0:T(8,128)(2,1)}) custom-call(s32[1]{0:T(128)} %bitcast.place_ref, s32[256]{0:T(256)S(1)} %reshape.19.send_ref, bf16[128,4096]{1,0:T(8,128)(2,1)S(1)} %fusion.pick_ref, bf16[33,16,128]{2,1,0:T(8,128)(2,1)S(1)} %get-tuple-element.28.refs_0_, ...), custom_call_target="tpu_custom_call" | custom-call | bytes 3000000 | tf_op jit(solution)/shard_map/pallas_call | solution.py:37
  92.4 7.1 %all-to-all-start.1 = ((bf16[288,16,128]{2,1,0:T(8,128)(2,1)}), bf16[288,16,128]{2,1,0:T(8,128)(2,1)S(1)}, u32[]{:S(2)}, u32[]{:S(2)}) async-start(bf16[288,16,128]{2,1,0:T(8,128)(2,1)} %get-tuple-element.29), calls=%async_computation.1 | async-start | bytes 2359296 | tf_op jit(solution)/shard_map/all_to_all | solution.py:652
  99.6 3.4 %copy-done.2 = bf16[256,128,128]{2,1,0:T(8,128)(2,1)S(1)} copy-done((bf16[256,128,128]{2,1,0:T(8,128)(2,1)S(1)}, bf16[256,128,128]{2,1,0:T(8,128)(2,1)}, u32[]{:S(2)}) %copy-start.2) | copy-done | bytes 8388632
  102.9 3.8 %shard_map.110 = (f32[33,16,128]{2,1,0:T(8,128)}, f32[33,16,128]{2,1,0:T(8,128)}) custom-call(s32[288]{0:T(512)S(1)} %get-tuple-element.24.list_ref, s32[3]{0:T(128)S(1)} %get-tuple-element.22.count_ref, bf16[256,16,128]{2,1,0:T(8,128)(2,1)} %get-tuple-element.31.part_ref, bf16[16,128]{1,0:T(8,128)(2,1)} %get-tuple-element.32.table_ref, ...), custom_call_target="tpu_custom_call" | custom-call | flops 268435456 | bytes 10000000 | tf_op jit(solution)/shard_map/pallas_call | solution.py:37
  106.8 11.2 %all-to-all-done.1.halo_ref = bf16[288,16,128]{2,1,0:T(8,128)(2,1)S(1)} async-done(((bf16[288,16,128]{2,1,0:T(8,128)(2,1)}), bf16[288,16,128]{2,1,0:T(8,128)(2,1)S(1)}, u32[]{:S(2)}, u32[]{:S(2)}) %all-to-all-start.1) | async-done | bytes 1179680 | tf_op jit(solution)/shard_map/all_to_all | solution.py:652
  118.0 3.4 %copy-done.3 = bf16[256,128,128]{2,1,0:T(8,128)(2,1)S(1)} copy-done((bf16[256,128,128]{2,1,0:T(8,128)(2,1)S(1)}, bf16[256,128,128]{2,1,0:T(8,128)(2,1)}, u32[]{:S(2)}) %copy-start.3) | copy-done | bytes 8388632
  121.4 5.5 %shard_map.111 = (f32[48,4096]{1,0:T(8,128)S(1)}, f32[48,4096]{1,0:T(8,128)S(1)}, f32[32,24,128]{2,1,0:T(8,128)S(1)}) custom-call(s32[288]{0:T(512)S(1)} %get-tuple-element.21.list_ref, s32[3]{0:T(128)S(1)} %get-tuple-element.22.count_ref, bf16[288,16,128]{2,1,0:T(8,128)(2,1)S(1)} %all-to-all-done.1.halo_ref, bf16[256,128,128]{2,1,0:T(8,128)(2,1)S(1)} %copy-done.3, ...), custom_call_target="tpu_custom_call" | custom-call | flops 134217728 | bytes 10000000 | tf_op jit(solution)/shard_map/pallas_call | solution.py:37
  126.9 14.0 %all_to_all.20.taken_ref = f32[32,24,128]{2,1,0:T(8,128)S(1)} all-to-all(f32[32,24,128]{2,1,0:T(8,128)S(1)} %get-tuple-element.37), channel_id=1, replica_groups=mesh['dom'=32,'row'=8] {'dom'}, dimensions={0} | all-to-all | bytes 786432 | tf_op jit(solution)/shard_map/all_to_all | solution.py:652
  140.9 10.4 %all_to_all.21.taken_ref = f32[8,24,128]{2,1,0:T(8,128)S(1)} all-to-all(f32[8,24,128]{2,1,0:T(8,128)S(1)} %shard_map.112), channel_id=1, replica_groups=mesh['dom'=32,'row'=8] {'row'}, dimensions={0} | all-to-all | bytes 196608 | tf_op jit(solution)/shard_map/all_to_all | solution.py:652
  151.3 4.7 %shard_map.113 = (f32[16,4096]{1,0:T(8,128)}, f32[16,4096]{1,0:T(8,128)}) custom-call(f32[8,24,128]{2,1,0:T(8,128)S(1)} %all_to_all.21.taken_ref, f32[48,4096]{1,0:T(8,128)S(1)} %get-tuple-element.38.stacked_ref, f32[48,4096]{1,0:T(8,128)S(1)} %get-tuple-element.39.stacked_image_ref), custom_call_target="tpu_custom_call" | custom-call | flops 1000000 | bytes 3000000 | tf_op jit(solution)/shard_map/pallas_call | solution.py:37
  (47 shorter events, 6.7 us)
Async XLA Ops:
  1.6 9.0 %collective-permute-start.1 = (bf16[36,16,128]{2,1,0:T(8,128)(2,1)S(1)}, bf16[36,16,128]{2,1,0:T(8,128)(2,1)S(1)}, u32[]{:S(2)}, u32[]{:S(2)}) collective-permute-start(bf16[36,16,128]{2,1,0:T(8,128)(2,1)S(1)} %shard_map.105.refs_0_), channel_id=1, source_target_pairs={{0,7},{1,0},{2,1},{3,2},{4,3},{5,4},{6,5},{7,6},{8,15},{9,8},{10,9... | collective-permute-start | bytes 442376 | tf_op jit(solution)/shard_map/ppermute | solution.py:164
  8.1 5.9 %collective-permute-start = (bf16[36,16,128]{2,1,0:T(8,128)(2,1)S(1)}, bf16[36,16,128]{2,1,0:T(8,128)(2,1)S(1)}, u32[]{:S(2)}, u32[]{:S(2)}) collective-permute-start(bf16[36,16,128]{2,1,0:T(8,128)(2,1)S(1)} %shard_map.105.refs_0_), channel_id=1, source_target_pairs={{0,1},{1,2},{2,3},{3,4},{4,5},{5,6},{6,7},{7,0},{8,9},{9,10},{10,1... | collective-permute-start | bytes 442376 | tf_op jit(solution)/shard_map/ppermute | solution.py:163
  10.6 5.5 %collective-permute-start.3 = (bf16[36,16,128]{2,1,0:T(8,128)(2,1)S(1)}, bf16[36,16,128]{2,1,0:T(8,128)(2,1)S(1)}, u32[]{:S(2)}, u32[]{:S(2)}) collective-permute-start(bf16[36,16,128]{2,1,0:T(8,128)(2,1)S(1)} %collective-permute-done.1.refs_2_), channel_id=1, source_target_pairs={{0,7},{1,0},{2,1},{3,2},{4,3},{5,4},{6,5},{7,6},{8,15},{9,8},{10,9... | collective-permute-start | bytes 442376 | tf_op jit(solution)/shard_map/ppermute | solution.py:164
  14.0 5.2 %collective-permute-start.2 = (bf16[36,16,128]{2,1,0:T(8,128)(2,1)S(1)}, bf16[36,16,128]{2,1,0:T(8,128)(2,1)S(1)}, u32[]{:S(2)}, u32[]{:S(2)}) collective-permute-start(bf16[36,16,128]{2,1,0:T(8,128)(2,1)S(1)} %collective-permute-done.refs_1_), channel_id=1, source_target_pairs={{0,1},{1,2},{2,3},{3,4},{4,5},{5,6},{6,7},{7,0},{8,9},{9,10},{10,1... | collective-permute-start | bytes 442376 | tf_op jit(solution)/shard_map/ppermute | solution.py:163
  16.1 5.2 %collective-permute-start.5 = (bf16[36,16,128]{2,1,0:T(8,128)(2,1)S(1)}, bf16[36,16,128]{2,1,0:T(8,128)(2,1)S(1)}, u32[]{:S(2)}, u32[]{:S(2)}) collective-permute-start(bf16[36,16,128]{2,1,0:T(8,128)(2,1)S(1)} %collective-permute-done.3.refs_4_), channel_id=1, source_target_pairs={{0,7},{1,0},{2,1},{3,2},{4,3},{5,4},{6,5},{7,6},{8,15},{9,8},{10,9... | collective-permute-start | bytes 442376 | tf_op jit(solution)/shard_map/ppermute | solution.py:164
  19.3 5.2 %collective-permute-start.4 = (bf16[36,16,128]{2,1,0:T(8,128)(2,1)S(1)}, bf16[36,16,128]{2,1,0:T(8,128)(2,1)S(1)}, u32[]{:S(2)}, u32[]{:S(2)}) collective-permute-start(bf16[36,16,128]{2,1,0:T(8,128)(2,1)S(1)} %collective-permute-done.2.refs_3_), channel_id=1, source_target_pairs={{0,1},{1,2},{2,3},{3,4},{4,5},{5,6},{6,7},{7,0},{8,9},{9,10},{10,1... | collective-permute-start | bytes 442376 | tf_op jit(solution)/shard_map/ppermute | solution.py:163
  21.4 4.5 %collective-permute-start.7 = (bf16[18,16,128]{2,1,0:T(8,128)(2,1)S(1)}, bf16[18,16,128]{2,1,0:T(8,128)(2,1)S(1)}, u32[]{:S(2)}, u32[]{:S(2)}) collective-permute-start(bf16[18,16,128]{2,1,0:T(8,128)(2,1)S(1)} %slice.22), channel_id=1, source_target_pairs={{0,7},{1,0},{2,1},{3,2},{4,3},{5,4},{6,5},{7,6},{8,15},{9,8},{10,9... | collective-permute-start | bytes 221192 | tf_op jit(solution)/shard_map/ppermute | solution.py:167
  24.5 4.5 %collective-permute-start.6 = (bf16[18,16,128]{2,1,0:T(8,128)(2,1)S(1)}, bf16[18,16,128]{2,1,0:T(8,128)(2,1)S(1)}, u32[]{:S(2)}, u32[]{:S(2)}) collective-permute-start(bf16[18,16,128]{2,1,0:T(8,128)(2,1)S(1)} %slice.21), channel_id=1, source_target_pairs={{0,1},{1,2},{2,3},{3,4},{4,5},{5,6},{6,7},{7,0},{8,9},{9,10},{10,1... | collective-permute-start | bytes 221192 | tf_op jit(solution)/shard_map/ppermute | solution.py:166
  31.1 13.1 %copy-start.6 = (s32[256]{0:T(256)S(1)}, s32[256]{0:T(256)}, u32[]{:S(2)}) copy-start(s32[256]{0:T(256)} %row_ref.1) | copy-start | bytes 3076
  31.1 13.0 %copy-start.7 = (s32[256]{0:T(256)S(1)}, s32[256]{0:T(256)}, u32[]{:S(2)}) copy-start(s32[256]{0:T(256)} %column_ref.1) | copy-start | bytes 3076
  31.1 30.7 %all-to-all-start = ((bf16[288,16,128]{2,1,0:T(8,128)(2,1)}), bf16[288,16,128]{2,1,0:T(8,128)(2,1)S(1)}, u32[]{:S(2)}, u32[]{:S(2)}) async-start(bf16[288,16,128]{2,1,0:T(8,128)(2,1)} %get-tuple-element.23), calls=%async_computation | async-start | bytes 2359296 | tf_op jit(solution)/shard_map/all_to_all | solution.py:652
  47.3 14.5 %copy-start.4 = (f32[16,4096]{1,0:T(8,128)S(1)}, f32[16,4096]{1,0:T(8,128)}, u32[]{:S(2)}) copy-start(f32[16,4096]{1,0:T(8,128)} %basis_hbm.1) | copy-start | bytes 786436
  47.3 14.5 %copy-start.5 = (f32[4096]{0:T(1024)S(1)}, f32[4096]{0:T(1024)}, u32[]{:S(2)}) copy-start(f32[4096]{0:T(1024)} %param.12) | copy-start | bytes 49156
  53.8 3.3 %copy-start = (bf16[256,128,128]{2,1,0:T(8,128)(2,1)}, bf16[256,128,128]{2,1,0:T(8,128)(2,1)S(1)}, u32[]{:S(2)}) copy-start(bf16[256,128,128]{2,1,0:T(8,128)(2,1)S(1)} %get-tuple-element.26.weights_ref) | copy-start | bytes 25165828
  61.8 3.4 %copy-start.1 = (bf16[256,128,128]{2,1,0:T(8,128)(2,1)S(1)}, bf16[256,128,128]{2,1,0:T(8,128)(2,1)}, u32[]{:S(2)}) copy-start(bf16[256,128,128]{2,1,0:T(8,128)(2,1)} %copy-done) | copy-start | bytes 25165828
  65.2 15.5 %copy-start.8 = (s32[1,32,8]{1,2,0:T(8,128)S(1)}, s32[1,32,8]{1,2,0:T(8,128)}, u32[]{:S(2)}) copy-start(s32[1,32,8]{1,2,0:T(8,128)} %param.16) | copy-start | bytes 3076
  68.2 5.5 %collective-permute-start.9 = (bf16[33,16,128]{2,1,0:T(8,128)(2,1)S(1)}, bf16[33,16,128]{2,1,0:T(8,128)(2,1)S(1)}, u32[]{:S(2)}, u32[]{:S(2)}) collective-permute-start(bf16[33,16,128]{2,1,0:T(8,128)(2,1)S(1)} %get-tuple-element.28.refs_0_), channel_id=1, source_target_pairs={{0,7},{1,0},{2,1},{3,2},{4,3},{5,4},{6,5},{7,6},{8,15},{9,8},{10,9... | collective-permute-start | bytes 405512 | tf_op jit(solution)/shard_map/ppermute | solution.py:164
  68.3 6.5 %collective-permute-start.8 = (bf16[33,16,128]{2,1,0:T(8,128)(2,1)S(1)}, bf16[33,16,128]{2,1,0:T(8,128)(2,1)S(1)}, u32[]{:S(2)}, u32[]{:S(2)}) collective-permute-start(bf16[33,16,128]{2,1,0:T(8,128)(2,1)S(1)} %get-tuple-element.28.refs_0_), channel_id=1, source_target_pairs={{0,1},{1,2},{2,3},{3,4},{4,5},{5,6},{6,7},{7,0},{8,9},{9,10},{10,1... | collective-permute-start | bytes 405512 | tf_op jit(solution)/shard_map/ppermute | solution.py:163
  73.6 5.0 %collective-permute-start.11 = (bf16[33,16,128]{2,1,0:T(8,128)(2,1)S(1)}, bf16[33,16,128]{2,1,0:T(8,128)(2,1)S(1)}, u32[]{:S(2)}, u32[]{:S(2)}) collective-permute-start(bf16[33,16,128]{2,1,0:T(8,128)(2,1)S(1)} %collective-permute-done.9.refs_2_), channel_id=1, source_target_pairs={{0,7},{1,0},{2,1},{3,2},{4,3},{5,4},{6,5},{7,6},{8,15},{9,8},{10,9... | collective-permute-start | bytes 405512 | tf_op jit(solution)/shard_map/ppermute | solution.py:164
  74.7 6.0 %collective-permute-start.10 = (bf16[33,16,128]{2,1,0:T(8,128)(2,1)S(1)}, bf16[33,16,128]{2,1,0:T(8,128)(2,1)S(1)}, u32[]{:S(2)}, u32[]{:S(2)}) collective-permute-start(bf16[33,16,128]{2,1,0:T(8,128)(2,1)S(1)} %collective-permute-done.8.refs_1_), channel_id=1, source_target_pairs={{0,1},{1,2},{2,3},{3,4},{4,5},{5,6},{6,7},{7,0},{8,9},{9,10},{10,1... | collective-permute-start | bytes 405512 | tf_op jit(solution)/shard_map/ppermute | solution.py:163
  78.7 3.9 %collective-permute-start.13 = (bf16[33,16,128]{2,1,0:T(8,128)(2,1)S(1)}, bf16[33,16,128]{2,1,0:T(8,128)(2,1)S(1)}, u32[]{:S(2)}, u32[]{:S(2)}) collective-permute-start(bf16[33,16,128]{2,1,0:T(8,128)(2,1)S(1)} %collective-permute-done.11.refs_4_), channel_id=1, source_target_pairs={{0,7},{1,0},{2,1},{3,2},{4,3},{5,4},{6,5},{7,6},{8,15},{9,8},{10,9... | collective-permute-start | bytes 405512 | tf_op jit(solution)/shard_map/ppermute | solution.py:164
  80.7 5.1 %collective-permute-start.12 = (bf16[33,16,128]{2,1,0:T(8,128)(2,1)S(1)}, bf16[33,16,128]{2,1,0:T(8,128)(2,1)S(1)}, u32[]{:S(2)}, u32[]{:S(2)}) collective-permute-start(bf16[33,16,128]{2,1,0:T(8,128)(2,1)S(1)} %collective-permute-done.10.refs_3_), channel_id=1, source_target_pairs={{0,1},{1,2},{2,3},{3,4},{4,5},{5,6},{6,7},{7,0},{8,9},{9,10},{10,1... | collective-permute-start | bytes 405512 | tf_op jit(solution)/shard_map/ppermute | solution.py:163
  82.5 7.6 %collective-permute-start.15 = (bf16[17,16,128]{2,1,0:T(8,128)(2,1)S(1)}, bf16[17,16,128]{2,1,0:T(8,128)(2,1)S(1)}, u32[]{:S(2)}, u32[]{:S(2)}) collective-permute-start(bf16[17,16,128]{2,1,0:T(8,128)(2,1)S(1)} %slice.24), channel_id=1, source_target_pairs={{0,7},{1,0},{2,1},{3,2},{4,3},{5,4},{6,5},{7,6},{8,15},{9,8},{10,9... | collective-permute-start | bytes 208904 | tf_op jit(solution)/shard_map/ppermute | solution.py:167
  85.8 4.3 %collective-permute-start.14 = (bf16[16,16,128]{2,1,0:T(8,128)(2,1)S(1)}, bf16[16,16,128]{2,1,0:T(8,128)(2,1)S(1)}, u32[]{:S(2)}, u32[]{:S(2)}) collective-permute-start(bf16[16,16,128]{2,1,0:T(8,128)(2,1)S(1)} %slice.23), channel_id=1, source_target_pairs={{0,1},{1,2},{2,3},{3,4},{4,5},{5,6},{6,7},{7,0},{8,9},{9,10},{10,1... | collective-permute-start | bytes 196616 | tf_op jit(solution)/shard_map/ppermute | solution.py:166
  92.4 25.6 %all-to-all-start.1 = ((bf16[288,16,128]{2,1,0:T(8,128)(2,1)}), bf16[288,16,128]{2,1,0:T(8,128)(2,1)S(1)}, u32[]{:S(2)}, u32[]{:S(2)}) async-start(bf16[288,16,128]{2,1,0:T(8,128)(2,1)} %get-tuple-element.29), calls=%async_computation.1 | async-start | bytes 2359296 | tf_op jit(solution)/shard_map/all_to_all | solution.py:652
  99.5 3.4 %copy-start.2 = (bf16[256,128,128]{2,1,0:T(8,128)(2,1)S(1)}, bf16[256,128,128]{2,1,0:T(8,128)(2,1)}, u32[]{:S(2)}) copy-start(bf16[256,128,128]{2,1,0:T(8,128)(2,1)} %copy-done) | copy-start | bytes 25165828
  118.0 3.4 %copy-start.3 = (bf16[256,128,128]{2,1,0:T(8,128)(2,1)S(1)}, bf16[256,128,128]{2,1,0:T(8,128)(2,1)}, u32[]{:S(2)}) copy-start(bf16[256,128,128]{2,1,0:T(8,128)(2,1)} %copy-done) | copy-start | bytes 25165828

commit v7 on v6

--- a/solution.py
+++ b/solution.py
@@ -15,7 +15,6 @@
 SEND = 8
 HALF = RB // 2
 EXTRA = SEND + 1
-CHUNK = 32
 GROUP = 32
 LEN = SLOTS + GROUP
 F32 = jnp.float32
@@ -297,24 +296,57 @@
     return (jnp.arange(BS, dtype=jnp.int32)[:, None] == target[None, :]).astype(BF16)
 
 
-def work(count, list_ref, weights_ref, load, add):
+def groups_of(count):
+    return lax.div(count + GROUP - 1, GROUP)
+
+
+def copy_group(source, target, sems, group):
+    span = pl.ds(group * GROUP, GROUP)
+    return pltpu.make_async_copy(source.at[span], target.at[span], sems.at[group])
+
+
+def start_groups(count, source, target, sems):
+    def start(group, carry):
+        copy_group(source, target, sems, group).start()
+        return carry
+
+    lax.fori_loop(0, groups_of(count), start, 0)
+
+
+def wait_groups(count, source, target, sems):
+    def wait(group, carry):
+        copy_group(source, target, sems, group).wait()
+        return carry
+
+    lax.fori_loop(0, groups_of(count), wait, 0)
+
+
+def products_of(entries, weights, load):
+    products = []
+    for at in range(0, GROUP, 2):
+        left = [load((entry >> 8) & 255) for entry in entries[at : at + 2]]
+        product = dot_nn(jnp.concatenate(left, axis=0), jnp.concatenate(weights[at : at + 2], axis=1))
+        rows = left[0].shape[0]
+        products += [product[:rows, :BS], product[rows:, BS:]]
+    return products
+
+
+def work(count, list_ref, weights_hbm, held, sems, load, add):
     def step(group, carry):
         base = group * GROUP
+        copy_group(weights_hbm, held, sems, group).wait()
         entries = [list_ref[base + j] for j in range(GROUP)]
-        products = []
-        for one, two in zip(entries[0::2], entries[1::2]):
-            left = [load((entry >> 8) & 255) for entry in (one, two)]
-            right = [weights_ref[entry & 255] for entry in (one, two)]
-            product = dot_nn(jnp.concatenate(left, axis=0), jnp.concatenate(right, axis=1))
-            rows = left[0].shape[0]
-            products += [product[:rows, :BS], product[rows:, BS:]]
+        products = products_of(entries, [held[base + j] for j in range(GROUP)], load)
         for entry, product in zip(entries, products):
             add(entry >> 16, (entry >> 8) & 255, product)
         return carry
 
-    lax.fori_loop(0, lax.div(count + GROUP - 1, GROUP), step, 0)
-
-
+    lax.fori_loop(0, groups_of(count), step, 0)
+
+
+WEIGHTS = pltpu.HBM((SLOTS, BS, BS), BF16)
+HELD = pltpu.VMEM((SLOTS, BS, BS), BF16)
+GROUP_SEMS = pltpu.SemaphoreType.DMA((SLOTS // GROUP,))
 ROWS = shaped((RB + 1, K, BS), F32)
 
 
@@ -322,62 +354,69 @@
     return (block.astype(F32) * inverse).astype(BF16)
 
 
-def first_own_kernel(list_ref, count_ref, part_ref, coupling_ref, acc_ref, weights_ref, held, sems):
-    chunks = lax.div(count_ref[2] + CHUNK - 1, CHUNK)
-
-    def copy_of(chunk):
-        span = pl.ds(chunk * CHUNK, CHUNK)
-        return pltpu.make_async_copy(coupling_ref.at[span], held.at[span], sems.at[chunk])
-
-    def start(chunk, carry):
-        copy_of(chunk).start()
+def first_own_kernel(
+    own_list, halo_list, count_ref, part_ref, coupling_ref, acc_ref, own_hbm, halo_hbm, held, own_held, halo_held, sems,
+    own_sems, halo_sems,
+):
+    live = count_ref[2]
+    start_groups(live, coupling_ref, held, sems)
+    acc_ref[...] = jnp.zeros_like(acc_ref)
+    wait_groups(live, coupling_ref, held, sems)
+
+    def own_step(group, carry):
+        base = group * GROUP
+        entries = [own_list[base + j] for j in range(GROUP)]
+        weights = [held[entry & 255].T for entry in entries]
+        for j in range(GROUP):
+            own_held[base + j] = weights[j]
+        copy_group(own_held, own_hbm, own_sems, group).start()
+        products = products_of(entries, weights, lambda block: part_ref[block])
+        for entry, product in zip(entries, products):
+            row = entry >> 16
+            acc_ref[row] = acc_ref[row] + product
         return carry
 
-    def turn(chunk, carry):
-        copy_of(chunk).wait()
-        for j in range(CHUNK):
-            weights_ref[chunk * CHUNK + j] = held[chunk * CHUNK + j].T
+    def halo_step(group, carry):
+        base = group * GROUP
+        for j in range(GROUP):
+            halo_held[base + j] = held[halo_list[base + j] & 255].T
+        copy_group(halo_held, halo_hbm, halo_sems, group).start()
         return carry
 
-    lax.fori_loop(0, chunks, start, 0)
-    lax.fori_loop(0, chunks, turn, 0)
-    acc_ref[...] = jnp.zeros_like(acc_ref)
+    lax.fori_loop(0, groups_of(count_ref[0]), own_step, 0)
+    lax.fori_loop(0, groups_of(count_ref[1]), halo_step, 0)
+    wait_groups(count_ref[0], own_held, own_hbm, own_sems)
+    wait_groups(count_ref[1], halo_held, halo_hbm, halo_sems)
+
+
+def first_own(own_list, halo_list, counts, part_tiles, coupling):
+    return call(
+        first_own_kernel,
+        (pltpu.HBM(ROWS.shape, F32), WEIGHTS, WEIGHTS),
+        [SMEM, SMEM, SMEM, VMEM, HBM],
+        (VMEM, HBM, HBM),
+        (HELD, HELD, HELD, GROUP_SEMS, GROUP_SEMS, GROUP_SEMS),
+        flops=2 * SLOTS * K * BS * BS,
+        moved=10000000,
+    )(own_list, halo_list, counts, in_hbm(part_tiles), in_hbm(coupling))
+
+
+def image_kernel(
+    list_ref, count_ref, halo_ref, weights_hbm, own_hbm, basis_ref, degree_ref, image_hbm, tiles_ref, halo_hbm, image_ref,
+    out_sems, acc_ref, held, sems,
+):
+    own = start_copies([(own_hbm, acc_ref)], out_sems, 2)
+    start_groups(count_ref[1], weights_hbm, held, sems)
+    copies = start_copies([(halo_ref, halo_hbm)], out_sems)
+    wait_all(own)
 
     def load(block):
-        return part_ref[block]
+        return halo_ref[block + (block >> 3)]
 
     def add(row, block, product):
         acc_ref[row] = acc_ref[row] + product
 
-    work(count_ref[0], list_ref, weights_ref, load, add)
-
-
-def first_own(own_list, counts, part_tiles, coupling):
-    return call(
-        first_own_kernel,
-        (ROWS, pltpu.VMEM((SLOTS, BS, BS), BF16)),
-        [SMEM, SMEM, VMEM, HBM],
-        (VMEM, VMEM),
-        (pltpu.VMEM((SLOTS, BS, BS), BF16), pltpu.SemaphoreType.DMA((SLOTS // CHUNK,))),
-        flops=2 * SLOTS * K * BS * BS,
-        moved=10000000,
-    )(own_list, counts, in_hbm(part_tiles), in_hbm(coupling))
-
-
-def image_kernel(
-    list_ref, count_ref, halo_ref, weights_ref, own_ref, basis_ref, degree_ref, image_hbm, tiles_ref, halo_hbm, image_ref,
-    out_sems, acc_ref,
-):
-    copies = start_copies([(halo_ref, halo_hbm)], out_sems)
-    acc_ref[...] = own_ref[...]
-
-    def load(block):
-        return halo_ref[block + (block >> 3)]
-
-    def add(row, block, product):
-        acc_ref[row] = acc_ref[row] + product
-
-    work(count_ref[1], list_ref, weights_ref, load, add)
+    work(count_ref[1], list_ref, weights_hbm, held, sems, load, add)
     top = jnp.zeros((K, BS), F32)
     bottom = jnp.zeros((K, BS), F32)
     for block in range(RB):
@@ -408,17 +447,25 @@
     return call(
         image_kernel,
         (pltpu.HBM(basis.shape, F32), shaped((RB + 1, K, BS), BF16), pltpu.HBM(halo_tiles.shape, BF16)),
-        [SMEM, SMEM, VMEM, VMEM, VMEM, VMEM, VMEM],
+        [SMEM, SMEM, VMEM, HBM, HBM, VMEM, VMEM],
         (HBM, VMEM, HBM),
-        (pltpu.VMEM(basis.shape, F32), pltpu.SemaphoreType.DMA((2,)), pltpu.VMEM((RB + 1, K, BS), F32)),
+        (
+            pltpu.VMEM(basis.shape, F32),
+            pltpu.SemaphoreType.DMA((3,)),
+            pltpu.VMEM((RB + 1, K, BS), F32),
+            HELD,
+            GROUP_SEMS,
+        ),
         flops=2 * SLOTS * K * BS * BS,
         moved=8000000,
-    )(halo_list, counts, halo_tiles, weights, own, basis, degree)
+    )(halo_list, counts, halo_tiles, in_hbm(weights), in_hbm(own), basis, degree)
 
 
 def second_own_kernel(
-    list_ref, count_ref, part_ref, table_ref, basis_part_ref, inverse_ref, weights_ref, acc_ref, scaled_ref, quotient_ref
+    list_ref, count_ref, part_ref, table_ref, basis_part_ref, inverse_ref, weights_hbm, acc_ref, scaled_ref, quotient_ref,
+    held, sems,
 ):
+    start_groups(count_ref[0], weights_hbm, held, sems)
     acc_ref[...] = jnp.zeros_like(acc_ref)
     scaled_ref[...] = jnp.zeros_like(scaled_ref)
     table = table_ref[...].astype(F32)
@@ -433,19 +480,19 @@
         acc_ref[row] = acc_ref[row] + (product[0:K] + quotient_ref[block >> 5] * product[K:])
         scaled_ref[row] = scaled_ref[row] + product[K:]
 
-    work(count_ref[0], list_ref, weights_ref, load, add)
+    work(count_ref[0], list_ref, weights_hbm, held, sems, load, add)
 
 
 def second_own(own_list, counts, part_tiles, table, basis_part, inverse, weights, n_row):
     return call(
         second_own_kernel,
         (pltpu.HBM(ROWS.shape, F32), pltpu.HBM(ROWS.shape, F32)),
-        [SMEM, SMEM, VMEM, VMEM, VMEM, VMEM, VMEM],
+        [SMEM, SMEM, VMEM, VMEM, VMEM, VMEM, HBM],
         (VMEM, VMEM),
-        (pltpu.VMEM((n_row, K, BS), F32),),
+        (pltpu.VMEM((n_row, K, BS), F32), HELD, GROUP_SEMS),
         flops=4 * SLOTS * K * BS * BS,
         moved=10000000,
-    )(own_list, counts, *map(in_hbm, (part_tiles, table, basis_part, inverse)), weights)
+    )(own_list, counts, *map(in_hbm, (part_tiles, table, basis_part, inverse, weights)))
 
 
 def spread_kernel(taken_ref, given_ref):
@@ -501,9 +548,9 @@
 
 
 def gram_kernel(
-    list_ref, count_ref, halo_ref, weights_ref, basis_halo_hbm, own_hbm, own_scaled_hbm, basis_hbm, image_hbm, degree_hbm,
+    list_ref, count_ref, halo_ref, weights_hbm, basis_halo_hbm, own_hbm, own_scaled_hbm, basis_hbm, image_hbm, degree_hbm,
     previous_hbm, previous_image_hbm, stacked, stacked_image, packed_ref, basis_halo_ref, acc_ref, scaled_ref, degree_ref,
-    in_sems, side_ref, quotient_ref, inverse_ref, wide_ref,
+    in_sems, held, sems, side_ref, quotient_ref, inverse_ref, wide_ref,
 ):
     early = [(basis_halo_hbm, basis_halo_ref), (own_hbm, acc_ref), (own_scaled_hbm, scaled_ref)]
     late = [
@@ -514,6 +561,7 @@
         (degree_hbm, degree_ref),
     ]
     early = start_copies(early, in_sems)
+    start_groups(count_ref[1], weights_hbm, held, sems)
     late = start_copies(late, in_sems, 3)
     peers = halo_ref.shape[0] // EXTRA
     total = jnp.zeros((K, BS), F32)
@@ -544,7 +592,7 @@
         acc_ref[row] = acc_ref[row] + (product[0:K] + quotient * product[K:])
         scaled_ref[row] = scaled_ref[row] + product[K:]
 
-    work(count_ref[1], list_ref, weights_ref, load, add)
+    work(count_ref[1], list_ref, weights_hbm, held, sems, load, add)
     wait_all(late)
     for block in range(RB):
         at = columns(block)
@@ -566,7 +614,7 @@
     return call(
         gram_kernel,
         (stack, stack, shaped((n_dom, 24, BS), F32)),
-        [SMEM, SMEM, VMEM, VMEM] + [HBM] * 8,
+        [SMEM, SMEM, VMEM] + [HBM] * 9,
         (VMEM, VMEM, VMEM),
         (
             pltpu.VMEM(basis_halo.shape, BF16),
@@ -574,6 +622,8 @@
             pltpu.VMEM((RB + 1, K, BS), F32),
             pltpu.VMEM(degree.shape, F32),
             pltpu.SemaphoreType.DMA((8,)),
+            HELD,
+            GROUP_SEMS,
             pltpu.VMEM((n_dom * K, BS), BF16),
             pltpu.VMEM((SEND, n_dom, K, BS), F32),
             pltpu.VMEM((n_dom * SEND, BS), F32),
@@ -582,8 +632,8 @@
         flops=2 * SLOTS * K * BS * BS,
         moved=10000000,
     )(
-        halo_list, counts, halo_tiles, weights,
-        *map(in_hbm, (basis_halo, own, scaled, basis, image, degree, previous, previous_image)),
+        halo_list, counts, halo_tiles,
+        *map(in_hbm, (weights, basis_halo, own, scaled, basis, image, degree, previous, previous_image)),
     )
 
 
@@ -665,15 +715,15 @@
     gathered = gather_row(cast_tiles(in_hbm(basis), in_hbm(degree)), n_row, HALF + 2)
     basis_part, inverse, chosen = first_select(gathered, place, send_list, n_row)
     halo_tiles = to_all(chosen, "dom")
-    own, weights = first_own(own_list, counts, basis_part, coupling)
-    image, tiles, basis_halo = make_image(halo_list, counts, halo_tiles, weights, own, basis, degree)
+    own, own_weights, halo_weights = first_own(own_list, halo_list, counts, basis_part, coupling)
+    image, tiles, basis_halo = make_image(halo_list, counts, halo_tiles, halo_weights, own, basis, degree)
 
     gathered = gather_row(tiles, n_row, HALF)
     part_tiles, chosen, table = second_select(gathered, place, send_list, picks(send_list), n_row)
     halo_tiles = to_all(chosen, "dom")
-    own, scaled = second_own(own_list, counts, part_tiles, table, basis_part, inverse, weights, n_row)
+    own, scaled = second_own(own_list, counts, part_tiles, table, basis_part, inverse, own_weights, n_row)
     stacked, stacked_image, packed = make_grams(
-        halo_list, counts, halo_tiles, weights, basis_halo, own, scaled, basis, image, degree, previous, previous_image,
+        halo_list, counts, halo_tiles, halo_weights, basis_halo, own, scaled, basis, image, degree, previous, previous_image,
         n_dom,
     )
     packed = to_all(add_and_repeat(to_all(packed, "dom"), n_row), "row")

time: 156 us -> 153 us (0.981)
  local copies, waits for them, and re-layouts: 14.5 us -> 1.65 us
  Pallas kernels: 31.9 us -> 39 us
  starting transfers between devices: 43.1 us -> 44.7 us
    unnamed x19 -> x23, local copies, waits for them, and re-layouts: 14.2 us -> 1.39 us
    pallas_call x10, Pallas kernels: 31.9 us -> 39 us  [run(): pl.pallas_call(kernel, out_shape=out_shape, in_specs=in_specs, out_specs=...]
  transfers between devices with their start and end apart: 18 -> 18, of which waited for: 14 -> 11; matrix products, arithmetic and copies ran while one was open for 1% -> 1% of each run, Pallas kernels for 9% -> 12%
where the time goes in v7:
time: 153 us; the launch traced here: 152 us
  starting transfers between devices  44.7 us (29%)
  waiting for transfers between devices  40.5 us (26%)
  Pallas kernels  39 us (25%)
  blocking collectives  24.6 us (16%)
  local copies, waits for them, and re-layouts  1.65 us (1%)
  between operations  1.53 us (1%)
    pallas_call x10, Pallas kernels, run(): pl.pallas_call(kernel, out_shape=out_shape, in_specs=in_specs, out_specs=...  39 us
    all_to_all x2, blocking collectives, to_all(): return lax.all_to_all(value, axis, split_axis=0, concat_axis=0, tiled=True)  24.6 us
    all_to_all x2, starting transfers between devices, to_all(): return lax.all_to_all(value, axis, split_axis=0, concat_axis=0, tiled=True)  19.8 us
    all_to_all x2, waiting for transfers between devices, to_all(): return lax.all_to_all(value, axis, split_axis=0, concat_axis=0, tiled=True)  17.2 us
    ppermute x6, starting transfers between devices, gather_row(): from_above = lax.ppermute(from_above, 'row', down)  16.9 us
    ppermute x6, waiting for transfers between devices, gather_row(): from_above = lax.ppermute(from_above, 'row', down)  15.7 us
    ppermute x2, waiting for transfers between devices, gather_row(): far_low = lax.ppermute(from_below[:half], 'row', up)  7.18 us
    ppermute x2, starting transfers between devices, gather_row(): far_high = lax.ppermute(from_above[half:], 'row', down)  6.19 us
  transfers between devices with their start and end apart: 18, of which 11 were waited for; matrix products, arithmetic and copies ran while one was open for 1% of the time, Pallas kernels for 12%

profile of v7, /device:TPU:1, one launch (start us, length us, event | category | flops | bytes accessed | tf_op | source)
XLA Modules:
  0.0 152.3 jit_solution(15178180384569931944)
XLA Ops:
  0.6 1.0 shard_map.105.refs_0_
  1.7 6.5 %collective-permute-start.1 = (bf16[36,16,128]{2,1,0:T(8,128)(2,1)S(1)}, bf16[36,16,128]{2,1,0:T(8,128)(2,1)S(1)}, u32[]{:S(2)}, u32[]{:S(2)}) collective-permute-start(bf16[36,16,128]{2,1,0:T(8,128)(2,1)S(1)} %shard_map.105.refs_0_), channel_id=1, source_target_pairs={{0,7},{1,0},{2,1},{3,2},{4,3},{5,4},{6,5},{7,6},{8,15},{9,8},{10,9... | collective-permute-start | bytes 442376 | tf_op jit(solution)/shard_map/ppermute | solution.py:163
  8.1 2.5 %collective-permute-done.1.refs_2_ = bf16[36,16,128]{2,1,0:T(8,128)(2,1)S(1)} collective-permute-done((bf16[36,16,128]{2,1,0:T(8,128)(2,1)S(1)}, bf16[36,16,128]{2,1,0:T(8,128)(2,1)S(1)}, u32[]{:S(2)}, u32[]{:S(2)}) %collective-permute-start.1) | collective-permute-done | bytes 147488 | tf_op jit(solution)/shard_map/ppermute | solution.py:163
  10.7 3.4 %collective-permute-start.3 = (bf16[36,16,128]{2,1,0:T(8,128)(2,1)S(1)}, bf16[36,16,128]{2,1,0:T(8,128)(2,1)S(1)}, u32[]{:S(2)}, u32[]{:S(2)}) collective-permute-start(bf16[36,16,128]{2,1,0:T(8,128)(2,1)S(1)} %collective-permute-done.1.refs_2_), channel_id=1, source_target_pairs={{0,7},{1,0},{2,1},{3,2},{4,3},{5,4},{6,5},{7,6},{8,15},{9,8},{10,9... | collective-permute-start | bytes 442376 | tf_op jit(solution)/shard_map/ppermute | solution.py:163
  14.1 2.1 %collective-permute-done.3.refs_4_ = bf16[36,16,128]{2,1,0:T(8,128)(2,1)S(1)} collective-permute-done((bf16[36,16,128]{2,1,0:T(8,128)(2,1)S(1)}, bf16[36,16,128]{2,1,0:T(8,128)(2,1)S(1)}, u32[]{:S(2)}, u32[]{:S(2)}) %collective-permute-start.3) | collective-permute-done | bytes 147488 | tf_op jit(solution)/shard_map/ppermute | solution.py:163
  16.2 3.1 %collective-permute-start.5 = (bf16[36,16,128]{2,1,0:T(8,128)(2,1)S(1)}, bf16[36,16,128]{2,1,0:T(8,128)(2,1)S(1)}, u32[]{:S(2)}, u32[]{:S(2)}) collective-permute-start(bf16[36,16,128]{2,1,0:T(8,128)(2,1)S(1)} %collective-permute-done.3.refs_4_), channel_id=1, source_target_pairs={{0,7},{1,0},{2,1},{3,2},{4,3},{5,4},{6,5},{7,6},{8,15},{9,8},{10,9... | collective-permute-start | bytes 442376 | tf_op jit(solution)/shard_map/ppermute | solution.py:163
  19.3 2.1 %collective-permute-done.5.refs_6_ = bf16[36,16,128]{2,1,0:T(8,128)(2,1)S(1)} collective-permute-done((bf16[36,16,128]{2,1,0:T(8,128)(2,1)S(1)}, bf16[36,16,128]{2,1,0:T(8,128)(2,1)S(1)}, u32[]{:S(2)}, u32[]{:S(2)}) %collective-permute-start.5) | collective-permute-done | bytes 147488 | tf_op jit(solution)/shard_map/ppermute | solution.py:163
  21.4 3.1 %collective-permute-start.7 = (bf16[18,16,128]{2,1,0:T(8,128)(2,1)S(1)}, bf16[18,16,128]{2,1,0:T(8,128)(2,1)S(1)}, u32[]{:S(2)}, u32[]{:S(2)}) collective-permute-start(bf16[18,16,128]{2,1,0:T(8,128)(2,1)S(1)} %slice.22), channel_id=1, source_target_pairs={{0,7},{1,0},{2,1},{3,2},{4,3},{5,4},{6,5},{7,6},{8,15},{9,8},{10,9... | collective-permute-start | bytes 221192 | tf_op jit(solution)/shard_map/ppermute | solution.py:166
  24.6 0.8 copy.12
  25.9 3.1 %collective-permute-done.6.refs_7_ = bf16[18,16,128]{2,1,0:T(8,128)(2,1)S(1)} collective-permute-done((bf16[18,16,128]{2,1,0:T(8,128)(2,1)S(1)}, bf16[18,16,128]{2,1,0:T(8,128)(2,1)S(1)}, u32[]{:S(2)}, u32[]{:S(2)}) %collective-permute-start.6) | collective-permute-done | bytes 73760 | tf_op jit(solution)/shard_map/ppermute | solution.py:165
  29.0 2.1 %shard_map.106 = (bf16[256,16,128]{2,1,0:T(8,128)(2,1)}, f32[256,128]{1,0:T(8,128)}, bf16[288,16,128]{2,1,0:T(8,128)(2,1)}) custom-call(s32[1]{0:T(128)} %bitcast.place_ref, s32[256]{0:T(256)S(1)} %reshape.19.send_ref, bf16[36,16,128]{2,1,0:T(8,128)(2,1)S(1)} %shard_map.105.refs_0_, bf16[36,16,128]{2,1,0:T(8,128)(2,1)S(1)} %collective-permute-done.refs_1_, ...), custom_call_target="tpu_custom_call" | custom-call | bytes 3000000 | tf_op jit(solution)/shard_map/pallas_call | solution.py:36
  31.1 12.4 %all-to-all-start = ((bf16[288,16,128]{2,1,0:T(8,128)(2,1)}), bf16[288,16,128]{2,1,0:T(8,128)(2,1)S(1)}, u32[]{:S(2)}, u32[]{:S(2)}) async-start(bf16[288,16,128]{2,1,0:T(8,128)(2,1)} %get-tuple-element.24), calls=%async_computation | async-start | bytes 2359296 | tf_op jit(solution)/shard_map/all_to_all | solution.py:702
  44.1 3.1 %shard_map.104 = (s32[288]{0:T(512)S(1)}, s32[288]{0:T(512)S(1)}, s32[3]{0:T(128)S(1)}) custom-call(s32[256]{0:T(256)S(1)} %copy-done.8, s32[256]{0:T(256)S(1)} %copy-done.9, s32[1]{0:T(128)S(6)} %copy.14.live_ref), custom_call_target="tpu_custom_call" | custom-call | bytes 20000 | tf_op jit(solution)/shard_map/pallas_call | solution.py:36
  47.9 10.1 %shard_map.107 = (f32[33,16,128]{2,1,0:T(8,128)}, bf16[256,128,128]{2,1,0:T(8,128)(2,1)}, bf16[256,128,128]{2,1,0:T(8,128)(2,1)}) custom-call(s32[288]{0:T(512)} %copy-done.4, s32[288]{0:T(512)} %copy-done.2, s32[3]{0:T(128)} %copy-done.6, bf16[256,16,128]{2,1,0:T(8,128)(2,1)} %get-tuple-element.26.part_ref.basis_part_ref, bf16[256,128,128]{2,1,0:T(8,128)(2,1)} %coupling_ref.1), custom_call_target="tpu_custom_call" | custom-call | flops 134217728 | bytes 10000000 | tf_op jit(solution)/shard_map/pallas_call | solution.py:36
  58.0 3.8 %all-to-all-done.halo_ref = bf16[288,16,128]{2,1,0:T(8,128)(2,1)S(1)} async-done(((bf16[288,16,128]{2,1,0:T(8,128)(2,1)}), bf16[288,16,128]{2,1,0:T(8,128)(2,1)S(1)}, u32[]{:S(2)}, u32[]{:S(2)}) %all-to-all-start) | async-done | bytes 1179680 | tf_op jit(solution)/shard_map/all_to_all | solution.py:702
  61.8 4.8 %shard_map.108 = (f32[16,4096]{1,0:T(8,128)}, bf16[33,16,128]{2,1,0:T(8,128)(2,1)S(1)}, bf16[288,16,128]{2,1,0:T(8,128)(2,1)}) custom-call(s32[288]{0:T(512)S(1)} %copy-done.3, s32[3]{0:T(128)S(1)} %copy-done.7, bf16[288,16,128]{2,1,0:T(8,128)(2,1)S(1)} %all-to-all-done.halo_ref, bf16[256,128,128]{2,1,0:T(8,128)(2,1)} %get-tuple-element.27.weights_hbm, ...), custom_call_target="tpu_custom_call" | custom-call | flops 134217728 | bytes 8000000 | tf_op jit(solution)/shard_map/pallas_call | solution.py:36
  66.7 1.5 collective-permute-start.8
  68.3 3.8 %collective-permute-done.9.refs_2_ = bf16[33,16,128]{2,1,0:T(8,128)(2,1)S(1)} collective-permute-done((bf16[33,16,128]{2,1,0:T(8,128)(2,1)S(1)}, bf16[33,16,128]{2,1,0:T(8,128)(2,1)S(1)}, u32[]{:S(2)}, u32[]{:S(2)}) %collective-permute-start.9) | collective-permute-done | bytes 135200 | tf_op jit(solution)/shard_map/ppermute | solution.py:163
  72.1 1.4 collective-permute-start.11
  73.8 3.4 %collective-permute-done.11.refs_4_ = bf16[33,16,128]{2,1,0:T(8,128)(2,1)S(1)} collective-permute-done((bf16[33,16,128]{2,1,0:T(8,128)(2,1)S(1)}, bf16[33,16,128]{2,1,0:T(8,128)(2,1)S(1)}, u32[]{:S(2)}, u32[]{:S(2)}) %collective-permute-start.11) | collective-permute-done | bytes 135200 | tf_op jit(solution)/shard_map/ppermute | solution.py:163
  77.1 2.4 %collective-permute-start.13 = (bf16[33,16,128]{2,1,0:T(8,128)(2,1)S(1)}, bf16[33,16,128]{2,1,0:T(8,128)(2,1)S(1)}, u32[]{:S(2)}, u32[]{:S(2)}) collective-permute-start(bf16[33,16,128]{2,1,0:T(8,128)(2,1)S(1)} %collective-permute-done.11.refs_4_), channel_id=1, source_target_pairs={{0,7},{1,0},{2,1},{3,2},{4,3},{5,4},{6,5},{7,6},{8,15},{9,8},{10,9... | collective-permute-start | bytes 405512 | tf_op jit(solution)/shard_map/ppermute | solution.py:163
  79.7 1.8 %collective-permute-done.13.refs_6_ = bf16[33,16,128]{2,1,0:T(8,128)(2,1)S(1)} collective-permute-done((bf16[33,16,128]{2,1,0:T(8,128)(2,1)S(1)}, bf16[33,16,128]{2,1,0:T(8,128)(2,1)S(1)}, u32[]{:S(2)}, u32[]{:S(2)}) %collective-permute-start.13) | collective-permute-done | bytes 135200 | tf_op jit(solution)/shard_map/ppermute | solution.py:163
  81.5 3.1 %collective-permute-start.15 = (bf16[17,16,128]{2,1,0:T(8,128)(2,1)S(1)}, bf16[17,16,128]{2,1,0:T(8,128)(2,1)S(1)}, u32[]{:S(2)}, u32[]{:S(2)}) collective-permute-start(bf16[17,16,128]{2,1,0:T(8,128)(2,1)S(1)} %slice.24), channel_id=1, source_target_pairs={{0,7},{1,0},{2,1},{3,2},{4,3},{5,4},{6,5},{7,6},{8,15},{9,8},{10,9... | collective-permute-start | bytes 208904 | tf_op jit(solution)/shard_map/ppermute | solution.py:166
  84.9 4.1 %collective-permute-done.14.refs_7_ = bf16[16,16,128]{2,1,0:T(8,128)(2,1)S(1)} collective-permute-done((bf16[16,16,128]{2,1,0:T(8,128)(2,1)S(1)}, bf16[16,16,128]{2,1,0:T(8,128)(2,1)S(1)}, u32[]{:S(2)}, u32[]{:S(2)}) %collective-permute-start.14) | collective-permute-done | bytes 65568 | tf_op jit(solution)/shard_map/ppermute | solution.py:165
  89.0 2.3 %shard_map.109 = (bf16[256,16,128]{2,1,0:T(8,128)(2,1)}, bf16[288,16,128]{2,1,0:T(8,128)(2,1)}, bf16[16,128]{1,0:T(8,128)(2,1)}) custom-call(s32[1]{0:T(128)} %bitcast.place_ref, s32[256]{0:T(256)S(1)} %reshape.19.send_ref, bf16[128,4096]{1,0:T(8,128)(2,1)S(1)} %fusion.pick_ref, bf16[33,16,128]{2,1,0:T(8,128)(2,1)S(1)} %get-tuple-element.29.refs_0_, ...), custom_call_target="tpu_custom_call" | custom-call | bytes 3000000 | tf_op jit(solution)/shard_map/pallas_call | solution.py:36
  91.3 7.4 %all-to-all-start.1 = ((bf16[288,16,128]{2,1,0:T(8,128)(2,1)}), bf16[288,16,128]{2,1,0:T(8,128)(2,1)S(1)}, u32[]{:S(2)}, u32[]{:S(2)}) async-start(bf16[288,16,128]{2,1,0:T(8,128)(2,1)} %get-tuple-element.30), calls=%async_computation.1 | async-start | bytes 2359296 | tf_op jit(solution)/shard_map/all_to_all | solution.py:702
  98.7 5.0 %shard_map.110 = (f32[33,16,128]{2,1,0:T(8,128)}, f32[33,16,128]{2,1,0:T(8,128)}) custom-call(s32[288]{0:T(512)S(1)} %copy-done.5, s32[3]{0:T(128)S(1)} %copy-done.7, bf16[256,16,128]{2,1,0:T(8,128)(2,1)} %get-tuple-element.32.part_ref, bf16[16,128]{1,0:T(8,128)(2,1)} %get-tuple-element.33.table_ref, ...), custom_call_target="tpu_custom_call" | custom-call | flops 268435456 | bytes 10000000 | tf_op jit(solution)/shard_map/pallas_call | solution.py:36
  103.8 13.4 %all-to-all-done.1.halo_ref = bf16[288,16,128]{2,1,0:T(8,128)(2,1)S(1)} async-done(((bf16[288,16,128]{2,1,0:T(8,128)(2,1)}), bf16[288,16,128]{2,1,0:T(8,128)(2,1)S(1)}, u32[]{:S(2)}, u32[]{:S(2)}) %all-to-all-start.1) | async-done | bytes 1179680 | tf_op jit(solution)/shard_map/all_to_all | solution.py:702
  117.2 5.8 %shard_map.111 = (f32[48,4096]{1,0:T(8,128)S(1)}, f32[48,4096]{1,0:T(8,128)S(1)}, f32[32,24,128]{2,1,0:T(8,128)S(1)}) custom-call(s32[288]{0:T(512)S(1)} %copy-done.3, s32[3]{0:T(128)S(1)} %copy-done.7, bf16[288,16,128]{2,1,0:T(8,128)(2,1)S(1)} %all-to-all-done.1.halo_ref, bf16[256,128,128]{2,1,0:T(8,128)(2,1)} %get-tuple-element.27.weights_hbm, ...), custom_call_target="tpu_custom_call" | custom-call | flops 134217728 | bytes 10000000 | tf_op jit(solution)/shard_map/pallas_call | solution.py:36
  123.0 13.4 %all_to_all.20.taken_ref = f32[32,24,128]{2,1,0:T(8,128)S(1)} all-to-all(f32[32,24,128]{2,1,0:T(8,128)S(1)} %get-tuple-element.39), channel_id=1, replica_groups=mesh['dom'=32,'row'=8] {'dom'}, dimensions={0} | all-to-all | bytes 786432 | tf_op jit(solution)/shard_map/all_to_all | solution.py:702
  136.4 11.2 %all_to_all.21.taken_ref = f32[8,24,128]{2,1,0:T(8,128)S(1)} all-to-all(f32[8,24,128]{2,1,0:T(8,128)S(1)} %shard_map.112), channel_id=1, replica_groups=mesh['dom'=32,'row'=8] {'row'}, dimensions={0} | all-to-all | bytes 196608 | tf_op jit(solution)/shard_map/all_to_all | solution.py:702
  147.6 4.7 %shard_map.113 = (f32[16,4096]{1,0:T(8,128)}, f32[16,4096]{1,0:T(8,128)}) custom-call(f32[8,24,128]{2,1,0:T(8,128)S(1)} %all_to_all.21.taken_ref, f32[48,4096]{1,0:T(8,128)S(1)} %get-tuple-element.40.stacked_ref, f32[48,4096]{1,0:T(8,128)S(1)} %get-tuple-element.41.stacked_image_ref), custom_call_target="tpu_custom_call" | custom-call | flops 1000000 | bytes 3000000 | tf_op jit(solution)/shard_map/pallas_call | solution.py:36
  (51 shorter events, 2.2 us)
Async XLA Ops:
  0.6 43.5 %copy-start.8 = (s32[256]{0:T(256)S(1)}, s32[256]{0:T(256)}, u32[]{:S(2)}) copy-start(s32[256]{0:T(256)} %row_ref.1) | copy-start | bytes 3076
  0.6 43.5 %copy-start.9 = (s32[256]{0:T(256)S(1)}, s32[256]{0:T(256)}, u32[]{:S(2)}) copy-start(s32[256]{0:T(256)} %column_ref.1) | copy-start | bytes 3076
  1.7 9.0 %collective-permute-start.1 = (bf16[36,16,128]{2,1,0:T(8,128)(2,1)S(1)}, bf16[36,16,128]{2,1,0:T(8,128)(2,1)S(1)}, u32[]{:S(2)}, u32[]{:S(2)}) collective-permute-start(bf16[36,16,128]{2,1,0:T(8,128)(2,1)S(1)} %shard_map.105.refs_0_), channel_id=1, source_target_pairs={{0,7},{1,0},{2,1},{3,2},{4,3},{5,4},{6,5},{7,6},{8,15},{9,8},{10,9... | collective-permute-start | bytes 442376 | tf_op jit(solution)/shard_map/ppermute | solution.py:163
  8.1 5.9 %collective-permute-start = (bf16[36,16,128]{2,1,0:T(8,128)(2,1)S(1)}, bf16[36,16,128]{2,1,0:T(8,128)(2,1)S(1)}, u32[]{:S(2)}, u32[]{:S(2)}) collective-permute-start(bf16[36,16,128]{2,1,0:T(8,128)(2,1)S(1)} %shard_map.105.refs_0_), channel_id=1, source_target_pairs={{0,1},{1,2},{2,3},{3,4},{4,5},{5,6},{6,7},{7,0},{8,9},{9,10},{10,1... | collective-permute-start | bytes 442376 | tf_op jit(solution)/shard_map/ppermute | solution.py:162
  10.7 5.5 %collective-permute-start.3 = (bf16[36,16,128]{2,1,0:T(8,128)(2,1)S(1)}, bf16[36,16,128]{2,1,0:T(8,128)(2,1)S(1)}, u32[]{:S(2)}, u32[]{:S(2)}) collective-permute-start(bf16[36,16,128]{2,1,0:T(8,128)(2,1)S(1)} %collective-permute-done.1.refs_2_), channel_id=1, source_target_pairs={{0,7},{1,0},{2,1},{3,2},{4,3},{5,4},{6,5},{7,6},{8,15},{9,8},{10,9... | collective-permute-start | bytes 442376 | tf_op jit(solution)/shard_map/ppermute | solution.py:163
  14.1 5.2 %collective-permute-start.2 = (bf16[36,16,128]{2,1,0:T(8,128)(2,1)S(1)}, bf16[36,16,128]{2,1,0:T(8,128)(2,1)S(1)}, u32[]{:S(2)}, u32[]{:S(2)}) collective-permute-start(bf16[36,16,128]{2,1,0:T(8,128)(2,1)S(1)} %collective-permute-done.refs_1_), channel_id=1, source_target_pairs={{0,1},{1,2},{2,3},{3,4},{4,5},{5,6},{6,7},{7,0},{8,9},{9,10},{10,1... | collective-permute-start | bytes 442376 | tf_op jit(solution)/shard_map/ppermute | solution.py:162
  16.2 5.2 %collective-permute-start.5 = (bf16[36,16,128]{2,1,0:T(8,128)(2,1)S(1)}, bf16[36,16,128]{2,1,0:T(8,128)(2,1)S(1)}, u32[]{:S(2)}, u32[]{:S(2)}) collective-permute-start(bf16[36,16,128]{2,1,0:T(8,128)(2,1)S(1)} %collective-permute-done.3.refs_4_), channel_id=1, source_target_pairs={{0,7},{1,0},{2,1},{3,2},{4,3},{5,4},{6,5},{7,6},{8,15},{9,8},{10,9... | collective-permute-start | bytes 442376 | tf_op jit(solution)/shard_map/ppermute | solution.py:163
  19.3 5.2 %collective-permute-start.4 = (bf16[36,16,128]{2,1,0:T(8,128)(2,1)S(1)}, bf16[36,16,128]{2,1,0:T(8,128)(2,1)S(1)}, u32[]{:S(2)}, u32[]{:S(2)}) collective-permute-start(bf16[36,16,128]{2,1,0:T(8,128)(2,1)S(1)} %collective-permute-done.2.refs_3_), channel_id=1, source_target_pairs={{0,1},{1,2},{2,3},{3,4},{4,5},{5,6},{6,7},{7,0},{8,9},{9,10},{10,1... | collective-permute-start | bytes 442376 | tf_op jit(solution)/shard_map/ppermute | solution.py:162
  21.4 4.5 %collective-permute-start.7 = (bf16[18,16,128]{2,1,0:T(8,128)(2,1)S(1)}, bf16[18,16,128]{2,1,0:T(8,128)(2,1)S(1)}, u32[]{:S(2)}, u32[]{:S(2)}) collective-permute-start(bf16[18,16,128]{2,1,0:T(8,128)(2,1)S(1)} %slice.22), channel_id=1, source_target_pairs={{0,7},{1,0},{2,1},{3,2},{4,3},{5,4},{6,5},{7,6},{8,15},{9,8},{10,9... | collective-permute-start | bytes 221192 | tf_op jit(solution)/shard_map/ppermute | solution.py:166
  24.5 4.5 %collective-permute-start.6 = (bf16[18,16,128]{2,1,0:T(8,128)(2,1)S(1)}, bf16[18,16,128]{2,1,0:T(8,128)(2,1)S(1)}, u32[]{:S(2)}, u32[]{:S(2)}) collective-permute-start(bf16[18,16,128]{2,1,0:T(8,128)(2,1)S(1)} %slice.21), channel_id=1, source_target_pairs={{0,1},{1,2},{2,3},{3,4},{4,5},{5,6},{6,7},{7,0},{8,9},{9,10},{10,1... | collective-permute-start | bytes 221192 | tf_op jit(solution)/shard_map/ppermute | solution.py:165
  31.1 30.7 %all-to-all-start = ((bf16[288,16,128]{2,1,0:T(8,128)(2,1)}), bf16[288,16,128]{2,1,0:T(8,128)(2,1)S(1)}, u32[]{:S(2)}, u32[]{:S(2)}) async-start(bf16[288,16,128]{2,1,0:T(8,128)(2,1)} %get-tuple-element.24), calls=%async_computation | async-start | bytes 2359296 | tf_op jit(solution)/shard_map/all_to_all | solution.py:702
  47.3 0.6 copy-start.2
  47.3 0.6 copy-start.4
  47.3 0.6 copy-start.6
  47.9 13.9 %copy-start = (f32[16,4096]{1,0:T(8,128)S(1)}, f32[16,4096]{1,0:T(8,128)}, u32[]{:S(2)}) copy-start(f32[16,4096]{1,0:T(8,128)} %basis_hbm.1) | copy-start | bytes 786436
  47.9 13.9 %copy-start.1 = (f32[4096]{0:T(1024)S(1)}, f32[4096]{0:T(1024)}, u32[]{:S(2)}) copy-start(f32[4096]{0:T(1024)} %param.12) | copy-start | bytes 49156
  47.9 13.9 %copy-start.3 = (s32[288]{0:T(512)S(1)}, s32[288]{0:T(512)}, u32[]{:S(2)}) copy-start(s32[288]{0:T(512)} %copy-done.2) | copy-start | bytes 3460
  47.9 13.9 %copy-start.7 = (s32[3]{0:T(128)S(1)}, s32[3]{0:T(128)}, u32[]{:S(2)}) copy-start(s32[3]{0:T(128)} %copy-done.6) | copy-start | bytes 40
  61.8 17.7 %copy-start.10 = (s32[1,32,8]{1,2,0:T(8,128)S(1)}, s32[1,32,8]{1,2,0:T(8,128)}, u32[]{:S(2)}) copy-start(s32[1,32,8]{1,2,0:T(8,128)} %param.16) | copy-start | bytes 3076
  66.6 5.4 %collective-permute-start.9 = (bf16[33,16,128]{2,1,0:T(8,128)(2,1)S(1)}, bf16[33,16,128]{2,1,0:T(8,128)(2,1)S(1)}, u32[]{:S(2)}, u32[]{:S(2)}) collective-permute-start(bf16[33,16,128]{2,1,0:T(8,128)(2,1)S(1)} %get-tuple-element.29.refs_0_), channel_id=1, source_target_pairs={{0,7},{1,0},{2,1},{3,2},{4,3},{5,4},{6,5},{7,6},{8,15},{9,8},{10,9... | collective-permute-start | bytes 405512 | tf_op jit(solution)/shard_map/ppermute | solution.py:163
  66.7 6.8 %collective-permute-start.8 = (bf16[33,16,128]{2,1,0:T(8,128)(2,1)S(1)}, bf16[33,16,128]{2,1,0:T(8,128)(2,1)S(1)}, u32[]{:S(2)}, u32[]{:S(2)}) collective-permute-start(bf16[33,16,128]{2,1,0:T(8,128)(2,1)S(1)} %get-tuple-element.29.refs_0_), channel_id=1, source_target_pairs={{0,1},{1,2},{2,3},{3,4},{4,5},{5,6},{6,7},{7,0},{8,9},{9,10},{10,1... | collective-permute-start | bytes 405512 | tf_op jit(solution)/shard_map/ppermute | solution.py:162
  72.1 5.0 %collective-permute-start.11 = (bf16[33,16,128]{2,1,0:T(8,128)(2,1)S(1)}, bf16[33,16,128]{2,1,0:T(8,128)(2,1)S(1)}, u32[]{:S(2)}, u32[]{:S(2)}) collective-permute-start(bf16[33,16,128]{2,1,0:T(8,128)(2,1)S(1)} %collective-permute-done.9.refs_2_), channel_id=1, source_target_pairs={{0,7},{1,0},{2,1},{3,2},{4,3},{5,4},{6,5},{7,6},{8,15},{9,8},{10,9... | collective-permute-start | bytes 405512 | tf_op jit(solution)/shard_map/ppermute | solution.py:163
  73.5 6.0 %collective-permute-start.10 = (bf16[33,16,128]{2,1,0:T(8,128)(2,1)S(1)}, bf16[33,16,128]{2,1,0:T(8,128)(2,1)S(1)}, u32[]{:S(2)}, u32[]{:S(2)}) collective-permute-start(bf16[33,16,128]{2,1,0:T(8,128)(2,1)S(1)} %collective-permute-done.8.refs_1_), channel_id=1, source_target_pairs={{0,1},{1,2},{2,3},{3,4},{4,5},{5,6},{6,7},{7,0},{8,9},{9,10},{10,1... | collective-permute-start | bytes 405512 | tf_op jit(solution)/shard_map/ppermute | solution.py:162
  77.1 4.4 %collective-permute-start.13 = (bf16[33,16,128]{2,1,0:T(8,128)(2,1)S(1)}, bf16[33,16,128]{2,1,0:T(8,128)(2,1)S(1)}, u32[]{:S(2)}, u32[]{:S(2)}) collective-permute-start(bf16[33,16,128]{2,1,0:T(8,128)(2,1)S(1)} %collective-permute-done.11.refs_4_), channel_id=1, source_target_pairs={{0,7},{1,0},{2,1},{3,2},{4,3},{5,4},{6,5},{7,6},{8,15},{9,8},{10,9... | collective-permute-start | bytes 405512 | tf_op jit(solution)/shard_map/ppermute | solution.py:163
  79.5 5.1 %collective-permute-start.12 = (bf16[33,16,128]{2,1,0:T(8,128)(2,1)S(1)}, bf16[33,16,128]{2,1,0:T(8,128)(2,1)S(1)}, u32[]{:S(2)}, u32[]{:S(2)}) collective-permute-start(bf16[33,16,128]{2,1,0:T(8,128)(2,1)S(1)} %collective-permute-done.10.refs_3_), channel_id=1, source_target_pairs={{0,1},{1,2},{2,3},{3,4},{4,5},{5,6},{6,7},{7,0},{8,9},{9,10},{10,1... | collective-permute-start | bytes 405512 | tf_op jit(solution)/shard_map/ppermute | solution.py:162
  81.5 7.5 %collective-permute-start.15 = (bf16[17,16,128]{2,1,0:T(8,128)(2,1)S(1)}, bf16[17,16,128]{2,1,0:T(8,128)(2,1)S(1)}, u32[]{:S(2)}, u32[]{:S(2)}) collective-permute-start(bf16[17,16,128]{2,1,0:T(8,128)(2,1)S(1)} %slice.24), channel_id=1, source_target_pairs={{0,7},{1,0},{2,1},{3,2},{4,3},{5,4},{6,5},{7,6},{8,15},{9,8},{10,9... | collective-permute-start | bytes 208904 | tf_op jit(solution)/shard_map/ppermute | solution.py:166
  84.6 4.4 %collective-permute-start.14 = (bf16[16,16,128]{2,1,0:T(8,128)(2,1)S(1)}, bf16[16,16,128]{2,1,0:T(8,128)(2,1)S(1)}, u32[]{:S(2)}, u32[]{:S(2)}) collective-permute-start(bf16[16,16,128]{2,1,0:T(8,128)(2,1)S(1)} %slice.23), channel_id=1, source_target_pairs={{0,1},{1,2},{2,3},{3,4},{4,5},{5,6},{6,7},{7,0},{8,9},{9,10},{10,1... | collective-permute-start | bytes 196616 | tf_op jit(solution)/shard_map/ppermute | solution.py:165
  84.9 13.8 %copy-start.5 = (s32[288]{0:T(512)S(1)}, s32[288]{0:T(512)}, u32[]{:S(2)}) copy-start(s32[288]{0:T(512)} %copy-done.4) | copy-start | bytes 3460
  91.3 25.9 %all-to-all-start.1 = ((bf16[288,16,128]{2,1,0:T(8,128)(2,1)}), bf16[288,16,128]{2,1,0:T(8,128)(2,1)S(1)}, u32[]{:S(2)}, u32[]{:S(2)}) async-start(bf16[288,16,128]{2,1,0:T(8,128)(2,1)} %get-tuple-element.30), calls=%async_computation.1 | async-start | bytes 2359296 | tf_op jit(solution)/shard_map/all_to_all | solution.py:702

commit v8 on v7

--- a/solution.py
+++ b/solution.py
@@ -153,18 +153,17 @@
     )(field, degree)
 
 
-def gather_row(tiles, n_row, half):
-    up = [(i, (i + 1) % n_row) for i in range(n_row)]
-    down = [(i, (i - 1) % n_row) for i in range(n_row)]
+def gather_row(tiles, n_row):
+    def shifted(value, shift):
+        return lax.ppermute(value, "row", [(i, (i + shift) % n_row) for i in range(n_row)])
+
     pieces = [(0, tiles)]
     from_below = from_above = tiles
     for step in range(1, n_row // 2):
-        from_below = lax.ppermute(from_below, "row", up)
-        from_above = lax.ppermute(from_above, "row", down)
+        from_below = shifted(from_below, 1)
+        from_above = shifted(from_above, -1)
         pieces += [(-step, from_below), (step, from_above)]
-    far_low = lax.ppermute(from_below[:half], "row", up)
-    far_high = lax.ppermute(from_above[half:], "row", down)
-    return pieces, far_low, far_high
+    return pieces + [(n_row // 2, shifted(tiles, n_row // 2))]
 
 
 def halves(offsets, pieces, half, n_row, place):
@@ -172,8 +171,7 @@
     for offset, piece in zip(offsets, pieces):
         owner = lax.rem(place + offset + n_row, n_row)
         parts += [(owner, 0, piece, 0), (owner, 1, piece, half)]
-    owner = lax.rem(place + n_row // 2, n_row)
-    return parts + [(owner, 0, pieces[-2], 0), (owner, 1, pieces[-1], 0)]
+    return parts
 
 
 def fill_and_send(fill, chosen_ref, chosen_hbm, sems):
@@ -181,12 +179,8 @@
     quarter = max(1, peers // 4)
     copies = []
     for at in range(peers // quarter):
-
-        def step(peer, carry):
+        for peer in range(at * quarter, (at + 1) * quarter):
             fill(peer)
-            return carry
-
-        lax.fori_loop(at * quarter, (at + 1) * quarter, step, 0)
         span = pl.ds(at * quarter * EXTRA, quarter * EXTRA)
         copies.append(pltpu.make_async_copy(chosen_ref.at[span], chosen_hbm.at[span], sems.at[at]))
         copies[-1].start()
@@ -220,13 +214,12 @@
 
 
 def first_select(gathered, place, send_list, n_row):
-    pieces, far_low, far_high = gathered
     part = n_row * RB
     peers = send_list.shape[0] // SEND
     return call(
-        functools.partial(first_select_kernel, [offset for offset, _ in pieces], n_row),
+        functools.partial(first_select_kernel, [offset for offset, _ in gathered], n_row),
         (pltpu.HBM((part, K, BS), BF16), pltpu.HBM((part, BS), F32), pltpu.HBM((peers * EXTRA, K, BS), BF16)),
-        [SMEM, SMEM] + [VMEM] * (len(pieces) + 2),
+        [SMEM, SMEM] + [VMEM] * len(gathered),
         (HBM, HBM, HBM),
         (
             pltpu.VMEM((part, K, BS), BF16),
@@ -236,7 +229,7 @@
             pltpu.SemaphoreType.DMA((6,)),
         ),
         moved=3000000,
-    )(place, send_list, *[piece for _, piece in pieces], far_low, far_high)
+    )(place, send_list, *[piece for _, piece in gathered])
 
 
 def second_select_kernel(offsets, n_row, place_ref, send_ref, pick_ref, *refs):
@@ -270,12 +263,11 @@
 
 
 def second_select(gathered, place, send_list, pick, n_row):
-    pieces, far_low, far_high = gathered
     peers = send_list.shape[0] // SEND
     return call(
-        functools.partial(second_select_kernel, [offset for offset, _ in pieces], n_row),
+        functools.partial(second_select_kernel, [offset for offset, _ in gathered], n_row),
         (pltpu.HBM((n_row * RB, K, BS), BF16), pltpu.HBM((peers * EXTRA, K, BS), BF16), pltpu.HBM((K, BS), BF16)),
-        [SMEM, SMEM] + [VMEM] * (len(pieces) + 3),
+        [SMEM, SMEM] + [VMEM] * (len(gathered) + 1),
         (HBM, HBM, HBM),
         (
             pltpu.VMEM((n_row * RB, K, BS), BF16),
@@ -284,7 +276,7 @@
             pltpu.SemaphoreType.DMA((6,)),
         ),
         moved=3000000,
-    )(place, send_list, pick, *[piece for _, piece in pieces], far_low, far_high)
+    )(place, send_list, pick, *[piece for _, piece in gathered])
 
 
 def picks(send_list):
@@ -712,13 +704,13 @@
     degree = degree.reshape(RB, BS)
     own_list, halo_list, counts = make_lists(slot_row, slot_column, live_slots, part)
 
-    gathered = gather_row(cast_tiles(in_hbm(basis), in_hbm(degree)), n_row, HALF + 2)
+    gathered = gather_row(cast_tiles(in_hbm(basis), in_hbm(degree)), n_row)
     basis_part, inverse, chosen = first_select(gathered, place, send_list, n_row)
     halo_tiles = to_all(chosen, "dom")
     own, own_weights, halo_weights = first_own(own_list, halo_list, counts, basis_part, coupling)
     image, tiles, basis_halo = make_image(halo_list, counts, halo_tiles, halo_weights, own, basis, degree)
 
-    gathered = gather_row(tiles, n_row, HALF)
+    gathered = gather_row(tiles, n_row)
     part_tiles, chosen, table = second_select(gathered, place, send_list, picks(send_list), n_row)
     halo_tiles = to_all(chosen, "dom")
     own, scaled = second_own(own_list, counts, part_tiles, table, basis_part, inverse, own_weights, n_row)

time: 153 us -> 152 us (level)
  Pallas kernels: 39 us -> 32.1 us
  waiting for transfers between devices: 40.5 us -> 47 us
  starting transfers between devices: 44.7 us -> 41.4 us
  blocking collectives: 24.6 us -> 27.6 us
    pallas_call x10, Pallas kernels: 39 us -> 32.1 us  [run(): pl.pallas_call(kernel, out_shape=out_shape, in_specs=in_specs, out_specs=...]
    all_to_all x2, waiting for transfers between devices: 17.2 us -> 21.8 us  [to_all(): return lax.all_to_all(value, axis, split_axis=0, concat_axis=0, tiled=True)]
    all_to_all x2, blocking collectives: 24.6 us -> 27.6 us  [to_all(): return lax.all_to_all(value, axis, split_axis=0, concat_axis=0, tiled=True)]
    ppermute x16 -> x14, starting transfers between devices: 24.9 us -> 23 us  [shifted(): lax.ppermute(value, 'row', [(i, (i + shift) % n_row) for i in range(n_row)])]
    ppermute x16 -> x14, waiting for transfers between devices: 23.3 us -> 25.1 us  [shifted(): lax.ppermute(value, 'row', [(i, (i + shift) % n_row) for i in range(n_row)])]
  transfers between devices with their start and end apart: 18 -> 16, of which waited for: 11 -> 10; matrix products, arithmetic and copies ran while one was open for 1% -> 1% of each run, Pallas kernels for 12% -> 9%
where the time goes in v8:
time: 152 us; the launch traced here: 151 us
  waiting for transfers between devices  47 us (31%)
  starting transfers between devices  41.4 us (27%)
  Pallas kernels  32.1 us (21%)
  blocking collectives  27.6 us (18%)
  local copies, waits for them, and re-layouts  1.61 us (1%)
  between operations  1.52 us (1%)
    pallas_call x10, Pallas kernels, run(): pl.pallas_call(kernel, out_shape=out_shape, in_specs=in_specs, out_specs=...  32.1 us
    all_to_all x2, blocking collectives, to_all(): return lax.all_to_all(value, axis, split_axis=0, concat_axis=0, tiled=True)  27.6 us
    ppermute x14, waiting for transfers between devices, shifted(): lax.ppermute(value, 'row', [(i, (i + shift) % n_row) for i in range(n_row)])  25.1 us
    ppermute x14, starting transfers between devices, shifted(): lax.ppermute(value, 'row', [(i, (i + shift) % n_row) for i in range(n_row)])  23 us
    all_to_all x2, waiting for transfers between devices, to_all(): return lax.all_to_all(value, axis, split_axis=0, concat_axis=0, tiled=True)  21.8 us
    all_to_all x2, starting transfers between devices, to_all(): return lax.all_to_all(value, axis, split_axis=0, concat_axis=0, tiled=True)  18.4 us
  transfers between devices with their start and end apart: 16, of which 10 were waited for; matrix products, arithmetic and copies ran while one was open for 1% of the time, Pallas kernels for 9%

profile of v8, /device:TPU:1, one launch (start us, length us, event | category | flops | bytes accessed | tf_op | source)
XLA Modules:
  0.0 151.5 jit_solution(1421555076777803329)
XLA Ops:
  0.6 1.0 shard_map.105.refs_0_
  1.7 6.5 %collective-permute-start.1 = (bf16[36,16,128]{2,1,0:T(8,128)(2,1)S(1)}, bf16[36,16,128]{2,1,0:T(8,128)(2,1)S(1)}, u32[]{:S(2)}, u32[]{:S(2)}) collective-permute-start(bf16[36,16,128]{2,1,0:T(8,128)(2,1)S(1)} %shard_map.105.refs_0_), channel_id=1, source_target_pairs={{0,7},{1,0},{2,1},{3,2},{4,3},{5,4},{6,5},{7,6},{8,15},{9,8},{10,9... | collective-permute-start | bytes 442376 | tf_op jit(solution)/shard_map/ppermute | solution.py:158
  8.1 2.5 %collective-permute-done.1.refs_2_ = bf16[36,16,128]{2,1,0:T(8,128)(2,1)S(1)} collective-permute-done((bf16[36,16,128]{2,1,0:T(8,128)(2,1)S(1)}, bf16[36,16,128]{2,1,0:T(8,128)(2,1)S(1)}, u32[]{:S(2)}, u32[]{:S(2)}) %collective-permute-start.1) | collective-permute-done | bytes 147488 | tf_op jit(solution)/shard_map/ppermute | solution.py:158
  10.7 3.4 %collective-permute-start.3 = (bf16[36,16,128]{2,1,0:T(8,128)(2,1)S(1)}, bf16[36,16,128]{2,1,0:T(8,128)(2,1)S(1)}, u32[]{:S(2)}, u32[]{:S(2)}) collective-permute-start(bf16[36,16,128]{2,1,0:T(8,128)(2,1)S(1)} %collective-permute-done.1.refs_2_), channel_id=1, source_target_pairs={{0,7},{1,0},{2,1},{3,2},{4,3},{5,4},{6,5},{7,6},{8,15},{9,8},{10,9... | collective-permute-start | bytes 442376 | tf_op jit(solution)/shard_map/ppermute | solution.py:158
  14.1 1.6 %collective-permute-start.6 = (bf16[36,16,128]{2,1,0:T(8,128)(2,1)S(1)}, bf16[36,16,128]{2,1,0:T(8,128)(2,1)S(1)}, u32[]{:S(2)}, u32[]{:S(2)}) collective-permute-start(bf16[36,16,128]{2,1,0:T(8,128)(2,1)S(1)} %shard_map.105.refs_0_), channel_id=1, source_target_pairs={{0,4},{1,5},{2,6},{3,7},{4,0},{5,1},{6,2},{7,3},{8,12},{9,13},{10,... | collective-permute-start | bytes 442376 | tf_op jit(solution)/shard_map/ppermute | solution.py:158
  16.2 3.1 %collective-permute-start.5 = (bf16[36,16,128]{2,1,0:T(8,128)(2,1)S(1)}, bf16[36,16,128]{2,1,0:T(8,128)(2,1)S(1)}, u32[]{:S(2)}, u32[]{:S(2)}) collective-permute-start(bf16[36,16,128]{2,1,0:T(8,128)(2,1)S(1)} %collective-permute-done.3.refs_4_), channel_id=1, source_target_pairs={{0,7},{1,0},{2,1},{3,2},{4,3},{5,4},{6,5},{7,6},{8,15},{9,8},{10,9... | collective-permute-start | bytes 442376 | tf_op jit(solution)/shard_map/ppermute | solution.py:158
  19.3 6.0 %collective-permute-done.2.refs_3_ = bf16[36,16,128]{2,1,0:T(8,128)(2,1)S(1)} collective-permute-done((bf16[36,16,128]{2,1,0:T(8,128)(2,1)S(1)}, bf16[36,16,128]{2,1,0:T(8,128)(2,1)S(1)}, u32[]{:S(2)}, u32[]{:S(2)}) %collective-permute-start.2) | collective-permute-done | bytes 147488 | tf_op jit(solution)/shard_map/ppermute | solution.py:158
  25.2 0.8 copy.12
  26.1 4.3 %collective-permute-done.4.refs_5_ = bf16[36,16,128]{2,1,0:T(8,128)(2,1)S(1)} collective-permute-done((bf16[36,16,128]{2,1,0:T(8,128)(2,1)S(1)}, bf16[36,16,128]{2,1,0:T(8,128)(2,1)S(1)}, u32[]{:S(2)}, u32[]{:S(2)}) %collective-permute-start.4) | collective-permute-done | bytes 147488 | tf_op jit(solution)/shard_map/ppermute | solution.py:158
  30.4 2.1 %shard_map.106 = (bf16[256,16,128]{2,1,0:T(8,128)(2,1)}, f32[256,128]{1,0:T(8,128)}, bf16[288,16,128]{2,1,0:T(8,128)(2,1)}) custom-call(s32[1]{0:T(128)} %bitcast.place_ref, s32[256]{0:T(256)S(1)} %reshape.19.send_ref, bf16[36,16,128]{2,1,0:T(8,128)(2,1)S(1)} %shard_map.105.refs_0_, bf16[36,16,128]{2,1,0:T(8,128)(2,1)S(1)} %collective-permute-done.refs_1_, ...), custom_call_target="tpu_custom_call" | custom-call | bytes 3000000 | tf_op jit(solution)/shard_map/pallas_call | solution.py:36
  32.5 10.1 %all-to-all-start = ((bf16[288,16,128]{2,1,0:T(8,128)(2,1)}), bf16[288,16,128]{2,1,0:T(8,128)(2,1)S(1)}, u32[]{:S(2)}, u32[]{:S(2)}) async-start(bf16[288,16,128]{2,1,0:T(8,128)(2,1)} %get-tuple-element.24), calls=%async_computation | async-start | bytes 2359296 | tf_op jit(solution)/shard_map/all_to_all | solution.py:694
  43.4 2.2 %shard_map.104 = (s32[288]{0:T(512)S(1)}, s32[288]{0:T(512)S(1)}, s32[3]{0:T(128)S(1)}) custom-call(s32[256]{0:T(256)S(1)} %copy-done.8, s32[256]{0:T(256)S(1)} %copy-done.9, s32[1]{0:T(128)S(6)} %copy.14.live_ref), custom_call_target="tpu_custom_call" | custom-call | bytes 20000 | tf_op jit(solution)/shard_map/pallas_call | solution.py:36
  45.7 0.5 copy-done.2
  46.3 7.0 %shard_map.107 = (f32[33,16,128]{2,1,0:T(8,128)}, bf16[256,128,128]{2,1,0:T(8,128)(2,1)}, bf16[256,128,128]{2,1,0:T(8,128)(2,1)}) custom-call(s32[288]{0:T(512)} %copy-done.4, s32[288]{0:T(512)} %copy-done.2, s32[3]{0:T(128)} %copy-done.6, bf16[256,16,128]{2,1,0:T(8,128)(2,1)} %get-tuple-element.26.part_ref.basis_part_ref, bf16[256,128,128]{2,1,0:T(8,128)(2,1)} %coupling_ref.1), custom_call_target="tpu_custom_call" | custom-call | flops 134217728 | bytes 10000000 | tf_op jit(solution)/shard_map/pallas_call | solution.py:36
  53.2 7.8 %all-to-all-done.halo_ref = bf16[288,16,128]{2,1,0:T(8,128)(2,1)S(1)} async-done(((bf16[288,16,128]{2,1,0:T(8,128)(2,1)}), bf16[288,16,128]{2,1,0:T(8,128)(2,1)S(1)}, u32[]{:S(2)}, u32[]{:S(2)}) %all-to-all-start) | async-done | bytes 1179680 | tf_op jit(solution)/shard_map/all_to_all | solution.py:694
  61.1 3.8 %shard_map.108 = (f32[16,4096]{1,0:T(8,128)}, bf16[33,16,128]{2,1,0:T(8,128)(2,1)S(1)}, bf16[288,16,128]{2,1,0:T(8,128)(2,1)}) custom-call(s32[288]{0:T(512)S(1)} %copy-done.3, s32[3]{0:T(128)S(1)} %copy-done.7, bf16[288,16,128]{2,1,0:T(8,128)(2,1)S(1)} %all-to-all-done.halo_ref, bf16[256,128,128]{2,1,0:T(8,128)(2,1)} %get-tuple-element.27.weights_hbm, ...), custom_call_target="tpu_custom_call" | custom-call | flops 134217728 | bytes 8000000 | tf_op jit(solution)/shard_map/pallas_call | solution.py:36
  65.0 1.5 collective-permute-start.7
  66.4 3.4 %collective-permute-done.8.refs_2_ = bf16[33,16,128]{2,1,0:T(8,128)(2,1)S(1)} collective-permute-done((bf16[33,16,128]{2,1,0:T(8,128)(2,1)S(1)}, bf16[33,16,128]{2,1,0:T(8,128)(2,1)S(1)}, u32[]{:S(2)}, u32[]{:S(2)}) %collective-permute-start.8) | collective-permute-done | bytes 135200 | tf_op jit(solution)/shard_map/ppermute | solution.py:158
  69.8 1.5 %collective-permute-start.10 = (bf16[33,16,128]{2,1,0:T(8,128)(2,1)S(1)}, bf16[33,16,128]{2,1,0:T(8,128)(2,1)S(1)}, u32[]{:S(2)}, u32[]{:S(2)}) collective-permute-start(bf16[33,16,128]{2,1,0:T(8,128)(2,1)S(1)} %collective-permute-done.8.refs_2_), channel_id=1, source_target_pairs={{0,7},{1,0},{2,1},{3,2},{4,3},{5,4},{6,5},{7,6},{8,15},{9,8},{10,9... | collective-permute-start | bytes 405512 | tf_op jit(solution)/shard_map/ppermute | solution.py:158
  71.6 2.3 %collective-permute-start.13 = (bf16[33,16,128]{2,1,0:T(8,128)(2,1)S(1)}, bf16[33,16,128]{2,1,0:T(8,128)(2,1)S(1)}, u32[]{:S(2)}, u32[]{:S(2)}) collective-permute-start(bf16[33,16,128]{2,1,0:T(8,128)(2,1)S(1)} %get-tuple-element.29.refs_0_), channel_id=1, source_target_pairs={{0,4},{1,5},{2,6},{3,7},{4,0},{5,1},{6,2},{7,3},{8,12},{9,13},{10,... | collective-permute-start | bytes 405512 | tf_op jit(solution)/shard_map/ppermute | solution.py:158
  73.9 3.0 %collective-permute-start.12 = (bf16[33,16,128]{2,1,0:T(8,128)(2,1)S(1)}, bf16[33,16,128]{2,1,0:T(8,128)(2,1)S(1)}, u32[]{:S(2)}, u32[]{:S(2)}) collective-permute-start(bf16[33,16,128]{2,1,0:T(8,128)(2,1)S(1)} %collective-permute-done.10.refs_4_), channel_id=1, source_target_pairs={{0,7},{1,0},{2,1},{3,2},{4,3},{5,4},{6,5},{7,6},{8,15},{9,8},{10,9... | collective-permute-start | bytes 405512 | tf_op jit(solution)/shard_map/ppermute | solution.py:158
  76.9 2.7 %collective-permute-done.9.refs_3_ = bf16[33,16,128]{2,1,0:T(8,128)(2,1)S(1)} collective-permute-done((bf16[33,16,128]{2,1,0:T(8,128)(2,1)S(1)}, bf16[33,16,128]{2,1,0:T(8,128)(2,1)S(1)}, u32[]{:S(2)}, u32[]{:S(2)}) %collective-permute-start.9) | collective-permute-done | bytes 135200 | tf_op jit(solution)/shard_map/ppermute | solution.py:158
  79.8 3.7 %collective-permute-done.13.refs_7_ = bf16[33,16,128]{2,1,0:T(8,128)(2,1)S(1)} collective-permute-done((bf16[33,16,128]{2,1,0:T(8,128)(2,1)S(1)}, bf16[33,16,128]{2,1,0:T(8,128)(2,1)S(1)}, u32[]{:S(2)}, u32[]{:S(2)}) %collective-permute-start.13) | collective-permute-done | bytes 135200 | tf_op jit(solution)/shard_map/ppermute | solution.py:158
  83.5 2.0 %collective-permute-done.11.refs_5_ = bf16[33,16,128]{2,1,0:T(8,128)(2,1)S(1)} collective-permute-done((bf16[33,16,128]{2,1,0:T(8,128)(2,1)S(1)}, bf16[33,16,128]{2,1,0:T(8,128)(2,1)S(1)}, u32[]{:S(2)}, u32[]{:S(2)}) %collective-permute-start.11) | collective-permute-done | bytes 135200 | tf_op jit(solution)/shard_map/ppermute | solution.py:158
  85.5 2.3 %shard_map.109 = (bf16[256,16,128]{2,1,0:T(8,128)(2,1)}, bf16[288,16,128]{2,1,0:T(8,128)(2,1)}, bf16[16,128]{1,0:T(8,128)(2,1)}) custom-call(s32[1]{0:T(128)} %bitcast.place_ref, s32[256]{0:T(256)S(1)} %reshape.19.send_ref, bf16[128,4096]{1,0:T(8,128)(2,1)S(1)} %fusion.pick_ref, bf16[33,16,128]{2,1,0:T(8,128)(2,1)S(1)} %get-tuple-element.29.refs_0_, ...), custom_call_target="tpu_custom_call" | custom-call | bytes 3000000 | tf_op jit(solution)/shard_map/pallas_call | solution.py:36
  87.8 8.2 %all-to-all-start.1 = ((bf16[288,16,128]{2,1,0:T(8,128)(2,1)}), bf16[288,16,128]{2,1,0:T(8,128)(2,1)S(1)}, u32[]{:S(2)}, u32[]{:S(2)}) async-start(bf16[288,16,128]{2,1,0:T(8,128)(2,1)} %get-tuple-element.30), calls=%async_computation.1 | async-start | bytes 2359296 | tf_op jit(solution)/shard_map/all_to_all | solution.py:694
  96.1 4.3 %shard_map.110 = (f32[33,16,128]{2,1,0:T(8,128)}, f32[33,16,128]{2,1,0:T(8,128)}) custom-call(s32[288]{0:T(512)S(1)} %copy-done.5, s32[3]{0:T(128)S(1)} %copy-done.7, bf16[256,16,128]{2,1,0:T(8,128)(2,1)} %get-tuple-element.32.part_ref, bf16[16,128]{1,0:T(8,128)(2,1)} %get-tuple-element.33.table_ref, ...), custom_call_target="tpu_custom_call" | custom-call | flops 268435456 | bytes 10000000 | tf_op jit(solution)/shard_map/pallas_call | solution.py:36
  100.4 14.0 %all-to-all-done.1.halo_ref = bf16[288,16,128]{2,1,0:T(8,128)(2,1)S(1)} async-done(((bf16[288,16,128]{2,1,0:T(8,128)(2,1)}), bf16[288,16,128]{2,1,0:T(8,128)(2,1)S(1)}, u32[]{:S(2)}, u32[]{:S(2)}) %all-to-all-start.1) | async-done | bytes 1179680 | tf_op jit(solution)/shard_map/all_to_all | solution.py:694
  114.4 4.7 %shard_map.111 = (f32[48,4096]{1,0:T(8,128)S(1)}, f32[48,4096]{1,0:T(8,128)S(1)}, f32[32,24,128]{2,1,0:T(8,128)S(1)}) custom-call(s32[288]{0:T(512)S(1)} %copy-done.3, s32[3]{0:T(128)S(1)} %copy-done.7, bf16[288,16,128]{2,1,0:T(8,128)(2,1)S(1)} %all-to-all-done.1.halo_ref, bf16[256,128,128]{2,1,0:T(8,128)(2,1)} %get-tuple-element.27.weights_hbm, ...), custom_call_target="tpu_custom_call" | custom-call | flops 134217728 | bytes 10000000 | tf_op jit(solution)/shard_map/pallas_call | solution.py:36
  119.2 15.0 %all_to_all.20.taken_ref = f32[32,24,128]{2,1,0:T(8,128)S(1)} all-to-all(f32[32,24,128]{2,1,0:T(8,128)S(1)} %get-tuple-element.39), channel_id=1, replica_groups=mesh['dom'=32,'row'=8] {'dom'}, dimensions={0} | all-to-all | bytes 786432 | tf_op jit(solution)/shard_map/all_to_all | solution.py:694
  134.3 12.5 %all_to_all.21.taken_ref = f32[8,24,128]{2,1,0:T(8,128)S(1)} all-to-all(f32[8,24,128]{2,1,0:T(8,128)S(1)} %shard_map.112), channel_id=1, replica_groups=mesh['dom'=32,'row'=8] {'row'}, dimensions={0} | all-to-all | bytes 196608 | tf_op jit(solution)/shard_map/all_to_all | solution.py:694
  146.8 4.7 %shard_map.113 = (f32[16,4096]{1,0:T(8,128)}, f32[16,4096]{1,0:T(8,128)}) custom-call(f32[8,24,128]{2,1,0:T(8,128)S(1)} %all_to_all.21.taken_ref, f32[48,4096]{1,0:T(8,128)S(1)} %get-tuple-element.40.stacked_ref, f32[48,4096]{1,0:T(8,128)S(1)} %get-tuple-element.41.stacked_image_ref), custom_call_target="tpu_custom_call" | custom-call | flops 1000000 | bytes 3000000 | tf_op jit(solution)/shard_map/pallas_call | solution.py:36
  (43 shorter events, 1.3 us)
Async XLA Ops:
  0.6 42.8 %copy-start.9 = (s32[256]{0:T(256)S(1)}, s32[256]{0:T(256)}, u32[]{:S(2)}) copy-start(s32[256]{0:T(256)} %column_ref.1) | copy-start | bytes 3076
  0.6 42.8 %copy-start.8 = (s32[256]{0:T(256)S(1)}, s32[256]{0:T(256)}, u32[]{:S(2)}) copy-start(s32[256]{0:T(256)} %row_ref.1) | copy-start | bytes 3076
  1.7 9.0 %collective-permute-start.1 = (bf16[36,16,128]{2,1,0:T(8,128)(2,1)S(1)}, bf16[36,16,128]{2,1,0:T(8,128)(2,1)S(1)}, u32[]{:S(2)}, u32[]{:S(2)}) collective-permute-start(bf16[36,16,128]{2,1,0:T(8,128)(2,1)S(1)} %shard_map.105.refs_0_), channel_id=1, source_target_pairs={{0,7},{1,0},{2,1},{3,2},{4,3},{5,4},{6,5},{7,6},{8,15},{9,8},{10,9... | collective-permute-start | bytes 442376 | tf_op jit(solution)/shard_map/ppermute | solution.py:158
  8.1 5.9 %collective-permute-start = (bf16[36,16,128]{2,1,0:T(8,128)(2,1)S(1)}, bf16[36,16,128]{2,1,0:T(8,128)(2,1)S(1)}, u32[]{:S(2)}, u32[]{:S(2)}) collective-permute-start(bf16[36,16,128]{2,1,0:T(8,128)(2,1)S(1)} %shard_map.105.refs_0_), channel_id=1, source_target_pairs={{0,1},{1,2},{2,3},{3,4},{4,5},{5,6},{6,7},{7,0},{8,9},{9,10},{10,1... | collective-permute-start | bytes 442376 | tf_op jit(solution)/shard_map/ppermute | solution.py:158
  10.7 5.5 %collective-permute-start.3 = (bf16[36,16,128]{2,1,0:T(8,128)(2,1)S(1)}, bf16[36,16,128]{2,1,0:T(8,128)(2,1)S(1)}, u32[]{:S(2)}, u32[]{:S(2)}) collective-permute-start(bf16[36,16,128]{2,1,0:T(8,128)(2,1)S(1)} %collective-permute-done.1.refs_2_), channel_id=1, source_target_pairs={{0,7},{1,0},{2,1},{3,2},{4,3},{5,4},{6,5},{7,6},{8,15},{9,8},{10,9... | collective-permute-start | bytes 442376 | tf_op jit(solution)/shard_map/ppermute | solution.py:158
  14.1 11.2 %collective-permute-start.2 = (bf16[36,16,128]{2,1,0:T(8,128)(2,1)S(1)}, bf16[36,16,128]{2,1,0:T(8,128)(2,1)S(1)}, u32[]{:S(2)}, u32[]{:S(2)}) collective-permute-start(bf16[36,16,128]{2,1,0:T(8,128)(2,1)S(1)} %collective-permute-done.refs_1_), channel_id=1, source_target_pairs={{0,1},{1,2},{2,3},{3,4},{4,5},{5,6},{6,7},{7,0},{8,9},{9,10},{10,1... | collective-permute-start | bytes 442376 | tf_op jit(solution)/shard_map/ppermute | solution.py:158
  14.1 12.0 %collective-permute-start.6 = (bf16[36,16,128]{2,1,0:T(8,128)(2,1)S(1)}, bf16[36,16,128]{2,1,0:T(8,128)(2,1)S(1)}, u32[]{:S(2)}, u32[]{:S(2)}) collective-permute-start(bf16[36,16,128]{2,1,0:T(8,128)(2,1)S(1)} %shard_map.105.refs_0_), channel_id=1, source_target_pairs={{0,4},{1,5},{2,6},{3,7},{4,0},{5,1},{6,2},{7,3},{8,12},{9,13},{10,... | collective-permute-start | bytes 442376 | tf_op jit(solution)/shard_map/ppermute | solution.py:158
  16.2 9.9 %collective-permute-start.5 = (bf16[36,16,128]{2,1,0:T(8,128)(2,1)S(1)}, bf16[36,16,128]{2,1,0:T(8,128)(2,1)S(1)}, u32[]{:S(2)}, u32[]{:S(2)}) collective-permute-start(bf16[36,16,128]{2,1,0:T(8,128)(2,1)S(1)} %collective-permute-done.3.refs_4_), channel_id=1, source_target_pairs={{0,7},{1,0},{2,1},{3,2},{4,3},{5,4},{6,5},{7,6},{8,15},{9,8},{10,9... | collective-permute-start | bytes 442376 | tf_op jit(solution)/shard_map/ppermute | solution.py:158
  25.2 5.2 %collective-permute-start.4 = (bf16[36,16,128]{2,1,0:T(8,128)(2,1)S(1)}, bf16[36,16,128]{2,1,0:T(8,128)(2,1)S(1)}, u32[]{:S(2)}, u32[]{:S(2)}) collective-permute-start(bf16[36,16,128]{2,1,0:T(8,128)(2,1)S(1)} %collective-permute-done.2.refs_3_), channel_id=1, source_target_pairs={{0,1},{1,2},{2,3},{3,4},{4,5},{5,6},{6,7},{7,0},{8,9},{9,10},{10,1... | collective-permute-start | bytes 442376 | tf_op jit(solution)/shard_map/ppermute | solution.py:158
  32.5 28.5 %all-to-all-start = ((bf16[288,16,128]{2,1,0:T(8,128)(2,1)}), bf16[288,16,128]{2,1,0:T(8,128)(2,1)S(1)}, u32[]{:S(2)}, u32[]{:S(2)}) async-start(bf16[288,16,128]{2,1,0:T(8,128)(2,1)} %get-tuple-element.24), calls=%async_computation | async-start | bytes 2359296 | tf_op jit(solution)/shard_map/all_to_all | solution.py:694
  45.6 0.6 copy-start.2
  45.7 0.6 copy-start.4
  45.7 0.6 copy-start.6
  46.2 14.8 %copy-start = (f32[16,4096]{1,0:T(8,128)S(1)}, f32[16,4096]{1,0:T(8,128)}, u32[]{:S(2)}) copy-start(f32[16,4096]{1,0:T(8,128)} %basis_hbm.1) | copy-start | bytes 786436
  46.2 14.8 %copy-start.1 = (f32[4096]{0:T(1024)S(1)}, f32[4096]{0:T(1024)}, u32[]{:S(2)}) copy-start(f32[4096]{0:T(1024)} %param.12) | copy-start | bytes 49156
  46.2 14.8 %copy-start.3 = (s32[288]{0:T(512)S(1)}, s32[288]{0:T(512)}, u32[]{:S(2)}) copy-start(s32[288]{0:T(512)} %copy-done.2) | copy-start | bytes 3460
  46.3 14.8 %copy-start.7 = (s32[3]{0:T(128)S(1)}, s32[3]{0:T(128)}, u32[]{:S(2)}) copy-start(s32[3]{0:T(128)} %copy-done.6) | copy-start | bytes 40
  61.1 10.3 %copy-start.10 = (s32[1,32,8]{1,2,0:T(8,128)S(1)}, s32[1,32,8]{1,2,0:T(8,128)}, u32[]{:S(2)}) copy-start(s32[1,32,8]{1,2,0:T(8,128)} %param.16) | copy-start | bytes 3076
  64.9 4.9 %collective-permute-start.8 = (bf16[33,16,128]{2,1,0:T(8,128)(2,1)S(1)}, bf16[33,16,128]{2,1,0:T(8,128)(2,1)S(1)}, u32[]{:S(2)}, u32[]{:S(2)}) collective-permute-start(bf16[33,16,128]{2,1,0:T(8,128)(2,1)S(1)} %get-tuple-element.29.refs_0_), channel_id=1, source_target_pairs={{0,7},{1,0},{2,1},{3,2},{4,3},{5,4},{6,5},{7,6},{8,15},{9,8},{10,9... | collective-permute-start | bytes 405512 | tf_op jit(solution)/shard_map/ppermute | solution.py:158
  65.0 6.4 %collective-permute-start.7 = (bf16[33,16,128]{2,1,0:T(8,128)(2,1)S(1)}, bf16[33,16,128]{2,1,0:T(8,128)(2,1)S(1)}, u32[]{:S(2)}, u32[]{:S(2)}) collective-permute-start(bf16[33,16,128]{2,1,0:T(8,128)(2,1)S(1)} %get-tuple-element.29.refs_0_), channel_id=1, source_target_pairs={{0,1},{1,2},{2,3},{3,4},{4,5},{5,6},{6,7},{7,0},{8,9},{9,10},{10,1... | collective-permute-start | bytes 405512 | tf_op jit(solution)/shard_map/ppermute | solution.py:158
  69.8 4.0 %collective-permute-start.10 = (bf16[33,16,128]{2,1,0:T(8,128)(2,1)S(1)}, bf16[33,16,128]{2,1,0:T(8,128)(2,1)S(1)}, u32[]{:S(2)}, u32[]{:S(2)}) collective-permute-start(bf16[33,16,128]{2,1,0:T(8,128)(2,1)S(1)} %collective-permute-done.8.refs_2_), channel_id=1, source_target_pairs={{0,7},{1,0},{2,1},{3,2},{4,3},{5,4},{6,5},{7,6},{8,15},{9,8},{10,9... | collective-permute-start | bytes 405512 | tf_op jit(solution)/shard_map/ppermute | solution.py:158
  71.4 8.2 %collective-permute-start.9 = (bf16[33,16,128]{2,1,0:T(8,128)(2,1)S(1)}, bf16[33,16,128]{2,1,0:T(8,128)(2,1)S(1)}, u32[]{:S(2)}, u32[]{:S(2)}) collective-permute-start(bf16[33,16,128]{2,1,0:T(8,128)(2,1)S(1)} %collective-permute-done.7.refs_1_), channel_id=1, source_target_pairs={{0,1},{1,2},{2,3},{3,4},{4,5},{5,6},{6,7},{7,0},{8,9},{9,10},{10,1... | collective-permute-start | bytes 405512 | tf_op jit(solution)/shard_map/ppermute | solution.py:158
  71.6 12.0 %collective-permute-start.13 = (bf16[33,16,128]{2,1,0:T(8,128)(2,1)S(1)}, bf16[33,16,128]{2,1,0:T(8,128)(2,1)S(1)}, u32[]{:S(2)}, u32[]{:S(2)}) collective-permute-start(bf16[33,16,128]{2,1,0:T(8,128)(2,1)S(1)} %get-tuple-element.29.refs_0_), channel_id=1, source_target_pairs={{0,4},{1,5},{2,6},{3,7},{4,0},{5,1},{6,2},{7,3},{8,12},{9,13},{10,... | collective-permute-start | bytes 405512 | tf_op jit(solution)/shard_map/ppermute | solution.py:158
  73.9 9.6 %collective-permute-start.12 = (bf16[33,16,128]{2,1,0:T(8,128)(2,1)S(1)}, bf16[33,16,128]{2,1,0:T(8,128)(2,1)S(1)}, u32[]{:S(2)}, u32[]{:S(2)}) collective-permute-start(bf16[33,16,128]{2,1,0:T(8,128)(2,1)S(1)} %collective-permute-done.10.refs_4_), channel_id=1, source_target_pairs={{0,7},{1,0},{2,1},{3,2},{4,3},{5,4},{6,5},{7,6},{8,15},{9,8},{10,9... | collective-permute-start | bytes 405512 | tf_op jit(solution)/shard_map/ppermute | solution.py:158
  79.6 5.9 %collective-permute-start.11 = (bf16[33,16,128]{2,1,0:T(8,128)(2,1)S(1)}, bf16[33,16,128]{2,1,0:T(8,128)(2,1)S(1)}, u32[]{:S(2)}, u32[]{:S(2)}) collective-permute-start(bf16[33,16,128]{2,1,0:T(8,128)(2,1)S(1)} %collective-permute-done.9.refs_3_), channel_id=1, source_target_pairs={{0,1},{1,2},{2,3},{3,4},{4,5},{5,6},{6,7},{7,0},{8,9},{9,10},{10,1... | collective-permute-start | bytes 405512 | tf_op jit(solution)/shard_map/ppermute | solution.py:158
  79.8 16.3 %copy-start.5 = (s32[288]{0:T(512)S(1)}, s32[288]{0:T(512)}, u32[]{:S(2)}) copy-start(s32[288]{0:T(512)} %copy-done.4) | copy-start | bytes 3460
  87.8 26.6 %all-to-all-start.1 = ((bf16[288,16,128]{2,1,0:T(8,128)(2,1)}), bf16[288,16,128]{2,1,0:T(8,128)(2,1)S(1)}, u32[]{:S(2)}, u32[]{:S(2)}) async-start(bf16[288,16,128]{2,1,0:T(8,128)(2,1)} %get-tuple-element.30), calls=%async_computation.1 | async-start | bytes 2359296 | tf_op jit(solution)/shard_map/all_to_all | solution.py:694

commit v9 on v8

--- a/solution.py
+++ b/solution.py
@@ -130,27 +130,21 @@
     return high, middle, (rest - middle).astype(BF16).astype(F32)
 
 
-def cast_kernel(field_hbm, degree_hbm, tiles_ref, field_ref, degree_ref, sems):
-    wait_all(start_copies([(field_hbm, field_ref), (degree_hbm, degree_ref)], sems))
+def cast_kernel(field_hbm, tiles_ref, field_ref, sems):
+    wait_all(start_copies([(field_hbm, field_ref)], sems))
     for block in range(RB):
-        tiles_ref[block + 2 * (block // HALF)] = field_ref[:, columns(block)].astype(BF16)
-    for half in range(2):
-        inverse = 1.0 / degree_ref[half * HALF : (half + 1) * HALF]
-        high = inverse.astype(BF16)
-        at = half * (HALF + 2) + HALF
-        tiles_ref[at] = high
-        tiles_ref[at + 1] = (inverse - high.astype(F32)).astype(BF16)
-
-
-def cast_tiles(field, degree):
+        tiles_ref[block] = field_ref[:, columns(block)].astype(BF16)
+
+
+def cast_tiles(field):
     return call(
         cast_kernel,
-        shaped((RB + 4, K, BS), BF16),
-        [HBM, HBM],
+        shaped((RB, K, BS), BF16),
+        [HBM],
         VMEM,
-        (pltpu.VMEM(field.shape, F32), pltpu.VMEM(degree.shape, F32), pltpu.SemaphoreType.DMA((2,))),
+        (pltpu.VMEM(field.shape, F32), pltpu.SemaphoreType.DMA((1,))),
         moved=400000,
-    )(field, degree)
+    )(field)
 
 
 def gather_row(tiles, n_row):
@@ -166,114 +160,106 @@
     return pieces + [(n_row // 2, shifted(tiles, n_row // 2))]
 
 
-def halves(offsets, pieces, half, n_row, place):
-    parts = []
-    for offset, piece in zip(offsets, pieces):
-        owner = lax.rem(place + offset + n_row, n_row)
-        parts += [(owner, 0, piece, 0), (owner, 1, piece, half)]
-    return parts
-
-
-def fill_and_send(fill, chosen_ref, chosen_hbm, sems):
-    peers = chosen_ref.shape[0] // EXTRA
+def placed(offsets, pieces, n_row, place):
+    return [(lax.rem(place + offset + n_row, n_row), piece) for offset, piece in zip(offsets, pieces)]
+
+
+def fill_and_send(fill, tiles, chosen_ref, chosen_hbm, sems):
+    peers = chosen_ref.shape[0] // tiles
     quarter = max(1, peers // 4)
     copies = []
     for at in range(peers // quarter):
         for peer in range(at * quarter, (at + 1) * quarter):
             fill(peer)
-        span = pl.ds(at * quarter * EXTRA, quarter * EXTRA)
+        span = pl.ds(at * quarter * tiles, quarter * tiles)
         copies.append(pltpu.make_async_copy(chosen_ref.at[span], chosen_hbm.at[span], sems.at[at]))
         copies[-1].start()
-    for copy in copies:
-        copy.wait()
+    wait_all(copies)
 
 
 def first_select_kernel(offsets, n_row, place_ref, send_ref, *refs):
-    pieces, (part_hbm, inverse_hbm, chosen_hbm) = refs[:-8], refs[-8:-5]
-    part_ref, inverse_ref, rows_ref, chosen_ref, sems = refs[-5:]
-    for owner, half, piece, start in halves(offsets, pieces, HALF + 2, n_row, place_ref[0]):
-        at = owner * RB + half * HALF
-        part_ref[pl.ds(at, HALF)] = piece[start : start + HALF]
-        inverse_ref[pl.ds(pl.multiple_of(at, HALF), HALF), :] = (
-            piece[start + HALF].astype(F32) + piece[start + HALF + 1].astype(F32)
-        )
-
-    copies = start_copies([(part_ref, part_hbm), (inverse_ref, inverse_hbm)], sems, 4)
+    pieces, (part_hbm, chosen_hbm, part_ref, chosen_ref, sems) = refs[:-5], refs[-5:]
+    for owner, piece in placed(offsets, pieces, n_row, place_ref[0]):
+        part_ref[pl.ds(owner * RB, RB)] = piece[...]
+    copies = start_copies([(part_ref, part_hbm)], sems, 4)
 
     def fill(peer):
         for j in range(SEND):
-            block = send_ref[peer * SEND + j]
-            chosen_ref[peer * EXTRA + j] = part_ref[block]
-            rows_ref[j : j + 1, :] = inverse_ref[pl.ds(block, 1), :]
-        rows = rows_ref[...]
-        high = rows.astype(BF16).astype(F32)
-        chosen_ref[peer * EXTRA + SEND] = jnp.concatenate([high, rows - high], axis=0).astype(BF16)
-
-    fill_and_send(fill, chosen_ref, chosen_hbm, sems)
+            chosen_ref[peer * SEND + j] = part_ref[send_ref[peer * SEND + j]]
+
+    fill_and_send(fill, SEND, chosen_ref, chosen_hbm, sems)
     wait_all(copies)
 
 
 def first_select(gathered, place, send_list, n_row):
     part = n_row * RB
-    peers = send_list.shape[0] // SEND
+    count = send_list.shape[0]
     return call(
         functools.partial(first_select_kernel, [offset for offset, _ in gathered], n_row),
-        (pltpu.HBM((part, K, BS), BF16), pltpu.HBM((part, BS), F32), pltpu.HBM((peers * EXTRA, K, BS), BF16)),
+        (pltpu.HBM((part, K, BS), BF16), pltpu.HBM((count, K, BS), BF16)),
         [SMEM, SMEM] + [VMEM] * len(gathered),
-        (HBM, HBM, HBM),
-        (
-            pltpu.VMEM((part, K, BS), BF16),
-            pltpu.VMEM((part, BS), F32),
-            pltpu.VMEM((SEND, BS), F32),
-            pltpu.VMEM((peers * EXTRA, K, BS), BF16),
-            pltpu.SemaphoreType.DMA((6,)),
-        ),
+        (HBM, HBM),
+        (pltpu.VMEM((part, K, BS), BF16), pltpu.VMEM((count, K, BS), BF16), pltpu.SemaphoreType.DMA((5,))),
         moved=3000000,
     )(place, send_list, *[piece for _, piece in gathered])
 
 
 def second_select_kernel(offsets, n_row, place_ref, send_ref, pick_ref, *refs):
-    pieces, (part_hbm, chosen_hbm, table_hbm, part_ref, chosen_ref, table_ref, sems) = refs[:-7], refs[-7:]
+    pieces, (part_hbm, chosen_hbm, table_hbm, inverse_hbm) = refs[:-10], refs[-10:-6]
+    part_ref, chosen_ref, table_ref, inverse_ref, rows_ref, sems = refs[-6:]
     lane = iota2((K, BS), 1)
     table = jnp.zeros((K, BS), F32)
     side_sum = jnp.zeros((K, BS), F32)
-    for owner, half, piece, start in halves(offsets, pieces, HALF, n_row, place_ref[0]):
-        part_ref[pl.ds(owner * RB + half * HALF, HALF)] = piece[start : start + HALF]
-        if half == 1:
-            side = piece[start + HALF].astype(F32)
-            table = jnp.where(lane == owner, side[:, 0:1], table)
-            side_sum = side_sum + side
+    for owner, piece in placed(offsets, pieces, n_row, place_ref[0]):
+        part_ref[pl.ds(owner * RB, RB)] = piece[0:RB]
+        for half in range(2):
+            at = pl.multiple_of(owner * RB + half * HALF, HALF)
+            inverse_ref[pl.ds(at, HALF), :] = piece[RB + 1 + half].astype(F32)
+        side = piece[RB].astype(F32)
+        table = jnp.where(lane == owner, side[:, 0:1], table)
+        side_sum = side_sum + side
     top = jnp.sum(jnp.where((lane >= 1) & (lane <= 3), side_sum, 0.0), axis=1, keepdims=True)
     bottom = jnp.sum(jnp.where((lane >= 4) & (lane <= 6), side_sum, 0.0), axis=1, keepdims=True)
     for at, value in enumerate(split3(top) + split3(bottom)):
         table = jnp.where(lane == 8 + at, value, table)
     table = table.astype(BF16)
     table_ref[...] = table
-    copies = start_copies([(part_ref, part_hbm), (table_ref, table_hbm)], sems, 4)
+    copies = start_copies([(part_ref, part_hbm), (table_ref, table_hbm), (inverse_ref, inverse_hbm)], sems, 4)
     sides = dot_nn(table, pick_ref[...])
-    for peer in range(chosen_ref.shape[0] // EXTRA):
-        chosen_ref[peer * EXTRA + SEND] = sides[:, columns(peer)].astype(BF16)
 
     def fill(peer):
         for j in range(SEND):
-            chosen_ref[peer * EXTRA + j] = part_ref[send_ref[peer * SEND + j]]
-
-    fill_and_send(fill, chosen_ref, chosen_hbm, sems)
+            block = send_ref[peer * SEND + j]
+            chosen_ref[peer * EXTRA + j] = part_ref[block]
+            rows_ref[j : j + 1, :] = inverse_ref[pl.ds(block, 1), :]
+        side = sides[:, columns(peer)]
+        folded = side[0:8] + pltpu.roll(side[8:16], 14, 1)
+        chosen_ref[peer * EXTRA + SEND] = jnp.concatenate([rows_ref[...], folded], axis=0).astype(BF16)
+
+    fill_and_send(fill, EXTRA, chosen_ref, chosen_hbm, sems)
     wait_all(copies)
 
 
 def second_select(gathered, place, send_list, pick, n_row):
+    part = n_row * RB
     peers = send_list.shape[0] // SEND
     return call(
         functools.partial(second_select_kernel, [offset for offset, _ in gathered], n_row),
-        (pltpu.HBM((n_row * RB, K, BS), BF16), pltpu.HBM((peers * EXTRA, K, BS), BF16), pltpu.HBM((K, BS), BF16)),
+        (
+            pltpu.HBM((part, K, BS), BF16),
+            pltpu.HBM((peers * EXTRA, K, BS), BF16),
+            pltpu.HBM((K, BS), BF16),
+            pltpu.HBM((part, BS), F32),
+        ),
         [SMEM, SMEM] + [VMEM] * (len(gathered) + 1),
-        (HBM, HBM, HBM),
+        (HBM, HBM, HBM, HBM),
         (
-            pltpu.VMEM((n_row * RB, K, BS), BF16),
+            pltpu.VMEM((part, K, BS), BF16),
             pltpu.VMEM((peers * EXTRA, K, BS), BF16),
             pltpu.VMEM((K, BS), BF16),
-            pltpu.SemaphoreType.DMA((6,)),
+            pltpu.VMEM((part, BS), F32),
+            pltpu.VMEM((SEND, BS), F32),
+            pltpu.SemaphoreType.DMA((7,)),
         ),
         moved=3000000,
     )(place, send_list, pick, *[piece for _, piece in gathered])
@@ -403,7 +389,7 @@
     wait_all(own)
 
     def load(block):
-        return halo_ref[block + (block >> 3)]
+        return halo_ref[block]
 
     def add(row, block, product):
         acc_ref[row] = acc_ref[row] + product
@@ -432,13 +418,15 @@
     for at, value in enumerate(split3(top) + split3(bottom)):
         side = jnp.where(lane == 1 + at, value, side)
     tiles_ref[RB] = side.astype(BF16)
+    for half in range(2):
+        tiles_ref[RB + 1 + half] = (1.0 / degree_ref[half * HALF : (half + 1) * HALF]).astype(BF16)
     wait_all(copies)
 
 
 def make_image(halo_list, counts, halo_tiles, weights, own, basis, degree):
     return call(
         image_kernel,
-        (pltpu.HBM(basis.shape, F32), shaped((RB + 1, K, BS), BF16), pltpu.HBM(halo_tiles.shape, BF16)),
+        (pltpu.HBM(basis.shape, F32), shaped((RB + 3, K, BS), BF16), pltpu.HBM(halo_tiles.shape, BF16)),
         [SMEM, SMEM, VMEM, HBM, HBM, VMEM, VMEM],
         (HBM, VMEM, HBM),
         (
@@ -508,12 +496,12 @@
     return wide_ref[...]
 
 
-def pack_grams(gram_b, gram_a, wide_ref):
-    wide_a = square(gram_a, wide_ref)
-    both = 0.5 * (wide_a + wide_a.T)
-    wide_b = square(gram_b, wide_ref)
+def pack_grams(wide):
     row = iota2((BS, BS), 0)
     lane = iota2((BS, BS), 1)
+    wide_b = jnp.where(lane < 48, wide, 0.0)
+    wide_a = jnp.where(lane < 48, pltpu.roll(wide, BS - 48, 1), 0.0)
+    both = 0.5 * (wide_a + wide_a.T)
     packed = jnp.where(row <= lane, wide_b, both)
     diagonal = jnp.sum(jnp.where(row == lane, both, 0.0), axis=1, keepdims=True)
     low, high = packed[0:24], pltpu.roll(packed[24:48], 48, 1)
@@ -541,43 +529,42 @@
 
 def gram_kernel(
     list_ref, count_ref, halo_ref, weights_hbm, basis_halo_hbm, own_hbm, own_scaled_hbm, basis_hbm, image_hbm, degree_hbm,
-    previous_hbm, previous_image_hbm, stacked, stacked_image, packed_ref, basis_halo_ref, acc_ref, scaled_ref, degree_ref,
+    previous_hbm, previous_image_hbm, stack, packed_ref, basis_halo_ref, acc_ref, scaled_ref, degree_ref,
     in_sems, held, sems, side_ref, quotient_ref, inverse_ref, wide_ref,
 ):
     early = [(basis_halo_hbm, basis_halo_ref), (own_hbm, acc_ref), (own_scaled_hbm, scaled_ref)]
     late = [
-        (basis_hbm, stacked.at[0:16]),
-        (previous_hbm, stacked.at[32:48]),
-        (image_hbm, stacked_image.at[0:16]),
-        (previous_image_hbm, stacked_image.at[32:48]),
+        (basis_hbm, stack.at[0:16]),
+        (previous_hbm, stack.at[32:48]),
+        (image_hbm, stack.at[48:64]),
+        (previous_image_hbm, stack.at[80:96]),
         (degree_hbm, degree_ref),
     ]
     early = start_copies(early, in_sems)
     start_groups(count_ref[1], weights_hbm, held, sems)
     late = start_copies(late, in_sems, 3)
     peers = halo_ref.shape[0] // EXTRA
+    lane = iota2((K, BS), 1)
     total = jnp.zeros((K, BS), F32)
     for peer in range(peers):
-        side = halo_ref[peer * EXTRA + SEND]
-        side_ref[peer * K : (peer + 1) * K, :] = side
-        total = total + side.astype(F32)
+        tile = halo_ref[peer * EXTRA + SEND].astype(F32)
+        inverse_ref[peer * SEND : (peer + 1) * SEND, :] = tile[0:8]
+        unfolded = [tile[8:16], pltpu.roll(tile[8:16], BS - 14, 1)]
+        side = jnp.where(lane < 14, jnp.concatenate(unfolded, axis=0), 0.0)
+        side_ref[peer * K : (peer + 1) * K, :] = side.astype(BF16)
+        total = total + side
     side = side_ref[...]
     for j in range(SEND):
         spread = (iota2((BS, BS), 0) == j).astype(F32).astype(BF16)
         quotient_ref[j] = dot_nn(side, spread).reshape(peers, K, BS)
-    lane = iota2((K, BS), 1)
     top = jnp.sum(jnp.where((lane >= 8) & (lane <= 10), total, 0.0), axis=1, keepdims=True)
     bottom = jnp.sum(jnp.where((lane >= 11) & (lane <= 13), total, 0.0), axis=1, keepdims=True)
     theta = top / bottom
     wait_all(early)
-    for peer in range(peers):
-        inverse = basis_halo_ref[peer * EXTRA + SEND].astype(F32)
-        inverse_ref[peer * SEND : (peer + 1) * SEND, :] = inverse[0:SEND] + inverse[SEND:]
 
     def load(block):
-        tile = block + (block >> 3)
-        scaled = scale_block(basis_halo_ref[tile], inverse_ref[pl.ds(block, 1), :])
-        return jnp.concatenate([halo_ref[tile], scaled], axis=0)
+        scaled = scale_block(basis_halo_ref[block], inverse_ref[pl.ds(block, 1), :])
+        return jnp.concatenate([halo_ref[block + (block >> 3)], scaled], axis=0)
 
     def add(row, block, product):
         quotient = quotient_ref[block & 7, block >> 3]
@@ -589,12 +576,10 @@
     for block in range(RB):
         at = columns(block)
         degree = degree_ref[block : block + 1, :]
-        residual = (stacked_image[0:16, at] - theta * stacked[0:16, at]) / degree
-        stacked[16:32, at] = residual
-        stacked_image[16:32, at] = degree * residual - (acc_ref[block] - theta * scaled_ref[block])
-    gram_b = dot_nt(stacked[...], stacked[...], HIGHEST)
-    gram_a = dot_nt(stacked[...], stacked_image[...], HIGHEST)
-    packed = pack_grams(gram_b, gram_a, wide_ref)
+        residual = (stack[48:64, at] - theta * stack[0:16, at]) / degree
+        stack[16:32, at] = residual
+        stack[64:80, at] = degree * residual - (acc_ref[block] - theta * scaled_ref[block])
+    packed = pack_grams(square(dot_nt(stack[0:48], stack[...], HIGHEST), wide_ref))
     for peer in range(packed_ref.shape[0]):
         packed_ref[peer] = packed
 
@@ -602,12 +587,11 @@
 def make_grams(
     halo_list, counts, halo_tiles, weights, basis_halo, own, scaled, basis, image, degree, previous, previous_image, n_dom
 ):
-    stack = shaped((3 * K, basis.shape[1]), F32)
     return call(
         gram_kernel,
-        (stack, stack, shaped((n_dom, 24, BS), F32)),
+        (shaped((6 * K, basis.shape[1]), F32), shaped((n_dom, 24, BS), F32)),
         [SMEM, SMEM, VMEM] + [HBM] * 9,
-        (VMEM, VMEM, VMEM),
+        (VMEM, VMEM),
         (
             pltpu.VMEM(basis_halo.shape, BF16),
             pltpu.VMEM((RB + 1, K, BS), F32),
@@ -650,7 +634,7 @@
 
 
 def final_kernel(
-    root_rows, taken_ref, stacked_ref, stacked_image_ref, new_basis_ref, new_image_ref, wide_ref
+    root_rows, taken_ref, stack_ref, new_basis_ref, new_image_ref, wide_ref
 ):
     packed = taken_ref[0]
     for peer in range(1, taken_ref.shape[0]):
@@ -673,21 +657,21 @@
     wide_ref[0:16, 0:16] = inner
     sub_inverse = inverse_factor(wide_ref[0:16, :], 16)[:, 0:16]
     coeff = dot_nn(dot_nn(sub_inverse, turned, HIGHEST), inverse, HIGHEST) * root_rows
-    new_basis_ref[...] = dot_nn(coeff, stacked_ref[...], HIGHEST)
-    new_image_ref[...] = dot_nn(coeff, stacked_image_ref[...], HIGHEST)
-
-
-def finish(root_rows, packed, stacked, stacked_image):
-    shape = (K, stacked.shape[1])
+    new_basis_ref[...] = dot_nn(coeff, stack_ref[0:48], HIGHEST)
+    new_image_ref[...] = dot_nn(coeff, stack_ref[48:96], HIGHEST)
+
+
+def finish(root_rows, packed, stack):
+    shape = (K, stack.shape[1])
     return call(
         functools.partial(final_kernel, root_rows),
         (shaped(shape, F32), shaped(shape, F32)),
-        [VMEM] * 3,
+        [VMEM] * 2,
         (VMEM, VMEM),
         (pltpu.VMEM((BS, BS), F32),),
         flops=1000000,
         moved=3000000,
-    )(packed, stacked, stacked_image)
+    )(packed, stack)
 
 
 def to_all(value, axis):
@@ -704,23 +688,23 @@
     degree = degree.reshape(RB, BS)
     own_list, halo_list, counts = make_lists(slot_row, slot_column, live_slots, part)
 
-    gathered = gather_row(cast_tiles(in_hbm(basis), in_hbm(degree)), n_row)
-    basis_part, inverse, chosen = first_select(gathered, place, send_list, n_row)
+    gathered = gather_row(cast_tiles(in_hbm(basis)), n_row)
+    basis_part, chosen = first_select(gathered, place, send_list, n_row)
     halo_tiles = to_all(chosen, "dom")
     own, own_weights, halo_weights = first_own(own_list, halo_list, counts, basis_part, coupling)
     image, tiles, basis_halo = make_image(halo_list, counts, halo_tiles, halo_weights, own, basis, degree)
 
     gathered = gather_row(tiles, n_row)
-    part_tiles, chosen, table = second_select(gathered, place, send_list, picks(send_list), n_row)
+    part_tiles, chosen, table, inverse = second_select(gathered, place, send_list, picks(send_list), n_row)
     halo_tiles = to_all(chosen, "dom")
     own, scaled = second_own(own_list, counts, part_tiles, table, basis_part, inverse, own_weights, n_row)
-    stacked, stacked_image, packed = make_grams(
+    stack, packed = make_grams(
         halo_list, counts, halo_tiles, halo_weights, basis_halo, own, scaled, basis, image, degree, previous, previous_image,
         n_dom,
     )
     packed = to_all(add_and_repeat(to_all(packed, "dom"), n_row), "row")
     root_rows = math.sqrt(basis.shape[1] * n_dom * n_row)
-    return finish(root_rows, packed, stacked, stacked_image)
+    return finish(root_rows, packed, stack)
 
 
 def solution(mesh):

time: 152 us -> 150 us (0.987)
  waiting for transfers between devices: 47 us -> 37.8 us
  Pallas kernels: 32.1 us -> 39.1 us
  starting transfers between devices: 41.4 us -> 43.2 us
    pallas_call x10, Pallas kernels: 32.1 us -> 39.1 us  [run(): pl.pallas_call(kernel, out_shape=out_shape, in_specs=in_specs, out_specs=...]
    all_to_all x2, waiting for transfers between devices: 21.8 us -> 15.1 us  [to_all(): return lax.all_to_all(value, axis, split_axis=0, concat_axis=0, tiled=True)]
    ppermute x14, waiting for transfers between devices: 25.1 us -> 22.8 us  [shifted(): lax.ppermute(value, 'row', [(i, (i + shift) % n_row) for i in range(n_row)])]
  transfers between devices with their start and end apart: 16 -> 16, of which waited for: 10 -> 10; matrix products, arithmetic and copies ran while one was open for 1% -> 1% of each run, Pallas kernels for 9% -> 13%
where the time goes in v9:
time: 150 us
  starting transfers between devices  43.2 us (29%)
  Pallas kernels  39.1 us (26%)
  waiting for transfers between devices  37.8 us (25%)
  blocking collectives  26.5 us (18%)
  local copies, waits for them, and re-layouts  1.62 us (1%)
  between operations  1.51 us (1%)
    pallas_call x10, Pallas kernels, run(): pl.pallas_call(kernel, out_shape=out_shape, in_specs=in_specs, out_specs=...  39.1 us
    all_to_all x2, blocking collectives, to_all(): return lax.all_to_all(value, axis, split_axis=0, concat_axis=0, tiled=True)  26.5 us
    ppermute x14, starting transfers between devices, shifted(): lax.ppermute(value, 'row', [(i, (i + shift) % n_row) for i in range(n_row)])  23.8 us
    ppermute x14, waiting for transfers between devices, shifted(): lax.ppermute(value, 'row', [(i, (i + shift) % n_row) for i in range(n_row)])  22.8 us
    all_to_all x2, starting transfers between devices, to_all(): return lax.all_to_all(value, axis, split_axis=0, concat_axis=0, tiled=True)  19.4 us
    all_to_all x2, waiting for transfers between devices, to_all(): return lax.all_to_all(value, axis, split_axis=0, concat_axis=0, tiled=True)  15.1 us
  transfers between devices with their start and end apart: 16, of which 10 were waited for; matrix products, arithmetic and copies ran while one was open for 1% of the time, Pallas kernels for 13%

profile of v9, /device:TPU:1, one launch (start us, length us, event | category | flops | bytes accessed | tf_op | source)
XLA Modules:
  0.0 150.0 jit_solution(14990092705094258941)
XLA Ops:
  0.6 1.0 shard_map.105.refs_0_
  1.6 6.5 %collective-permute-start.1 = (bf16[32,16,128]{2,1,0:T(8,128)(2,1)S(1)}, bf16[32,16,128]{2,1,0:T(8,128)(2,1)S(1)}, u32[]{:S(2)}, u32[]{:S(2)}) collective-permute-start(bf16[32,16,128]{2,1,0:T(8,128)(2,1)S(1)} %shard_map.105.refs_0_), channel_id=1, source_target_pairs={{0,7},{1,0},{2,1},{3,2},{4,3},{5,4},{6,5},{7,6},{8,15},{9,8},{10,9... | collective-permute-start | bytes 393224 | tf_op jit(solution)/shard_map/ppermute | solution.py:152
  8.1 2.2 %collective-permute-done.1.refs_2_ = bf16[32,16,128]{2,1,0:T(8,128)(2,1)S(1)} collective-permute-done((bf16[32,16,128]{2,1,0:T(8,128)(2,1)S(1)}, bf16[32,16,128]{2,1,0:T(8,128)(2,1)S(1)}, u32[]{:S(2)}, u32[]{:S(2)}) %collective-permute-start.1) | collective-permute-done | bytes 131104 | tf_op jit(solution)/shard_map/ppermute | solution.py:152
  10.3 3.4 %collective-permute-start.3 = (bf16[32,16,128]{2,1,0:T(8,128)(2,1)S(1)}, bf16[32,16,128]{2,1,0:T(8,128)(2,1)S(1)}, u32[]{:S(2)}, u32[]{:S(2)}) collective-permute-start(bf16[32,16,128]{2,1,0:T(8,128)(2,1)S(1)} %collective-permute-done.1.refs_2_), channel_id=1, source_target_pairs={{0,7},{1,0},{2,1},{3,2},{4,3},{5,4},{6,5},{7,6},{8,15},{9,8},{10,9... | collective-permute-start | bytes 393224 | tf_op jit(solution)/shard_map/ppermute | solution.py:152
  13.7 1.6 %collective-permute-start.6 = (bf16[32,16,128]{2,1,0:T(8,128)(2,1)S(1)}, bf16[32,16,128]{2,1,0:T(8,128)(2,1)S(1)}, u32[]{:S(2)}, u32[]{:S(2)}) collective-permute-start(bf16[32,16,128]{2,1,0:T(8,128)(2,1)S(1)} %shard_map.105.refs_0_), channel_id=1, source_target_pairs={{0,4},{1,5},{2,6},{3,7},{4,0},{5,1},{6,2},{7,3},{8,12},{9,13},{10,... | collective-permute-start | bytes 393224 | tf_op jit(solution)/shard_map/ppermute | solution.py:152
  15.6 3.1 %collective-permute-start.5 = (bf16[32,16,128]{2,1,0:T(8,128)(2,1)S(1)}, bf16[32,16,128]{2,1,0:T(8,128)(2,1)S(1)}, u32[]{:S(2)}, u32[]{:S(2)}) collective-permute-start(bf16[32,16,128]{2,1,0:T(8,128)(2,1)S(1)} %collective-permute-done.3.refs_4_), channel_id=1, source_target_pairs={{0,7},{1,0},{2,1},{3,2},{4,3},{5,4},{6,5},{7,6},{8,15},{9,8},{10,9... | collective-permute-start | bytes 393224 | tf_op jit(solution)/shard_map/ppermute | solution.py:152
  18.7 4.5 %collective-permute-done.2.refs_3_ = bf16[32,16,128]{2,1,0:T(8,128)(2,1)S(1)} collective-permute-done((bf16[32,16,128]{2,1,0:T(8,128)(2,1)S(1)}, bf16[32,16,128]{2,1,0:T(8,128)(2,1)S(1)}, u32[]{:S(2)}, u32[]{:S(2)}) %collective-permute-start.2) | collective-permute-done | bytes 131104 | tf_op jit(solution)/shard_map/ppermute | solution.py:152
  23.2 0.8 copy.12
  24.1 4.3 %collective-permute-done.4.refs_5_ = bf16[32,16,128]{2,1,0:T(8,128)(2,1)S(1)} collective-permute-done((bf16[32,16,128]{2,1,0:T(8,128)(2,1)S(1)}, bf16[32,16,128]{2,1,0:T(8,128)(2,1)S(1)}, u32[]{:S(2)}, u32[]{:S(2)}) %collective-permute-start.4) | collective-permute-done | bytes 131104 | tf_op jit(solution)/shard_map/ppermute | solution.py:152
  28.4 2.0 %shard_map.106 = (bf16[256,16,128]{2,1,0:T(8,128)(2,1)}, bf16[256,16,128]{2,1,0:T(8,128)(2,1)}) custom-call(s32[1]{0:T(128)} %bitcast.place_ref, s32[256]{0:T(256)S(1)} %reshape.19.send_ref, bf16[32,16,128]{2,1,0:T(8,128)(2,1)S(1)} %shard_map.105.refs_0_, bf16[32,16,128]{2,1,0:T(8,128)(2,1)S(1)} %collective-permute-done.refs_1_, ...), custom_call_target="tpu_custom_call" | custom-call | bytes 3000000 | tf_op jit(solution)/shard_map/pallas_call | solution.py:36
  30.4 10.5 %all-to-all-start = ((bf16[256,16,128]{2,1,0:T(8,128)(2,1)}), bf16[256,16,128]{2,1,0:T(8,128)(2,1)S(1)}, u32[]{:S(2)}, u32[]{:S(2)}) async-start(bf16[256,16,128]{2,1,0:T(8,128)(2,1)} %get-tuple-element.23), calls=%async_computation | async-start | bytes 2097152 | tf_op jit(solution)/shard_map/all_to_all | solution.py:678
  41.6 3.1 %shard_map.104 = (s32[288]{0:T(512)S(1)}, s32[288]{0:T(512)S(1)}, s32[3]{0:T(128)S(1)}) custom-call(s32[256]{0:T(256)S(1)} %copy-done.8, s32[256]{0:T(256)S(1)} %copy-done.9, s32[1]{0:T(128)S(6)} %copy.14.live_ref), custom_call_target="tpu_custom_call" | custom-call | bytes 20000 | tf_op jit(solution)/shard_map/pallas_call | solution.py:36
  44.8 0.5 copy-done.2
  45.4 10.2 %shard_map.107 = (f32[33,16,128]{2,1,0:T(8,128)}, bf16[256,128,128]{2,1,0:T(8,128)(2,1)}, bf16[256,128,128]{2,1,0:T(8,128)(2,1)}) custom-call(s32[288]{0:T(512)} %copy-done.4, s32[288]{0:T(512)} %copy-done.2, s32[3]{0:T(128)} %copy-done.6, bf16[256,16,128]{2,1,0:T(8,128)(2,1)} %get-tuple-element.25.part_ref.basis_part_ref, bf16[256,128,128]{2,1,0:T(8,128)(2,1)} %coupling_ref.1), custom_call_target="tpu_custom_call" | custom-call | flops 134217728 | bytes 10000000 | tf_op jit(solution)/shard_map/pallas_call | solution.py:36
  55.6 2.2 %all-to-all-done.halo_ref = bf16[256,16,128]{2,1,0:T(8,128)(2,1)S(1)} async-done(((bf16[256,16,128]{2,1,0:T(8,128)(2,1)}), bf16[256,16,128]{2,1,0:T(8,128)(2,1)S(1)}, u32[]{:S(2)}, u32[]{:S(2)}) %all-to-all-start) | async-done | bytes 1048608 | tf_op jit(solution)/shard_map/all_to_all | solution.py:678
  57.8 4.4 %shard_map.108 = (f32[16,4096]{1,0:T(8,128)}, bf16[35,16,128]{2,1,0:T(8,128)(2,1)S(1)}, bf16[256,16,128]{2,1,0:T(8,128)(2,1)}) custom-call(s32[288]{0:T(512)S(1)} %copy-done.3, s32[3]{0:T(128)S(1)} %copy-done.7, bf16[256,16,128]{2,1,0:T(8,128)(2,1)S(1)} %all-to-all-done.halo_ref, bf16[256,128,128]{2,1,0:T(8,128)(2,1)} %get-tuple-element.26.weights_hbm, ...), custom_call_target="tpu_custom_call" | custom-call | flops 134217728 | bytes 8000000 | tf_op jit(solution)/shard_map/pallas_call | solution.py:36
  62.3 1.5 collective-permute-start.7
  63.8 3.7 %collective-permute-done.8.refs_2_ = bf16[35,16,128]{2,1,0:T(8,128)(2,1)S(1)} collective-permute-done((bf16[35,16,128]{2,1,0:T(8,128)(2,1)S(1)}, bf16[35,16,128]{2,1,0:T(8,128)(2,1)S(1)}, u32[]{:S(2)}, u32[]{:S(2)}) %collective-permute-start.8) | collective-permute-done | bytes 143392 | tf_op jit(solution)/shard_map/ppermute | solution.py:152
  67.5 1.5 collective-permute-start.10
  69.2 3.6 %collective-permute-start.13 = (bf16[35,16,128]{2,1,0:T(8,128)(2,1)S(1)}, bf16[35,16,128]{2,1,0:T(8,128)(2,1)S(1)}, u32[]{:S(2)}, u32[]{:S(2)}) collective-permute-start(bf16[35,16,128]{2,1,0:T(8,128)(2,1)S(1)} %get-tuple-element.28.refs_0_), channel_id=1, source_target_pairs={{0,4},{1,5},{2,6},{3,7},{4,0},{5,1},{6,2},{7,3},{8,12},{9,13},{10,... | collective-permute-start | bytes 430088 | tf_op jit(solution)/shard_map/ppermute | solution.py:152
  72.7 2.7 %collective-permute-start.12 = (bf16[35,16,128]{2,1,0:T(8,128)(2,1)S(1)}, bf16[35,16,128]{2,1,0:T(8,128)(2,1)S(1)}, u32[]{:S(2)}, u32[]{:S(2)}) collective-permute-start(bf16[35,16,128]{2,1,0:T(8,128)(2,1)S(1)} %collective-permute-done.10.refs_4_), channel_id=1, source_target_pairs={{0,7},{1,0},{2,1},{3,2},{4,3},{5,4},{6,5},{7,6},{8,15},{9,8},{10,9... | collective-permute-start | bytes 430088 | tf_op jit(solution)/shard_map/ppermute | solution.py:152
  75.6 4.6 %collective-permute-done.13.refs_7_ = bf16[35,16,128]{2,1,0:T(8,128)(2,1)S(1)} collective-permute-done((bf16[35,16,128]{2,1,0:T(8,128)(2,1)S(1)}, bf16[35,16,128]{2,1,0:T(8,128)(2,1)S(1)}, u32[]{:S(2)}, u32[]{:S(2)}) %collective-permute-start.13) | collective-permute-done | bytes 143392 | tf_op jit(solution)/shard_map/ppermute | solution.py:152
  80.2 1.4 collective-permute-done.12.refs_6_
  81.6 1.8 %collective-permute-done.11.refs_5_ = bf16[35,16,128]{2,1,0:T(8,128)(2,1)S(1)} collective-permute-done((bf16[35,16,128]{2,1,0:T(8,128)(2,1)S(1)}, bf16[35,16,128]{2,1,0:T(8,128)(2,1)S(1)}, u32[]{:S(2)}, u32[]{:S(2)}) %collective-permute-start.11) | collective-permute-done | bytes 143392 | tf_op jit(solution)/shard_map/ppermute | solution.py:152
  83.4 2.4 %shard_map.109 = (bf16[256,16,128]{2,1,0:T(8,128)(2,1)}, bf16[288,16,128]{2,1,0:T(8,128)(2,1)}, bf16[16,128]{1,0:T(8,128)(2,1)}, f32[256,128]{1,0:T(8,128)}) custom-call(s32[1]{0:T(128)} %bitcast.place_ref, s32[256]{0:T(256)S(1)} %reshape.19.send_ref, bf16[128,4096]{1,0:T(8,128)(2,1)S(1)} %fusion.pick_ref, ...), custom_call_target="tpu_custom_call" | custom-call | bytes 3000000 | tf_op jit(solution)/shard_map/pallas_call | solution.py:36
  85.7 8.8 %all-to-all-start.1 = ((bf16[288,16,128]{2,1,0:T(8,128)(2,1)}), bf16[288,16,128]{2,1,0:T(8,128)(2,1)S(1)}, u32[]{:S(2)}, u32[]{:S(2)}) async-start(bf16[288,16,128]{2,1,0:T(8,128)(2,1)} %get-tuple-element.29), calls=%async_computation.1 | async-start | bytes 2359296 | tf_op jit(solution)/shard_map/all_to_all | solution.py:678
  94.6 5.4 %shard_map.110 = (f32[33,16,128]{2,1,0:T(8,128)}, f32[33,16,128]{2,1,0:T(8,128)}) custom-call(s32[288]{0:T(512)S(1)} %copy-done.5, s32[3]{0:T(128)S(1)} %copy-done.7, bf16[256,16,128]{2,1,0:T(8,128)(2,1)} %get-tuple-element.31.part_ref, bf16[16,128]{1,0:T(8,128)(2,1)} %get-tuple-element.32.table_ref, ...), custom_call_target="tpu_custom_call" | custom-call | flops 268435456 | bytes 10000000 | tf_op jit(solution)/shard_map/pallas_call | solution.py:36
  100.0 12.9 %all-to-all-done.1.halo_ref = bf16[288,16,128]{2,1,0:T(8,128)(2,1)S(1)} async-done(((bf16[288,16,128]{2,1,0:T(8,128)(2,1)}), bf16[288,16,128]{2,1,0:T(8,128)(2,1)S(1)}, u32[]{:S(2)}, u32[]{:S(2)}) %all-to-all-start.1) | async-done | bytes 1179680 | tf_op jit(solution)/shard_map/all_to_all | solution.py:678
  112.9 5.8 %shard_map.111 = (f32[96,4096]{1,0:T(8,128)S(1)}, f32[32,24,128]{2,1,0:T(8,128)S(1)}) custom-call(s32[288]{0:T(512)S(1)} %copy-done.3, s32[3]{0:T(128)S(1)} %copy-done.7, bf16[288,16,128]{2,1,0:T(8,128)(2,1)S(1)} %all-to-all-done.1.halo_ref, bf16[256,128,128]{2,1,0:T(8,128)(2,1)} %get-tuple-element.26.weights_hbm, ...), custom_call_target="tpu_custom_call" | custom-call | flops 134217728 | bytes 10000000 | tf_op jit(solution)/shard_map/pallas_call | solution.py:36
  118.8 14.4 %all_to_all.20.taken_ref = f32[32,24,128]{2,1,0:T(8,128)S(1)} all-to-all(f32[32,24,128]{2,1,0:T(8,128)S(1)} %get-tuple-element.38), channel_id=1, replica_groups=mesh['dom'=32,'row'=8] {'dom'}, dimensions={0} | all-to-all | bytes 786432 | tf_op jit(solution)/shard_map/all_to_all | solution.py:678
  133.2 12.1 %all_to_all.21.taken_ref = f32[8,24,128]{2,1,0:T(8,128)S(1)} all-to-all(f32[8,24,128]{2,1,0:T(8,128)S(1)} %shard_map.112), channel_id=1, replica_groups=mesh['dom'=32,'row'=8] {'row'}, dimensions={0} | all-to-all | bytes 196608 | tf_op jit(solution)/shard_map/all_to_all | solution.py:678
  145.3 4.7 %shard_map.113 = (f32[16,4096]{1,0:T(8,128)}, f32[16,4096]{1,0:T(8,128)}) custom-call(f32[8,24,128]{2,1,0:T(8,128)S(1)} %all_to_all.21.taken_ref, f32[96,4096]{1,0:T(8,128)S(1)} %get-tuple-element.39.stack_ref), custom_call_target="tpu_custom_call" | custom-call | flops 1000000 | bytes 3000000 | tf_op jit(solution)/shard_map/pallas_call | solution.py:36
  (43 shorter events, 1.1 us)
Async XLA Ops:
  0.6 41.0 %copy-start.9 = (s32[256]{0:T(256)S(1)}, s32[256]{0:T(256)}, u32[]{:S(2)}) copy-start(s32[256]{0:T(256)} %column_ref.1) | copy-start | bytes 3076
  0.6 41.0 %copy-start.8 = (s32[256]{0:T(256)S(1)}, s32[256]{0:T(256)}, u32[]{:S(2)}) copy-start(s32[256]{0:T(256)} %row_ref.1) | copy-start | bytes 3076
  1.6 8.6 %collective-permute-start.1 = (bf16[32,16,128]{2,1,0:T(8,128)(2,1)S(1)}, bf16[32,16,128]{2,1,0:T(8,128)(2,1)S(1)}, u32[]{:S(2)}, u32[]{:S(2)}) collective-permute-start(bf16[32,16,128]{2,1,0:T(8,128)(2,1)S(1)} %shard_map.105.refs_0_), channel_id=1, source_target_pairs={{0,7},{1,0},{2,1},{3,2},{4,3},{5,4},{6,5},{7,6},{8,15},{9,8},{10,9... | collective-permute-start | bytes 393224 | tf_op jit(solution)/shard_map/ppermute | solution.py:152
  8.1 5.6 %collective-permute-start = (bf16[32,16,128]{2,1,0:T(8,128)(2,1)S(1)}, bf16[32,16,128]{2,1,0:T(8,128)(2,1)S(1)}, u32[]{:S(2)}, u32[]{:S(2)}) collective-permute-start(bf16[32,16,128]{2,1,0:T(8,128)(2,1)S(1)} %shard_map.105.refs_0_), channel_id=1, source_target_pairs={{0,1},{1,2},{2,3},{3,4},{4,5},{5,6},{6,7},{7,0},{8,9},{9,10},{10,1... | collective-permute-start | bytes 393224 | tf_op jit(solution)/shard_map/ppermute | solution.py:152
  10.3 5.4 %collective-permute-start.3 = (bf16[32,16,128]{2,1,0:T(8,128)(2,1)S(1)}, bf16[32,16,128]{2,1,0:T(8,128)(2,1)S(1)}, u32[]{:S(2)}, u32[]{:S(2)}) collective-permute-start(bf16[32,16,128]{2,1,0:T(8,128)(2,1)S(1)} %collective-permute-done.1.refs_2_), channel_id=1, source_target_pairs={{0,7},{1,0},{2,1},{3,2},{4,3},{5,4},{6,5},{7,6},{8,15},{9,8},{10,9... | collective-permute-start | bytes 393224 | tf_op jit(solution)/shard_map/ppermute | solution.py:152
  13.7 9.5 %collective-permute-start.2 = (bf16[32,16,128]{2,1,0:T(8,128)(2,1)S(1)}, bf16[32,16,128]{2,1,0:T(8,128)(2,1)S(1)}, u32[]{:S(2)}, u32[]{:S(2)}) collective-permute-start(bf16[32,16,128]{2,1,0:T(8,128)(2,1)S(1)} %collective-permute-done.refs_1_), channel_id=1, source_target_pairs={{0,1},{1,2},{2,3},{3,4},{4,5},{5,6},{6,7},{7,0},{8,9},{9,10},{10,1... | collective-permute-start | bytes 393224 | tf_op jit(solution)/shard_map/ppermute | solution.py:152
  13.7 10.4 %collective-permute-start.6 = (bf16[32,16,128]{2,1,0:T(8,128)(2,1)S(1)}, bf16[32,16,128]{2,1,0:T(8,128)(2,1)S(1)}, u32[]{:S(2)}, u32[]{:S(2)}) collective-permute-start(bf16[32,16,128]{2,1,0:T(8,128)(2,1)S(1)} %shard_map.105.refs_0_), channel_id=1, source_target_pairs={{0,4},{1,5},{2,6},{3,7},{4,0},{5,1},{6,2},{7,3},{8,12},{9,13},{10,... | collective-permute-start | bytes 393224 | tf_op jit(solution)/shard_map/ppermute | solution.py:152
  15.6 8.4 %collective-permute-start.5 = (bf16[32,16,128]{2,1,0:T(8,128)(2,1)S(1)}, bf16[32,16,128]{2,1,0:T(8,128)(2,1)S(1)}, u32[]{:S(2)}, u32[]{:S(2)}) collective-permute-start(bf16[32,16,128]{2,1,0:T(8,128)(2,1)S(1)} %collective-permute-done.3.refs_4_), channel_id=1, source_target_pairs={{0,7},{1,0},{2,1},{3,2},{4,3},{5,4},{6,5},{7,6},{8,15},{9,8},{10,9... | collective-permute-start | bytes 393224 | tf_op jit(solution)/shard_map/ppermute | solution.py:152
  23.2 5.2 %collective-permute-start.4 = (bf16[32,16,128]{2,1,0:T(8,128)(2,1)S(1)}, bf16[32,16,128]{2,1,0:T(8,128)(2,1)S(1)}, u32[]{:S(2)}, u32[]{:S(2)}) collective-permute-start(bf16[32,16,128]{2,1,0:T(8,128)(2,1)S(1)} %collective-permute-done.2.refs_3_), channel_id=1, source_target_pairs={{0,1},{1,2},{2,3},{3,4},{4,5},{5,6},{6,7},{7,0},{8,9},{9,10},{10,1... | collective-permute-start | bytes 393224 | tf_op jit(solution)/shard_map/ppermute | solution.py:152
  30.4 27.4 %all-to-all-start = ((bf16[256,16,128]{2,1,0:T(8,128)(2,1)}), bf16[256,16,128]{2,1,0:T(8,128)(2,1)S(1)}, u32[]{:S(2)}, u32[]{:S(2)}) async-start(bf16[256,16,128]{2,1,0:T(8,128)(2,1)} %get-tuple-element.23), calls=%async_computation | async-start | bytes 2097152 | tf_op jit(solution)/shard_map/all_to_all | solution.py:678
  44.8 0.6 copy-start.2
  44.8 0.6 copy-start.4
  44.8 0.6 copy-start.6
  45.4 12.4 %copy-start = (f32[16,4096]{1,0:T(8,128)S(1)}, f32[16,4096]{1,0:T(8,128)}, u32[]{:S(2)}) copy-start(f32[16,4096]{1,0:T(8,128)} %basis_hbm.1) | copy-start | bytes 786436
  45.4 12.4 %copy-start.1 = (f32[4096]{0:T(1024)S(1)}, f32[4096]{0:T(1024)}, u32[]{:S(2)}) copy-start(f32[4096]{0:T(1024)} %param.12) | copy-start | bytes 49156
  45.4 12.4 %copy-start.3 = (s32[288]{0:T(512)S(1)}, s32[288]{0:T(512)}, u32[]{:S(2)}) copy-start(s32[288]{0:T(512)} %copy-done.2) | copy-start | bytes 3460
  45.4 12.4 %copy-start.7 = (s32[3]{0:T(128)S(1)}, s32[3]{0:T(128)}, u32[]{:S(2)}) copy-start(s32[3]{0:T(128)} %copy-done.6) | copy-start | bytes 40
  57.8 11.2 %copy-start.10 = (s32[1,32,8]{1,2,0:T(8,128)S(1)}, s32[1,32,8]{1,2,0:T(8,128)}, u32[]{:S(2)}) copy-start(s32[1,32,8]{1,2,0:T(8,128)} %param.16) | copy-start | bytes 3076
  62.2 5.3 %collective-permute-start.8 = (bf16[35,16,128]{2,1,0:T(8,128)(2,1)S(1)}, bf16[35,16,128]{2,1,0:T(8,128)(2,1)S(1)}, u32[]{:S(2)}, u32[]{:S(2)}) collective-permute-start(bf16[35,16,128]{2,1,0:T(8,128)(2,1)S(1)} %get-tuple-element.28.refs_0_), channel_id=1, source_target_pairs={{0,7},{1,0},{2,1},{3,2},{4,3},{5,4},{6,5},{7,6},{8,15},{9,8},{10,9... | collective-permute-start | bytes 430088 | tf_op jit(solution)/shard_map/ppermute | solution.py:152
  62.3 6.7 %collective-permute-start.7 = (bf16[35,16,128]{2,1,0:T(8,128)(2,1)S(1)}, bf16[35,16,128]{2,1,0:T(8,128)(2,1)S(1)}, u32[]{:S(2)}, u32[]{:S(2)}) collective-permute-start(bf16[35,16,128]{2,1,0:T(8,128)(2,1)S(1)} %get-tuple-element.28.refs_0_), channel_id=1, source_target_pairs={{0,1},{1,2},{2,3},{3,4},{4,5},{5,6},{6,7},{7,0},{8,9},{9,10},{10,1... | collective-permute-start | bytes 430088 | tf_op jit(solution)/shard_map/ppermute | solution.py:152
  67.5 5.2 %collective-permute-start.10 = (bf16[35,16,128]{2,1,0:T(8,128)(2,1)S(1)}, bf16[35,16,128]{2,1,0:T(8,128)(2,1)S(1)}, u32[]{:S(2)}, u32[]{:S(2)}) collective-permute-start(bf16[35,16,128]{2,1,0:T(8,128)(2,1)S(1)} %collective-permute-done.8.refs_2_), channel_id=1, source_target_pairs={{0,7},{1,0},{2,1},{3,2},{4,3},{5,4},{6,5},{7,6},{8,15},{9,8},{10,9... | collective-permute-start | bytes 430088 | tf_op jit(solution)/shard_map/ppermute | solution.py:152
  69.0 6.4 %collective-permute-start.9 = (bf16[35,16,128]{2,1,0:T(8,128)(2,1)S(1)}, bf16[35,16,128]{2,1,0:T(8,128)(2,1)S(1)}, u32[]{:S(2)}, u32[]{:S(2)}) collective-permute-start(bf16[35,16,128]{2,1,0:T(8,128)(2,1)S(1)} %collective-permute-done.7.refs_1_), channel_id=1, source_target_pairs={{0,1},{1,2},{2,3},{3,4},{4,5},{5,6},{6,7},{7,0},{8,9},{9,10},{10,1... | collective-permute-start | bytes 430088 | tf_op jit(solution)/shard_map/ppermute | solution.py:152
  69.2 11.0 %collective-permute-start.13 = (bf16[35,16,128]{2,1,0:T(8,128)(2,1)S(1)}, bf16[35,16,128]{2,1,0:T(8,128)(2,1)S(1)}, u32[]{:S(2)}, u32[]{:S(2)}) collective-permute-start(bf16[35,16,128]{2,1,0:T(8,128)(2,1)S(1)} %get-tuple-element.28.refs_0_), channel_id=1, source_target_pairs={{0,4},{1,5},{2,6},{3,7},{4,0},{5,1},{6,2},{7,3},{8,12},{9,13},{10,... | collective-permute-start | bytes 430088 | tf_op jit(solution)/shard_map/ppermute | solution.py:152
  72.7 8.8 %collective-permute-start.12 = (bf16[35,16,128]{2,1,0:T(8,128)(2,1)S(1)}, bf16[35,16,128]{2,1,0:T(8,128)(2,1)S(1)}, u32[]{:S(2)}, u32[]{:S(2)}) collective-permute-start(bf16[35,16,128]{2,1,0:T(8,128)(2,1)S(1)} %collective-permute-done.10.refs_4_), channel_id=1, source_target_pairs={{0,7},{1,0},{2,1},{3,2},{4,3},{5,4},{6,5},{7,6},{8,15},{9,8},{10,9... | collective-permute-start | bytes 430088 | tf_op jit(solution)/shard_map/ppermute | solution.py:152
  75.4 8.0 %collective-permute-start.11 = (bf16[35,16,128]{2,1,0:T(8,128)(2,1)S(1)}, bf16[35,16,128]{2,1,0:T(8,128)(2,1)S(1)}, u32[]{:S(2)}, u32[]{:S(2)}) collective-permute-start(bf16[35,16,128]{2,1,0:T(8,128)(2,1)S(1)} %collective-permute-done.9.refs_3_), channel_id=1, source_target_pairs={{0,1},{1,2},{2,3},{3,4},{4,5},{5,6},{6,7},{7,0},{8,9},{9,10},{10,1... | collective-permute-start | bytes 430088 | tf_op jit(solution)/shard_map/ppermute | solution.py:152
  75.6 19.0 %copy-start.5 = (s32[288]{0:T(512)S(1)}, s32[288]{0:T(512)}, u32[]{:S(2)}) copy-start(s32[288]{0:T(512)} %copy-done.4) | copy-start | bytes 3460
  85.7 27.2 %all-to-all-start.1 = ((bf16[288,16,128]{2,1,0:T(8,128)(2,1)}), bf16[288,16,128]{2,1,0:T(8,128)(2,1)S(1)}, u32[]{:S(2)}, u32[]{:S(2)}) async-start(bf16[288,16,128]{2,1,0:T(8,128)(2,1)} %get-tuple-element.29), calls=%async_computation.1 | async-start | bytes 2359296 | tf_op jit(solution)/shard_map/all_to_all | solution.py:678

commit v10 on v9

--- a/solution.py
+++ b/solution.py
@@ -164,7 +164,7 @@
     return [(lax.rem(place + offset + n_row, n_row), piece) for offset, piece in zip(offsets, pieces)]
 
 
-def fill_and_send(fill, tiles, chosen_ref, chosen_hbm, sems):
+def fill_and_send(fill, tiles, chosen_ref, chosen_hbm, sems, others):
     peers = chosen_ref.shape[0] // tiles
     quarter = max(1, peers // 4)
     copies = []
@@ -174,6 +174,8 @@
         span = pl.ds(at * quarter * tiles, quarter * tiles)
         copies.append(pltpu.make_async_copy(chosen_ref.at[span], chosen_hbm.at[span], sems.at[at]))
         copies[-1].start()
+        if at == 0:
+            copies += start_copies(others, sems, 4)
     wait_all(copies)
 
 
@@ -181,14 +183,12 @@
     pieces, (part_hbm, chosen_hbm, part_ref, chosen_ref, sems) = refs[:-5], refs[-5:]
     for owner, piece in placed(offsets, pieces, n_row, place_ref[0]):
         part_ref[pl.ds(owner * RB, RB)] = piece[...]
-    copies = start_copies([(part_ref, part_hbm)], sems, 4)
 
     def fill(peer):
         for j in range(SEND):
             chosen_ref[peer * SEND + j] = part_ref[send_ref[peer * SEND + j]]
 
-    fill_and_send(fill, SEND, chosen_ref, chosen_hbm, sems)
-    wait_all(copies)
+    fill_and_send(fill, SEND, chosen_ref, chosen_hbm, sems, [(part_ref, part_hbm)])
 
 
 def first_select(gathered, place, send_list, n_row):
@@ -224,7 +224,6 @@
         table = jnp.where(lane == 8 + at, value, table)
     table = table.astype(BF16)
     table_ref[...] = table
-    copies = start_copies([(part_ref, part_hbm), (table_ref, table_hbm), (inverse_ref, inverse_hbm)], sems, 4)
     sides = dot_nn(table, pick_ref[...])
 
     def fill(peer):
@@ -236,8 +235,8 @@
         folded = side[0:8] + pltpu.roll(side[8:16], 14, 1)
         chosen_ref[peer * EXTRA + SEND] = jnp.concatenate([rows_ref[...], folded], axis=0).astype(BF16)
 
-    fill_and_send(fill, EXTRA, chosen_ref, chosen_hbm, sems)
-    wait_all(copies)
+    others = [(part_ref, part_hbm), (table_ref, table_hbm), (inverse_ref, inverse_hbm)]
+    fill_and_send(fill, EXTRA, chosen_ref, chosen_hbm, sems, others)
 
 
 def second_select(gathered, place, send_list, pick, n_row):
@@ -381,12 +380,12 @@
 
 def image_kernel(
     list_ref, count_ref, halo_ref, weights_hbm, own_hbm, basis_ref, degree_ref, image_hbm, tiles_ref, halo_hbm, image_ref,
-    out_sems, acc_ref, held, sems,
+    out_sems, own_ref, acc_ref, held, sems,
 ):
-    own = start_copies([(own_hbm, acc_ref)], out_sems, 2)
     start_groups(count_ref[1], weights_hbm, held, sems)
+    own = start_copies([(own_hbm, own_ref)], out_sems, 2)
     copies = start_copies([(halo_ref, halo_hbm)], out_sems)
-    wait_all(own)
+    acc_ref[...] = jnp.zeros_like(acc_ref)
 
     def load(block):
         return halo_ref[block]
@@ -395,12 +394,13 @@
         acc_ref[row] = acc_ref[row] + product
 
     work(count_ref[1], list_ref, weights_hbm, held, sems, load, add)
+    wait_all(own)
     top = jnp.zeros((K, BS), F32)
     bottom = jnp.zeros((K, BS), F32)
     for block in range(RB):
         at = columns(block)
         basis = basis_ref[:, at]
-        image = degree_ref[block : block + 1, :] * basis - acc_ref[block]
+        image = degree_ref[block : block + 1, :] * basis - (own_ref[block] + acc_ref[block])
         image_ref[:, at] = image
         top = top + basis * image
         bottom = bottom + basis * basis
@@ -433,6 +433,7 @@
             pltpu.VMEM(basis.shape, F32),
             pltpu.SemaphoreType.DMA((3,)),
             pltpu.VMEM((RB + 1, K, BS), F32),
+            pltpu.VMEM((RB + 1, K, BS), F32),
             HELD,
             GROUP_SEMS,
         ),
@@ -529,11 +530,14 @@
 
 def gram_kernel(
     list_ref, count_ref, halo_ref, weights_hbm, basis_halo_hbm, own_hbm, own_scaled_hbm, basis_hbm, image_hbm, degree_hbm,
-    previous_hbm, previous_image_hbm, stack, packed_ref, basis_halo_ref, acc_ref, scaled_ref, degree_ref,
+    previous_hbm, previous_image_hbm, stack, packed_ref, basis_halo_ref, own_ref, own_scaled_ref, acc_ref,
+    scaled_ref, degree_ref,
     in_sems, held, sems, side_ref, quotient_ref, inverse_ref, wide_ref,
 ):
-    early = [(basis_halo_hbm, basis_halo_ref), (own_hbm, acc_ref), (own_scaled_hbm, scaled_ref)]
+    early = [(basis_halo_hbm, basis_halo_ref)]
     late = [
+        (own_hbm, own_ref),
+        (own_scaled_hbm, own_scaled_ref),
         (basis_hbm, stack.at[0:16]),
         (previous_hbm, stack.at[32:48]),
         (image_hbm, stack.at[48:64]),
@@ -542,7 +546,9 @@
     ]
     early = start_copies(early, in_sems)
     start_groups(count_ref[1], weights_hbm, held, sems)
-    late = start_copies(late, in_sems, 3)
+    late = start_copies(late, in_sems, 1)
+    acc_ref[...] = jnp.zeros_like(acc_ref)
+    scaled_ref[...] = jnp.zeros_like(scaled_ref)
     peers = halo_ref.shape[0] // EXTRA
     lane = iota2((K, BS), 1)
     total = jnp.zeros((K, BS), F32)
@@ -578,7 +584,9 @@
         degree = degree_ref[block : block + 1, :]
         residual = (stack[48:64, at] - theta * stack[0:16, at]) / degree
         stack[16:32, at] = residual
-        stack[64:80, at] = degree * residual - (acc_ref[block] - theta * scaled_ref[block])
+        stack[64:80, at] = degree * residual - (
+            own_ref[block] + acc_ref[block] - theta * (own_scaled_ref[block] + scaled_ref[block])
+        )
     packed = pack_grams(square(dot_nt(stack[0:48], stack[...], HIGHEST), wide_ref))
     for peer in range(packed_ref.shape[0]):
         packed_ref[peer] = packed
@@ -594,6 +602,8 @@
         (VMEM, VMEM),
         (
             pltpu.VMEM(basis_halo.shape, BF16),
+            pltpu.VMEM((RB + 1, K, BS), F32),
+            pltpu.VMEM((RB + 1, K, BS), F32),
             pltpu.VMEM((RB + 1, K, BS), F32),
             pltpu.VMEM((RB + 1, K, BS), F32),
             pltpu.VMEM(degree.shape, F32),
@@ -634,7 +644,7 @@
 
 
 def final_kernel(
-    root_rows, taken_ref, stack_ref, new_basis_ref, new_image_ref, wide_ref
+    root_rows, taken_ref, stack_ref, new_basis_hbm, new_image_hbm, wide_ref, new_basis_ref, new_image_ref, sems
 ):
     packed = taken_ref[0]
     for peer in range(1, taken_ref.shape[0]):
@@ -649,26 +659,38 @@
     row = iota2((48, 48), 0)
     lane = iota2((48, 48), 1)
     filter_mat = (jnp.where(row == lane, spread, 0.0) - reduced) / (2.0 * spread)
-    turned = filter_mat[0:16, :]
-    for repeat in range(3):
-        turned = dot_nn(turned, filter_mat, HIGHEST)
+    squared = dot_nn(filter_mat, filter_mat, HIGHEST)
+    turned = dot_nn(squared[0:16, :], squared, HIGHEST)
+    back = dot_nn(turned, inverse, HIGHEST)
     inner = dot_nt(turned, turned, HIGHEST)
     wide_ref[...] = jnp.zeros_like(wide_ref)
     wide_ref[0:16, 0:16] = inner
     sub_inverse = inverse_factor(wide_ref[0:16, :], 16)[:, 0:16]
-    coeff = dot_nn(dot_nn(sub_inverse, turned, HIGHEST), inverse, HIGHEST) * root_rows
-    new_basis_ref[...] = dot_nn(coeff, stack_ref[0:48], HIGHEST)
-    new_image_ref[...] = dot_nn(coeff, stack_ref[48:96], HIGHEST)
+    coeff = dot_nn(sub_inverse, back, HIGHEST) * root_rows
+    copies = []
+    half = stack_ref.shape[1] // 2
+    for rows, out_ref, out_hbm in ((0, new_basis_ref, new_basis_hbm), (48, new_image_ref, new_image_hbm)):
+        for start in (0, half):
+            span = slice(start, start + half)
+            out_ref[:, span] = dot_nn(coeff, stack_ref[rows : rows + 48, span], HIGHEST)
+            span = pl.ds(start, half)
+            copies += start_copies([(out_ref.at[:, span], out_hbm.at[:, span])], sems, len(copies))
+    wait_all(copies)
 
 
 def finish(root_rows, packed, stack):
     shape = (K, stack.shape[1])
     return call(
         functools.partial(final_kernel, root_rows),
-        (shaped(shape, F32), shaped(shape, F32)),
+        (pltpu.HBM(shape, F32), pltpu.HBM(shape, F32)),
         [VMEM] * 2,
-        (VMEM, VMEM),
-        (pltpu.VMEM((BS, BS), F32),),
+        (HBM, HBM),
+        (
+            pltpu.VMEM((BS, BS), F32),
+            pltpu.VMEM(shape, F32),
+            pltpu.VMEM(shape, F32),
+            pltpu.SemaphoreType.DMA((4,)),
+        ),
         flops=1000000,
         moved=3000000,
     )(packed, stack)

time: 150 us -> 151 us (level)
  waiting for transfers between devices: 37.8 us -> 41.1 us
  starting transfers between devices: 43.2 us -> 40.9 us
    ppermute x14, waiting for transfers between devices: 22.8 us -> 26 us  [shifted(): lax.ppermute(value, 'row', [(i, (i + shift) % n_row) for i in range(n_row)])]
    ppermute x14, starting transfers between devices: 23.8 us -> 21 us  [shifted(): lax.ppermute(value, 'row', [(i, (i + shift) % n_row) for i in range(n_row)])]
  transfers between devices with their start and end apart: 16 -> 16, of which waited for: 10 -> 11; matrix products, arithmetic and copies ran while one was open for 1% -> 1% of each run, Pallas kernels for 13% -> 12%
where the time goes in v10:
time: 151 us
  waiting for transfers between devices  41.1 us (27%)
  starting transfers between devices  40.9 us (27%)
  Pallas kernels  38.7 us (26%)
  blocking collectives  26.4 us (17%)
  between operations  1.67 us (1%)
  local copies, waits for them, and re-layouts  1.62 us (1%)
    pallas_call x10, Pallas kernels, run(): pl.pallas_call(kernel, out_shape=out_shape, in_specs=in_specs, out_specs=...  38.7 us
    all_to_all x2, blocking collectives, to_all(): return lax.all_to_all(value, axis, split_axis=0, concat_axis=0, tiled=True)  26.4 us
    ppermute x14, waiting for transfers between devices, shifted(): lax.ppermute(value, 'row', [(i, (i + shift) % n_row) for i in range(n_row)])  26 us
    ppermute x14, starting transfers between devices, shifted(): lax.ppermute(value, 'row', [(i, (i + shift) % n_row) for i in range(n_row)])  21 us
    all_to_all x2, starting transfers between devices, to_all(): return lax.all_to_all(value, axis, split_axis=0, concat_axis=0, tiled=True)  19.9 us
    all_to_all x2, waiting for transfers between devices, to_all(): return lax.all_to_all(value, axis, split_axis=0, concat_axis=0, tiled=True)  15.1 us
  transfers between devices with their start and end apart: 16, of which 11 were waited for; matrix products, arithmetic and copies ran while one was open for 1% of the time, Pallas kernels for 12%

profile of v10, /device:TPU:1, one launch (start us, length us, event | category | flops | bytes accessed | tf_op | source)
XLA Modules:
  0.0 150.6 jit_solution(15972445708819946973)
XLA Ops:
  0.6 1.0 shard_map.105.refs_0_
  1.6 6.5 %collective-permute-start.1 = (bf16[32,16,128]{2,1,0:T(8,128)(2,1)S(1)}, bf16[32,16,128]{2,1,0:T(8,128)(2,1)S(1)}, u32[]{:S(2)}, u32[]{:S(2)}) collective-permute-start(bf16[32,16,128]{2,1,0:T(8,128)(2,1)S(1)} %shard_map.105.refs_0_), channel_id=1, source_target_pairs={{0,7},{1,0},{2,1},{3,2},{4,3},{5,4},{6,5},{7,6},{8,15},{9,8},{10,9... | collective-permute-start | bytes 393224 | tf_op jit(solution)/shard_map/ppermute | solution.py:152
  8.1 2.2 %collective-permute-done.1.refs_2_ = bf16[32,16,128]{2,1,0:T(8,128)(2,1)S(1)} collective-permute-done((bf16[32,16,128]{2,1,0:T(8,128)(2,1)S(1)}, bf16[32,16,128]{2,1,0:T(8,128)(2,1)S(1)}, u32[]{:S(2)}, u32[]{:S(2)}) %collective-permute-start.1) | collective-permute-done | bytes 131104 | tf_op jit(solution)/shard_map/ppermute | solution.py:152
  10.3 3.4 %collective-permute-start.3 = (bf16[32,16,128]{2,1,0:T(8,128)(2,1)S(1)}, bf16[32,16,128]{2,1,0:T(8,128)(2,1)S(1)}, u32[]{:S(2)}, u32[]{:S(2)}) collective-permute-start(bf16[32,16,128]{2,1,0:T(8,128)(2,1)S(1)} %collective-permute-done.1.refs_2_), channel_id=1, source_target_pairs={{0,7},{1,0},{2,1},{3,2},{4,3},{5,4},{6,5},{7,6},{8,15},{9,8},{10,9... | collective-permute-start | bytes 393224 | tf_op jit(solution)/shard_map/ppermute | solution.py:152
  13.7 1.6 %collective-permute-start.6 = (bf16[32,16,128]{2,1,0:T(8,128)(2,1)S(1)}, bf16[32,16,128]{2,1,0:T(8,128)(2,1)S(1)}, u32[]{:S(2)}, u32[]{:S(2)}) collective-permute-start(bf16[32,16,128]{2,1,0:T(8,128)(2,1)S(1)} %shard_map.105.refs_0_), channel_id=1, source_target_pairs={{0,4},{1,5},{2,6},{3,7},{4,0},{5,1},{6,2},{7,3},{8,12},{9,13},{10,... | collective-permute-start | bytes 393224 | tf_op jit(solution)/shard_map/ppermute | solution.py:152
  15.6 3.1 %collective-permute-start.5 = (bf16[32,16,128]{2,1,0:T(8,128)(2,1)S(1)}, bf16[32,16,128]{2,1,0:T(8,128)(2,1)S(1)}, u32[]{:S(2)}, u32[]{:S(2)}) collective-permute-start(bf16[32,16,128]{2,1,0:T(8,128)(2,1)S(1)} %collective-permute-done.3.refs_4_), channel_id=1, source_target_pairs={{0,7},{1,0},{2,1},{3,2},{4,3},{5,4},{6,5},{7,6},{8,15},{9,8},{10,9... | collective-permute-start | bytes 393224 | tf_op jit(solution)/shard_map/ppermute | solution.py:152
  18.7 4.5 %collective-permute-done.2.refs_3_ = bf16[32,16,128]{2,1,0:T(8,128)(2,1)S(1)} collective-permute-done((bf16[32,16,128]{2,1,0:T(8,128)(2,1)S(1)}, bf16[32,16,128]{2,1,0:T(8,128)(2,1)S(1)}, u32[]{:S(2)}, u32[]{:S(2)}) %collective-permute-start.2) | collective-permute-done | bytes 131104 | tf_op jit(solution)/shard_map/ppermute | solution.py:152
  23.2 0.8 copy.12
  24.1 4.3 %collective-permute-done.4.refs_5_ = bf16[32,16,128]{2,1,0:T(8,128)(2,1)S(1)} collective-permute-done((bf16[32,16,128]{2,1,0:T(8,128)(2,1)S(1)}, bf16[32,16,128]{2,1,0:T(8,128)(2,1)S(1)}, u32[]{:S(2)}, u32[]{:S(2)}) %collective-permute-start.4) | collective-permute-done | bytes 131104 | tf_op jit(solution)/shard_map/ppermute | solution.py:152
  28.4 2.0 %shard_map.106 = (bf16[256,16,128]{2,1,0:T(8,128)(2,1)}, bf16[256,16,128]{2,1,0:T(8,128)(2,1)}) custom-call(s32[1]{0:T(128)} %bitcast.place_ref, s32[256]{0:T(256)S(1)} %reshape.19.send_ref, bf16[32,16,128]{2,1,0:T(8,128)(2,1)S(1)} %shard_map.105.refs_0_, bf16[32,16,128]{2,1,0:T(8,128)(2,1)S(1)} %collective-permute-done.refs_1_, ...), custom_call_target="tpu_custom_call" | custom-call | bytes 3000000 | tf_op jit(solution)/shard_map/pallas_call | solution.py:36
  30.4 10.5 %all-to-all-start = ((bf16[256,16,128]{2,1,0:T(8,128)(2,1)}), bf16[256,16,128]{2,1,0:T(8,128)(2,1)S(1)}, u32[]{:S(2)}, u32[]{:S(2)}) async-start(bf16[256,16,128]{2,1,0:T(8,128)(2,1)} %get-tuple-element.23), calls=%async_computation | async-start | bytes 2097152 | tf_op jit(solution)/shard_map/all_to_all | solution.py:700
  41.7 3.1 %shard_map.104 = (s32[288]{0:T(512)S(1)}, s32[288]{0:T(512)S(1)}, s32[3]{0:T(128)S(1)}) custom-call(s32[256]{0:T(256)S(1)} %copy-done.8, s32[256]{0:T(256)S(1)} %copy-done.9, s32[1]{0:T(128)S(6)} %copy.14.live_ref), custom_call_target="tpu_custom_call" | custom-call | bytes 20000 | tf_op jit(solution)/shard_map/pallas_call | solution.py:36
  45.5 10.2 %shard_map.107 = (f32[33,16,128]{2,1,0:T(8,128)}, bf16[256,128,128]{2,1,0:T(8,128)(2,1)}, bf16[256,128,128]{2,1,0:T(8,128)(2,1)}) custom-call(s32[288]{0:T(512)} %copy-done.4, s32[288]{0:T(512)} %copy-done.2, s32[3]{0:T(128)} %copy-done.6, bf16[256,16,128]{2,1,0:T(8,128)(2,1)} %get-tuple-element.25.part_ref.basis_part_ref, bf16[256,128,128]{2,1,0:T(8,128)(2,1)} %coupling_ref.1), custom_call_target="tpu_custom_call" | custom-call | flops 134217728 | bytes 10000000 | tf_op jit(solution)/shard_map/pallas_call | solution.py:36
  55.7 2.2 %all-to-all-done.halo_ref = bf16[256,16,128]{2,1,0:T(8,128)(2,1)S(1)} async-done(((bf16[256,16,128]{2,1,0:T(8,128)(2,1)}), bf16[256,16,128]{2,1,0:T(8,128)(2,1)S(1)}, u32[]{:S(2)}, u32[]{:S(2)}) %all-to-all-start) | async-done | bytes 1048608 | tf_op jit(solution)/shard_map/all_to_all | solution.py:700
  57.9 4.3 %shard_map.108 = (f32[16,4096]{1,0:T(8,128)}, bf16[35,16,128]{2,1,0:T(8,128)(2,1)S(1)}, bf16[256,16,128]{2,1,0:T(8,128)(2,1)}) custom-call(s32[288]{0:T(512)S(1)} %copy-done.3, s32[3]{0:T(128)S(1)} %copy-done.7, bf16[256,16,128]{2,1,0:T(8,128)(2,1)S(1)} %all-to-all-done.halo_ref, bf16[256,128,128]{2,1,0:T(8,128)(2,1)} %get-tuple-element.26.weights_hbm, ...), custom_call_target="tpu_custom_call" | custom-call | flops 134217728 | bytes 8000000 | tf_op jit(solution)/shard_map/pallas_call | solution.py:36
  62.3 1.5 collective-permute-start.7
  63.8 4.3 %collective-permute-done.8.refs_2_ = bf16[35,16,128]{2,1,0:T(8,128)(2,1)S(1)} collective-permute-done((bf16[35,16,128]{2,1,0:T(8,128)(2,1)S(1)}, bf16[35,16,128]{2,1,0:T(8,128)(2,1)S(1)}, u32[]{:S(2)}, u32[]{:S(2)}) %collective-permute-start.8) | collective-permute-done | bytes 143392 | tf_op jit(solution)/shard_map/ppermute | solution.py:152
  68.1 1.0 collective-permute-start.10
  69.7 1.5 %collective-permute-start.13 = (bf16[35,16,128]{2,1,0:T(8,128)(2,1)S(1)}, bf16[35,16,128]{2,1,0:T(8,128)(2,1)S(1)}, u32[]{:S(2)}, u32[]{:S(2)}) collective-permute-start(bf16[35,16,128]{2,1,0:T(8,128)(2,1)S(1)} %get-tuple-element.28.refs_0_), channel_id=1, source_target_pairs={{0,4},{1,5},{2,6},{3,7},{4,0},{5,1},{6,2},{7,3},{8,12},{9,13},{10,... | collective-permute-start | bytes 430088 | tf_op jit(solution)/shard_map/ppermute | solution.py:152
  71.3 1.8 %collective-permute-done.10.refs_4_ = bf16[35,16,128]{2,1,0:T(8,128)(2,1)S(1)} collective-permute-done((bf16[35,16,128]{2,1,0:T(8,128)(2,1)S(1)}, bf16[35,16,128]{2,1,0:T(8,128)(2,1)S(1)}, u32[]{:S(2)}, u32[]{:S(2)}) %collective-permute-start.10) | collective-permute-done | bytes 143392 | tf_op jit(solution)/shard_map/ppermute | solution.py:152
  73.1 1.9 %collective-permute-start.12 = (bf16[35,16,128]{2,1,0:T(8,128)(2,1)S(1)}, bf16[35,16,128]{2,1,0:T(8,128)(2,1)S(1)}, u32[]{:S(2)}, u32[]{:S(2)}) collective-permute-start(bf16[35,16,128]{2,1,0:T(8,128)(2,1)S(1)} %collective-permute-done.10.refs_4_), channel_id=1, source_target_pairs={{0,7},{1,0},{2,1},{3,2},{4,3},{5,4},{6,5},{7,6},{8,15},{9,8},{10,9... | collective-permute-start | bytes 430088 | tf_op jit(solution)/shard_map/ppermute | solution.py:152
  75.0 2.9 %collective-permute-done.9.refs_3_ = bf16[35,16,128]{2,1,0:T(8,128)(2,1)S(1)} collective-permute-done((bf16[35,16,128]{2,1,0:T(8,128)(2,1)S(1)}, bf16[35,16,128]{2,1,0:T(8,128)(2,1)S(1)}, u32[]{:S(2)}, u32[]{:S(2)}) %collective-permute-start.9) | collective-permute-done | bytes 143392 | tf_op jit(solution)/shard_map/ppermute | solution.py:152
  78.1 3.8 %collective-permute-done.13.refs_7_ = bf16[35,16,128]{2,1,0:T(8,128)(2,1)S(1)} collective-permute-done((bf16[35,16,128]{2,1,0:T(8,128)(2,1)S(1)}, bf16[35,16,128]{2,1,0:T(8,128)(2,1)S(1)}, u32[]{:S(2)}, u32[]{:S(2)}) %collective-permute-start.13) | collective-permute-done | bytes 143392 | tf_op jit(solution)/shard_map/ppermute | solution.py:152
  81.9 1.9 %collective-permute-done.11.refs_5_ = bf16[35,16,128]{2,1,0:T(8,128)(2,1)S(1)} collective-permute-done((bf16[35,16,128]{2,1,0:T(8,128)(2,1)S(1)}, bf16[35,16,128]{2,1,0:T(8,128)(2,1)S(1)}, u32[]{:S(2)}, u32[]{:S(2)}) %collective-permute-start.11) | collective-permute-done | bytes 143392 | tf_op jit(solution)/shard_map/ppermute | solution.py:152
  83.8 2.5 %shard_map.109 = (bf16[256,16,128]{2,1,0:T(8,128)(2,1)}, bf16[288,16,128]{2,1,0:T(8,128)(2,1)}, bf16[16,128]{1,0:T(8,128)(2,1)}, f32[256,128]{1,0:T(8,128)}) custom-call(s32[1]{0:T(128)} %bitcast.place_ref, s32[256]{0:T(256)S(1)} %reshape.19.send_ref, bf16[128,4096]{1,0:T(8,128)(2,1)S(1)} %fusion.pick_ref, ...), custom_call_target="tpu_custom_call" | custom-call | bytes 3000000 | tf_op jit(solution)/shard_map/pallas_call | solution.py:36
  86.3 9.3 %all-to-all-start.1 = ((bf16[288,16,128]{2,1,0:T(8,128)(2,1)}), bf16[288,16,128]{2,1,0:T(8,128)(2,1)S(1)}, u32[]{:S(2)}, u32[]{:S(2)}) async-start(bf16[288,16,128]{2,1,0:T(8,128)(2,1)} %get-tuple-element.29), calls=%async_computation.1 | async-start | bytes 2359296 | tf_op jit(solution)/shard_map/all_to_all | solution.py:700
  95.6 5.4 %shard_map.110 = (f32[33,16,128]{2,1,0:T(8,128)}, f32[33,16,128]{2,1,0:T(8,128)}) custom-call(s32[288]{0:T(512)S(1)} %copy-done.5, s32[3]{0:T(128)S(1)} %copy-done.7, bf16[256,16,128]{2,1,0:T(8,128)(2,1)} %get-tuple-element.31.part_ref, bf16[16,128]{1,0:T(8,128)(2,1)} %get-tuple-element.32.table_ref, ...), custom_call_target="tpu_custom_call" | custom-call | flops 268435456 | bytes 10000000 | tf_op jit(solution)/shard_map/pallas_call | solution.py:36
  101.0 12.9 %all-to-all-done.1.halo_ref = bf16[288,16,128]{2,1,0:T(8,128)(2,1)S(1)} async-done(((bf16[288,16,128]{2,1,0:T(8,128)(2,1)}), bf16[288,16,128]{2,1,0:T(8,128)(2,1)S(1)}, u32[]{:S(2)}, u32[]{:S(2)}) %all-to-all-start.1) | async-done | bytes 1179680 | tf_op jit(solution)/shard_map/all_to_all | solution.py:700
  114.0 5.7 %shard_map.111 = (f32[96,4096]{1,0:T(8,128)S(1)}, f32[32,24,128]{2,1,0:T(8,128)S(1)}) custom-call(s32[288]{0:T(512)S(1)} %copy-done.3, s32[3]{0:T(128)S(1)} %copy-done.7, bf16[288,16,128]{2,1,0:T(8,128)(2,1)S(1)} %all-to-all-done.1.halo_ref, bf16[256,128,128]{2,1,0:T(8,128)(2,1)} %get-tuple-element.26.weights_hbm, ...), custom_call_target="tpu_custom_call" | custom-call | flops 134217728 | bytes 10000000 | tf_op jit(solution)/shard_map/pallas_call | solution.py:36
  119.6 14.0 %all_to_all.20.taken_ref = f32[32,24,128]{2,1,0:T(8,128)S(1)} all-to-all(f32[32,24,128]{2,1,0:T(8,128)S(1)} %get-tuple-element.38), channel_id=1, replica_groups=mesh['dom'=32,'row'=8] {'dom'}, dimensions={0} | all-to-all | bytes 786432 | tf_op jit(solution)/shard_map/all_to_all | solution.py:700
  133.7 12.4 %all_to_all.21.taken_ref = f32[8,24,128]{2,1,0:T(8,128)S(1)} all-to-all(f32[8,24,128]{2,1,0:T(8,128)S(1)} %shard_map.112), channel_id=1, replica_groups=mesh['dom'=32,'row'=8] {'row'}, dimensions={0} | all-to-all | bytes 196608 | tf_op jit(solution)/shard_map/all_to_all | solution.py:700
  146.1 4.4 %shard_map.113 = (f32[16,4096]{1,0:T(8,128)}, f32[16,4096]{1,0:T(8,128)}) custom-call(f32[8,24,128]{2,1,0:T(8,128)S(1)} %all_to_all.21.taken_ref, f32[96,4096]{1,0:T(8,128)S(1)} %get-tuple-element.39.stack_ref), custom_call_target="tpu_custom_call" | custom-call | flops 1000000 | bytes 3000000 | tf_op jit(solution)/shard_map/pallas_call | solution.py:36
  (43 shorter events, 2.1 us)
Async XLA Ops:
  0.6 41.1 %copy-start.9 = (s32[256]{0:T(256)S(1)}, s32[256]{0:T(256)}, u32[]{:S(2)}) copy-start(s32[256]{0:T(256)} %column_ref.1) | copy-start | bytes 3076
  0.6 41.0 %copy-start.8 = (s32[256]{0:T(256)S(1)}, s32[256]{0:T(256)}, u32[]{:S(2)}) copy-start(s32[256]{0:T(256)} %row_ref.1) | copy-start | bytes 3076
  1.6 8.6 %collective-permute-start.1 = (bf16[32,16,128]{2,1,0:T(8,128)(2,1)S(1)}, bf16[32,16,128]{2,1,0:T(8,128)(2,1)S(1)}, u32[]{:S(2)}, u32[]{:S(2)}) collective-permute-start(bf16[32,16,128]{2,1,0:T(8,128)(2,1)S(1)} %shard_map.105.refs_0_), channel_id=1, source_target_pairs={{0,7},{1,0},{2,1},{3,2},{4,3},{5,4},{6,5},{7,6},{8,15},{9,8},{10,9... | collective-permute-start | bytes 393224 | tf_op jit(solution)/shard_map/ppermute | solution.py:152
  8.1 5.6 %collective-permute-start = (bf16[32,16,128]{2,1,0:T(8,128)(2,1)S(1)}, bf16[32,16,128]{2,1,0:T(8,128)(2,1)S(1)}, u32[]{:S(2)}, u32[]{:S(2)}) collective-permute-start(bf16[32,16,128]{2,1,0:T(8,128)(2,1)S(1)} %shard_map.105.refs_0_), channel_id=1, source_target_pairs={{0,1},{1,2},{2,3},{3,4},{4,5},{5,6},{6,7},{7,0},{8,9},{9,10},{10,1... | collective-permute-start | bytes 393224 | tf_op jit(solution)/shard_map/ppermute | solution.py:152
  10.3 5.4 %collective-permute-start.3 = (bf16[32,16,128]{2,1,0:T(8,128)(2,1)S(1)}, bf16[32,16,128]{2,1,0:T(8,128)(2,1)S(1)}, u32[]{:S(2)}, u32[]{:S(2)}) collective-permute-start(bf16[32,16,128]{2,1,0:T(8,128)(2,1)S(1)} %collective-permute-done.1.refs_2_), channel_id=1, source_target_pairs={{0,7},{1,0},{2,1},{3,2},{4,3},{5,4},{6,5},{7,6},{8,15},{9,8},{10,9... | collective-permute-start | bytes 393224 | tf_op jit(solution)/shard_map/ppermute | solution.py:152
  13.7 9.5 %collective-permute-start.2 = (bf16[32,16,128]{2,1,0:T(8,128)(2,1)S(1)}, bf16[32,16,128]{2,1,0:T(8,128)(2,1)S(1)}, u32[]{:S(2)}, u32[]{:S(2)}) collective-permute-start(bf16[32,16,128]{2,1,0:T(8,128)(2,1)S(1)} %collective-permute-done.refs_1_), channel_id=1, source_target_pairs={{0,1},{1,2},{2,3},{3,4},{4,5},{5,6},{6,7},{7,0},{8,9},{9,10},{10,1... | collective-permute-start | bytes 393224 | tf_op jit(solution)/shard_map/ppermute | solution.py:152
  13.7 10.4 %collective-permute-start.6 = (bf16[32,16,128]{2,1,0:T(8,128)(2,1)S(1)}, bf16[32,16,128]{2,1,0:T(8,128)(2,1)S(1)}, u32[]{:S(2)}, u32[]{:S(2)}) collective-permute-start(bf16[32,16,128]{2,1,0:T(8,128)(2,1)S(1)} %shard_map.105.refs_0_), channel_id=1, source_target_pairs={{0,4},{1,5},{2,6},{3,7},{4,0},{5,1},{6,2},{7,3},{8,12},{9,13},{10,... | collective-permute-start | bytes 393224 | tf_op jit(solution)/shard_map/ppermute | solution.py:152
  15.6 8.4 %collective-permute-start.5 = (bf16[32,16,128]{2,1,0:T(8,128)(2,1)S(1)}, bf16[32,16,128]{2,1,0:T(8,128)(2,1)S(1)}, u32[]{:S(2)}, u32[]{:S(2)}) collective-permute-start(bf16[32,16,128]{2,1,0:T(8,128)(2,1)S(1)} %collective-permute-done.3.refs_4_), channel_id=1, source_target_pairs={{0,7},{1,0},{2,1},{3,2},{4,3},{5,4},{6,5},{7,6},{8,15},{9,8},{10,9... | collective-permute-start | bytes 393224 | tf_op jit(solution)/shard_map/ppermute | solution.py:152
  23.2 5.2 %collective-permute-start.4 = (bf16[32,16,128]{2,1,0:T(8,128)(2,1)S(1)}, bf16[32,16,128]{2,1,0:T(8,128)(2,1)S(1)}, u32[]{:S(2)}, u32[]{:S(2)}) collective-permute-start(bf16[32,16,128]{2,1,0:T(8,128)(2,1)S(1)} %collective-permute-done.2.refs_3_), channel_id=1, source_target_pairs={{0,1},{1,2},{2,3},{3,4},{4,5},{5,6},{6,7},{7,0},{8,9},{9,10},{10,1... | collective-permute-start | bytes 393224 | tf_op jit(solution)/shard_map/ppermute | solution.py:152
  30.4 27.4 %all-to-all-start = ((bf16[256,16,128]{2,1,0:T(8,128)(2,1)}), bf16[256,16,128]{2,1,0:T(8,128)(2,1)S(1)}, u32[]{:S(2)}, u32[]{:S(2)}) async-start(bf16[256,16,128]{2,1,0:T(8,128)(2,1)} %get-tuple-element.23), calls=%async_computation | async-start | bytes 2097152 | tf_op jit(solution)/shard_map/all_to_all | solution.py:700
  44.8 0.6 copy-start.2
  44.9 0.6 copy-start.4
  44.9 0.6 copy-start.6
  45.4 12.4 %copy-start = (f32[16,4096]{1,0:T(8,128)S(1)}, f32[16,4096]{1,0:T(8,128)}, u32[]{:S(2)}) copy-start(f32[16,4096]{1,0:T(8,128)} %basis_hbm.1) | copy-start | bytes 786436
  45.5 12.4 %copy-start.1 = (f32[4096]{0:T(1024)S(1)}, f32[4096]{0:T(1024)}, u32[]{:S(2)}) copy-start(f32[4096]{0:T(1024)} %param.12) | copy-start | bytes 49156
  45.5 12.4 %copy-start.3 = (s32[288]{0:T(512)S(1)}, s32[288]{0:T(512)}, u32[]{:S(2)}) copy-start(s32[288]{0:T(512)} %copy-done.2) | copy-start | bytes 3460
  45.5 12.4 %copy-start.7 = (s32[3]{0:T(128)S(1)}, s32[3]{0:T(128)}, u32[]{:S(2)}) copy-start(s32[3]{0:T(128)} %copy-done.6) | copy-start | bytes 40
  57.9 11.7 %copy-start.10 = (s32[1,32,8]{1,2,0:T(8,128)S(1)}, s32[1,32,8]{1,2,0:T(8,128)}, u32[]{:S(2)}) copy-start(s32[1,32,8]{1,2,0:T(8,128)} %param.16) | copy-start | bytes 3076
  62.2 5.8 %collective-permute-start.8 = (bf16[35,16,128]{2,1,0:T(8,128)(2,1)S(1)}, bf16[35,16,128]{2,1,0:T(8,128)(2,1)S(1)}, u32[]{:S(2)}, u32[]{:S(2)}) collective-permute-start(bf16[35,16,128]{2,1,0:T(8,128)(2,1)S(1)} %get-tuple-element.28.refs_0_), channel_id=1, source_target_pairs={{0,7},{1,0},{2,1},{3,2},{4,3},{5,4},{6,5},{7,6},{8,15},{9,8},{10,9... | collective-permute-start | bytes 430088 | tf_op jit(solution)/shard_map/ppermute | solution.py:152
  62.3 6.7 %collective-permute-start.7 = (bf16[35,16,128]{2,1,0:T(8,128)(2,1)S(1)}, bf16[35,16,128]{2,1,0:T(8,128)(2,1)S(1)}, u32[]{:S(2)}, u32[]{:S(2)}) collective-permute-start(bf16[35,16,128]{2,1,0:T(8,128)(2,1)S(1)} %get-tuple-element.28.refs_0_), channel_id=1, source_target_pairs={{0,1},{1,2},{2,3},{3,4},{4,5},{5,6},{6,7},{7,0},{8,9},{9,10},{10,1... | collective-permute-start | bytes 430088 | tf_op jit(solution)/shard_map/ppermute | solution.py:152
  68.1 5.0 %collective-permute-start.10 = (bf16[35,16,128]{2,1,0:T(8,128)(2,1)S(1)}, bf16[35,16,128]{2,1,0:T(8,128)(2,1)S(1)}, u32[]{:S(2)}, u32[]{:S(2)}) collective-permute-start(bf16[35,16,128]{2,1,0:T(8,128)(2,1)S(1)} %collective-permute-done.8.refs_2_), channel_id=1, source_target_pairs={{0,7},{1,0},{2,1},{3,2},{4,3},{5,4},{6,5},{7,6},{8,15},{9,8},{10,9... | collective-permute-start | bytes 430088 | tf_op jit(solution)/shard_map/ppermute | solution.py:152
  69.1 8.8 %collective-permute-start.9 = (bf16[35,16,128]{2,1,0:T(8,128)(2,1)S(1)}, bf16[35,16,128]{2,1,0:T(8,128)(2,1)S(1)}, u32[]{:S(2)}, u32[]{:S(2)}) collective-permute-start(bf16[35,16,128]{2,1,0:T(8,128)(2,1)S(1)} %collective-permute-done.7.refs_1_), channel_id=1, source_target_pairs={{0,1},{1,2},{2,3},{3,4},{4,5},{5,6},{6,7},{7,0},{8,9},{9,10},{10,1... | collective-permute-start | bytes 430088 | tf_op jit(solution)/shard_map/ppermute | solution.py:152
  69.7 12.2 %collective-permute-start.13 = (bf16[35,16,128]{2,1,0:T(8,128)(2,1)S(1)}, bf16[35,16,128]{2,1,0:T(8,128)(2,1)S(1)}, u32[]{:S(2)}, u32[]{:S(2)}) collective-permute-start(bf16[35,16,128]{2,1,0:T(8,128)(2,1)S(1)} %get-tuple-element.28.refs_0_), channel_id=1, source_target_pairs={{0,4},{1,5},{2,6},{3,7},{4,0},{5,1},{6,2},{7,3},{8,12},{9,13},{10,... | collective-permute-start | bytes 430088 | tf_op jit(solution)/shard_map/ppermute | solution.py:152
  73.1 8.9 %collective-permute-start.12 = (bf16[35,16,128]{2,1,0:T(8,128)(2,1)S(1)}, bf16[35,16,128]{2,1,0:T(8,128)(2,1)S(1)}, u32[]{:S(2)}, u32[]{:S(2)}) collective-permute-start(bf16[35,16,128]{2,1,0:T(8,128)(2,1)S(1)} %collective-permute-done.10.refs_4_), channel_id=1, source_target_pairs={{0,7},{1,0},{2,1},{3,2},{4,3},{5,4},{6,5},{7,6},{8,15},{9,8},{10,9... | collective-permute-start | bytes 430088 | tf_op jit(solution)/shard_map/ppermute | solution.py:152
  77.8 6.0 %collective-permute-start.11 = (bf16[35,16,128]{2,1,0:T(8,128)(2,1)S(1)}, bf16[35,16,128]{2,1,0:T(8,128)(2,1)S(1)}, u32[]{:S(2)}, u32[]{:S(2)}) collective-permute-start(bf16[35,16,128]{2,1,0:T(8,128)(2,1)S(1)} %collective-permute-done.9.refs_3_), channel_id=1, source_target_pairs={{0,1},{1,2},{2,3},{3,4},{4,5},{5,6},{6,7},{7,0},{8,9},{9,10},{10,1... | collective-permute-start | bytes 430088 | tf_op jit(solution)/shard_map/ppermute | solution.py:152
  78.1 17.6 %copy-start.5 = (s32[288]{0:T(512)S(1)}, s32[288]{0:T(512)}, u32[]{:S(2)}) copy-start(s32[288]{0:T(512)} %copy-done.4) | copy-start | bytes 3460
  86.3 27.7 %all-to-all-start.1 = ((bf16[288,16,128]{2,1,0:T(8,128)(2,1)}), bf16[288,16,128]{2,1,0:T(8,128)(2,1)S(1)}, u32[]{:S(2)}, u32[]{:S(2)}) async-start(bf16[288,16,128]{2,1,0:T(8,128)(2,1)} %get-tuple-element.29), calls=%async_computation.1 | async-start | bytes 2359296 | tf_op jit(solution)/shard_map/all_to_all | solution.py:700
